TPU v7x, 32 devices: a whole 2x2x4 slice. The times are simulated.
32 devices in a mesh: step: 8 (over z, y), space: 4 (over x, core).
Axes of the slice: x: 2, y: 2, z: 4, core: 2. Of those that a mesh axis runs over, the one named last changes fastest.
Arguments:
- guesses: float32 [8, 64, 4, 2560], P('step', None, None, 'space'), may hold values from -6 to 6
- noise: float32 [8, 64, 4, 2560], P('step', None, None, 'space'), may hold values from -6 to 6
- timesteps: int32 [8, 2], P('step'), may hold values from 1 to 999, as said below
- conv_first: bfloat16 [3, 256, 576], replicated, may hold values from -0.15625 to 0.15625
- conv_second: bfloat16 [3, 64, 2304], replicated, may hold values from -0.078125 to 0.078125
- time_weight: float32 [64, 256], replicated, may hold values from -0.75 to 0.75
Outputs:
- states: float32 [8, 64, 4, 2560], P('step', None, None, 'space')
- changes: float32 [8], P('step')
Inputs may be any that keep to these rules, and one draw needn't show every extreme that they name: Row k holds the timesteps before and after step k: the first entry of row 0 is 999, the second entry of the last row is 1, each row's second entry equals the next row's first, and the first entries fall strictly.
All inputs are finite; a program needn't handle non-finite values.
Results may differ from a plain program's by a relative error of at most 0.0019.
Values may be sent and summed in bfloat16 or wider, within the bound.
No kernel may reach another device: no remote copies, remote signals or barrier semaphores. Data moves between devices by JAX's collectives and lax.ppermute only.
A program may use at most 64 MiB of HBM per device.

v0:
```python
import math

import jax
import jax.numpy as jnp
from jax import lax
from jax.sharding import PartitionSpec as P

C = 64
COLS = 80


def padded_2(cells, sides, width):
    for axis, dim in sides:
        count = lax.axis_size(axis)
        ends = count - 1
        head = lax.slice_in_dim(cells, 0, width, axis=dim)
        tail = lax.slice_in_dim(cells, cells.shape[dim] - width, cells.shape[dim], axis=dim)
        cells = jnp.concatenate(
            [
                lax.ppermute(tail, axis, [(i, (i + 1) % count) for i in range(ends)]),
                cells,
                lax.ppermute(head, axis, [((i + 1) % count, i) for i in range(ends)]),
            ],
            axis=dim,
        )
    return cells


def plan(timestep):
    scaled = timestep.astype(jnp.float32) / 1000.0
    return -(0.1 * scaled + 9.95 * scaled * scaled)


def coefficients(timestep_pair):
    log_from = plan(timestep_pair[0])
    log_to = plan(timestep_pair[1])
    half_gap = 0.5 * (log_to - log_from)
    decay_gain = jnp.expm1(half_gap)
    remain_from = -jnp.expm1(log_from)
    remain_to = -jnp.expm1(log_to)
    ratio_term = -jnp.expm1(log_from - log_to)
    noise_gain = -jnp.exp(half_gap) * jnp.sqrt(remain_from) + remain_to * jnp.exp(
        -half_gap
    ) / jnp.sqrt(remain_from)
    spread_gain = jnp.sqrt(remain_to / remain_from * ratio_term)
    return (decay_gain, noise_gain, spread_gain)


def time_embed(timestep, time_weight):
    half_count = C // 2
    frequency = jnp.exp(-math.log(10000.0) * jnp.arange(half_count, dtype=jnp.float32) / half_count)
    angles = timestep.astype(jnp.float32) * frequency
    features = jnp.concatenate([jnp.sin(angles), jnp.cos(angles)])
    return jnp.dot(
        features, time_weight, preferred_element_type=jnp.float32, precision=lax.Precision.HIGHEST
    )


def convolve(padded, weight, rows_out):
    length = rows_out * COLS
    extended = jnp.pad(padded, ((0, 0), (0, 0), (1, 1)))
    column = jnp.arange(length) % COLS
    zero_value = jnp.zeros((), padded.dtype)
    pieces = []
    for row_shift in range(3):
        for col_shift in range(3):
            offset_start = 1 + row_shift * COLS + col_shift - 1
            window_piece = extended[:, :, offset_start : offset_start + length]
            if col_shift == 0:
                window_piece = jnp.where(column >= 1, window_piece, zero_value)
            if col_shift == 2:
                window_piece = jnp.where(column <= COLS - 2, window_piece, zero_value)
            pieces.append(window_piece)
    stacked = jnp.concatenate(pieces, axis=0)
    framed = jnp.pad(stacked, ((0, 0), (1, 1), (0, 0)))
    frame_count = padded.shape[1]
    result = jnp.einsum(
        "oj,jfp->ofp", weight[0], framed[:, 0:frame_count], preferred_element_type=jnp.float32
    )
    for frame_shift in range(1, 3):
        result = result + jnp.einsum(
            "oj,jfp->ofp",
            weight[frame_shift],
            framed[:, frame_shift : frame_shift + frame_count],
            preferred_element_type=jnp.float32,
        )
    return result


def earlier_total(column_block):
    step_count = column_block.shape[0]
    later_index = jnp.arange(step_count)[:, None]
    earlier_index = jnp.arange(step_count)[None, :]
    lower_table = (earlier_index < later_index).astype(jnp.float32)
    return jnp.einsum("kj,j...->k...", lower_table, column_block, precision=lax.Precision.HIGHEST)


def local(guesses, noise, timesteps, conv_first, conv_second, time_weight):
    step_index = lax.axis_index("step")
    row_block = lax.axis_index("space")
    space_count = lax.axis_size("space")
    start_latent = guesses[0]
    noise_step = noise[0]
    timestep_pair = timesteps[0]
    decay_gain, noise_gain, spread_gain = coefficients(timestep_pair)
    temb = time_embed(timestep_pair[0], time_weight)
    row_count = start_latent.shape[2] // COLS
    is_anchor = step_index == 0

    def denoise(latent):
        rounded = latent.astype(jnp.bfloat16)
        deep_padded = padded_2(rounded, (("space", 2),), 2 * COLS)
        preact = convolve(deep_padded, conv_first, row_count + 2) + temb[:, None, None]
        global_rows = row_block * row_count - 1 + jnp.arange(row_count + 2)
        inside_rows = (global_rows >= 0) & (global_rows < row_count * space_count)
        inside_mask = jnp.repeat(inside_rows, COLS)
        hidden = jnp.where(inside_mask, jax.nn.silu(preact), 0.0).astype(jnp.bfloat16)
        return convolve(hidden, conv_second, row_count)

    def prefix(scan_term):
        before_sum = earlier_total(
            lax.all_to_all(scan_term[None], "step", split_axis=1, concat_axis=0, tiled=True)
        )
        return lax.all_to_all(before_sum, "step", split_axis=0, concat_axis=1, tiled=True)[0]

    def picard_sweep(latent):
        drift = decay_gain * latent + noise_gain * denoise(latent) + spread_gain * noise_step
        scan_term = drift + jnp.where(is_anchor, latent, 0.0)
        before_sum = prefix(scan_term)
        advanced = jnp.where(is_anchor, latent, before_sum)
        return (advanced, advanced + drift)

    entering_one, reached_one = picard_sweep(start_latent)
    entering_two, reached_two = picard_sweep(entering_one)
    difference = reached_two - reached_one
    local_sum = jnp.sum(difference * difference)
    norm_total = lax.psum(local_sum, "space")
    cell_count = difference.shape[0] * difference.shape[1] * difference.shape[2] * space_count
    changes = jnp.sqrt(norm_total / cell_count).reshape(1)
    return (reached_two[None], changes)


def solution(mesh):
    in_specs = (
        P("step", None, None, "space"),
        P("step", None, None, "space"),
        P("step", None),
        P(),
        P(),
        P(),
    )
    out_specs = (P("step", None, None, "space"), P("step"))
    return jax.shard_map(local, mesh=mesh, in_specs=in_specs, out_specs=out_specs, check_vma=False)
```

profile of v0, /device:TPU:0, one launch (start us, length us, event | category | flops | bytes accessed | tf_op | source)
XLA Modules:
  0.0 157.5 jit_solution(16990002324655541962)
XLA Ops:
  0.6 1.2 copy.140
  1.9 2.4 %collective-permute-start = (bf16[64,4,160]{2,0,1:T(8,128)(2,1)S(1)}, bf16[64,4,160]{2,0,1:T(8,128)(2,1)S(1)}, u32[]{:S(2)}, u32[]{:S(2)}) collective-permute-start(bf16[64,4,160]{2,0,1:T(8,128)(2,1)S(1)} %get-tuple-element.16), channel_id=1, source_target_pairs={{0,1},{1,2},{2,3},{4,5},{5,6},{6,7},{8,9},{9,10},{10,11},{12,13},{... | collective-permute-start | bytes 245768 | tf_op jit(solution)/shard_map/ppermute | solution.py:20
  4.3 1.3 collective-permute-start.1
  5.6 1.3 fusion.110
  9.2 0.4 collective-permute-done.1
  9.6 0.3 pad_maximum_fusion
  10.6 0.2 fusion.55
  11.3 0.2 fusion.53
  11.8 1.5 fusion.73
  13.3 1.5 fusion.69
  14.8 1.9 %fusion.8 = bf16[256,4,800]{0,2,1:T(8,128)(2,1)S(1)} fusion(f32[4,800,256]{2,1,0:T(8,128)S(1)} %fusion.73, f32[4,800,256]{2,1,0:T(8,128)S(1)} %fusion.69, bf16[576,4,800]{2,0,1:T(8,128)(2,1)S(1)} %fusion.44, f32[256]{0:T(256)S(1)} %bitcast.145, pred[800]{0:T(1024)(128)(4,1)S(1)} %reshape.40, bf16[3,256,576]{1,2,0:T(8,128)(2,1)S(1)} %copy-done.4), kind=kOutput, calls=%fused_computation.12 | convolution fusion | flops 715161600 | bytes 12617728 | tf_op jit(solution)/shard_map/oj,jfp->ofp/dot_general | solution.py:81
  16.7 0.4 fusion.11
  17.2 0.4 fusion.25
  17.7 0.4 fusion.24
  18.2 0.4 fusion.23
  18.7 0.4 fusion.22
  19.2 0.4 fusion.13
  19.8 3.6 %fusion.61 = f32[4,640,64]{1,2,0:T(8,128)S(1)} fusion(bf16[2304,4,640]{0,2,1:T(8,128)(2,1)S(1)} %fusion.13, bf16[3,64,2304]{2,1,0:T(8,128)(2,1)S(1)} %copy-done.3), kind=kOutput, calls=%fused_computation.115 | convolution fusion | flops 754974720 | bytes 12746752 | tf_op jit(solution)/shard_map/oj,jfp->ofp/dot_general | solution.py:81
  23.5 3.2 %convolution_add_fusion.3 = f32[4,640,64]{1,2,0:T(8,128)S(1)} fusion(f32[4,640,64]{1,2,0:T(8,128)S(1)} %fusion.61, bf16[2304,4,640]{0,2,1:T(8,128)(2,1)S(1)} %fusion.13, bf16[3,64,2304]{2,1,0:T(8,128)(2,1)S(1)} %copy-done.3), kind=kOutput, calls=%fused_computation.59 | convolution fusion | flops 566394880 | bytes 13402112 | tf_op jit(solution)/shard_map/oj,jfp->ofp/dot_general | solution.py:77
  26.7 2.9 %fusion.33 = f32[64,4,640]{2,0,1:T(8,128)S(1)} fusion(f32[4,640,64]{1,2,0:T(8,128)S(1)} %convolution_add_fusion.3, bf16[2304,4,640]{0,2,1:T(8,128)(2,1)S(1)} %fusion.13, f32[1,64,4,640]{3,2,1,0:T(4,128)S(1)} %copy-done.5, f32[1,64,4,640]{3,2,1,0:T(4,128)S(1)} %copy-done.2, f32[]{:T(128)S(6)} %sqrt.11, f32[]{:T(128)S(6)} %add.185, f32[]{:T(128)S(6)} %expm1.12, ...), kind=kOutput, calls=%fused_computation.58 | convolution fusion | flops 567214080 | bytes 14712844 | tf_op jit(solution)/shard_map/oj,jfp->ofp/dot_general | solution.py:81
  29.8 0.4 copy.85
  30.2 23.3 %all_to_all.42 = f32[1,64,4,640]{3,2,0,1:T(4,128)S(1)} all-to-all(f32[1,64,4,640]{3,2,0,1:T(4,128)S(1)} %copy.85), channel_id=1, replica_groups=mesh['step'=8,'space'=4] {'step'}, dimensions={1} | all-to-all | bytes 1310720 | tf_op jit(solution)/shard_map/all_to_all | solution.py:122
  53.5 0.8 fusion.37
  54.5 22.5 %all_to_all.43 = f32[8,8,4,640]{3,2,1,0:T(4,128)S(1)} all-to-all(f32[8,8,4,640]{3,2,1,0:T(4,128)S(1)} %copy.88), channel_id=1, replica_groups=mesh['step'=8,'space'=4] {'step'}, dimensions={0} | all-to-all | bytes 1310720 | tf_op jit(solution)/shard_map/all_to_all | solution.py:124
  77.2 1.3 collective-permute-start.2
  78.5 1.3 collective-permute-start.3
  79.8 3.3 %collective-permute-done.3 = bf16[64,4,160]{2,0,1:T(8,128)(2,1)S(1)} collective-permute-done((bf16[64,4,160]{2,0,1:T(8,128)(2,1)S(1)}, bf16[64,4,160]{2,0,1:T(8,128)(2,1)S(1)}, u32[]{:S(2)}, u32[]{:S(2)}) %collective-permute-start.3) | collective-permute-done | bytes 81952 | tf_op jit(solution)/shard_map/ppermute | solution.py:22
  83.1 0.3 pad_maximum_fusion.1
  84.7 0.2 fusion.49
  85.2 1.5 fusion.71
  86.7 1.5 fusion.67
  88.2 1.9 %fusion.9 = bf16[256,4,800]{0,2,1:T(8,128)(2,1)S(1)} fusion(f32[4,800,256]{2,1,0:T(8,128)S(1)} %fusion.71, f32[4,800,256]{2,1,0:T(8,128)S(1)} %fusion.67, bf16[576,4,800]{2,0,1:T(8,128)(2,1)S(1)} %fusion.48, f32[256]{0:T(256)S(1)} %bitcast.146, pred[800]{0:T(1024)(128)(4,1)S(1)} %reshape.40, bf16[3,256,576]{1,2,0:T(8,128)(2,1)S(1)} %copy-done.4), kind=kOutput, calls=%fused_computation.13 | convolution fusion | flops 715161600 | bytes 12617728 | tf_op jit(solution)/shard_map/oj,jfp->ofp/dot_general | solution.py:81
  90.1 0.4 fusion.15
  90.7 0.4 fusion.21
  91.1 0.4 fusion.20
  91.6 0.4 fusion.19
  92.1 0.4 fusion.18
  92.6 0.4 fusion.17
  93.0 3.6 %fusion.59 = f32[4,640,64]{1,2,0:T(8,128)S(1)} fusion(bf16[2304,4,640]{0,2,1:T(8,128)(2,1)S(1)} %fusion.17, bf16[3,64,2304]{2,1,0:T(8,128)(2,1)S(1)} %copy-done.3), kind=kOutput, calls=%fused_computation.113 | convolution fusion | flops 754974720 | bytes 12746752 | tf_op jit(solution)/shard_map/oj,jfp->ofp/dot_general | solution.py:81
  96.7 3.3 %convolution_add_fusion.1 = f32[4,640,64]{1,2,0:T(8,128)S(1)} fusion(f32[4,640,64]{1,2,0:T(8,128)S(1)} %fusion.59, bf16[2304,4,640]{0,2,1:T(8,128)(2,1)S(1)} %fusion.17, bf16[3,64,2304]{2,1,0:T(8,128)(2,1)S(1)} %copy-done.3), kind=kOutput, calls=%fused_computation.53 | convolution fusion | flops 566394880 | bytes 13402112 | tf_op jit(solution)/shard_map/oj,jfp->ofp/dot_general | solution.py:77
  100.0 2.9 %fusion.29 = f32[64,4,640]{2,0,1:T(8,128)S(1)} fusion(f32[4,640,64]{1,2,0:T(8,128)S(1)} %convolution_add_fusion.1, bf16[2304,4,640]{0,2,1:T(8,128)(2,1)S(1)} %fusion.17, f32[64,4,640]{2,0,1:T(8,128)S(1)} %get-tuple-element.11, f32[1,64,4,640]{3,2,1,0:T(4,128)S(1)} %copy-done.5, f32[]{:T(128)S(6)} %sqrt.11, f32[]{:T(128)S(6)} %add.185, f32[]{:T(128)S(6)} %expm1.12, ...), kind=kOutput, calls=%fused_computation.52 | convolution fusion | flops 567214080 | bytes 14712844 | tf_op jit(solution)/shard_map/oj,jfp->ofp/dot_general | solution.py:81
  103.0 0.4 copy.96
  103.5 20.1 %all_to_all.44 = f32[1,64,4,640]{3,2,0,1:T(4,128)S(1)} all-to-all(f32[1,64,4,640]{3,2,0,1:T(4,128)S(1)} %copy.96), channel_id=1, replica_groups=mesh['step'=8,'space'=4] {'step'}, dimensions={1} | all-to-all | bytes 1310720 | tf_op jit(solution)/shard_map/all_to_all | solution.py:122
  123.6 0.8 fusion.35
  124.6 22.7 %all_to_all.45 = f32[8,8,4,640]{3,2,1,0:T(4,128)S(1)} all-to-all(f32[8,8,4,640]{3,2,1,0:T(4,128)S(1)} %copy.99), channel_id=1, replica_groups=mesh['step'=8,'space'=4] {'step'}, dimensions={0} | all-to-all | bytes 1310720 | tf_op jit(solution)/shard_map/all_to_all | solution.py:124
  147.2 0.8 multiply_reduce_fusion
  148.1 6.4 %psum.7 = f32[]{:T(128)} all-reduce(f32[]{:T(128)} %get-tuple-element.12), channel_id=1, replica_groups=mesh['step'=8,'space'=4] {'space'}, use_global_device_ids=true, to_apply=%region_1.2 | all-reduce | flops 1 | bytes 8 | tf_op jit(solution)/shard_map/psum | solution.py:137
  155.1 1.3 copy.101
  (51 shorter events, 5.0 us)
Async XLA Ops:
  0.6 8.3 %copy-start = (f32[64,256]{1,0:T(8,128)S(1)}, f32[64,256]{1,0:T(8,128)}, u32[]{:S(2)}) copy-start(f32[64,256]{1,0:T(8,128)} %param.11) | copy-start | bytes 196612
  1.9 7.3 %collective-permute-start = (bf16[64,4,160]{2,0,1:T(8,128)(2,1)S(1)}, bf16[64,4,160]{2,0,1:T(8,128)(2,1)S(1)}, u32[]{:S(2)}, u32[]{:S(2)}) collective-permute-start(bf16[64,4,160]{2,0,1:T(8,128)(2,1)S(1)} %get-tuple-element.16), channel_id=1, source_target_pairs={{0,1},{1,2},{2,3},{4,5},{5,6},{6,7},{8,9},{9,10},{10,11},{12,13},{... | collective-permute-start | bytes 245768 | tf_op jit(solution)/shard_map/ppermute | solution.py:20
  4.3 5.3 %collective-permute-start.1 = (bf16[64,4,160]{2,0,1:T(8,128)(2,1)S(1)}, bf16[64,4,160]{2,0,1:T(8,128)(2,1)S(1)}, u32[]{:S(2)}, u32[]{:S(2)}) collective-permute-start(bf16[64,4,160]{2,0,1:T(8,128)(2,1)S(1)} %get-tuple-element.17), channel_id=1, source_target_pairs={{1,0},{2,1},{3,2},{5,4},{6,5},{7,6},{9,8},{10,9},{11,10},{13,12},{... | collective-permute-start | bytes 245768 | tf_op jit(solution)/shard_map/ppermute | solution.py:22
  9.9 1.9 %copy-start.4 = (bf16[3,256,576]{1,2,0:T(8,128)(2,1)S(1)}, bf16[3,256,576]{1,2,0:T(8,128)(2,1)}, u32[]{:S(2)}) copy-start(bf16[3,256,576]{1,2,0:T(8,128)(2,1)} %param.9) | copy-start | bytes 2654212
  18.6 1.2 copy-start.3
  23.5 3.3 %copy-start.2 = (f32[1,64,4,640]{3,2,1,0:T(4,128)S(1)}, f32[1,64,4,640]{3,2,1,0:T(4,128)}, u32[]{:S(2)}) copy-start(f32[1,64,4,640]{3,2,1,0:T(4,128)} %param.6) | copy-start | bytes 1966084
  23.5 3.3 %copy-start.5 = (f32[1,64,4,640]{3,2,1,0:T(4,128)S(1)}, f32[1,64,4,640]{3,2,1,0:T(4,128)}, u32[]{:S(2)}) copy-start(f32[1,64,4,640]{3,2,1,0:T(4,128)} %param.7) | copy-start | bytes 1966084
  77.2 2.6 %collective-permute-start.2 = (bf16[64,4,160]{2,0,1:T(8,128)(2,1)S(1)}, bf16[64,4,160]{2,0,1:T(8,128)(2,1)S(1)}, u32[]{:S(2)}, u32[]{:S(2)}) collective-permute-start(bf16[64,4,160]{2,0,1:T(8,128)(2,1)S(1)} %get-tuple-element.14), channel_id=1, source_target_pairs={{0,1},{1,2},{2,3},{4,5},{5,6},{6,7},{8,9},{9,10},{10,11},{12,13},{... | collective-permute-start | bytes 245768 | tf_op jit(solution)/shard_map/ppermute | solution.py:20
  78.5 4.6 %collective-permute-start.3 = (bf16[64,4,160]{2,0,1:T(8,128)(2,1)S(1)}, bf16[64,4,160]{2,0,1:T(8,128)(2,1)S(1)}, u32[]{:S(2)}, u32[]{:S(2)}) collective-permute-start(bf16[64,4,160]{2,0,1:T(8,128)(2,1)S(1)} %get-tuple-element.15), channel_id=1, source_target_pairs={{1,0},{2,1},{3,2},{5,4},{6,5},{7,6},{9,8},{10,9},{11,10},{13,12},{... | collective-permute-start | bytes 245768 | tf_op jit(solution)/shard_map/ppermute | solution.py:22
  123.6 32.8 %copy-start.1 = (f32[64,256]{1,0:T(8,128)S(1)}, f32[64,256]{1,0:T(8,128)}, u32[]{:S(2)}) copy-start(f32[64,256]{1,0:T(8,128)} %param.11) | copy-start | bytes 196612
where the time goes:
time: 158 us
  blocking collectives  95 us (60%)
  matrix products  31.2 us (20%)
  other arithmetic  10.1 us (6%)
  local copies, waits for them, and re-layouts  6.46 us (4%)
  starting transfers between devices  6.25 us (4%)
  between operations  4.74 us (3%)
  waiting for transfers between devices  3.72 us (2%)
    all_to_all x2, blocking collectives, prefix(): lax.all_to_all(before_sum, 'step', split_axis=0, concat_axis=1, tiled=True)  45.2 us
    all_to_all x2, blocking collectives, prefix(): lax.all_to_all(scan_term[None], 'step', split_axis=1, concat_axis=0, tile...  43.5 us
    dot_general x8, matrix products, convolve(): jnp.einsum('oj,jfp->ofp', weight[frame_shift], framed[:, frame_shift:fram...  20 us
    dot_general x4, matrix products, convolve(): jnp.einsum('oj,jfp->ofp', weight[0], framed[:, 0:frame_count], preferred_...  9.47 us
    unnamed x24, other arithmetic  7.08 us
    psum x1, blocking collectives, local(): norm_total = lax.psum(local_sum, 'space')  6.36 us
    ppermute x2, waiting for transfers between devices, padded_2(): lax.ppermute(head, axis, [((i + 1) % count, i) for i in range(ends)])  3.72 us
    ppermute x2, starting transfers between devices, padded_2(): lax.ppermute(tail, axis, [(i, (i + 1) % count) for i in range(ends)])  3.66 us
  transfers between devices with their start and end apart: 4, of which 2 were waited for; matrix products, arithmetic and copies ran while one was open for 1% of the time, Pallas kernels for 0%

commit v1 on v0

v1 whole, which is shorter than its diff:
```python
import math

import jax
import jax.numpy as jnp
from jax import lax
from jax.experimental import pallas as pl
from jax.experimental.pallas import tpu as pltpu
from jax.sharding import PartitionSpec as P

C = 64
COLS = 80
LANES = 256
NT = (((1,), (1,)), ((), ()))


def plan(timestep):
    scaled = timestep.astype(jnp.float32) / 1000.0
    return -(0.1 * scaled + 9.95 * scaled * scaled)


def coefficients(timestep_pair):
    log_from = plan(timestep_pair[0])
    log_to = plan(timestep_pair[1])
    half_gap = 0.5 * (log_to - log_from)
    decay_gain = jnp.expm1(half_gap)
    remain_from = -jnp.expm1(log_from)
    remain_to = -jnp.expm1(log_to)
    ratio_term = -jnp.expm1(log_from - log_to)
    noise_gain = -jnp.exp(half_gap) * jnp.sqrt(remain_from) + remain_to * jnp.exp(
        -half_gap
    ) / jnp.sqrt(remain_from)
    spread_gain = jnp.sqrt(remain_to / remain_from * ratio_term)
    return (decay_gain, noise_gain, spread_gain)


def time_embed(timestep, time_weight):
    half_count = C // 2
    frequency = jnp.exp(-math.log(10000.0) * jnp.arange(half_count, dtype=jnp.float32) / half_count)
    angles = timestep.astype(jnp.float32) * frequency
    features = jnp.concatenate([jnp.sin(angles), jnp.cos(angles)])
    return jnp.dot(
        features, time_weight, preferred_element_type=jnp.float32, precision=lax.Precision.HIGHEST
    )


def denoise_kernel(scalars, latent, inner, outer, noise, first, second, temb, drift, largest, shifted, hidden):
    channels, frames, length = latent.shape
    count = temb.shape[1]
    edge = 2 * COLS
    extended = length + 2 * COLS
    chunk = extended // 2
    keep, gain, spread = scalars[0], scalars[1], scalars[2]
    top, bottom = scalars[3], scalars[4]
    even = scalars[5] > 0.5

    def spread_columns(values, at, frame):
        width = values.shape[1]
        column = lax.broadcasted_iota(jnp.int32, (1, width), 1) % COLS
        before = jnp.where(column >= 1, pltpu.roll(values, 1, 1), 0.0)
        after = jnp.where(column <= COLS - 2, pltpu.roll(values, width - 1, 1), 0.0)
        stack = jnp.concatenate([before, values, after, jnp.zeros_like(values)], axis=0)
        shifted[frame, pl.ds(at, width), :] = stack.astype(jnp.bfloat16).T

    def taps_of(frame):
        return [(a, b) for a in range(3) if 0 <= frame + a - 1 < frames for b in range(3)]

    def first_conv(frame):
        taps = taps_of(frame)
        weights = jnp.concatenate([first[a, :, b * LANES : (b + 1) * LANES] for a, b in taps], axis=1)
        for start in range(0, extended, chunk):
            cells = jnp.concatenate(
                [shifted[frame + a - 1, pl.ds(b * COLS + start, chunk), :] for a, b in taps], axis=1
            )
            value = lax.dot_general(cells, weights, NT, preferred_element_type=jnp.float32) + temb[...]
            active = value / (1.0 + jnp.exp(-value))
            place = start + lax.broadcasted_iota(jnp.int32, (chunk, 1), 0)
            inside = jnp.where(place < COLS, 1.0 - top, jnp.where(place >= extended - COLS, 1.0 - bottom, 1.0))
            active = jnp.where(inside > 0.5, active, 0.0)
            hidden[frame, pl.ds(start, chunk), :] = active.astype(jnp.bfloat16)

    def second_conv(frame):
        taps = taps_of(frame)
        cells = jnp.concatenate([hidden[frame + a - 1, pl.ds(b * COLS, length), :] for a, b in taps], axis=1)
        weights = jnp.concatenate(
            [
                jnp.concatenate(
                    [second[a, :, (b * 3 + e) * count : (b * 3 + e + 1) * count] for e in range(3)], axis=0
                )
                for a, b in taps
            ],
            axis=1,
        )
        parts = lax.dot_general(cells, weights, NT, preferred_element_type=jnp.float32).T
        column = lax.broadcasted_iota(jnp.int32, (1, length), 1) % COLS
        before = jnp.where(column >= 1, pltpu.roll(parts[:channels], 1, 1), 0.0)
        after = jnp.where(
            column <= COLS - 2, pltpu.roll(parts[2 * channels : 3 * channels], length - 1, 1), 0.0
        )
        predicted = before + parts[channels : 2 * channels] + after
        result = keep * latent[:, frame, :] + gain * predicted + spread * noise[:, frame, :]
        drift[:, frame, :] = result
        return jnp.max(jnp.abs(result), axis=0, keepdims=True)

    for frame in range(frames):
        near = inner[:, frame, :].astype(jnp.float32)
        far = outer[:, frame, :].astype(jnp.float32)
        spread_columns(jnp.where(even, far, near), 0, frame)
        spread_columns(latent[:, frame, :], edge, frame)
        spread_columns(jnp.where(even, near, far), edge + length, frame)
    peaks = []
    for frame in range(frames):
        first_conv(frame)
        if frame >= 1:
            peaks.append(second_conv(frame - 1))
    peaks.append(second_conv(frames - 1))
    peak = peaks[0]
    for other in peaks[1:]:
        peak = jnp.maximum(peak, other)
    largest[0] = jnp.max(peak)


def denoise(scalars, latent, inner, outer, noise, first, second, temb):
    channels, frames, length = latent.shape
    whole = pl.BlockSpec(memory_space=pltpu.VMEM)
    words = pl.BlockSpec(memory_space=pltpu.SMEM)
    return pl.pallas_call(
        denoise_kernel,
        out_shape=(
            jax.ShapeDtypeStruct(latent.shape, jnp.float32),
            jax.ShapeDtypeStruct((1,), jnp.float32),
        ),
        in_specs=[words] + [whole] * 7,
        out_specs=(whole, words),
        scratch_shapes=[
            pltpu.VMEM((frames, length + 4 * COLS, LANES), jnp.bfloat16),
            pltpu.VMEM((frames, length + 2 * COLS, temb.shape[1]), jnp.bfloat16),
        ],
        compiler_params=pltpu.CompilerParams(vmem_limit_bytes=24 * 2**20),
        cost_estimate=pl.CostEstimate(
            flops=5_000_000_000, bytes_accessed=4_000_000, transcendentals=1_000_000
        ),
        name="denoise",
    )(scalars, latent, inner, outer, noise, first, second, temb)


def exponent_of(largest):
    return jnp.clip(jnp.ceil(jnp.log2(largest)) + 1.0, -100.0, 126.0)


def send(values, exponent, pairs):
    small = (values * jnp.exp2(14.0 - exponent)).astype(jnp.float16)
    mark = jnp.full((1,) + values.shape[1:], exponent, jnp.float16)
    return lax.ppermute(jnp.concatenate([small, mark], axis=0), "step", pairs)


def receive(message):
    exponent = message[-1, 0, 0].astype(jnp.float32)
    return message[:-1].astype(jnp.float32) * jnp.exp2(exponent - 14.0), exponent


def prefix(term, largest, step_index):
    steps = lax.axis_size("step")
    half = term.shape[0] // 2
    odd = step_index % 2
    swap = [(i, i ^ 1) for i in range(steps)]
    exponent = exponent_of(largest)
    mine = lax.dynamic_slice_in_dim(term, odd * half, half, 0)
    yours = lax.dynamic_slice_in_dim(term, (1 - odd) * half, half, 0)
    partner, partner_exponent = receive(send(yours, exponent, swap))
    total = mine + partner
    reach = jnp.maximum(exponent, partner_exponent) + 1.0
    before = jnp.zeros_like(total)
    distance = 2
    while distance < steps:
        pairs = [(i, i + distance) for i in range(steps - distance)]
        got, got_exponent = receive(send(total, reach, pairs))
        total = total + got
        before = before + got
        reach = jnp.maximum(reach, got_exponent) + 1.0
        distance *= 2
    keep = before + jnp.where(odd == 1, partner, 0.0)
    give = before + jnp.where(odd == 0, mine, 0.0)
    other, _ = receive(send(give, reach, swap))
    low = jnp.where(odd == 0, keep, other)
    high = jnp.where(odd == 0, other, keep)
    return jnp.concatenate([low, high], axis=0)


def local(guesses, noise, timesteps, conv_first, conv_second, time_weight):
    step_index = lax.axis_index("step")
    row_block = lax.axis_index("space")
    space = lax.axis_size("space")
    start_latent = guesses[0]
    noise_step = noise[0]
    timestep_pair = timesteps[0]
    is_anchor = step_index == 0
    even = row_block % 2 == 0
    inner_pairs = [pair for i in range(0, space - 1, 2) for pair in ((i, i + 1), (i + 1, i))]
    outer_pairs = [pair for i in range(1, space - 1, 2) for pair in ((i, i + 1), (i + 1, i))]

    decay_gain, noise_gain, spread_gain = coefficients(timestep_pair)
    temb = time_embed(timestep_pair[0], time_weight).reshape(1, -1)
    scalars = jnp.stack(
        [
            decay_gain,
            noise_gain,
            spread_gain,
            (row_block == 0).astype(jnp.float32),
            (row_block == space - 1).astype(jnp.float32),
            even.astype(jnp.float32),
        ]
    )
    offsets, count, _ = conv_first.shape
    first = jnp.pad(
        conv_first.reshape(offsets, count, 3, 3 * C), ((0, 0), (0, 0), (0, 0), (0, LANES - 3 * C))
    ).reshape(offsets, count, 3 * LANES)

    def sweep(latent):
        edge = 2 * COLS
        head = latent[:, :, :edge].astype(jnp.bfloat16)
        tail = latent[:, :, latent.shape[2] - edge :].astype(jnp.bfloat16)
        inner = lax.ppermute(jnp.where(even, tail, head), "space", inner_pairs)
        outer = lax.ppermute(jnp.where(even, head, tail), "space", outer_pairs)
        drift, largest = denoise(scalars, latent, inner, outer, noise_step, first, conv_second, temb)
        term = drift + jnp.where(is_anchor, latent, 0.0)
        before = prefix(term, largest[0] + 8.0, step_index)
        entering = jnp.where(is_anchor, latent, before)
        return entering, entering + drift

    entering_one, reached_one = sweep(start_latent)
    _, reached_two = sweep(entering_one)
    difference = reached_two - reached_one
    norm_total = lax.psum(jnp.sum(difference * difference), "space")
    cell_count = difference.shape[0] * difference.shape[1] * difference.shape[2] * space
    changes = jnp.sqrt(norm_total / cell_count).reshape(1)
    return (reached_two[None], changes)


def solution(mesh):
    in_specs = (
        P("step", None, None, "space"),
        P("step", None, None, "space"),
        P("step", None),
        P(),
        P(),
        P(),
    )
    out_specs = (P("step", None, None, "space"), P("step"))
    return jax.shard_map(local, mesh=mesh, in_specs=in_specs, out_specs=out_specs, check_vma=False)
```

time: 158 us -> 130 us (0.82)
  the two profiles are of different devices: /device:TPU:0 before, /device:TPU:28 now
where the time goes in v1:
time: 130 us; the launch traced here: 129 us
  waiting for transfers between devices  56 us (43%)
  Pallas kernels  18 us (14%)
  starting transfers between devices  15.6 us (12%)
  local copies, waits for them, and re-layouts  12.2 us (9%)
  between operations  11.9 us (9%)
  other arithmetic  8.97 us (7%)
  blocking collectives  6.36 us (5%)
    ppermute x8, waiting for transfers between devices, send(): return lax.ppermute(jnp.concatenate([small, mark], axis=0), 'step', pairs)  55.1 us
    pallas_call x2, Pallas kernels, denoise(): pl.pallas_call(denoise_kernel, out_shape=(jax.ShapeDtypeStruct(latent.sha...  18 us
    ppermute x8, starting transfers between devices, send(): return lax.ppermute(jnp.concatenate([small, mark], axis=0), 'step', pairs)  7.35 us
    ppermute x2, starting transfers between devices, sweep(): inner = lax.ppermute(jnp.where(even, tail, head), 'space', inner_pairs)  6.69 us
    psum x1, blocking collectives, local(): norm_total = lax.psum(jnp.sum(difference * difference), 'space')  6.36 us
    slice x8, local copies, waits for them, and re-layouts, receive(): exponent = message[-1, 0, 0].astype(jnp.float32)  4.79 us
    convert_element_type x8, other arithmetic, send(): small = (values * jnp.exp2(14.0 - exponent)).astype(jnp.float16)  3.2 us
  transfers between devices with their start and end apart: 12, of which 9 were waited for; matrix products, arithmetic and copies ran while one was open for 3% of the time, Pallas kernels for 0%

profile of v1, /device:TPU:28, one launch (start us, length us, event | category | flops | bytes accessed | tf_op | source)
XLA Modules:
  0.0 129.3 jit_solution(6978857201893639019)
XLA Ops:
  0.7 1.3 bitcast_convert_fusion
  2.2 0.7 collective-permute-start.1
  2.8 2.9 %collective-permute-start = (bf16[64,4,160]{2,1,0:T(4,128)(2,1)S(1)}, bf16[64,4,160]{2,1,0:T(4,128)(2,1)S(1)}, u32[]{:S(2)}, u32[]{:S(2)}) collective-permute-start(bf16[64,4,160]{2,1,0:T(4,128)(2,1)S(1)} %get-tuple-element.21), channel_id=1, source_target_pairs={{0,1},{1,0},{2,3},{3,2},{4,5},{5,4},{6,7},{7,6},{8,9},{9,8},{10,11... | collective-permute-start | bytes 245768 | tf_op jit(solution)/shard_map/ppermute | solution.py:222
  5.8 0.6 fusion.15
  8.4 1.1 pad.12
  9.5 1.7 %copy.9.first = bf16[3,256,768]{2,1,0:T(8,128)(2,1)S(1)} copy(bf16[3,256,768]{1,2,0:T(8,128)(2,1)} %bitcast.43) | data formatting | bytes 2359296 | tf_op jit(solution)/shard_map/reshape | solution.py:216
  11.3 1.2 copy-done.2
  12.5 9.0 %denoise.2 = (f32[64,4,640]{2,1,0:T(4,128)S(1)}, f32[1]{0:T(128)}) custom-call(f32[6]{0:T(128)S(1)} %stack.39.scalars, f32[64,4,640]{2,1,0:T(4,128)S(1)} %bitcast.40, bf16[64,4,160]{2,1,0:T(4,128)(2,1)S(1)} %collective-permute-done.inner, bf16[64,4,160]{2,1,0:T(4,128)(2,1)S(1)} %collective-permute-done.1.outer, f32[64,4,640]{2,1,0:T(4,128)S(1)} %bitcast.41, ...), custom_call_target="tpu_custom_call" | custom-call | flops 5000000000 | bytes 4000000 | tf_op jit(solution)/shard_map/denoise/pallas_call | solution.py:126
  22.2 0.2 select_add_fusion.1
  22.6 0.8 concatenate.34
  23.3 0.5 collective-permute-start.2
  23.8 5.9 %collective-permute-done.2 = f16[33,4,640]{2,1,0:T(4,128)(2,1)S(1)} collective-permute-done((f16[33,4,640]{2,1,0:T(4,128)(2,1)}, f16[33,4,640]{2,1,0:T(4,128)(2,1)S(1)}, u32[]{:S(2)}, u32[]{:S(2)}) %collective-permute-start.2) | collective-permute-done | bytes 168992 | tf_op jit(solution)/shard_map/ppermute | solution.py:153
  29.8 0.5 slice.98
  31.3 1.3 collective-permute-start.3
  32.6 6.0 %collective-permute-done.3 = f16[33,4,640]{2,1,0:T(4,128)(2,1)S(1)} collective-permute-done((f16[33,4,640]{2,1,0:T(4,128)(2,1)S(1)}, f16[33,4,640]{2,1,0:T(4,128)(2,1)S(1)}, u32[]{:S(2)}, u32[]{:S(2)}) %collective-permute-start.3) | collective-permute-done | bytes 168992 | tf_op jit(solution)/shard_map/ppermute | solution.py:153
  38.6 0.7 copy-done.6
  39.2 0.5 slice.100
  40.5 1.1 multiply_convert_fusion.5
  41.6 0.8 concatenate.36
  42.4 1.3 collective-permute-start.4
  43.7 9.5 %collective-permute-done.4 = f16[33,4,640]{2,1,0:T(4,128)(2,1)} collective-permute-done((f16[33,4,640]{2,1,0:T(4,128)(2,1)}, f16[33,4,640]{2,1,0:T(4,128)(2,1)}, u32[]{:S(2)}, u32[]{:S(2)}) %collective-permute-start.4) | collective-permute-done | bytes 168992 | tf_op jit(solution)/shard_map/ppermute | solution.py:153
  53.2 1.2 slice.102
  55.1 1.2 multiply_convert_fusion.4
  56.5 0.6 collective-permute-start.5
  57.0 4.9 %collective-permute-done.5 = f16[33,4,640]{2,1,0:T(4,128)(2,1)S(1)} collective-permute-done((f16[33,4,640]{2,1,0:T(4,128)(2,1)S(1)}, f16[33,4,640]{2,1,0:T(4,128)(2,1)S(1)}, u32[]{:S(2)}, u32[]{:S(2)}) %collective-permute-start.5) | collective-permute-done | bytes 168992 | tf_op jit(solution)/shard_map/ppermute | solution.py:153
  61.9 0.5 slice.104
  63.1 1.3 fusion.5
  64.4 0.3 fusion.14
  64.9 0.8 collective-permute-start.7
  65.8 3.8 %collective-permute-start.6 = (bf16[64,4,160]{2,1,0:T(4,128)(2,1)S(1)}, bf16[64,4,160]{2,1,0:T(4,128)(2,1)S(1)}, u32[]{:S(2)}, u32[]{:S(2)}) collective-permute-start(bf16[64,4,160]{2,1,0:T(4,128)(2,1)S(1)} %get-tuple-element.19), channel_id=1, source_target_pairs={{0,1},{1,0},{2,3},{3,2},{4,5},{5,4},{6,7},{7,6},{8,9},{9,8},{10,11... | collective-permute-start | bytes 245768 | tf_op jit(solution)/shard_map/ppermute | solution.py:222
  69.6 1.0 collective-permute-done.6.inner
  70.5 9.0 %denoise.3 = (f32[64,4,640]{2,1,0:T(4,128)S(1)}, f32[1]{0:T(128)}) custom-call(f32[6]{0:T(128)S(1)} %stack.39.scalars, f32[64,4,640]{2,1,0:T(4,128)S(1)} %get-tuple-element.11.latent, bf16[64,4,160]{2,1,0:T(4,128)(2,1)S(1)} %collective-permute-done.6.inner, bf16[64,4,160]{2,1,0:T(4,128)(2,1)S(1)} %collective-permute-done.7.outer, ...), custom_call_target="tpu_custom_call" | custom-call | flops 5000000000 | bytes 4000000 | tf_op jit(solution)/shard_map/denoise/pallas_call | solution.py:126
  80.7 0.6 collective-permute-start.8
  81.3 6.3 %collective-permute-done.8 = f16[33,4,640]{2,1,0:T(4,128)(2,1)S(1)} collective-permute-done((f16[33,4,640]{2,1,0:T(4,128)(2,1)S(1)}, f16[33,4,640]{2,1,0:T(4,128)(2,1)S(1)}, u32[]{:S(2)}, u32[]{:S(2)}) %collective-permute-start.8) | collective-permute-done | bytes 168992 | tf_op jit(solution)/shard_map/ppermute | solution.py:153
  87.6 0.5 slice.108
  89.1 1.3 collective-permute-start.9
  90.4 7.0 %collective-permute-done.9 = f16[33,4,640]{2,1,0:T(4,128)(2,1)S(1)} collective-permute-done((f16[33,4,640]{2,1,0:T(4,128)(2,1)S(1)}, f16[33,4,640]{2,1,0:T(4,128)(2,1)S(1)}, u32[]{:S(2)}, u32[]{:S(2)}) %collective-permute-start.9) | collective-permute-done | bytes 168992 | tf_op jit(solution)/shard_map/ppermute | solution.py:153
  97.4 0.5 slice.110
  99.0 1.3 collective-permute-start.10
  100.3 9.7 %collective-permute-done.10 = f16[33,4,640]{2,1,0:T(4,128)(2,1)S(1)} collective-permute-done((f16[33,4,640]{2,1,0:T(4,128)(2,1)S(1)}, f16[33,4,640]{2,1,0:T(4,128)(2,1)S(1)}, u32[]{:S(2)}, u32[]{:S(2)}) %collective-permute-start.10) | collective-permute-done | bytes 168992 | tf_op jit(solution)/shard_map/ppermute | solution.py:153
  109.9 0.5 slice.112
  111.2 0.2 multiply_convert_fusion
  111.5 0.6 collective-permute-start.11
  112.1 5.7 %collective-permute-done.11 = f16[33,4,640]{2,1,0:T(4,128)(2,1)S(1)} collective-permute-done((f16[33,4,640]{2,1,0:T(4,128)(2,1)S(1)}, f16[33,4,640]{2,1,0:T(4,128)(2,1)S(1)}, u32[]{:S(2)}, u32[]{:S(2)}) %collective-permute-start.11) | collective-permute-done | bytes 168992 | tf_op jit(solution)/shard_map/ppermute | solution.py:153
  117.8 0.5 slice.114
  119.0 0.3 fusion.2
  119.3 1.8 %multiply_reduce_fusion = (f32[]{:T(128)}, f32[1,64,4,640]{3,2,1,0:T(4,128)}) fusion(f32[64,4,640]{2,1,0:T(4,128)S(1)} %get-tuple-element.11.latent, f32[64,4,640]{2,1,0:T(4,128)S(1)} %get-tuple-element.6, f32[64,4,640]{2,1,0:T(4,128)S(1)} %get-tuple-element.8, f32[32,4,640]{2,1,0:T(4,128)S(1)} %get-tuple-element.15, f32[32,4,640]{2,1,0:T(4,128)S(1)} %get-tuple-element.14, ...), kind=kLoop, calls=%fused_computation.3 | loop fusion | flops 1146879 | bytes 3276805 | tf_op jit(solution)/shard_map/reduce_sum | solution.py:233
  121.1 6.4 %psum.7 = f32[]{:T(128)} all-reduce(f32[]{:T(128)} %get-tuple-element.12), channel_id=1, replica_groups=mesh['step'=8,'space'=4] {'space'}, use_global_device_ids=true, to_apply=%region_1.2 | all-reduce | flops 1 | bytes 8 | tf_op jit(solution)/shard_map/psum | solution.py:233
  (36 shorter events, 2.2 us)
Async XLA Ops:
  0.6 6.4 %copy-start = (f32[64,256]{1,0:T(8,128)S(1)}, f32[64,256]{1,0:T(8,128)}, u32[]{:S(2)}) copy-start(f32[64,256]{1,0:T(8,128)} %param.11) | copy-start | bytes 196612
  0.6 5.1 %copy-start.8 = (s32[1,2]{1,0:T(1,128)S(1)}, s32[1,2]{1,0:T(1,128)}, u32[]{:S(2)}) copy-start(s32[1,2]{1,0:T(1,128)} %param.8) | copy-start | bytes 28
  0.7 7.7 %copy-start.7 = (bf16[3,256,576]{1,2,0:T(8,128)(2,1)S(1)}, bf16[3,256,576]{1,2,0:T(8,128)(2,1)}, u32[]{:S(2)}) copy-start(bf16[3,256,576]{1,2,0:T(8,128)(2,1)} %param.9) | copy-start | bytes 2654212
  2.2 9.1 %collective-permute-start.1 = (bf16[64,4,160]{2,1,0:T(4,128)(2,1)S(1)}, bf16[64,4,160]{2,1,0:T(4,128)(2,1)S(1)}, u32[]{:S(2)}, u32[]{:S(2)}) collective-permute-start(bf16[64,4,160]{2,1,0:T(4,128)(2,1)S(1)} %get-tuple-element.20), channel_id=1, source_target_pairs={{1,2},{2,1},{5,6},{6,5},{9,10},{10,9},{13,14},{14,13},{17,18},{18,... | collective-permute-start | bytes 245768 | tf_op jit(solution)/shard_map/ppermute | solution.py:223
  2.8 8.5 %collective-permute-start = (bf16[64,4,160]{2,1,0:T(4,128)(2,1)S(1)}, bf16[64,4,160]{2,1,0:T(4,128)(2,1)S(1)}, u32[]{:S(2)}, u32[]{:S(2)}) collective-permute-start(bf16[64,4,160]{2,1,0:T(4,128)(2,1)S(1)} %get-tuple-element.21), channel_id=1, source_target_pairs={{0,1},{1,0},{2,3},{3,2},{4,5},{5,4},{6,7},{7,6},{8,9},{9,8},{10,11... | collective-permute-start | bytes 245768 | tf_op jit(solution)/shard_map/ppermute | solution.py:222
  9.5 1.8 %copy-start.1 = (f32[1,64,4,640]{3,2,1,0:T(4,128)S(1)}, f32[1,64,4,640]{3,2,1,0:T(4,128)}, u32[]{:S(2)}) copy-start(f32[1,64,4,640]{3,2,1,0:T(4,128)} %param.6) | copy-start | bytes 1966084
  9.5 1.8 %copy-start.4 = (f32[1,64,4,640]{3,2,1,0:T(4,128)S(1)}, f32[1,64,4,640]{3,2,1,0:T(4,128)}, u32[]{:S(2)}) copy-start(f32[1,64,4,640]{3,2,1,0:T(4,128)} %param.7) | copy-start | bytes 1966084
  11.3 1.2 copy-start.2
  23.3 6.4 %collective-permute-start.2 = (f16[33,4,640]{2,1,0:T(4,128)(2,1)}, f16[33,4,640]{2,1,0:T(4,128)(2,1)S(1)}, u32[]{:S(2)}, u32[]{:S(2)}) collective-permute-start(f16[33,4,640]{2,1,0:T(4,128)(2,1)} %concatenate.34), channel_id=1, source_target_pairs={{0,4},{4,0},{8,12},{12,8},{16,20},{20,16},{24,28},{28,24},{1,5},{5... | collective-permute-start | bytes 506888 | tf_op jit(solution)/shard_map/ppermute | solution.py:153
  31.3 7.3 %collective-permute-start.3 = (f16[33,4,640]{2,1,0:T(4,128)(2,1)S(1)}, f16[33,4,640]{2,1,0:T(4,128)(2,1)S(1)}, u32[]{:S(2)}, u32[]{:S(2)}) collective-permute-start(f16[33,4,640]{2,1,0:T(4,128)(2,1)S(1)} %concatenate.35), channel_id=1, source_target_pairs={{0,8},{4,12},{8,16},{12,20},{16,24},{20,28},{1,9},{5,13},{9,17},{1... | collective-permute-start | bytes 506888 | tf_op jit(solution)/shard_map/ppermute | solution.py:153
  38.6 0.7 copy-start.6
  42.4 10.8 %collective-permute-start.4 = (f16[33,4,640]{2,1,0:T(4,128)(2,1)}, f16[33,4,640]{2,1,0:T(4,128)(2,1)}, u32[]{:S(2)}, u32[]{:S(2)}) collective-permute-start(f16[33,4,640]{2,1,0:T(4,128)(2,1)} %concatenate.36), channel_id=1, source_target_pairs={{0,16},{4,20},{8,24},{12,28},{1,17},{5,21},{9,25},{13,29},{2,18},{... | collective-permute-start | bytes 506888 | tf_op jit(solution)/shard_map/ppermute | solution.py:153
  56.5 5.4 %collective-permute-start.5 = (f16[33,4,640]{2,1,0:T(4,128)(2,1)S(1)}, f16[33,4,640]{2,1,0:T(4,128)(2,1)S(1)}, u32[]{:S(2)}, u32[]{:S(2)}) collective-permute-start(f16[33,4,640]{2,1,0:T(4,128)(2,1)S(1)} %concatenate.37), channel_id=1, source_target_pairs={{0,4},{4,0},{8,12},{12,8},{16,20},{20,16},{24,28},{28,24},{1,5},{5... | collective-permute-start | bytes 506888 | tf_op jit(solution)/shard_map/ppermute | solution.py:153
  64.4 6.1 %copy-start.3 = (bf16[3,64,2304]{2,1,0:T(8,128)(2,1)S(1)}, bf16[3,64,2304]{2,1,0:T(8,128)(2,1)}, u32[]{:S(2)}) copy-start(bf16[3,64,2304]{2,1,0:T(8,128)(2,1)} %second.3) | copy-start | bytes 2654212
  64.4 6.1 %copy-start.5 = (f32[1,64,4,640]{3,2,1,0:T(4,128)S(1)}, f32[1,64,4,640]{3,2,1,0:T(4,128)}, u32[]{:S(2)}) copy-start(f32[1,64,4,640]{3,2,1,0:T(4,128)} %param.7) | copy-start | bytes 1966084
  64.9 4.6 %collective-permute-start.7 = (bf16[64,4,160]{2,1,0:T(4,128)(2,1)S(1)}, bf16[64,4,160]{2,1,0:T(4,128)(2,1)S(1)}, u32[]{:S(2)}, u32[]{:S(2)}) collective-permute-start(bf16[64,4,160]{2,1,0:T(4,128)(2,1)S(1)} %get-tuple-element.18), channel_id=1, source_target_pairs={{1,2},{2,1},{5,6},{6,5},{9,10},{10,9},{13,14},{14,13},{17,18},{18,... | collective-permute-start | bytes 245768 | tf_op jit(solution)/shard_map/ppermute | solution.py:223
  65.8 4.8 %collective-permute-start.6 = (bf16[64,4,160]{2,1,0:T(4,128)(2,1)S(1)}, bf16[64,4,160]{2,1,0:T(4,128)(2,1)S(1)}, u32[]{:S(2)}, u32[]{:S(2)}) collective-permute-start(bf16[64,4,160]{2,1,0:T(4,128)(2,1)S(1)} %get-tuple-element.19), channel_id=1, source_target_pairs={{0,1},{1,0},{2,3},{3,2},{4,5},{5,4},{6,7},{7,6},{8,9},{9,8},{10,11... | collective-permute-start | bytes 245768 | tf_op jit(solution)/shard_map/ppermute | solution.py:222
  80.7 6.9 %collective-permute-start.8 = (f16[33,4,640]{2,1,0:T(4,128)(2,1)S(1)}, f16[33,4,640]{2,1,0:T(4,128)(2,1)S(1)}, u32[]{:S(2)}, u32[]{:S(2)}) collective-permute-start(f16[33,4,640]{2,1,0:T(4,128)(2,1)S(1)} %concatenate.39), channel_id=1, source_target_pairs={{0,4},{4,0},{8,12},{12,8},{16,20},{20,16},{24,28},{28,24},{1,5},{5... | collective-permute-start | bytes 506888 | tf_op jit(solution)/shard_map/ppermute | solution.py:153
  89.1 8.3 %collective-permute-start.9 = (f16[33,4,640]{2,1,0:T(4,128)(2,1)S(1)}, f16[33,4,640]{2,1,0:T(4,128)(2,1)S(1)}, u32[]{:S(2)}, u32[]{:S(2)}) collective-permute-start(f16[33,4,640]{2,1,0:T(4,128)(2,1)S(1)} %concatenate.40), channel_id=1, source_target_pairs={{0,8},{4,12},{8,16},{12,20},{16,24},{20,28},{1,9},{5,13},{9,17},{1... | collective-permute-start | bytes 506888 | tf_op jit(solution)/shard_map/ppermute | solution.py:153
  99.0 11.0 %collective-permute-start.10 = (f16[33,4,640]{2,1,0:T(4,128)(2,1)S(1)}, f16[33,4,640]{2,1,0:T(4,128)(2,1)S(1)}, u32[]{:S(2)}, u32[]{:S(2)}) collective-permute-start(f16[33,4,640]{2,1,0:T(4,128)(2,1)S(1)} %concatenate.41), channel_id=1, source_target_pairs={{0,16},{4,20},{8,24},{12,28},{1,17},{5,21},{9,25},{13,29},{2,18},{... | collective-permute-start | bytes 506888 | tf_op jit(solution)/shard_map/ppermute | solution.py:153
  111.5 6.3 %collective-permute-start.11 = (f16[33,4,640]{2,1,0:T(4,128)(2,1)S(1)}, f16[33,4,640]{2,1,0:T(4,128)(2,1)S(1)}, u32[]{:S(2)}, u32[]{:S(2)}) collective-permute-start(f16[33,4,640]{2,1,0:T(4,128)(2,1)S(1)} %concatenate.42), channel_id=1, source_target_pairs={{0,4},{4,0},{8,12},{12,8},{16,20},{20,16},{24,28},{28,24},{1,5},{5... | collective-permute-start | bytes 506888 | tf_op jit(solution)/shard_map/ppermute | solution.py:153

commit v2 on v0

v2 whole, which is shorter than its diff:
```python
import functools
import math

import jax
import jax.numpy as jnp
from jax import lax
from jax.experimental import pallas as pl
from jax.experimental.pallas import tpu as pltpu
from jax.sharding import PartitionSpec as P

C = 64
COLS = 80
SUB = 8
NT = (((1,), (1,)), ((), ()))
MEGA = 2**20


def plan(timestep):
    scaled = timestep.astype(jnp.float32) / 1000.0
    return -(0.1 * scaled + 9.95 * scaled * scaled)


def coefficients(timestep_pair):
    log_from = plan(timestep_pair[0])
    log_to = plan(timestep_pair[1])
    half_gap = 0.5 * (log_to - log_from)
    decay_gain = jnp.expm1(half_gap)
    remain_from = -jnp.expm1(log_from)
    remain_to = -jnp.expm1(log_to)
    ratio_term = -jnp.expm1(log_from - log_to)
    noise_gain = -jnp.exp(half_gap) * jnp.sqrt(remain_from) + remain_to * jnp.exp(
        -half_gap
    ) / jnp.sqrt(remain_from)
    spread_gain = jnp.sqrt(remain_to / remain_from * ratio_term)
    return (decay_gain, noise_gain, spread_gain)


def time_embed(timestep, time_weight):
    half_count = C // 2
    frequency = jnp.exp(-math.log(10000.0) * jnp.arange(half_count, dtype=jnp.float32) / half_count)
    angles = timestep.astype(jnp.float32) * frequency
    features = jnp.concatenate([jnp.sin(angles), jnp.cos(angles)])
    return jnp.dot(
        features, time_weight, preferred_element_type=jnp.float32, precision=lax.Precision.HIGHEST
    )


class Frames:
    def __init__(self, odd, parity):
        self.odd, self.parity = odd, parity

    def pick(self, ref, v):
        count = ref.shape[1]
        return jnp.where(self.odd, ref[:, v, :], ref[:, count - 1 - v, :])

    def slot(self, v):
        return jnp.where(self.parity == 1, v % 2, (v + 1) % 2)

    def load(self, ref, v):
        tiles = C // SUB
        return ref[pl.ds(self.slot(v) * tiles, tiles)].reshape(C, ref.shape[2])

    def store(self, ref, v, value):
        tiles = C // SUB
        ref[pl.ds(self.slot(v) * tiles, tiles)] = value.reshape(tiles, SUB, ref.shape[2])

    def tap(self, a):
        return jnp.where(self.parity == 1, a, 2 - a)


def entering_of(frames, flags, guesses, halves, v):
    start = frames.pick(guesses, v)
    if halves is None:
        return start
    other, keep = halves
    return jnp.where(flags.anchor, start, frames.load(other if v < 2 else keep, v))


class Flags:
    def __init__(self, whole, real):
        self.parity = whole[0]
        self.odd = whole[0] == 1
        self.even_block = whole[1] == 0
        self.anchor = whole[2] == 1
        self.keep, self.gain, self.spread = real[0], real[1], real[2]
        self.top, self.bottom = whole[3], whole[4]


def denoise_kernel(later, whole, real, guesses, *refs):
    halves = None
    if later:
        other, keep, *refs = refs
        halves = (other, keep)
    inner, outer, noise, first, second, temb, yours, mine, shifted, hidden = refs
    flags = Flags(whole, real)
    frames = Frames(flags.odd, flags.parity)
    channels, count, length = guesses.shape
    width = temb.shape[1]
    edge = 2 * COLS
    extended = length + 2 * COLS
    chunk = extended // 2
    top, bottom = flags.top == 1, flags.bottom == 1

    def spread_columns(values, at, v):
        n = values.shape[1]
        column = lax.broadcasted_iota(jnp.int32, (1, n), 1) % COLS
        before = jnp.where(column >= 1, pltpu.roll(values, 1, 1), 0.0).astype(jnp.bfloat16)
        after = jnp.where(column <= COLS - 2, pltpu.roll(values, n - 1, 1), 0.0).astype(jnp.bfloat16)
        center = values.astype(jnp.bfloat16)
        shifted[v, pl.ds(at, n), 0:128] = jnp.concatenate([before, center], axis=0).T
        shifted[v, pl.ds(at, n), 256:384] = jnp.concatenate([center, after], axis=0).T
        mixed = jnp.concatenate([after, before], axis=0).T
        shifted[v, pl.ds(at, n), 128:192] = mixed[:, :64]
        if at >= COLS:
            shifted[v, pl.ds(at - COLS, n), 192:256] = mixed[:, 64:]
        else:
            shifted[v, pl.ds(0, n - COLS), 192:256] = mixed[COLS:, 64:]

    def halo(ref, v):
        tiles = C // SUB
        at = (0 if v < 2 else 2 * tiles) + frames.slot(v) * tiles
        return ref[pl.ds(at, tiles)].astype(jnp.float32).reshape(C, ref.shape[2])

    def prepare(v):
        shifted[v, pl.ds(length + 3 * COLS, COLS), 128:256] = jnp.zeros((COLS, 128), jnp.bfloat16)
        near, far = halo(inner, v), halo(outer, v)
        spread_columns(jnp.where(flags.even_block, far, near), 0, v)
        spread_columns(entering_of(frames, flags, guesses, halves, v), edge, v)
        spread_columns(jnp.where(flags.even_block, near, far), edge + length, v)

    def near_frames(v):
        return [a for a in range(3) if 0 <= v + a - 1 < count]

    def first_conv(v):
        weights = []
        for a in near_frames(v):
            w = first[frames.tap(a)]
            weights += [w[:, :512], w[:, 512:], jnp.zeros((width, 64), jnp.bfloat16)]
        weights = jnp.concatenate(weights, axis=1)
        for start in range(0, extended, chunk):
            cells = []
            for a in near_frames(v):
                for b, low, high in ((0, 0, 256), (1, 256, 384), (2, 0, 256)):
                    cells.append(shifted[v + a - 1, pl.ds(b * COLS + start, chunk), low:high])
            cells = jnp.concatenate(cells, axis=1)
            value = lax.dot_general(cells, weights, NT, preferred_element_type=jnp.float32) + temb[...]
            active = value / (1.0 + jnp.exp(-value))
            place = start + lax.broadcasted_iota(jnp.int32, (chunk, 1), 0)
            outside = jnp.logical_or(
                jnp.logical_and(place < COLS, top), jnp.logical_and(place >= extended - COLS, bottom)
            )
            hidden[v, pl.ds(start, chunk), :] = jnp.where(outside, 0.0, active).astype(jnp.bfloat16)

    def second_conv(v):
        taps = [(a, b) for a in near_frames(v) for b in range(3)]
        cells = jnp.concatenate([hidden[v + a - 1, pl.ds(b * COLS, length), :] for a, b in taps], axis=1)
        weights = jnp.concatenate(
            [
                jnp.concatenate(
                    [
                        second[frames.tap(a), :, (b * 3 + e) * width : (b * 3 + e + 1) * width]
                        for e in range(3)
                    ],
                    axis=0,
                )
                for a, b in taps
            ],
            axis=1,
        )
        parts = lax.dot_general(cells, weights, NT, preferred_element_type=jnp.float32).T
        column = lax.broadcasted_iota(jnp.int32, (1, length), 1) % COLS
        before = jnp.where(column >= 1, pltpu.roll(parts[:channels], 1, 1), 0.0)
        after = jnp.where(
            column <= COLS - 2, pltpu.roll(parts[2 * channels : 3 * channels], length - 1, 1), 0.0
        )
        predicted = before + parts[channels : 2 * channels] + after
        latent = entering_of(frames, flags, guesses, halves, v)
        result = flags.keep * latent + flags.gain * predicted + flags.spread * frames.pick(noise, v)
        result = result + jnp.where(flags.anchor, latent, 0.0)
        frames.store(yours if v < 2 else mine, v, result)
        return jnp.max(jnp.abs(result), axis=0, keepdims=True)

    def mark(ref, peaks):
        peak = jnp.max(functools.reduce(jnp.maximum, peaks), axis=1, keepdims=True)
        exponent = jnp.clip(jnp.ceil(jnp.log(peak) * (1.0 / math.log(2.0))) + 1.0, -100.0, 126.0)
        ref[ref.shape[0] - 1] = jnp.broadcast_to(exponent, (SUB, length))

    prepare(0)
    prepare(1)
    peaks = []
    for v in range(count):
        first_conv(v)
        if v + 2 < count:
            prepare(v + 2)
        if v >= 1:
            peaks.append(second_conv(v - 1))
    peaks.append(second_conv(count - 1))
    mark(yours, peaks[: count // 2])
    mark(mine, peaks[count // 2 :])


WHOLE = pl.BlockSpec(memory_space=pltpu.VMEM)
WORDS = pl.BlockSpec(memory_space=pltpu.SMEM)


def denoise(whole, real, guesses, halves, inner, outer, noise, first, second, temb):
    channels, frames, length = guesses.shape
    half = jax.ShapeDtypeStruct((frames // 2 * channels // SUB + 1, SUB, length), jnp.float32)
    later = halves is not None
    operands = (whole, real, guesses) + (halves if later else ()) + (inner, outer, noise, first, second, temb)
    return pl.pallas_call(
        functools.partial(denoise_kernel, later),
        out_shape=(half, half),
        in_specs=[WORDS] * 2 + [WHOLE] * (len(operands) - 2),
        out_specs=(WHOLE, WHOLE),
        scratch_shapes=[
            pltpu.VMEM((frames, length + 4 * COLS, 384), jnp.bfloat16),
            pltpu.VMEM((frames, length + 2 * COLS, temb.shape[1]), jnp.bfloat16),
        ],
        compiler_params=pltpu.CompilerParams(vmem_limit_bytes=24 * MEGA),
        cost_estimate=pl.CostEstimate(flops=5_000_000_000, bytes_accessed=4_000_000, transcendentals=1_000_000),
        name="denoise",
    )(*operands)


def finish_kernel(whole, real, guesses, other1, keep1, yours1, mine1, other2, keep2, yours2, mine2, states, total):
    flags = Flags(whole, real)
    frames = Frames(flags.odd, flags.parity)
    count = guesses.shape[1]
    square = jnp.zeros((C, guesses.shape[2]), jnp.float32)
    for frame in range(count):
        low = frame < count // 2
        slot = (frame % 2) * (C // SUB)

        def part(first_ref, second_ref):
            one = first_ref[pl.ds(slot, C // SUB)].reshape(C, guesses.shape[2])
            two = second_ref[pl.ds(slot, C // SUB)].reshape(C, guesses.shape[2])
            return jnp.where(flags.odd, one, two) if low else jnp.where(flags.odd, two, one)

        before1 = jnp.where(flags.anchor, 0.0, part(other1, keep1))
        before2 = jnp.where(flags.anchor, 0.0, part(other2, keep2))
        reached1 = before1 + part(yours1, mine1)
        reached2 = before2 + part(yours2, mine2)
        states[:, frame, :] = reached2
        change = reached2 - reached1
        square = square + change * change
    total[...] = jnp.broadcast_to(jnp.sum(jnp.sum(square, axis=0, keepdims=True), axis=1, keepdims=True), total.shape)


def finish(whole, real, guesses, *halves):
    return pl.pallas_call(
        finish_kernel,
        out_shape=(
            jax.ShapeDtypeStruct(guesses.shape, jnp.float32),
            jax.ShapeDtypeStruct((SUB, 128), jnp.float32),
        ),
        in_specs=[WORDS] * 2 + [WHOLE] * 9,
        out_specs=(WHOLE, WHOLE),
        compiler_params=pltpu.CompilerParams(vmem_limit_bytes=24 * MEGA),
        cost_estimate=pl.CostEstimate(flops=4_000_000, bytes_accessed=7_000_000, transcendentals=0),
        name="finish",
    )(whole, real, guesses, *halves)


def is_mark(half):
    return lax.broadcasted_iota(jnp.int32, half.shape, 0) == half.shape[0] - 1


def coded(half):
    exponent = half[-1:]
    return jnp.where(is_mark(half), half, half * jnp.exp2(14.0 - exponent)).astype(jnp.float16)


def decoded(message):
    half = message.astype(jnp.float32)
    return jnp.where(is_mark(half), half, half * jnp.exp2(half[-1:] - 14.0))


def added(one, two):
    return jnp.where(is_mark(one), jnp.maximum(one, two) + 1.0, one + two)


def masked(half, condition):
    return jnp.where(condition, half, jnp.where(is_mark(half), -100.0, 0.0))


def exchange(half, distance):
    steps = lax.axis_size("step")
    return decoded(lax.ppermute(coded(half), "step", [(i, i ^ distance) for i in range(steps)]))


def prefix(yours, mine, step_index):
    steps = lax.axis_size("step")
    odd = step_index % 2 == 1
    partner = exchange(yours, 1)
    total = added(mine, partner)
    before = masked(total, False)
    distance = 2
    while distance < steps:
        got = exchange(total, distance)
        before = added(before, masked(got, (step_index // distance) % 2 == 1))
        total = added(total, got)
        distance *= 2
    keep = added(before, masked(partner, odd))
    give = added(before, masked(mine, jnp.logical_not(odd)))
    return exchange(give, 1), keep


def local(guesses, noise, timesteps, conv_first, conv_second, time_weight):
    step_index = lax.axis_index("step")
    row_block = lax.axis_index("space")
    space = lax.axis_size("space")
    start_latent = guesses[0]
    noise_step = noise[0]
    timestep_pair = timesteps[0]
    edge = 2 * COLS
    length = start_latent.shape[2]
    even = row_block % 2 == 0
    inner_pairs = [pair for i in range(0, space - 1, 2) for pair in ((i, i + 1), (i + 1, i))]
    outer_pairs = [pair for i in range(1, space - 1, 2) for pair in ((i, i + 1), (i + 1, i))]

    real = jnp.stack(coefficients(timestep_pair))
    temb = time_embed(timestep_pair[0], time_weight).reshape(1, -1)
    whole = jnp.stack([step_index % 2, row_block % 2, step_index == 0, row_block == 0, row_block == space - 1])
    whole = whole.astype(jnp.int32)

    def halos(head, tail):
        inner = lax.ppermute(jnp.where(even, tail, head), "space", inner_pairs)
        outer = lax.ppermute(jnp.where(even, head, tail), "space", outer_pairs)
        return inner, outer

    def ends(values):
        rounded = values.astype(jnp.bfloat16)
        return rounded[..., :edge], rounded[..., length - edge :]

    def ordered(values):
        moved = values.transpose(1, 0, 2)
        count = moved.shape[0] // 2
        turned = jnp.concatenate([moved[count:], moved[:count]], axis=0)
        return jnp.where(step_index % 2 == 1, moved, turned).reshape(-1, SUB, edge)

    head1, tail1 = (ordered(side) for side in ends(start_latent))
    inner, outer = halos(head1, tail1)
    yours1, mine1 = denoise(whole, real, start_latent, None, inner, outer, noise_step, conv_first, conv_second, temb)
    other1, keep1 = prefix(yours1, mine1, step_index)
    heads, tails = zip(ends(other1[:-1]), ends(keep1[:-1]))
    is_anchor = step_index == 0
    head2 = jnp.where(is_anchor, head1, jnp.concatenate(heads, axis=0))
    tail2 = jnp.where(is_anchor, tail1, jnp.concatenate(tails, axis=0))
    inner2, outer2 = halos(head2, tail2)
    yours2, mine2 = denoise(
        whole, real, start_latent, (other1, keep1), inner2, outer2, noise_step, conv_first, conv_second, temb
    )
    other2, keep2 = prefix(yours2, mine2, step_index)
    states, total = finish(whole, real, start_latent, other1, keep1, yours1, mine1, other2, keep2, yours2, mine2)
    norm_total = lax.psum(total[0, 0], "space")
    cell_count = start_latent.size * space
    changes = jnp.sqrt(norm_total / cell_count).reshape(1)
    return (states[None], changes)


def solution(mesh):
    in_specs = (
        P("step", None, None, "space"),
        P("step", None, None, "space"),
        P("step", None),
        P(),
        P(),
        P(),
    )
    out_specs = (P("step", None, None, "space"), P("step"))
    return jax.shard_map(local, mesh=mesh, in_specs=in_specs, out_specs=out_specs, check_vma=False)
```

time: 158 us -> 113 us (0.72)
  blocking collectives: 95 us -> 6.36 us
  waiting for transfers between devices: 3.72 us -> 43.3 us
  matrix products: 31.2 us -> 0.2 us
  Pallas kernels: 0 us -> 18.9 us
  starting transfers between devices: 6.25 us -> 23.5 us
  other arithmetic: 10.1 us -> 7.26 us
  local copies, waits for them, and re-layouts: 6.46 us -> 8.73 us
    all_to_all x4 -> x0, blocking collectives: 88.6 us -> none  [the longest x2 45.2 us: prefix(): lax.all_to_all(before_sum, 'step', split_axis=0, concat_axis=1, tiled=True)]
    ppermute x4 -> x12, waiting for transfers between devices: 3.72 us -> 43.3 us  [the longest x8 42.3 us: exchange(): lax.ppermute(coded(half), 'step', [(i, i ^ distance) for i in range(steps)])]
    dot_general x14 -> x0, matrix products: 31 us -> none  [the longest x8 20 us: convolve(): jnp.einsum('oj,jfp->ofp', weight[frame_shift], framed[:, frame_shift:fram...]
    pallas_call x0 -> x3, Pallas kernels: none -> 18.9 us  [the longest x2 16.9 us: denoise(): pl.pallas_call(functools.partial(denoise_kernel, later), out_shape=(half,...]
    ppermute x4 -> x12, starting transfers between devices: 6.25 us -> 23.5 us  [the longest x8 14.7 us: exchange(): lax.ppermute(coded(half), 'step', [(i, i ^ distance) for i in range(steps)])]
    unnamed x24 -> x0, other arithmetic: 7.08 us -> none
    convert_element_type x1 -> x17, other arithmetic: 0.09 us -> 3.83 us  [the longest x8 1.51 us: coded(): jnp.where(is_mark(half), half, half * jnp.exp2(14.0 - exponent))]
    unnamed x22 -> x29, local copies, waits for them, and re-layouts: 3.58 us -> 6.99 us
  transfers between devices with their start and end apart: 4 -> 12, of which waited for: 2 -> 9; matrix products, arithmetic and copies ran while one was open for 1% -> 2% of each run, Pallas kernels for 0% -> 0%
where the time goes in v2:
time: 113 us
  waiting for transfers between devices  43.3 us (38%)
  starting transfers between devices  23.5 us (21%)
  Pallas kernels  18.9 us (17%)
  local copies, waits for them, and re-layouts  8.73 us (8%)
  other arithmetic  7.26 us (6%)
  blocking collectives  6.36 us (6%)
  between operations  4.65 us (4%)
    ppermute x8, waiting for transfers between devices, exchange(): lax.ppermute(coded(half), 'step', [(i, i ^ distance) for i in range(steps)])  42.3 us
    pallas_call x2, Pallas kernels, denoise(): pl.pallas_call(functools.partial(denoise_kernel, later), out_shape=(half,...  16.9 us
    ppermute x8, starting transfers between devices, exchange(): lax.ppermute(coded(half), 'step', [(i, i ^ distance) for i in range(steps)])  14.7 us
    ppermute x2, starting transfers between devices, halos(): inner = lax.ppermute(jnp.where(even, tail, head), 'space', inner_pairs)  7.25 us
    unnamed x29, local copies, waits for them, and re-layouts  6.99 us
    psum x1, blocking collectives, local(): norm_total = lax.psum(total[0, 0], 'space')  6.36 us
  transfers between devices with their start and end apart: 12, of which 9 were waited for; matrix products, arithmetic and copies ran while one was open for 2% of the time, Pallas kernels for 0%

profile of v2, /device:TPU:0, one launch (start us, length us, event | category | flops | bytes accessed | tf_op | source)
XLA Modules:
  0.0 112.9 jit_solution(16790801364369069194)
XLA Ops:
  0.7 1.2 %bitcast_convert_fusion = bf16[64,4,640]{2,1,0:T(4,128)(2,1)S(1)} fusion(f32[1,64,4,640]{3,2,1,0:T(4,128)} %param.6), kind=kLoop, calls=%fused_computation.115 | loop fusion | flops 163840 | bytes 983040 | tf_op jit(solution)/shard_map/convert_element_type | solution.py:333
  1.9 0.1 slice_bitcast_fusion
  2.0 0.2 fusion.62
  2.2 0.4 maximum_select_fusion.1
  2.7 0.6 copy-done.9
  3.4 0.7 collective-permute-start.1
  4.0 4.4 %collective-permute-start = (bf16[32,8,160]{2,1,0:T(8,128)(2,1)S(1)}, bf16[32,8,160]{2,1,0:T(8,128)(2,1)S(1)}, u32[]{:S(2)}, u32[]{:S(2)}) collective-permute-start(bf16[32,8,160]{2,1,0:T(8,128)(2,1)S(1)} %get-tuple-element.26), channel_id=1, source_target_pairs={{0,1},{1,0},{2,3},{3,2},{4,5},{5,4},{6,7},{7,6},{8,9},{9,8},{10,11... | collective-permute-start | bytes 245768 | tf_op jit(solution)/shard_map/ppermute | solution.py:328
  8.4 0.6 copy-done.13
  9.1 0.6 fusion.64
  11.5 1.6 %copy.10.refs_3_.refs_5_ = bf16[3,256,576]{2,1,0:T(8,128)(2,1)S(1)} copy(bf16[3,256,576]{1,2,0:T(8,128)(2,1)} %param.9) | data formatting | bytes 1769472 | tf_op args[3]
  13.2 0.2 fusion.52.refs_5_.refs_7_
  13.6 0.7 copy-done.5
  14.2 1.1 copy-done.3
  15.3 0.9 copy-done.6
  16.2 8.7 %denoise.2 = (f32[17,8,640]{2,1,0:T(8,128)S(1)}, f32[17,8,640]{2,1,0:T(8,128)S(1)}) custom-call(s32[5]{0:T(128)S(1)} %stack.47.whole, f32[3]{0:T(128)S(1)} %pad_maximum_fusion.real, f32[64,4,640]{2,1,0:T(4,128)S(1)} %bitcast.63, bf16[32,8,160]{2,1,0:T(8,128)(2,1)S(1)} %copy-done.6, bf16[32,8,160]{2,1,0:T(8,128)(2,1)S(1)} %collective-permute-done.1.refs_1_, ...), custom_call_target="tpu_custom_call" | custom-call | flops 5000000000 | bytes 4000000 | tf_op jit(solution)/shard_map/denoise/pallas_call | solution.py:211
  25.0 1.6 %collective-permute-start.2 = (f16[17,8,640]{2,1,0:T(8,128)(2,1)S(1)}, f16[17,8,640]{2,1,0:T(8,128)(2,1)S(1)}, u32[]{:S(2)}, u32[]{:S(2)}) collective-permute-start(f16[17,8,640]{2,1,0:T(8,128)(2,1)S(1)} %fusion), channel_id=1, source_target_pairs={{0,4},{4,0},{8,12},{12,8},{16,20},{20,16},{24,28},{28,24},{1,5},{5... | collective-permute-start | bytes 522248 | tf_op jit(solution)/shard_map/ppermute | solution.py:289
  26.6 4.8 %collective-permute-done.2 = f16[17,8,640]{2,1,0:T(8,128)(2,1)S(1)} collective-permute-done((f16[17,8,640]{2,1,0:T(8,128)(2,1)S(1)}, f16[17,8,640]{2,1,0:T(8,128)(2,1)S(1)}, u32[]{:S(2)}, u32[]{:S(2)}) %collective-permute-start.2) | collective-permute-done | bytes 174112 | tf_op jit(solution)/shard_map/ppermute | solution.py:289
  31.5 0.1 add_select_fusion.9
  31.7 1.6 %collective-permute-start.3 = (f16[17,8,640]{2,1,0:T(8,128)(2,1)S(1)}, f16[17,8,640]{2,1,0:T(8,128)(2,1)S(1)}, u32[]{:S(2)}, u32[]{:S(2)}) collective-permute-start(f16[17,8,640]{2,1,0:T(8,128)(2,1)S(1)} %fusion.1), channel_id=1, source_target_pairs={{0,8},{4,12},{8,0},{12,4},{16,24},{20,28},{24,16},{28,20},{1,9},{5... | collective-permute-start | bytes 522248 | tf_op jit(solution)/shard_map/ppermute | solution.py:289
  33.4 3.9 %collective-permute-done.3 = f16[17,8,640]{2,1,0:T(8,128)(2,1)S(1)} collective-permute-done((f16[17,8,640]{2,1,0:T(8,128)(2,1)S(1)}, f16[17,8,640]{2,1,0:T(8,128)(2,1)S(1)}, u32[]{:S(2)}, u32[]{:S(2)}) %collective-permute-start.3) | collective-permute-done | bytes 174112 | tf_op jit(solution)/shard_map/ppermute | solution.py:289
  37.4 0.6 copy-done.7
  38.0 0.1 add_select_fusion.8
  38.2 0.8 fusion.2
  38.9 2.6 %collective-permute-start.4 = (f16[17,8,640]{2,1,0:T(8,128)(2,1)}, f16[17,8,640]{2,1,0:T(8,128)(2,1)}, u32[]{:S(2)}, u32[]{:S(2)}) collective-permute-start(f16[17,8,640]{2,1,0:T(8,128)(2,1)} %fusion.2), channel_id=1, source_target_pairs={{0,16},{4,20},{8,24},{12,28},{16,0},{20,4},{24,8},{28,12},{1,17},{... | collective-permute-start | bytes 522248 | tf_op jit(solution)/shard_map/ppermute | solution.py:289
  41.5 6.9 %collective-permute-done.4 = f16[17,8,640]{2,1,0:T(8,128)(2,1)} collective-permute-done((f16[17,8,640]{2,1,0:T(8,128)(2,1)}, f16[17,8,640]{2,1,0:T(8,128)(2,1)}, u32[]{:S(2)}, u32[]{:S(2)}) %collective-permute-start.4) | collective-permute-done | bytes 174112 | tf_op jit(solution)/shard_map/ppermute | solution.py:289
  48.5 0.9 convert_element_type.76
  49.4 1.4 %fusion.59 = (bf16[17,8,640]{2,1,0:T(8,128)(2,1)S(1)}, f32[17,8,640]{2,1,0:T(8,128)S(1)}, f32[17,8,640]{2,1,0:T(8,128)S(1)}) fusion(f32[8,640]{1,0:T(8,128)S(1)} %fusion.51, f16[17,8,640]{2,1,0:T(8,128)(2,1)S(1)} %collective-permute-done.2, pred[]{:T(512)S(6)} %eq.164, f32[8,640]{1,0:T(8,128)S(1)} %fusion.39, f16[17,8,640]{2,1,0:T(8,128)(2,1)} %collective-permute-done.4, ...), kind=kLoop, calls=%fused_computation.117 | loop fusion | flops 2611200 | bytes 1802329 | tf_op jit(solution)/shard_map/convert.3
  50.9 1.3 %collective-permute-start.5 = (f16[17,8,640]{2,1,0:T(8,128)(2,1)S(1)}, f16[17,8,640]{2,1,0:T(8,128)(2,1)S(1)}, u32[]{:S(2)}, u32[]{:S(2)}) collective-permute-start(f16[17,8,640]{2,1,0:T(8,128)(2,1)S(1)} %fusion.4), channel_id=1, source_target_pairs={{0,4},{4,0},{8,12},{12,8},{16,20},{20,16},{24,28},{28,24},{1,5},{5... | collective-permute-start | bytes 522248 | tf_op jit(solution)/shard_map/ppermute | solution.py:289
  52.3 4.1 %collective-permute-done.5 = f16[17,8,640]{2,1,0:T(8,128)(2,1)S(1)} collective-permute-done((f16[17,8,640]{2,1,0:T(8,128)(2,1)S(1)}, f16[17,8,640]{2,1,0:T(8,128)(2,1)S(1)}, u32[]{:S(2)}, u32[]{:S(2)}) %collective-permute-start.5) | collective-permute-done | bytes 174112 | tf_op jit(solution)/shard_map/ppermute | solution.py:289
  56.7 0.7 copy-done.10
  57.5 0.8 collective-permute-start.7
  58.4 2.9 %collective-permute-start.6 = (bf16[32,8,160]{2,1,0:T(8,128)(2,1)S(1)}, bf16[32,8,160]{2,1,0:T(8,128)(2,1)S(1)}, u32[]{:S(2)}, u32[]{:S(2)}) collective-permute-start(bf16[32,8,160]{2,1,0:T(8,128)(2,1)S(1)} %get-tuple-element.17), channel_id=1, source_target_pairs={{0,1},{1,0},{2,3},{3,2},{4,5},{5,4},{6,7},{7,6},{8,9},{9,8},{10,11... | collective-permute-start | bytes 245768 | tf_op jit(solution)/shard_map/ppermute | solution.py:328
  61.3 1.0 collective-permute-done.6.refs_2_
  62.2 8.3 %denoise.3 = (f32[17,8,640]{2,1,0:T(8,128)S(1)}, f32[17,8,640]{2,1,0:T(8,128)S(1)}) custom-call(s32[5]{0:T(128)S(1)} %stack.47.whole, f32[3]{0:T(128)S(1)} %pad_maximum_fusion.real, f32[64,4,640]{2,1,0:T(4,128)S(1)} %bitcast.64, f32[17,8,640]{2,1,0:T(8,128)S(1)} %get-tuple-element.28.refs_0_.other1, f32[17,8,640]{2,1,0:T(8,128)S(1)} %get-tuple-element.15.refs_1_.keep1, ...), custom_call_target="tpu_custom_call" | custom-call | flops 5000000000 | bytes 4000000 | tf_op jit(solution)/shard_map/denoise/pallas_call | solution.py:211
  70.6 1.6 %collective-permute-start.8 = (f16[17,8,640]{2,1,0:T(8,128)(2,1)S(1)}, f16[17,8,640]{2,1,0:T(8,128)(2,1)S(1)}, u32[]{:S(2)}, u32[]{:S(2)}) collective-permute-start(f16[17,8,640]{2,1,0:T(8,128)(2,1)S(1)} %fusion.5), channel_id=1, source_target_pairs={{0,4},{4,0},{8,12},{12,8},{16,20},{20,16},{24,28},{28,24},{1,5},{5... | collective-permute-start | bytes 522248 | tf_op jit(solution)/shard_map/ppermute | solution.py:289
  72.2 5.4 %collective-permute-done.8 = f16[17,8,640]{2,1,0:T(8,128)(2,1)S(1)} collective-permute-done((f16[17,8,640]{2,1,0:T(8,128)(2,1)S(1)}, f16[17,8,640]{2,1,0:T(8,128)(2,1)S(1)}, u32[]{:S(2)}, u32[]{:S(2)}) %collective-permute-start.8) | collective-permute-done | bytes 174112 | tf_op jit(solution)/shard_map/ppermute | solution.py:289
  77.7 0.2 add_select_fusion.4
  78.0 1.4 %collective-permute-start.9 = (f16[17,8,640]{2,1,0:T(8,128)(2,1)S(1)}, f16[17,8,640]{2,1,0:T(8,128)(2,1)S(1)}, u32[]{:S(2)}, u32[]{:S(2)}) collective-permute-start(f16[17,8,640]{2,1,0:T(8,128)(2,1)S(1)} %fusion.6), channel_id=1, source_target_pairs={{0,8},{4,12},{8,0},{12,4},{16,24},{20,28},{24,16},{28,20},{1,9},{5... | collective-permute-start | bytes 522248 | tf_op jit(solution)/shard_map/ppermute | solution.py:289
  79.3 5.2 %collective-permute-done.9 = f16[17,8,640]{2,1,0:T(8,128)(2,1)S(1)} collective-permute-done((f16[17,8,640]{2,1,0:T(8,128)(2,1)S(1)}, f16[17,8,640]{2,1,0:T(8,128)(2,1)S(1)}, u32[]{:S(2)}, u32[]{:S(2)}) %collective-permute-start.9) | collective-permute-done | bytes 174112 | tf_op jit(solution)/shard_map/ppermute | solution.py:289
  84.6 0.1 add_select_fusion.3
  84.9 3.0 %collective-permute-start.10 = (f16[17,8,640]{2,1,0:T(8,128)(2,1)S(1)}, f16[17,8,640]{2,1,0:T(8,128)(2,1)S(1)}, u32[]{:S(2)}, u32[]{:S(2)}) collective-permute-start(f16[17,8,640]{2,1,0:T(8,128)(2,1)S(1)} %fusion.7), channel_id=1, source_target_pairs={{0,16},{4,20},{8,24},{12,28},{16,0},{20,4},{24,8},{28,12},{1,17},{... | collective-permute-start | bytes 522248 | tf_op jit(solution)/shard_map/ppermute | solution.py:289
  87.9 8.0 %collective-permute-done.10 = f16[17,8,640]{2,1,0:T(8,128)(2,1)S(1)} collective-permute-done((f16[17,8,640]{2,1,0:T(8,128)(2,1)S(1)}, f16[17,8,640]{2,1,0:T(8,128)(2,1)S(1)}, u32[]{:S(2)}, u32[]{:S(2)}) %collective-permute-start.10) | collective-permute-done | bytes 174112 | tf_op jit(solution)/shard_map/ppermute | solution.py:289
  95.9 0.4 add_select_fusion
  96.5 1.7 %collective-permute-start.11 = (f16[17,8,640]{2,1,0:T(8,128)(2,1)S(1)}, f16[17,8,640]{2,1,0:T(8,128)(2,1)S(1)}, u32[]{:S(2)}, u32[]{:S(2)}) collective-permute-start(f16[17,8,640]{2,1,0:T(8,128)(2,1)S(1)} %fusion.9), channel_id=1, source_target_pairs={{0,4},{4,0},{8,12},{12,8},{16,20},{20,16},{24,28},{28,24},{1,5},{5... | collective-permute-start | bytes 522248 | tf_op jit(solution)/shard_map/ppermute | solution.py:289
  98.1 3.9 %collective-permute-done.11 = f16[17,8,640]{2,1,0:T(8,128)(2,1)S(1)} collective-permute-done((f16[17,8,640]{2,1,0:T(8,128)(2,1)S(1)}, f16[17,8,640]{2,1,0:T(8,128)(2,1)S(1)}, u32[]{:S(2)}, u32[]{:S(2)}) %collective-permute-start.11) | collective-permute-done | bytes 174112 | tf_op jit(solution)/shard_map/ppermute | solution.py:289
  102.2 2.0 %finish.1 = (f32[64,4,640]{2,1,0:T(4,128)}, f32[8,128]{1,0:T(8,128)S(1)}) custom-call(s32[5]{0:T(128)S(1)} %stack.47.whole, f32[3]{0:T(128)S(1)} %pad_maximum_fusion.real, f32[64,4,640]{2,1,0:T(4,128)S(1)} %bitcast.65, f32[17,8,640]{2,1,0:T(8,128)S(1)} %get-tuple-element.28.refs_0_.other1, f32[17,8,640]{2,1,0:T(8,128)S(1)} %get-tuple-element.15.refs_1_.keep1, ...), custom_call_target="tpu_custom_call" | custom-call | flops 4000000 | bytes 7000000 | tf_op jit(solution)/shard_map/finish/pallas_call | solution.py:251
  104.2 0.5 slice.126
  104.7 6.4 %psum.7 = f32[]{:T(128)} all-reduce(f32[]{:T(128)} %bitcast.35), channel_id=1, replica_groups=mesh['step'=8,'space'=4] {'space'}, use_global_device_ids=true, to_apply=%region_0.1 | all-reduce | flops 1 | bytes 8 | tf_op jit(solution)/shard_map/psum | solution.py:356
  (67 shorter events, 2.0 us)
Async XLA Ops:
  0.6 12.5 %copy-start = (f32[64,256]{1,0:T(8,128)S(1)}, f32[64,256]{1,0:T(8,128)}, u32[]{:S(2)}) copy-start(f32[64,256]{1,0:T(8,128)} %param.11) | copy-start | bytes 196612
  2.7 0.6 copy-start.9
  2.7 0.7 copy-start.11
  3.4 10.2 %collective-permute-start.1 = (bf16[32,8,160]{2,1,0:T(8,128)(2,1)S(1)}, bf16[32,8,160]{2,1,0:T(8,128)(2,1)S(1)}, u32[]{:S(2)}, u32[]{:S(2)}) collective-permute-start(bf16[32,8,160]{2,1,0:T(8,128)(2,1)S(1)} %get-tuple-element.25), channel_id=1, source_target_pairs={{1,2},{2,1},{5,6},{6,5},{9,10},{10,9},{13,14},{14,13},{17,18},{18,... | collective-permute-start | bytes 245768 | tf_op jit(solution)/shard_map/ppermute | solution.py:329
  4.0 9.5 %collective-permute-start = (bf16[32,8,160]{2,1,0:T(8,128)(2,1)S(1)}, bf16[32,8,160]{2,1,0:T(8,128)(2,1)S(1)}, u32[]{:S(2)}, u32[]{:S(2)}) collective-permute-start(bf16[32,8,160]{2,1,0:T(8,128)(2,1)S(1)} %get-tuple-element.26), channel_id=1, source_target_pairs={{0,1},{1,0},{2,3},{3,2},{4,5},{5,4},{6,7},{7,6},{8,9},{9,8},{10,11... | collective-permute-start | bytes 245768 | tf_op jit(solution)/shard_map/ppermute | solution.py:328
  8.4 0.7 copy-start.13
  11.5 2.7 %copy-start.1 = (f32[1,64,4,640]{3,2,1,0:T(4,128)S(1)}, f32[1,64,4,640]{3,2,1,0:T(4,128)}, u32[]{:S(2)}) copy-start(f32[1,64,4,640]{3,2,1,0:T(4,128)} %param.6) | copy-start | bytes 1966084
  11.5 2.7 %copy-start.2 = (bf16[3,64,2304]{2,1,0:T(8,128)(2,1)S(1)}, bf16[3,64,2304]{2,1,0:T(8,128)(2,1)}, u32[]{:S(2)}) copy-start(bf16[3,64,2304]{2,1,0:T(8,128)(2,1)} %refs_6_.1) | copy-start | bytes 2654212
  13.5 0.7 copy-start.5
  14.2 1.1 copy-start.3
  15.3 0.9 copy-start.6
  25.0 6.4 %collective-permute-start.2 = (f16[17,8,640]{2,1,0:T(8,128)(2,1)S(1)}, f16[17,8,640]{2,1,0:T(8,128)(2,1)S(1)}, u32[]{:S(2)}, u32[]{:S(2)}) collective-permute-start(f16[17,8,640]{2,1,0:T(8,128)(2,1)S(1)} %fusion), channel_id=1, source_target_pairs={{0,4},{4,0},{8,12},{12,8},{16,20},{20,16},{24,28},{28,24},{1,5},{5... | collective-permute-start | bytes 522248 | tf_op jit(solution)/shard_map/ppermute | solution.py:289
  31.7 5.6 %collective-permute-start.3 = (f16[17,8,640]{2,1,0:T(8,128)(2,1)S(1)}, f16[17,8,640]{2,1,0:T(8,128)(2,1)S(1)}, u32[]{:S(2)}, u32[]{:S(2)}) collective-permute-start(f16[17,8,640]{2,1,0:T(8,128)(2,1)S(1)} %fusion.1), channel_id=1, source_target_pairs={{0,8},{4,12},{8,0},{12,4},{16,24},{20,28},{24,16},{28,20},{1,9},{5... | collective-permute-start | bytes 522248 | tf_op jit(solution)/shard_map/ppermute | solution.py:289
  37.3 0.7 copy-start.7
  38.9 9.5 %collective-permute-start.4 = (f16[17,8,640]{2,1,0:T(8,128)(2,1)}, f16[17,8,640]{2,1,0:T(8,128)(2,1)}, u32[]{:S(2)}, u32[]{:S(2)}) collective-permute-start(f16[17,8,640]{2,1,0:T(8,128)(2,1)} %fusion.2), channel_id=1, source_target_pairs={{0,16},{4,20},{8,24},{12,28},{16,0},{20,4},{24,8},{28,12},{1,17},{... | collective-permute-start | bytes 522248 | tf_op jit(solution)/shard_map/ppermute | solution.py:289
  41.5 7.9 %copy-start.8 = (f16[17,8,640]{2,1,0:T(8,128)(2,1)S(1)}, f16[17,8,640]{2,1,0:T(8,128)(2,1)}, u32[]{:S(2)}) copy-start(f16[17,8,640]{2,1,0:T(8,128)(2,1)} %copy-done.7) | copy-start | bytes 522244
  50.9 5.5 %collective-permute-start.5 = (f16[17,8,640]{2,1,0:T(8,128)(2,1)S(1)}, f16[17,8,640]{2,1,0:T(8,128)(2,1)S(1)}, u32[]{:S(2)}, u32[]{:S(2)}) collective-permute-start(f16[17,8,640]{2,1,0:T(8,128)(2,1)S(1)} %fusion.4), channel_id=1, source_target_pairs={{0,4},{4,0},{8,12},{12,8},{16,20},{20,16},{24,28},{28,24},{1,5},{5... | collective-permute-start | bytes 522248 | tf_op jit(solution)/shard_map/ppermute | solution.py:289
  56.5 0.9 copy-start.10
  56.5 1.0 copy-start.12
  56.6 5.6 %copy-start.4 = (f32[1,64,4,640]{3,2,1,0:T(4,128)S(1)}, f32[1,64,4,640]{3,2,1,0:T(4,128)}, u32[]{:S(2)}) copy-start(f32[1,64,4,640]{3,2,1,0:T(4,128)} %param.7) | copy-start | bytes 1966084
  57.5 3.8 %collective-permute-start.7 = (bf16[32,8,160]{2,1,0:T(8,128)(2,1)S(1)}, bf16[32,8,160]{2,1,0:T(8,128)(2,1)S(1)}, u32[]{:S(2)}, u32[]{:S(2)}) collective-permute-start(bf16[32,8,160]{2,1,0:T(8,128)(2,1)S(1)} %get-tuple-element.16), channel_id=1, source_target_pairs={{1,2},{2,1},{5,6},{6,5},{9,10},{10,9},{13,14},{14,13},{17,18},{18,... | collective-permute-start | bytes 245768 | tf_op jit(solution)/shard_map/ppermute | solution.py:329
  58.4 3.9 %collective-permute-start.6 = (bf16[32,8,160]{2,1,0:T(8,128)(2,1)S(1)}, bf16[32,8,160]{2,1,0:T(8,128)(2,1)S(1)}, u32[]{:S(2)}, u32[]{:S(2)}) collective-permute-start(bf16[32,8,160]{2,1,0:T(8,128)(2,1)S(1)} %get-tuple-element.17), channel_id=1, source_target_pairs={{0,1},{1,0},{2,3},{3,2},{4,5},{5,4},{6,7},{7,6},{8,9},{9,8},{10,11... | collective-permute-start | bytes 245768 | tf_op jit(solution)/shard_map/ppermute | solution.py:328
  70.6 7.0 %collective-permute-start.8 = (f16[17,8,640]{2,1,0:T(8,128)(2,1)S(1)}, f16[17,8,640]{2,1,0:T(8,128)(2,1)S(1)}, u32[]{:S(2)}, u32[]{:S(2)}) collective-permute-start(f16[17,8,640]{2,1,0:T(8,128)(2,1)S(1)} %fusion.5), channel_id=1, source_target_pairs={{0,4},{4,0},{8,12},{12,8},{16,20},{20,16},{24,28},{28,24},{1,5},{5... | collective-permute-start | bytes 522248 | tf_op jit(solution)/shard_map/ppermute | solution.py:289
  78.0 6.6 %collective-permute-start.9 = (f16[17,8,640]{2,1,0:T(8,128)(2,1)S(1)}, f16[17,8,640]{2,1,0:T(8,128)(2,1)S(1)}, u32[]{:S(2)}, u32[]{:S(2)}) collective-permute-start(f16[17,8,640]{2,1,0:T(8,128)(2,1)S(1)} %fusion.6), channel_id=1, source_target_pairs={{0,8},{4,12},{8,0},{12,4},{16,24},{20,28},{24,16},{28,20},{1,9},{5... | collective-permute-start | bytes 522248 | tf_op jit(solution)/shard_map/ppermute | solution.py:289
  84.9 11.0 %collective-permute-start.10 = (f16[17,8,640]{2,1,0:T(8,128)(2,1)S(1)}, f16[17,8,640]{2,1,0:T(8,128)(2,1)S(1)}, u32[]{:S(2)}, u32[]{:S(2)}) collective-permute-start(f16[17,8,640]{2,1,0:T(8,128)(2,1)S(1)} %fusion.7), channel_id=1, source_target_pairs={{0,16},{4,20},{8,24},{12,28},{16,0},{20,4},{24,8},{28,12},{1,17},{... | collective-permute-start | bytes 522248 | tf_op jit(solution)/shard_map/ppermute | solution.py:289
  96.5 5.5 %collective-permute-start.11 = (f16[17,8,640]{2,1,0:T(8,128)(2,1)S(1)}, f16[17,8,640]{2,1,0:T(8,128)(2,1)S(1)}, u32[]{:S(2)}, u32[]{:S(2)}) collective-permute-start(f16[17,8,640]{2,1,0:T(8,128)(2,1)S(1)} %fusion.9), channel_id=1, source_target_pairs={{0,4},{4,0},{8,12},{12,8},{16,20},{20,16},{24,28},{28,24},{1,5},{5... | collective-permute-start | bytes 522248 | tf_op jit(solution)/shard_map/ppermute | solution.py:289

commit v3 on v2

v3 whole, which is shorter than its diff:
```python
import functools
import math

import jax
import jax.numpy as jnp
from jax import lax
from jax.experimental import pallas as pl
from jax.experimental.pallas import tpu as pltpu
from jax.sharding import PartitionSpec as P

C = 64
COLS = 80
SUB = 8
NT = (((1,), (1,)), ((), ()))
MEGA = 2**20


def plan(timestep):
    scaled = timestep.astype(jnp.float32) / 1000.0
    return -(0.1 * scaled + 9.95 * scaled * scaled)


def coefficients(timestep_pair):
    log_from = plan(timestep_pair[0])
    log_to = plan(timestep_pair[1])
    half_gap = 0.5 * (log_to - log_from)
    decay_gain = jnp.expm1(half_gap)
    remain_from = -jnp.expm1(log_from)
    remain_to = -jnp.expm1(log_to)
    ratio_term = -jnp.expm1(log_from - log_to)
    noise_gain = -jnp.exp(half_gap) * jnp.sqrt(remain_from) + remain_to * jnp.exp(
        -half_gap
    ) / jnp.sqrt(remain_from)
    spread_gain = jnp.sqrt(remain_to / remain_from * ratio_term)
    return (decay_gain, noise_gain, spread_gain)


def time_embed(timestep, time_weight):
    half_count = C // 2
    frequency = jnp.exp(-math.log(10000.0) * jnp.arange(half_count, dtype=jnp.float32) / half_count)
    angles = timestep.astype(jnp.float32) * frequency
    features = jnp.concatenate([jnp.sin(angles), jnp.cos(angles)])
    return jnp.dot(
        features, time_weight, preferred_element_type=jnp.float32, precision=lax.Precision.HIGHEST
    )


class Frames:
    def __init__(self, odd, parity):
        self.odd, self.parity = odd, parity

    def pick(self, ref, v):
        count = ref.shape[1]
        return jnp.where(self.odd, ref[:, v, :], ref[:, count - 1 - v, :])

    def slot(self, v):
        return jnp.where(self.parity == 1, v % 2, (v + 1) % 2)

    def load(self, ref, v):
        tiles = C // SUB
        return ref[pl.ds(self.slot(v) * tiles, tiles)].reshape(C, ref.shape[2])

    def store(self, ref, v, value):
        tiles = C // SUB
        ref[pl.ds(self.slot(v) * tiles, tiles)] = value.reshape(tiles, SUB, ref.shape[2])

    def tap(self, a):
        return jnp.where(self.parity == 1, a, 2 - a)


def entering_of(frames, flags, guesses, halves, v):
    start = frames.pick(guesses, v)
    if halves is None:
        return start
    other, keep = halves
    return jnp.where(flags.anchor, start, frames.load(other if v < 2 else keep, v))


class Flags:
    def __init__(self, whole, real):
        self.parity = whole[0]
        self.odd = whole[0] == 1
        self.even_block = whole[1] == 0
        self.anchor = whole[2] == 1
        self.keep, self.gain, self.spread = real[0], real[1], real[2]
        self.top, self.bottom = whole[3], whole[4]


def halo_slot(frames, v):
    tiles = C // SUB
    return pl.ds((0 if v < 2 else 2 * tiles) + frames.slot(v) * tiles, tiles)


def edges_kernel(later, whole, real, guesses, *refs):
    halves = None
    if later:
        other, keep, *refs = refs
        halves = (other, keep)
    inner, outer = refs
    flags = Flags(whole, real)
    frames = Frames(flags.odd, flags.parity)
    count, length = guesses.shape[1:]
    edge = 2 * COLS
    for v in range(count):
        latent = entering_of(frames, flags, guesses, halves, v).astype(jnp.bfloat16)
        shape = (C // SUB, SUB, edge)
        head, tail = latent[:, :edge].reshape(shape), latent[:, length - edge :].reshape(shape)
        at = halo_slot(frames, v)
        inner[at] = jnp.where(flags.even_block, tail, head)
        outer[at] = jnp.where(flags.even_block, head, tail)


class Shared:
    def __init__(self, flags, frames, halves, guesses, noise, first, second, temb, shifted, hidden):
        self.flags, self.frames, self.halves, self.guesses, self.noise = flags, frames, halves, guesses, noise
        self.first, self.second, self.temb, self.shifted, self.hidden = first, second, temb, shifted, hidden
        self.channels, self.count, self.length = guesses.shape
        self.width = temb.shape[1]
        self.extended = self.length + 2 * COLS

    def entering(self, v):
        return entering_of(self.frames, self.flags, self.guesses, self.halves, v)

    def spread_columns(self, values, at, v):
        ref, i = self.shifted[v]
        n = values.shape[1]
        column = lax.broadcasted_iota(jnp.int32, (1, n), 1) % COLS
        before = jnp.where(column >= 1, pltpu.roll(values, 1, 1), 0.0).astype(jnp.bfloat16)
        after = jnp.where(column <= COLS - 2, pltpu.roll(values, n - 1, 1), 0.0).astype(jnp.bfloat16)
        center = values.astype(jnp.bfloat16)
        ref[i, pl.ds(at, n), 0:128] = jnp.concatenate([before, center], axis=0).T
        ref[i, pl.ds(at, n), 256:384] = jnp.concatenate([center, after], axis=0).T
        mixed = jnp.concatenate([after, before], axis=0).T
        ref[i, pl.ds(at, n), 128:192] = mixed[:, :64]
        if at >= COLS:
            ref[i, pl.ds(at - COLS, n), 192:256] = mixed[:, 64:]
        else:
            ref[i, pl.ds(0, n - COLS), 192:256] = mixed[COLS:, 64:]

    def prepare(self, v, inner, outer):
        ref, i = self.shifted[v]
        ref[i, pl.ds(self.length + 3 * COLS, COLS), 128:256] = jnp.zeros((COLS, 128), jnp.bfloat16)
        at = halo_slot(self.frames, v)
        edge = 2 * COLS
        near = inner[at].astype(jnp.float32).reshape(C, edge)
        far = outer[at].astype(jnp.float32).reshape(C, edge)
        even = self.flags.even_block
        self.spread_columns(jnp.where(even, far, near), 0, v)
        self.spread_columns(self.entering(v), edge, v)
        self.spread_columns(jnp.where(even, near, far), edge + self.length, v)

    def near_frames(self, v):
        return [a for a in range(3) if 0 <= v + a - 1 < self.count]

    def first_conv(self, v):
        extended, chunk = self.extended, self.extended // 2
        top, bottom = self.flags.top == 1, self.flags.bottom == 1
        weights = []
        for a in self.near_frames(v):
            weights += [self.first[self.frames.tap(a)], jnp.zeros((64, self.width), jnp.bfloat16)]
        weights = jnp.concatenate(weights, axis=0)
        out, place_of = self.hidden[v]
        for start in range(0, extended, chunk):
            cells = []
            for a in self.near_frames(v):
                ref, i = self.shifted[v + a - 1]
                for b, low, high in ((0, 0, 256), (1, 256, 384), (2, 0, 256)):
                    cells.append(ref[i, pl.ds(b * COLS + start, chunk), low:high])
            cells = jnp.concatenate(cells, axis=1)
            value = jnp.dot(cells, weights, preferred_element_type=jnp.float32) + self.temb[...]
            active = value / (1.0 + jnp.exp(-value))
            place = start + lax.broadcasted_iota(jnp.int32, (chunk, 1), 0)
            outside = jnp.logical_or(
                jnp.logical_and(place < COLS, top), jnp.logical_and(place >= extended - COLS, bottom)
            )
            out[place_of, pl.ds(start, chunk), :] = jnp.where(outside, 0.0, active).astype(jnp.bfloat16)

    def second_conv(self, v, out):
        channels, length, width, flags = self.channels, self.length, self.width, self.flags
        cells, weights = [], []
        for a in self.near_frames(v):
            ref, i = self.hidden[v + a - 1]
            tap = self.frames.tap(a)
            for b in range(3):
                cells.append(ref[i, pl.ds(b * COLS, length), :])
                columns = [
                    self.second[tap, :, (b * 3 + e) * width : (b * 3 + e + 1) * width] for e in range(3)
                ]
                weights.append(jnp.concatenate(columns, axis=0))
        cells, weights = jnp.concatenate(cells, axis=1), jnp.concatenate(weights, axis=1)
        parts = lax.dot_general(cells, weights, NT, preferred_element_type=jnp.float32).T
        column = lax.broadcasted_iota(jnp.int32, (1, length), 1) % COLS
        before = jnp.where(column >= 1, pltpu.roll(parts[:channels], 1, 1), 0.0)
        after = jnp.where(
            column <= COLS - 2, pltpu.roll(parts[2 * channels : 3 * channels], length - 1, 1), 0.0
        )
        predicted = before + parts[channels : 2 * channels] + after
        latent = self.entering(v)
        result = flags.keep * latent + flags.gain * predicted + flags.spread * self.frames.pick(self.noise, v)
        result = result + jnp.where(flags.anchor, latent, 0.0)
        self.frames.store(out, v, result)
        return jnp.max(jnp.abs(result), axis=0, keepdims=True)

    def mark(self, ref, peaks):
        peak = jnp.max(functools.reduce(jnp.maximum, peaks), axis=1, keepdims=True)
        exponent = jnp.clip(jnp.ceil(jnp.log(peak) * (1.0 / math.log(2.0))) + 1.0, -100.0, 126.0)
        ref[ref.shape[0] - 1] = jnp.broadcast_to(exponent, (SUB, self.length))


def sending_kernel(later, whole, real, guesses, *refs):
    halves = None
    if later:
        other, keep, *refs = refs
        halves = (other, keep)
    inner, outer, noise, first, second, temb, yours, spread_out, hidden_out, spread_own, hidden_own = refs
    flags = Flags(whole, real)
    frames = Frames(flags.odd, flags.parity)
    shifted = {0: (spread_own, 0), 1: (spread_own, 1), 2: (spread_out, 0), 3: (spread_out, 1)}
    hidden = {0: (hidden_own, 0), 1: (hidden_out, 0), 2: (hidden_out, 1)}
    work = Shared(flags, frames, halves, guesses, noise, first, second, temb, shifted, hidden)
    work.prepare(0, inner, outer)
    work.prepare(1, inner, outer)
    work.first_conv(0)
    work.prepare(2, inner, outer)
    work.first_conv(1)
    work.prepare(3, inner, outer)
    peaks = [work.second_conv(0, yours)]
    work.first_conv(2)
    peaks.append(work.second_conv(1, yours))
    work.mark(yours, peaks)


def keeping_kernel(later, whole, real, guesses, *refs):
    halves = None
    if later:
        other, keep, *refs = refs
        halves = (other, keep)
    spread_in, hidden_in, noise, first, second, temb, mine, hidden_own = refs
    flags = Flags(whole, real)
    frames = Frames(flags.odd, flags.parity)
    shifted = {2: (spread_in, 0), 3: (spread_in, 1)}
    hidden = {1: (hidden_in, 0), 2: (hidden_in, 1), 3: (hidden_own, 0)}
    work = Shared(flags, frames, halves, guesses, noise, first, second, temb, shifted, hidden)
    work.first_conv(3)
    peaks = [work.second_conv(2, mine), work.second_conv(3, mine)]
    work.mark(mine, peaks)


WHOLE = pl.BlockSpec(memory_space=pltpu.VMEM)
WORDS = pl.BlockSpec(memory_space=pltpu.SMEM)


def call(kernel, name, operands, out_shape, scratch, flops):
    return pl.pallas_call(
        kernel,
        out_shape=out_shape,
        in_specs=[WORDS] * 2 + [WHOLE] * (len(operands) - 2),
        out_specs=tuple(WHOLE for _ in out_shape),
        scratch_shapes=scratch,
        compiler_params=pltpu.CompilerParams(vmem_limit_bytes=24 * MEGA),
        cost_estimate=pl.CostEstimate(flops=flops, bytes_accessed=4_000_000, transcendentals=100_000),
        name=name,
    )(*operands)


def edges(whole, real, guesses, halves):
    channels, frames, _ = guesses.shape
    shape = jax.ShapeDtypeStruct((frames * channels // SUB, SUB, 2 * COLS), jnp.bfloat16)
    operands = (whole, real, guesses) + (halves or ())
    return call(functools.partial(edges_kernel, halves is not None), "edges", operands, (shape, shape), [], 100_000)


def denoise(whole, real, guesses, halves, inner, outer, noise, first, second, temb):
    channels, frames, length = guesses.shape
    half = jax.ShapeDtypeStruct((frames // 2 * channels // SUB + 1, SUB, length), jnp.float32)
    spread = (2, length + 4 * COLS, 384)
    hidden = (2, length + 2 * COLS, temb.shape[1])
    later = halves is not None
    start = (whole, real, guesses) + (halves or ())
    yours, spread_mid, hidden_mid = call(
        functools.partial(sending_kernel, later),
        "sending",
        start + (inner, outer, noise, first, second, temb),
        (half, jax.ShapeDtypeStruct(spread, jnp.bfloat16), jax.ShapeDtypeStruct(hidden, jnp.bfloat16)),
        [pltpu.VMEM(spread, jnp.bfloat16), pltpu.VMEM((1,) + hidden[1:], jnp.bfloat16)],
        3_000_000_000,
    )
    (mine,) = call(
        functools.partial(keeping_kernel, later),
        "keeping",
        start + (spread_mid, hidden_mid, noise, first, second, temb),
        (half,),
        [pltpu.VMEM((1,) + hidden[1:], jnp.bfloat16)],
        2_000_000_000,
    )
    return yours, mine


def finish_kernel(whole, real, guesses, other, keep, yours, mine, states):
    flags = Flags(whole, real)
    count, length = guesses.shape[1:]
    tiles = C // SUB
    for frame in range(count):
        low = frame < count // 2
        at = pl.ds((frame % 2) * tiles, tiles)

        def part(first_ref, second_ref):
            one, two = first_ref[at].reshape(C, length), second_ref[at].reshape(C, length)
            return jnp.where(flags.odd, one, two) if low else jnp.where(flags.odd, two, one)

        before = jnp.where(flags.anchor, 0.0, part(other, keep))
        states[:, frame, :] = before + part(yours, mine)


def finish(whole, real, guesses, *halves):
    shape = jax.ShapeDtypeStruct(guesses.shape, jnp.float32)
    (states,) = call(finish_kernel, "finish", (whole, real, guesses) + halves, (shape,), [], 1_000_000)
    return states


def changes_kernel(whole, real, *refs):
    *sweeps, own, theirs = refs
    tiles = 2 * C // SUB

    def reached(before, term):
        return before[pl.ds(0, tiles)] + term[pl.ds(0, tiles)]

    for out, at in ((own, 0), (theirs, 2)):
        change = reached(sweeps[4 + at], sweeps[5 + at]) - reached(sweeps[at], sweeps[1 + at])
        square = jnp.sum(change * change, axis=0)
        total = jnp.sum(jnp.sum(square, axis=0, keepdims=True), axis=1, keepdims=True)
        out[...] = jnp.broadcast_to(total, out.shape)


def change_sums(whole, real, one, two):
    shape = jax.ShapeDtypeStruct((SUB, 128), jnp.float32)
    return call(changes_kernel, "changes", (whole, real) + one + two, (shape, shape), [], 1_000_000)


def is_mark(half):
    return lax.broadcasted_iota(jnp.int32, half.shape, 0) == half.shape[0] - 1


def coded(half):
    exponent = half[-1:]
    return jnp.where(is_mark(half), half, half * jnp.exp2(14.0 - exponent)).astype(jnp.float16)


def decoded(message):
    half = message.astype(jnp.float32)
    return jnp.where(is_mark(half), half, half * jnp.exp2(half[-1:] - 14.0))


def added(one, two):
    return jnp.where(is_mark(one), jnp.maximum(one, two) + 1.0, one + two)


def masked(half, condition):
    return jnp.where(condition, half, jnp.where(is_mark(half), -100.0, 0.0))


def exchange(half, distance):
    steps = lax.axis_size("step")
    return decoded(lax.ppermute(coded(half), "step", [(i, i ^ distance) for i in range(steps)]))


def prefix(yours, mine, step_index):
    steps = lax.axis_size("step")
    odd = step_index % 2 == 1
    partner = exchange(yours, 1)
    total = added(mine, partner)
    before = masked(total, False)
    distance = 2
    while distance < steps:
        got = exchange(total, distance)
        before = added(before, masked(got, (step_index // distance) % 2 == 1))
        total = added(total, got)
        distance *= 2
    keep = added(before, masked(partner, odd))
    give = added(before, masked(mine, jnp.logical_not(odd)))
    return exchange(give, 1), keep, (keep, mine, give, partner)


def local(guesses, noise, timesteps, conv_first, conv_second, time_weight):
    step_index = lax.axis_index("step")
    row_block = lax.axis_index("space")
    space = lax.axis_size("space")
    start_latent = guesses[0]
    noise_step = noise[0]
    timestep_pair = timesteps[0]
    inner_pairs = [pair for i in range(0, space - 1, 2) for pair in ((i, i + 1), (i + 1, i))]
    outer_pairs = [pair for i in range(1, space - 1, 2) for pair in ((i, i + 1), (i + 1, i))]

    real = jnp.stack(coefficients(timestep_pair))
    temb = time_embed(timestep_pair[0], time_weight).reshape(1, -1)
    whole = jnp.stack([step_index % 2, row_block % 2, step_index == 0, row_block == 0, row_block == space - 1])
    whole = whole.astype(jnp.int32)

    first = conv_first.transpose(0, 2, 1)

    def sweep(halves):
        near, far = edges(whole, real, start_latent, halves)
        inner = lax.ppermute(near, "space", inner_pairs)
        outer = lax.ppermute(far, "space", outer_pairs)
        yours, mine = denoise(
            whole, real, start_latent, halves, inner, outer, noise_step, first, conv_second, temb
        )
        return yours, mine, prefix(yours, mine, step_index)

    _, _, (other1, keep1, reached1) = sweep(None)
    yours2, mine2, (other2, keep2, reached2) = sweep((other1, keep1))
    own, theirs = change_sums(whole, real, reached1, reached2)
    total = own + lax.ppermute(theirs, "step", [(i, i ^ 1) for i in range(lax.axis_size("step"))])
    if space & (space - 1):
        total = lax.psum(total, "space")
    else:
        distance = 1
        while distance < space:
            total = total + lax.ppermute(total, "space", [(i, i ^ distance) for i in range(space)])
            distance *= 2
    states = finish(whole, real, start_latent, other2, keep2, yours2, mine2)
    cell_count = start_latent.size * space
    changes = jnp.sqrt(total[0, :1] / cell_count)
    return (states[None], changes)


def solution(mesh):
    in_specs = (
        P("step", None, None, "space"),
        P("step", None, None, "space"),
        P("step", None),
        P(),
        P(),
        P(),
    )
    out_specs = (P("step", None, None, "space"), P("step"))
    return jax.shard_map(local, mesh=mesh, in_specs=in_specs, out_specs=out_specs, check_vma=False)
```

time: 113 us -> 101 us (0.89)
  waiting for transfers between devices: 43.3 us -> 29.3 us
  starting transfers between devices: 23.5 us -> 32 us
  Pallas kernels: 18.9 us -> 25.3 us
  blocking collectives: 6.36 us -> 0 us
  other arithmetic: 7.26 us -> 3.03 us
  local copies, waits for them, and re-layouts: 8.73 us -> 6.45 us
    ppermute x8, waiting for transfers between devices: 42.3 us -> 22.9 us  [exchange(): lax.ppermute(coded(half), 'step', [(i, i ^ distance) for i in range(steps)])]
    ppermute x8, starting transfers between devices: 14.7 us -> 21.4 us  [exchange(): lax.ppermute(coded(half), 'step', [(i, i ^ distance) for i in range(steps)])]
    psum x1 -> x0, blocking collectives: 6.36 us -> none  [local(): norm_total = lax.psum(total[0, 0], 'space')]
    pallas_call x3 -> x8, Pallas kernels: 18.9 us -> 25.3 us  [call(): pl.pallas_call(kernel, out_shape=out_shape, in_specs=[WORDS] * 2 + [WHOLE...]
    ppermute x4 -> x7, waiting for transfers between devices: 0.99 us -> 6.41 us  [the longest x1 3.59 us: local(): lax.ppermute(theirs, 'step', [(i, i ^ 1) for i in range(lax.axis_size('st...]
    unnamed x29 -> x18, local copies, waits for them, and re-layouts: 6.99 us -> 4.54 us
    ppermute x4 -> x7, starting transfers between devices: 8.76 us -> 10.6 us  [the longest x2 8.38 us: local(): lax.ppermute(total, 'space', [(i, i ^ distance) for i in range(space)])]
    another operation x2 -> x0, other arithmetic: 1.47 us -> none
  transfers between devices with their start and end apart: 12 -> 15, of which waited for: 9 -> 9; matrix products, arithmetic and copies ran while one was open for 2% -> 1% of each run, Pallas kernels for 0% -> 8%
where the time goes in v3:
time: 101 us
  starting transfers between devices  32 us (32%)
  waiting for transfers between devices  29.3 us (29%)
  Pallas kernels  25.3 us (25%)
  local copies, waits for them, and re-layouts  6.45 us (6%)
  between operations  4.58 us (5%)
  other arithmetic  3.03 us (3%)
    pallas_call x8, Pallas kernels, call(): pl.pallas_call(kernel, out_shape=out_shape, in_specs=[WORDS] * 2 + [WHOLE...  25.3 us
    ppermute x8, waiting for transfers between devices, exchange(): lax.ppermute(coded(half), 'step', [(i, i ^ distance) for i in range(steps)])  22.9 us
    ppermute x8, starting transfers between devices, exchange(): lax.ppermute(coded(half), 'step', [(i, i ^ distance) for i in range(steps)])  21.4 us
    ppermute x2, starting transfers between devices, local(): lax.ppermute(total, 'space', [(i, i ^ distance) for i in range(space)])  8.38 us
    unnamed x18, local copies, waits for them, and re-layouts  4.54 us
    ppermute x1, waiting for transfers between devices, local(): lax.ppermute(theirs, 'step', [(i, i ^ 1) for i in range(lax.axis_size('st...  3.59 us
    ppermute x2, waiting for transfers between devices, local(): lax.ppermute(total, 'space', [(i, i ^ distance) for i in range(space)])  2.41 us
  transfers between devices with their start and end apart: 15, of which 9 were waited for; matrix products, arithmetic and copies ran while one was open for 1% of the time, Pallas kernels for 8%

profile of v3, /device:TPU:0, one launch (start us, length us, event | category | flops | bytes accessed | tf_op | source)
XLA Modules:
  0.0 100.8 jit_solution(11261179293580523414)
XLA Ops:
  0.7 1.3 %fusion.58 = (s32[1,1]{1,0:T(1,128)}, s32[1,1]{1,0:T(1,128)}) fusion(s32[1,2]{1,0:T(1,128)} %param.8), kind=kLoop, calls=%fused_computation.105 | loop fusion | bytes 16 | tf_op jit(solution)/shard_map/slice | solution.py:24
  3.9 1.1 %copy-done.1 = f32[1,64,4,640]{3,2,1,0:T(4,128)S(1)} copy-done((f32[1,64,4,640]{3,2,1,0:T(4,128)S(1)}, f32[1,64,4,640]{3,2,1,0:T(4,128)}, u32[]{:S(2)}) %copy-start.1) | copy-done | bytes 655384
  5.0 2.1 %edges.2 = (bf16[32,8,160]{2,1,0:T(8,128)(2,1)S(1)}, bf16[32,8,160]{2,1,0:T(8,128)(2,1)S(1)}) custom-call(s32[5]{0:T(128)S(1)} %stack.47.whole, f32[3]{0:T(128)S(1)} %pad_maximum_fusion.real, f32[64,4,640]{2,1,0:T(4,128)S(1)} %bitcast.52), custom_call_target="tpu_custom_call" | custom-call | flops 100000 | bytes 4000000 | tf_op jit(solution)/shard_map/edges/pallas_call | solution.py:254
  7.1 0.5 collective-permute-start
  7.6 0.7 collective-permute-start.1
  8.3 0.2 fusion.52.refs_5_.refs_7_
  8.6 1.2 %copy-done.3 = bf16[3,256,576]{1,2,0:T(8,128)(2,1)S(1)} copy-done((bf16[3,256,576]{1,2,0:T(8,128)(2,1)S(1)}, bf16[3,256,576]{1,2,0:T(8,128)(2,1)}, u32[]{:S(2)}) %copy-start.3) | copy-done | bytes 884760
  9.7 1.2 %copy-done.5 = bf16[3,64,2304]{2,1,0:T(8,128)(2,1)S(1)} copy-done((bf16[3,64,2304]{2,1,0:T(8,128)(2,1)S(1)}, bf16[3,64,2304]{2,1,0:T(8,128)(2,1)}, u32[]{:S(2)}) %copy-start.5) | copy-done | bytes 884760
  10.9 1.1 %copy-done.7 = f32[1,64,4,640]{3,2,1,0:T(4,128)S(1)} copy-done((f32[1,64,4,640]{3,2,1,0:T(4,128)S(1)}, f32[1,64,4,640]{3,2,1,0:T(4,128)}, u32[]{:S(2)}) %copy-start.7) | copy-done | bytes 655384
  12.0 6.5 %sending.2 = (f32[17,8,640]{2,1,0:T(8,128)S(1)}, bf16[2,960,384]{2,1,0:T(8,128)(2,1)S(1)}, bf16[2,800,256]{2,1,0:T(8,128)(2,1)S(1)}) custom-call(s32[5]{0:T(128)S(1)} %stack.47.whole, f32[3]{0:T(128)S(1)} %pad_maximum_fusion.real, f32[64,4,640]{2,1,0:T(4,128)S(1)} %bitcast.53, bf16[32,8,160]{2,1,0:T(8,128)(2,1)S(1)} %collective-permute-done.refs_0_, ...), custom_call_target="tpu_custom_call" | custom-call | flops 3000000000 | bytes 4000000 | tf_op jit(solution)/shard_map/sending/pallas_call | solution.py:254
  18.5 0.1 fusion
  18.7 2.9 %collective-permute-start.2 = (f16[17,8,640]{2,1,0:T(8,128)(2,1)S(1)}, f16[17,8,640]{2,1,0:T(8,128)(2,1)S(1)}, u32[]{:S(2)}, u32[]{:S(2)}) collective-permute-start(f16[17,8,640]{2,1,0:T(8,128)(2,1)S(1)} %fusion), channel_id=1, source_target_pairs={{0,4},{4,0},{8,12},{12,8},{16,20},{20,16},{24,28},{28,24},{1,5},{5... | collective-permute-start | bytes 522248 | tf_op jit(solution)/shard_map/ppermute | solution.py:364
  21.6 3.5 %keeping.2.refs_1_ = f32[17,8,640]{2,1,0:T(8,128)S(1)} custom-call(s32[5]{0:T(128)S(1)} %stack.47.whole, f32[3]{0:T(128)S(1)} %pad_maximum_fusion.real, f32[64,4,640]{2,1,0:T(4,128)S(1)} %bitcast.54, bf16[2,960,384]{2,1,0:T(8,128)(2,1)S(1)} %get-tuple-element.16.refs_0_, bf16[2,800,256]{2,1,0:T(8,128)(2,1)S(1)} %get-tuple-element.17.refs_1_, ...), custom_call_target="tpu_custom_call" | custom-call | flops 2000000000 | bytes 4000000 | tf_op jit(solution)/shard_map/keeping/pallas_call | solution.py:254
  25.2 0.1 multiply_select_fusion.14
  25.3 0.1 fusion.1
  25.4 2.0 %collective-permute-start.3 = (f16[17,8,640]{2,1,0:T(8,128)(2,1)S(1)}, f16[17,8,640]{2,1,0:T(8,128)(2,1)S(1)}, u32[]{:S(2)}, u32[]{:S(2)}) collective-permute-start(f16[17,8,640]{2,1,0:T(8,128)(2,1)S(1)} %fusion.1), channel_id=1, source_target_pairs={{0,8},{4,12},{8,0},{12,4},{16,24},{20,28},{24,16},{28,20},{1,9},{5... | collective-permute-start | bytes 522248 | tf_op jit(solution)/shard_map/ppermute | solution.py:364
  27.5 3.5 %collective-permute-done.3 = f16[17,8,640]{2,1,0:T(8,128)(2,1)S(1)} collective-permute-done((f16[17,8,640]{2,1,0:T(8,128)(2,1)S(1)}, f16[17,8,640]{2,1,0:T(8,128)(2,1)S(1)}, u32[]{:S(2)}, u32[]{:S(2)}) %collective-permute-start.3) | collective-permute-done | bytes 174112 | tf_op jit(solution)/shard_map/ppermute | solution.py:364
  31.0 0.1 add_select_fusion.8
  31.1 0.1 fusion.2
  31.3 3.0 %collective-permute-start.4 = (f16[17,8,640]{2,1,0:T(8,128)(2,1)S(1)}, f16[17,8,640]{2,1,0:T(8,128)(2,1)S(1)}, u32[]{:S(2)}, u32[]{:S(2)}) collective-permute-start(f16[17,8,640]{2,1,0:T(8,128)(2,1)S(1)} %fusion.2), channel_id=1, source_target_pairs={{0,16},{4,20},{8,24},{12,28},{16,0},{20,4},{24,8},{28,12},{1,17},{... | collective-permute-start | bytes 522248 | tf_op jit(solution)/shard_map/ppermute | solution.py:364
  34.3 5.6 %collective-permute-done.4 = f16[17,8,640]{2,1,0:T(8,128)(2,1)S(1)} collective-permute-done((f16[17,8,640]{2,1,0:T(8,128)(2,1)S(1)}, f16[17,8,640]{2,1,0:T(8,128)(2,1)S(1)}, u32[]{:S(2)}, u32[]{:S(2)}) %collective-permute-start.4) | collective-permute-done | bytes 174112 | tf_op jit(solution)/shard_map/ppermute | solution.py:364
  40.0 0.4 add_select_fusion.5
  40.5 0.1 fusion.4
  40.6 4.1 %collective-permute-start.5 = (f16[17,8,640]{2,1,0:T(8,128)(2,1)S(1)}, f16[17,8,640]{2,1,0:T(8,128)(2,1)S(1)}, u32[]{:S(2)}, u32[]{:S(2)}) collective-permute-start(f16[17,8,640]{2,1,0:T(8,128)(2,1)S(1)} %fusion.4), channel_id=1, source_target_pairs={{0,4},{4,0},{8,12},{12,8},{16,20},{20,16},{24,28},{28,24},{1,5},{5... | collective-permute-start | bytes 522248 | tf_op jit(solution)/shard_map/ppermute | solution.py:364
  44.7 5.0 %collective-permute-done.5 = f16[17,8,640]{2,1,0:T(8,128)(2,1)S(1)} collective-permute-done((f16[17,8,640]{2,1,0:T(8,128)(2,1)S(1)}, f16[17,8,640]{2,1,0:T(8,128)(2,1)S(1)}, u32[]{:S(2)}, u32[]{:S(2)}) %collective-permute-start.5) | collective-permute-done | bytes 174112 | tf_op jit(solution)/shard_map/ppermute | solution.py:364
  49.8 0.9 edges.3
  50.7 0.2 collective-permute-start.6
  50.9 0.8 collective-permute-start.7
  51.8 0.4 collective-permute-done.6.refs_2_
  52.1 6.2 %sending.3 = (f32[17,8,640]{2,1,0:T(8,128)S(1)}, bf16[2,960,384]{2,1,0:T(8,128)(2,1)S(1)}, bf16[2,800,256]{2,1,0:T(8,128)(2,1)S(1)}) custom-call(s32[5]{0:T(128)S(1)} %stack.47.whole, f32[3]{0:T(128)S(1)} %pad_maximum_fusion.real, f32[64,4,640]{2,1,0:T(4,128)S(1)} %bitcast.56, f32[17,8,640]{2,1,0:T(8,128)S(1)} %multiply_select_fusion.8.refs_0_, ...), custom_call_target="tpu_custom_call" | custom-call | flops 3000000000 | bytes 4000000 | tf_op jit(solution)/shard_map/sending/pallas_call | solution.py:254
  58.5 2.4 %collective-permute-start.8 = (f16[17,8,640]{2,1,0:T(8,128)(2,1)S(1)}, f16[17,8,640]{2,1,0:T(8,128)(2,1)S(1)}, u32[]{:S(2)}, u32[]{:S(2)}) collective-permute-start(f16[17,8,640]{2,1,0:T(8,128)(2,1)S(1)} %fusion.5), channel_id=1, source_target_pairs={{0,4},{4,0},{8,12},{12,8},{16,20},{20,16},{24,28},{28,24},{1,5},{5... | collective-permute-start | bytes 522248 | tf_op jit(solution)/shard_map/ppermute | solution.py:364
  60.9 3.5 %keeping.3.mine.refs_5_ = f32[17,8,640]{2,1,0:T(8,128)S(1)} custom-call(s32[5]{0:T(128)S(1)} %stack.47.whole, f32[3]{0:T(128)S(1)} %pad_maximum_fusion.real, f32[64,4,640]{2,1,0:T(4,128)S(1)} %bitcast.57, f32[17,8,640]{2,1,0:T(8,128)S(1)} %multiply_select_fusion.8.refs_0_, f32[17,8,640]{2,1,0:T(8,128)S(1)} %get-tuple-element.28.refs_1_.refs_0_, ...), custom_call_target="tpu_custom_call" | custom-call | flops 2000000000 | bytes 4000000 | tf_op jit(solution)/shard_map/keeping/pallas_call | solution.py:254
  64.4 0.1 multiply_select_fusion.6
  64.7 1.3 %collective-permute-start.9 = (f16[17,8,640]{2,1,0:T(8,128)(2,1)S(1)}, f16[17,8,640]{2,1,0:T(8,128)(2,1)S(1)}, u32[]{:S(2)}, u32[]{:S(2)}) collective-permute-start(f16[17,8,640]{2,1,0:T(8,128)(2,1)S(1)} %fusion.6), channel_id=1, source_target_pairs={{0,8},{4,12},{8,0},{12,4},{16,24},{20,28},{24,16},{28,20},{1,9},{5... | collective-permute-start | bytes 522248 | tf_op jit(solution)/shard_map/ppermute | solution.py:364
  66.0 4.2 %collective-permute-done.9 = f16[17,8,640]{2,1,0:T(8,128)(2,1)S(1)} collective-permute-done((f16[17,8,640]{2,1,0:T(8,128)(2,1)S(1)}, f16[17,8,640]{2,1,0:T(8,128)(2,1)S(1)}, u32[]{:S(2)}, u32[]{:S(2)}) %collective-permute-start.9) | collective-permute-done | bytes 174112 | tf_op jit(solution)/shard_map/ppermute | solution.py:364
  70.2 0.1 add_select_fusion.3
  70.5 2.6 %collective-permute-start.10 = (f16[17,8,640]{2,1,0:T(8,128)(2,1)S(1)}, f16[17,8,640]{2,1,0:T(8,128)(2,1)S(1)}, u32[]{:S(2)}, u32[]{:S(2)}) collective-permute-start(f16[17,8,640]{2,1,0:T(8,128)(2,1)S(1)} %fusion.7), channel_id=1, source_target_pairs={{0,16},{4,20},{8,24},{12,28},{16,0},{20,4},{24,8},{28,12},{1,17},{... | collective-permute-start | bytes 522248 | tf_op jit(solution)/shard_map/ppermute | solution.py:364
  73.1 4.7 %collective-permute-done.10 = f16[17,8,640]{2,1,0:T(8,128)(2,1)S(1)} collective-permute-done((f16[17,8,640]{2,1,0:T(8,128)(2,1)S(1)}, f16[17,8,640]{2,1,0:T(8,128)(2,1)S(1)}, u32[]{:S(2)}, u32[]{:S(2)}) %collective-permute-start.10) | collective-permute-done | bytes 174112 | tf_op jit(solution)/shard_map/ppermute | solution.py:364
  77.8 0.4 add_select_fusion
  78.4 3.0 %collective-permute-start.11 = (f16[17,8,640]{2,1,0:T(8,128)(2,1)S(1)}, f16[17,8,640]{2,1,0:T(8,128)(2,1)S(1)}, u32[]{:S(2)}, u32[]{:S(2)}) collective-permute-start(f16[17,8,640]{2,1,0:T(8,128)(2,1)S(1)} %fusion.9), channel_id=1, source_target_pairs={{0,4},{4,0},{8,12},{12,8},{16,20},{20,16},{24,28},{28,24},{1,5},{5... | collective-permute-start | bytes 522248 | tf_op jit(solution)/shard_map/ppermute | solution.py:364
  81.4 0.9 changes.1
  82.3 3.6 %collective-permute-done.12 = f32[8,128]{1,0:T(8,128)S(1)} collective-permute-done((f32[8,128]{1,0:T(8,128)S(1)}, f32[8,128]{1,0:T(8,128)S(1)}, u32[]{:S(2)}, u32[]{:S(2)}) %collective-permute-start.12) | collective-permute-done | bytes 4128 | tf_op jit(solution)/shard_map/ppermute | solution.py:413
  85.9 2.4 %collective-permute-start.13 = (f32[8,128]{1,0:T(8,128)S(1)}, f32[8,128]{1,0:T(8,128)S(1)}, u32[]{:S(2)}, u32[]{:S(2)}) collective-permute-start(f32[8,128]{1,0:T(8,128)S(1)} %add.152), channel_id=1, source_target_pairs={{0,1},{1,0},{2,3},{3,2},{4,5},{5,4},{6,7},{7,6},{8,9},{9,8},{10,11... | collective-permute-start | bytes 12296 | tf_op jit(solution)/shard_map/ppermute | solution.py:419
  88.2 0.8 collective-permute-done.13
  89.1 6.0 %collective-permute-start.14 = (f32[8,128]{1,0:T(8,128)S(1)}, f32[8,128]{1,0:T(8,128)S(1)}, u32[]{:S(2)}, u32[]{:S(2)}) collective-permute-start(f32[8,128]{1,0:T(8,128)S(1)} %add.153), channel_id=1, source_target_pairs={{0,2},{1,3},{2,0},{3,1},{4,6},{5,7},{6,4},{7,5},{8,10},{9,11},{10,... | collective-permute-start | bytes 12296 | tf_op jit(solution)/shard_map/ppermute | solution.py:419
  95.1 1.6 %collective-permute-done.14 = f32[8,128]{1,0:T(8,128)S(1)} collective-permute-done((f32[8,128]{1,0:T(8,128)S(1)}, f32[8,128]{1,0:T(8,128)S(1)}, u32[]{:S(2)}, u32[]{:S(2)}) %collective-permute-start.14) | collective-permute-done | bytes 4128 | tf_op jit(solution)/shard_map/ppermute | solution.py:419
  96.7 0.5 slice.78
  98.0 1.7 %finish.1 = f32[64,4,640]{2,1,0:T(4,128)} custom-call(s32[5]{0:T(128)S(1)} %stack.47.whole, f32[3]{0:T(128)S(1)} %pad_maximum_fusion.real, f32[64,4,640]{2,1,0:T(4,128)S(1)} %bitcast.58, f32[17,8,640]{2,1,0:T(8,128)S(1)} %multiply_select_fusion.other, f32[17,8,640]{2,1,0:T(8,128)S(1)} %get-tuple-element.26.keep.refs_4_, ...), custom_call_target="tpu_custom_call" | custom-call | flops 1000000 | bytes 4000000 | tf_op jit(solution)/shard_map/finish/pallas_call | solution.py:254
  (59 shorter events, 1.3 us)
Async XLA Ops:
  0.6 7.7 %copy-start = (f32[64,256]{1,0:T(8,128)S(1)}, f32[64,256]{1,0:T(8,128)}, u32[]{:S(2)}) copy-start(f32[64,256]{1,0:T(8,128)} %param.11) | copy-start | bytes 196612
  3.9 1.1 %copy-start.1 = (f32[1,64,4,640]{3,2,1,0:T(4,128)S(1)}, f32[1,64,4,640]{3,2,1,0:T(4,128)}, u32[]{:S(2)}) copy-start(f32[1,64,4,640]{3,2,1,0:T(4,128)} %param.6) | copy-start | bytes 1966084
  7.1 1.5 %collective-permute-start = (bf16[32,8,160]{2,1,0:T(8,128)(2,1)S(1)}, bf16[32,8,160]{2,1,0:T(8,128)(2,1)S(1)}, u32[]{:S(2)}, u32[]{:S(2)}) collective-permute-start(bf16[32,8,160]{2,1,0:T(8,128)(2,1)S(1)} %get-tuple-element.14), channel_id=1, source_target_pairs={{0,1},{1,0},{2,3},{3,2},{4,5},{5,4},{6,7},{7,6},{8,9},{9,8},{10,11... | collective-permute-start | bytes 245768 | tf_op jit(solution)/shard_map/ppermute | solution.py:403
  7.6 1.0 collective-permute-start.1
  8.6 1.2 %copy-start.3 = (bf16[3,256,576]{1,2,0:T(8,128)(2,1)S(1)}, bf16[3,256,576]{1,2,0:T(8,128)(2,1)}, u32[]{:S(2)}) copy-start(bf16[3,256,576]{1,2,0:T(8,128)(2,1)} %param.9) | copy-start | bytes 2654212
  9.7 1.2 %copy-start.5 = (bf16[3,64,2304]{2,1,0:T(8,128)(2,1)S(1)}, bf16[3,64,2304]{2,1,0:T(8,128)(2,1)}, u32[]{:S(2)}) copy-start(bf16[3,64,2304]{2,1,0:T(8,128)(2,1)} %refs_6_.3) | copy-start | bytes 2654212
  10.9 1.1 %copy-start.7 = (f32[1,64,4,640]{3,2,1,0:T(4,128)S(1)}, f32[1,64,4,640]{3,2,1,0:T(4,128)}, u32[]{:S(2)}) copy-start(f32[1,64,4,640]{3,2,1,0:T(4,128)} %param.7) | copy-start | bytes 1966084
  12.0 9.6 %copy-start.4 = (bf16[3,256,576]{1,2,0:T(8,128)(2,1)S(1)}, bf16[3,256,576]{1,2,0:T(8,128)(2,1)}, u32[]{:S(2)}) copy-start(bf16[3,256,576]{1,2,0:T(8,128)(2,1)} %param.9) | copy-start | bytes 2654212
  12.0 9.6 %copy-start.6 = (bf16[3,64,2304]{2,1,0:T(8,128)(2,1)S(1)}, bf16[3,64,2304]{2,1,0:T(8,128)(2,1)}, u32[]{:S(2)}) copy-start(bf16[3,64,2304]{2,1,0:T(8,128)(2,1)} %refs_6_.3) | copy-start | bytes 2654212
  18.7 6.4 %collective-permute-start.2 = (f16[17,8,640]{2,1,0:T(8,128)(2,1)S(1)}, f16[17,8,640]{2,1,0:T(8,128)(2,1)S(1)}, u32[]{:S(2)}, u32[]{:S(2)}) collective-permute-start(f16[17,8,640]{2,1,0:T(8,128)(2,1)S(1)} %fusion), channel_id=1, source_target_pairs={{0,4},{4,0},{8,12},{12,8},{16,20},{20,16},{24,28},{28,24},{1,5},{5... | collective-permute-start | bytes 522248 | tf_op jit(solution)/shard_map/ppermute | solution.py:364
  25.4 5.5 %collective-permute-start.3 = (f16[17,8,640]{2,1,0:T(8,128)(2,1)S(1)}, f16[17,8,640]{2,1,0:T(8,128)(2,1)S(1)}, u32[]{:S(2)}, u32[]{:S(2)}) collective-permute-start(f16[17,8,640]{2,1,0:T(8,128)(2,1)S(1)} %fusion.1), channel_id=1, source_target_pairs={{0,8},{4,12},{8,0},{12,4},{16,24},{20,28},{24,16},{28,20},{1,9},{5... | collective-permute-start | bytes 522248 | tf_op jit(solution)/shard_map/ppermute | solution.py:364
  31.3 8.7 %collective-permute-start.4 = (f16[17,8,640]{2,1,0:T(8,128)(2,1)S(1)}, f16[17,8,640]{2,1,0:T(8,128)(2,1)S(1)}, u32[]{:S(2)}, u32[]{:S(2)}) collective-permute-start(f16[17,8,640]{2,1,0:T(8,128)(2,1)S(1)} %fusion.2), channel_id=1, source_target_pairs={{0,16},{4,20},{8,24},{12,28},{16,0},{20,4},{24,8},{28,12},{1,17},{... | collective-permute-start | bytes 522248 | tf_op jit(solution)/shard_map/ppermute | solution.py:364
  40.0 9.8 %copy-start.2 = (f32[1,64,4,640]{3,2,1,0:T(4,128)S(1)}, f32[1,64,4,640]{3,2,1,0:T(4,128)}, u32[]{:S(2)}) copy-start(f32[1,64,4,640]{3,2,1,0:T(4,128)} %param.6) | copy-start | bytes 1966084
  40.5 11.7 %copy-start.8 = (f32[1,64,4,640]{3,2,1,0:T(4,128)S(1)}, f32[1,64,4,640]{3,2,1,0:T(4,128)}, u32[]{:S(2)}) copy-start(f32[1,64,4,640]{3,2,1,0:T(4,128)} %param.7) | copy-start | bytes 1966084
  40.6 9.1 %collective-permute-start.5 = (f16[17,8,640]{2,1,0:T(8,128)(2,1)S(1)}, f16[17,8,640]{2,1,0:T(8,128)(2,1)S(1)}, u32[]{:S(2)}, u32[]{:S(2)}) collective-permute-start(f16[17,8,640]{2,1,0:T(8,128)(2,1)S(1)} %fusion.4), channel_id=1, source_target_pairs={{0,4},{4,0},{8,12},{12,8},{16,20},{20,16},{24,28},{28,24},{1,5},{5... | collective-permute-start | bytes 522248 | tf_op jit(solution)/shard_map/ppermute | solution.py:364
  50.7 1.4 %collective-permute-start.6 = (bf16[32,8,160]{2,1,0:T(8,128)(2,1)S(1)}, bf16[32,8,160]{2,1,0:T(8,128)(2,1)S(1)}, u32[]{:S(2)}, u32[]{:S(2)}) collective-permute-start(bf16[32,8,160]{2,1,0:T(8,128)(2,1)S(1)} %get-tuple-element.19), channel_id=1, source_target_pairs={{0,1},{1,0},{2,3},{3,2},{4,5},{5,4},{6,7},{7,6},{8,9},{9,8},{10,11... | collective-permute-start | bytes 245768 | tf_op jit(solution)/shard_map/ppermute | solution.py:403
  50.9 1.2 %collective-permute-start.7 = (bf16[32,8,160]{2,1,0:T(8,128)(2,1)S(1)}, bf16[32,8,160]{2,1,0:T(8,128)(2,1)S(1)}, u32[]{:S(2)}, u32[]{:S(2)}) collective-permute-start(bf16[32,8,160]{2,1,0:T(8,128)(2,1)S(1)} %get-tuple-element.20), channel_id=1, source_target_pairs={{1,2},{2,1},{5,6},{6,5},{9,10},{10,9},{13,14},{14,13},{17,18},{18,... | collective-permute-start | bytes 245768 | tf_op jit(solution)/shard_map/ppermute | solution.py:404
  58.5 5.9 %collective-permute-start.8 = (f16[17,8,640]{2,1,0:T(8,128)(2,1)S(1)}, f16[17,8,640]{2,1,0:T(8,128)(2,1)S(1)}, u32[]{:S(2)}, u32[]{:S(2)}) collective-permute-start(f16[17,8,640]{2,1,0:T(8,128)(2,1)S(1)} %fusion.5), channel_id=1, source_target_pairs={{0,4},{4,0},{8,12},{12,8},{16,20},{20,16},{24,28},{28,24},{1,5},{5... | collective-permute-start | bytes 522248 | tf_op jit(solution)/shard_map/ppermute | solution.py:364
  64.7 5.5 %collective-permute-start.9 = (f16[17,8,640]{2,1,0:T(8,128)(2,1)S(1)}, f16[17,8,640]{2,1,0:T(8,128)(2,1)S(1)}, u32[]{:S(2)}, u32[]{:S(2)}) collective-permute-start(f16[17,8,640]{2,1,0:T(8,128)(2,1)S(1)} %fusion.6), channel_id=1, source_target_pairs={{0,8},{4,12},{8,0},{12,4},{16,24},{20,28},{24,16},{28,20},{1,9},{5... | collective-permute-start | bytes 522248 | tf_op jit(solution)/shard_map/ppermute | solution.py:364
  70.5 7.2 %collective-permute-start.10 = (f16[17,8,640]{2,1,0:T(8,128)(2,1)S(1)}, f16[17,8,640]{2,1,0:T(8,128)(2,1)S(1)}, u32[]{:S(2)}, u32[]{:S(2)}) collective-permute-start(f16[17,8,640]{2,1,0:T(8,128)(2,1)S(1)} %fusion.7), channel_id=1, source_target_pairs={{0,16},{4,20},{8,24},{12,28},{16,0},{20,4},{24,8},{28,12},{1,17},{... | collective-permute-start | bytes 522248 | tf_op jit(solution)/shard_map/ppermute | solution.py:364
  78.4 19.5 %collective-permute-start.11 = (f16[17,8,640]{2,1,0:T(8,128)(2,1)S(1)}, f16[17,8,640]{2,1,0:T(8,128)(2,1)S(1)}, u32[]{:S(2)}, u32[]{:S(2)}) collective-permute-start(f16[17,8,640]{2,1,0:T(8,128)(2,1)S(1)} %fusion.9), channel_id=1, source_target_pairs={{0,4},{4,0},{8,12},{12,8},{16,20},{20,16},{24,28},{28,24},{1,5},{5... | collective-permute-start | bytes 522248 | tf_op jit(solution)/shard_map/ppermute | solution.py:364
  82.3 3.6 %collective-permute-start.12 = (f32[8,128]{1,0:T(8,128)S(1)}, f32[8,128]{1,0:T(8,128)S(1)}, u32[]{:S(2)}, u32[]{:S(2)}) collective-permute-start(f32[8,128]{1,0:T(8,128)S(1)} %get-tuple-element.25), channel_id=1, source_target_pairs={{0,4},{4,0},{8,12},{12,8},{16,20},{20,16},{24,28},{28,24},{1,5},{5... | collective-permute-start | bytes 12296 | tf_op jit(solution)/shard_map/ppermute | solution.py:413
  85.9 3.2 %collective-permute-start.13 = (f32[8,128]{1,0:T(8,128)S(1)}, f32[8,128]{1,0:T(8,128)S(1)}, u32[]{:S(2)}, u32[]{:S(2)}) collective-permute-start(f32[8,128]{1,0:T(8,128)S(1)} %add.152), channel_id=1, source_target_pairs={{0,1},{1,0},{2,3},{3,2},{4,5},{5,4},{6,7},{7,6},{8,9},{9,8},{10,11... | collective-permute-start | bytes 12296 | tf_op jit(solution)/shard_map/ppermute | solution.py:419
  89.1 7.6 %collective-permute-start.14 = (f32[8,128]{1,0:T(8,128)S(1)}, f32[8,128]{1,0:T(8,128)S(1)}, u32[]{:S(2)}, u32[]{:S(2)}) collective-permute-start(f32[8,128]{1,0:T(8,128)S(1)} %add.153), channel_id=1, source_target_pairs={{0,2},{1,3},{2,0},{3,1},{4,6},{5,7},{6,4},{7,5},{8,10},{9,11},{10,... | collective-permute-start | bytes 12296 | tf_op jit(solution)/shard_map/ppermute | solution.py:419

commit v4 on v3

v4 whole, which is shorter than its diff:
```python
import functools
import math

import jax
import jax.numpy as jnp
from jax import lax
from jax.experimental import pallas as pl
from jax.experimental.pallas import tpu as pltpu
from jax.sharding import PartitionSpec as P

C = 64
COLS = 80
SUB = 8
NT = (((1,), (1,)), ((), ()))
MEGA = 2**20


def plan(timestep):
    scaled = timestep.astype(jnp.float32) / 1000.0
    return -(0.1 * scaled + 9.95 * scaled * scaled)


def coefficients(timestep_pair):
    log_from = plan(timestep_pair[0])
    log_to = plan(timestep_pair[1])
    half_gap = 0.5 * (log_to - log_from)
    decay_gain = jnp.expm1(half_gap)
    remain_from = -jnp.expm1(log_from)
    remain_to = -jnp.expm1(log_to)
    ratio_term = -jnp.expm1(log_from - log_to)
    noise_gain = -jnp.exp(half_gap) * jnp.sqrt(remain_from) + remain_to * jnp.exp(
        -half_gap
    ) / jnp.sqrt(remain_from)
    spread_gain = jnp.sqrt(remain_to / remain_from * ratio_term)
    return (decay_gain, noise_gain, spread_gain)


def time_embed(timestep, time_weight):
    half_count = C // 2
    frequency = jnp.exp(-math.log(10000.0) * jnp.arange(half_count, dtype=jnp.float32) / half_count)
    angles = timestep.astype(jnp.float32) * frequency
    features = jnp.concatenate([jnp.sin(angles), jnp.cos(angles)])
    return jnp.dot(
        features, time_weight, preferred_element_type=jnp.float32, precision=lax.Precision.HIGHEST
    )


class Frames:
    def __init__(self, odd, parity):
        self.odd, self.parity = odd, parity

    def pick(self, ref, v):
        count = ref.shape[1]
        return jnp.where(self.odd, ref[:, v, :], ref[:, count - 1 - v, :])

    def slot(self, v):
        return jnp.where(self.parity == 1, v % 2, (v + 1) % 2)

    def load(self, ref, v):
        tiles = C // SUB
        return ref[pl.ds(self.slot(v) * tiles, tiles)].reshape(C, ref.shape[2])

    def store(self, ref, v, value):
        tiles = C // SUB
        ref[pl.ds(self.slot(v) * tiles, tiles)] = value.reshape(tiles, SUB, ref.shape[2])

    def tap(self, a):
        return jnp.where(self.parity == 1, a, 2 - a)


def entering_of(frames, flags, guesses, halves, v):
    start = frames.pick(guesses, v)
    if halves is None:
        return start
    other, keep = halves
    return jnp.where(flags.anchor, start, frames.load(other if v < 2 else keep, v))


class Flags:
    def __init__(self, real=None):
        step, block = lax.axis_index("step"), lax.axis_index("space")
        self.parity = lax.rem(step, 2)
        self.odd = self.parity == 1
        self.even_block = lax.rem(block, 2) == 0
        self.anchor = step == 0
        if real is not None:
            self.keep, self.gain, self.spread = (real[i : i + 1, 0:1] for i in range(3))
        self.top, self.bottom = block == 0, block == lax.axis_size("space") - 1


def halo_slot(frames, v):
    return (0 if v < 2 else 2) + frames.slot(v)


def edges_kernel(later, *refs):
    flags = Flags()
    frames = Frames(flags.odd, flags.parity)
    edge = 2 * COLS
    if later:
        guesses, other, keep, inner, outer = refs
        count, length = guesses.shape[1:]
    else:
        low, high, inner, outer = refs
        count, wide = low.shape[1:]
    for v in range(count):
        if later:
            latent = entering_of(frames, flags, guesses, (other, keep), v)
            head, tail = latent[:, :edge], latent[:, length - edge :]
        else:
            head = frames.pick(low, v)[:, :edge]
            tail = frames.pick(high, v)[:, wide - edge :]
        head, tail = head.astype(jnp.bfloat16), tail.astype(jnp.bfloat16)
        at = halo_slot(frames, v)
        inner[at] = jnp.where(flags.even_block, tail, head)
        outer[at] = jnp.where(flags.even_block, head, tail)


def near_frames(v, count):
    return [a for a in range(3) if 0 <= v + a - 1 < count]


def spread_columns(values):
    n = values.shape[1]
    column = lax.broadcasted_iota(jnp.int32, (1, n), 1) % COLS
    before = jnp.where(column >= 1, pltpu.roll(values, 1, 1), 0.0).astype(jnp.bfloat16)
    after = jnp.where(column <= COLS - 2, pltpu.roll(values, n - 1, 1), 0.0).astype(jnp.bfloat16)
    center = values.astype(jnp.bfloat16)
    pairs = ((before, center), (after, before), (center, after))
    return [jnp.concatenate(pair, axis=0).T for pair in pairs]


def first_weights(frames, first, v, count):
    return jnp.concatenate([first[frames.tap(a)] for a in near_frames(v, count)], axis=0)


WINDOWS = ((0, 0, 256), (1, 256, 384), (2, 0, 256))


def silu(value):
    return value / (1.0 + jnp.exp(-value))


def interior_kernel(later, guesses, *refs):
    flags = Flags()
    frames = Frames(flags.odd, flags.parity)
    halves, refs = split(later, refs)
    first, temb, hidden, own, spread = refs
    count, length = guesses.shape[1:]
    edge = 2 * COLS
    inside = length - edge

    def prepare(v):
        left, mixed, right = spread_columns(entering_of(frames, flags, guesses, halves, v))
        spread[v, :, 0:128] = left
        spread[v, :, 128:192] = mixed[:, :64]
        spread[v, pl.ds(0, length - COLS), 192:256] = mixed[COLS:, 64:]
        spread[v, pl.ds(length - COLS, COLS), 192:256] = jnp.zeros((COLS, 64), jnp.bfloat16)
        spread[v, :, 256:384] = right

    prepare(0)
    prepare(1)
    for v in range(count):
        if v + 2 < count:
            prepare(v + 2)
        cells = jnp.concatenate(
            [
                spread[v + a - 1, pl.ds(b * COLS, inside), low:high]
                for a in near_frames(v, count)
                for b, low, high in WINDOWS
            ],
            axis=1,
        )
        value = jnp.dot(cells, first_weights(frames, first, v, count), preferred_element_type=jnp.float32)
        hidden[v] = silu(value + temb[...]).astype(jnp.bfloat16)
        own[v, pl.ds(0, edge), :] = spread[v, pl.ds(0, edge), :]
        own[v, pl.ds(edge, edge), :] = spread[v, pl.ds(inside, edge), :]


class Rest:
    def __init__(self, real, guesses, halves, noise, first, second, temb, inside, ends):
        self.flags = Flags(real)
        self.frames = Frames(self.flags.odd, self.flags.parity)
        self.guesses, self.halves, self.noise = guesses, halves, noise
        self.first, self.second, self.temb, self.inside, self.ends = first, second, temb, inside, ends
        self.channels, self.count, self.length = guesses.shape

    def entering(self, v):
        return entering_of(self.frames, self.flags, self.guesses, self.halves, v)

    def prepare(self, v, inner, outer, own, spread):
        edge = 2 * COLS
        at = halo_slot(self.frames, v)
        near, far = inner[at].astype(jnp.float32), outer[at].astype(jnp.float32)
        even = self.flags.even_block
        both = jnp.concatenate([jnp.where(even, far, near), jnp.where(even, near, far)], axis=1)
        left, mixed, right = spread_columns(both)
        spread[v, pl.ds(edge, 2 * edge), :] = own[v]
        for low, high, rows in ((0, 128, left), (128, 192, mixed[:, :64]), (256, 384, right)):
            spread[v, pl.ds(0, edge), low:high] = rows[:edge]
            spread[v, pl.ds(3 * edge, edge), low:high] = rows[edge:]
        spread[v, pl.ds(0, COLS), 192:256] = mixed[COLS:edge, 64:]
        spread[v, pl.ds(COLS, COLS), 192:256] = own[v, pl.ds(0, COLS), 0:64]
        spread[v, pl.ds(3 * edge - COLS, edge), 192:256] = mixed[edge:, 64:]
        spread[v, pl.ds(3 * edge + COLS, COLS), 192:256] = jnp.zeros((COLS, 64), jnp.bfloat16)

    def edge_rows(self, v, spread):
        edge = 2 * COLS
        top, bottom = self.flags.top, self.flags.bottom
        rows = []
        for group in (0, 2 * edge):
            rows.append(
                jnp.concatenate(
                    [
                        spread[v + a - 1, pl.ds(group + b * COLS, edge), low:high]
                        for a in near_frames(v, self.count)
                        for b, low, high in WINDOWS
                    ],
                    axis=1,
                )
            )
        weights = first_weights(self.frames, self.first, v, self.count)
        value = jnp.dot(jnp.concatenate(rows, axis=0), weights, preferred_element_type=jnp.float32)
        active = silu(value + self.temb[...])
        place = lax.broadcasted_iota(jnp.int32, (2 * edge, 1), 0)
        outside = jnp.logical_or(
            jnp.logical_and(place < COLS, top), jnp.logical_and(place >= 2 * edge - COLS, bottom)
        )
        ref, i = self.ends[v]
        ref[i] = jnp.where(outside, 0.0, active).astype(jnp.bfloat16)

    def second_conv(self, v, out):
        channels, length, flags = self.channels, self.length, self.flags
        width = self.temb.shape[1]
        edge = 2 * COLS
        taps = [(a, b) for a in near_frames(v, self.count) for b in range(3)]
        weights = jnp.concatenate(
            [
                jnp.concatenate(
                    [
                        self.second[self.frames.tap(a), :, (b * 3 + e) * width : (b * 3 + e + 1) * width]
                        for e in range(3)
                    ],
                    axis=0,
                )
                for a, b in taps
            ],
            axis=1,
        )
        latent, noise = self.entering(v), self.frames.pick(self.noise, v)
        base = flags.keep * latent + flags.spread * noise + jnp.where(flags.anchor, latent, 0.0)
        chunk = length // 2
        column = lax.broadcasted_iota(jnp.int32, (1, chunk), 1) % COLS
        predicted = []
        for start in range(0, length, chunk):
            cells = []
            for a, b in taps:
                ref, i = self.ends[v + a - 1]
                low, high = start + b * COLS, start + b * COLS + chunk
                rows = []
                if low < edge:
                    rows.append(ref[i, pl.ds(low, edge - low), :])
                at, end = max(low, edge), min(high, length)
                rows.append(self.inside[v + a - 1, pl.ds(at - edge, end - at), :])
                if high > length:
                    rows.append(ref[i, pl.ds(edge, high - length), :])
                cells.append(jnp.concatenate(rows, axis=0))
            cells = jnp.concatenate(cells, axis=1)
            parts = lax.dot_general(cells, weights, NT, preferred_element_type=jnp.float32).T
            before = jnp.where(column >= 1, pltpu.roll(parts[:channels], 1, 1), 0.0)
            after = jnp.where(
                column <= COLS - 2, pltpu.roll(parts[2 * channels : 3 * channels], chunk - 1, 1), 0.0
            )
            predicted.append(before + parts[channels : 2 * channels] + after)
        result = base + flags.gain * jnp.concatenate(predicted, axis=1)
        self.frames.store(out, v, result)
        return jnp.max(jnp.abs(result), axis=0, keepdims=True)

    def mark(self, ref, peaks):
        peak = jnp.max(functools.reduce(jnp.maximum, peaks), axis=1, keepdims=True)
        exponent = jnp.clip(jnp.ceil(jnp.log(peak) * (1.0 / math.log(2.0))) + 1.0, -100.0, 126.0)
        ref[ref.shape[0] - 1] = jnp.broadcast_to(exponent, (SUB, self.length))


def split(later, refs):
    return (tuple(refs[:2]), refs[2:]) if later else (None, refs)


def sending_kernel(later, real, guesses, *refs):
    halves, refs = split(later, refs)
    inner, outer, noise, first, second, temb, inside, own, yours, ends_out, ends_own, spread = refs
    ends = {0: (ends_own, 0), 1: (ends_out, 0), 2: (ends_out, 1), 3: (ends_out, 2)}
    work = Rest(real, guesses, halves, noise, first, second, temb, inside, ends)
    work.prepare(0, inner, outer, own, spread)
    work.prepare(1, inner, outer, own, spread)
    work.edge_rows(0, spread)
    work.prepare(2, inner, outer, own, spread)
    work.edge_rows(1, spread)
    peaks = [work.second_conv(0, yours)]
    work.prepare(3, inner, outer, own, spread)
    work.edge_rows(2, spread)
    peaks.append(work.second_conv(1, yours))
    work.edge_rows(3, spread)
    work.mark(yours, peaks)


def keeping_kernel(later, real, guesses, *refs):
    halves, refs = split(later, refs)
    noise, second, temb, inside, ends_in, mine = refs
    ends = {1: (ends_in, 0), 2: (ends_in, 1), 3: (ends_in, 2)}
    work = Rest(real, guesses, halves, noise, None, second, temb, inside, ends)
    work.mark(mine, [work.second_conv(2, mine), work.second_conv(3, mine)])


WHOLE = pl.BlockSpec(memory_space=pltpu.VMEM)


def call(kernel, name, arrays, out_shape, scratch=(), flops=1_000_000, limit=4):
    return pl.pallas_call(
        kernel,
        out_shape=out_shape,
        in_specs=[WHOLE] * len(arrays),
        out_specs=tuple(WHOLE for _ in out_shape),
        scratch_shapes=list(scratch),
        compiler_params=pltpu.CompilerParams(vmem_limit_bytes=limit * MEGA),
        cost_estimate=pl.CostEstimate(flops=flops, bytes_accessed=4_000_000, transcendentals=100_000),
        name=name,
    )(*arrays)


def edges(guesses, halves):
    channels, frames, length = guesses.shape
    shape = jax.ShapeDtypeStruct((frames, channels, 2 * COLS), jnp.bfloat16)
    kernel = functools.partial(edges_kernel, halves is not None)
    if halves is not None:
        return call(kernel, "edges", (guesses,) + halves, (shape, shape))
    wide = -(-2 * COLS // 128) * 128
    return call(kernel, "edges", (guesses[..., :wide], guesses[..., length - wide :]), (shape, shape))


def denoise(real, guesses, halves, inner, outer, noise, first, second, temb):
    channels, frames, length = guesses.shape
    width = temb.shape[1]
    half = jax.ShapeDtypeStruct((frames // 2 * channels // SUB + 1, SUB, length), jnp.float32)
    later = halves is not None
    start = (guesses,) + (halves or ())
    inside, own = call(
        functools.partial(interior_kernel, later),
        "interior",
        start + (first, temb),
        (
            jax.ShapeDtypeStruct((frames, length - 2 * COLS, width), jnp.bfloat16),
            jax.ShapeDtypeStruct((frames, 4 * COLS, 384), jnp.bfloat16),
        ),
        [pltpu.VMEM((frames, length, 384), jnp.bfloat16)],
        2_000_000_000,
        limit=6,
    )
    ends = (4 * COLS, width)
    yours, ends_mid = call(
        functools.partial(sending_kernel, later),
        "sending",
        (real,) + start + (inner, outer, noise, first, second, temb, inside, own),
        (half, jax.ShapeDtypeStruct((3,) + ends, jnp.bfloat16)),
        [pltpu.VMEM((1,) + ends, jnp.bfloat16), pltpu.VMEM((frames, 8 * COLS, 384), jnp.bfloat16)],
        2_000_000_000,
        limit=6,
    )
    (mine,) = call(
        functools.partial(keeping_kernel, later),
        "keeping",
        (real,) + start + (noise, second, temb, inside, ends_mid),
        (half,),
        flops=2_000_000_000,
        limit=6,
    )
    return yours, mine


def finish_kernel(other, keep, yours, mine, out, states, done):
    flags = Flags()
    channels, count, length = states.shape
    tiles = C // SUB
    group = channels // 4
    copies = []
    for at in range(0, channels, group):
        for frame in range(count):
            low = frame < count // 2
            slabs = pl.ds((frame % 2) * tiles + at // SUB, group // SUB)

            def part(first_ref, second_ref):
                one, two = first_ref[slabs].reshape(group, length), second_ref[slabs].reshape(group, length)
                return jnp.where(flags.odd, one, two) if low else jnp.where(flags.odd, two, one)

            before = jnp.where(flags.anchor, 0.0, part(other, keep))
            states[pl.ds(at, group), frame, :] = before + part(yours, mine)
        place = pl.ds(at, group)
        copies.append(pltpu.make_async_copy(states.at[place], out.at[place], done.at[len(copies)]))
        copies[-1].start()
    for copy in copies:
        copy.wait()


def finish(guesses, *halves):
    return pl.pallas_call(
        finish_kernel,
        out_shape=jax.ShapeDtypeStruct(guesses.shape, jnp.float32),
        in_specs=[WHOLE] * len(halves),
        out_specs=pl.BlockSpec(memory_space=pl.ANY),
        scratch_shapes=[pltpu.VMEM(guesses.shape, jnp.float32), pltpu.SemaphoreType.DMA((4,))],
        compiler_params=pltpu.CompilerParams(vmem_limit_bytes=4 * MEGA),
        cost_estimate=pl.CostEstimate(flops=8_000_000_000, bytes_accessed=4_000_000, transcendentals=0),
        name="finish",
    )(*halves)


def changes_kernel(*refs):
    *sweeps, sums = refs
    tiles = 2 * C // SUB

    def reached(before, term):
        return before[pl.ds(0, tiles)] + term[pl.ds(0, tiles)]

    for i, at in enumerate((0, 2)):
        change = reached(sweeps[4 + at], sweeps[5 + at]) - reached(sweeps[at], sweeps[1 + at])
        square = jnp.sum(change * change, axis=0)
        total = jnp.sum(jnp.sum(square, axis=0, keepdims=True), axis=1, keepdims=True)
        sums[i] = jnp.broadcast_to(total, sums.shape[1:])


def change_sums(one, two):
    shape = jax.ShapeDtypeStruct((2, SUB, 128), jnp.float32)
    (sums,) = call(changes_kernel, "changes", one + two, (shape,))
    return sums


def is_mark(half):
    return lax.broadcasted_iota(jnp.int32, half.shape, 0) == half.shape[0] - 1


def coded(half):
    exponent = half[-1:]
    return jnp.where(is_mark(half), half, half * jnp.exp2(14.0 - exponent)).astype(jnp.float16)


def decoded(message):
    half = message.astype(jnp.float32)
    return jnp.where(is_mark(half), half, half * jnp.exp2(half[-1:] - 14.0))


def added(one, two):
    return jnp.where(is_mark(one), jnp.maximum(one, two) + 1.0, one + two)


def masked(half, condition):
    return jnp.where(condition, half, jnp.where(is_mark(half), -100.0, 0.0))


def exchange(half, distance):
    steps = lax.axis_size("step")
    return decoded(lax.ppermute(coded(half), "step", [(i, i ^ distance) for i in range(steps)]))


def prefix(yours, mine, step_index):
    steps = lax.axis_size("step")
    odd = step_index % 2 == 1
    partner = exchange(yours, 1)
    total = added(mine, partner)
    before = masked(total, False)
    distance = 2
    while distance < steps:
        got = exchange(total, distance)
        before = added(before, masked(got, (step_index // distance) % 2 == 1))
        total = added(total, got)
        distance *= 2
    keep = added(before, masked(partner, odd))
    give = added(before, masked(mine, jnp.logical_not(odd)))
    return exchange(give, 1), keep, (keep, mine, give, partner)


def local(guesses, noise, timesteps, conv_first, conv_second, time_weight):
    step_index = lax.axis_index("step")
    row_block = lax.axis_index("space")
    space = lax.axis_size("space")
    start_latent = guesses[0]
    noise_step = noise[0]
    timestep_pair = timesteps[0]
    inner_pairs = [pair for i in range(0, space - 1, 2) for pair in ((i, i + 1), (i + 1, i))]
    outer_pairs = [pair for i in range(1, space - 1, 2) for pair in ((i, i + 1), (i + 1, i))]

    pair = lax.optimization_barrier(jnp.broadcast_to(timestep_pair[:, None], (2, 128)))
    real = jnp.stack(coefficients(pair))
    temb = time_embed(pair[0, : C // 2], time_weight).reshape(1, -1)
    first = jnp.pad(conv_first.transpose(0, 2, 1), ((0, 0), (0, C), (0, 0)))

    def sweep(halves):
        near, far = edges(start_latent, halves)
        inner = lax.ppermute(near, "space", inner_pairs)
        outer = lax.ppermute(far, "space", outer_pairs)
        yours, mine = denoise(
            real, start_latent, halves, inner, outer, noise_step, first, conv_second, temb
        )
        return yours, mine, prefix(yours, mine, step_index)

    _, _, (other1, keep1, reached1) = sweep(None)
    yours2, mine2, (other2, keep2, reached2) = sweep((other1, keep1))
    sums = change_sums(reached1, reached2)
    steps = lax.axis_size("step")
    cell_count = start_latent.size * space
    distance = 1
    while 2 * distance < space:
        sums = sums + lax.ppermute(sums, "space", [(i, i ^ distance) for i in range(space)])
        distance *= 2
    swap = [(k * space + s, (k ^ 1) * space + s) for k in range(steps) for s in range(space)]
    cross = [(k * space + s, (k ^ 1) * space + (s ^ distance)) for k in range(steps) for s in range(space)]
    far = [(i, i ^ distance) for i in range(space)]
    near_sum, other2 = lax.optimization_barrier((sums[0], other2))
    if space == 1:
        others = (lax.ppermute(sums[1], ("step", "space"), swap),)
    else:
        others = (
            lax.ppermute(sums[1], ("step", "space"), swap),
            lax.ppermute(sums[1], ("step", "space"), cross),
            lax.ppermute(near_sum, "space", far),
        )
    states = finish(start_latent, other2, keep2, yours2, mine2)
    total = functools.reduce(jnp.add, others, sums[0])
    changes = lax.optimization_barrier(jnp.sqrt(total / cell_count))[0, :1]
    return (states[None], changes)


def solution(mesh):
    in_specs = (
        P("step", None, None, "space"),
        P("step", None, None, "space"),
        P("step", None),
        P(),
        P(),
        P(),
    )
    out_specs = (P("step", None, None, "space"), P("step"))
    return jax.shard_map(local, mesh=mesh, in_specs=in_specs, out_specs=out_specs, check_vma=False)
```

time: 101 us -> 90.9 us (0.900)
  waiting for transfers between devices: 29.3 us -> 43 us
  starting transfers between devices: 32 us -> 19 us
  Pallas kernels: 25.3 us -> 21 us
  local copies, waits for them, and re-layouts: 6.45 us -> 2.64 us
  between operations: 4.58 us -> 1.11 us
    ppermute x8, waiting for transfers between devices: 22.9 us -> 40.4 us  [exchange(): lax.ppermute(coded(half), 'step', [(i, i ^ distance) for i in range(steps)])]
    ppermute x3 -> x4, starting transfers between devices: 8.4 us -> 1.09 us  [the longest x1 0.84 us: local(): lax.ppermute(sums[1], ('step', 'space'), swap)]
    ppermute x8, starting transfers between devices: 21.4 us -> 15.5 us  [exchange(): lax.ppermute(coded(half), 'step', [(i, i ^ distance) for i in range(steps)])]
    pallas_call x8 -> x10, Pallas kernels: 25.3 us -> 21 us  [the longest x9 20.1 us: call(): pl.pallas_call(kernel, out_shape=out_shape, in_specs=[WHOLE] * len(arrays...]
    unnamed x18 -> x14, local copies, waits for them, and re-layouts: 4.54 us -> 0.82 us
    ppermute x3 -> x4, waiting for transfers between devices: 6 us -> 2.6 us  [the longest x1 2.59 us: local(): lax.ppermute(near_sum, 'space', far)]
  transfers between devices with their start and end apart: 15 -> 16, of which waited for: 9 -> 9; matrix products, arithmetic and copies ran while one was open for 1% -> 1% of each run, Pallas kernels for 8% -> 12%
where the time goes in v4:
time: 90.9 us; the launch traced here: 90.7 us
  waiting for transfers between devices  43 us (47%)
  Pallas kernels  21 us (23%)
  starting transfers between devices  19 us (21%)
  other arithmetic  3.67 us (4%)
  local copies, waits for them, and re-layouts  2.64 us (3%)
  between operations  1.11 us (1%)
    ppermute x8, waiting for transfers between devices, exchange(): lax.ppermute(coded(half), 'step', [(i, i ^ distance) for i in range(steps)])  40.4 us
    pallas_call x9, Pallas kernels, call(): pl.pallas_call(kernel, out_shape=out_shape, in_specs=[WHOLE] * len(arrays...  20.1 us
    ppermute x8, starting transfers between devices, exchange(): lax.ppermute(coded(half), 'step', [(i, i ^ distance) for i in range(steps)])  15.5 us
    ppermute x1, waiting for transfers between devices, local(): lax.ppermute(near_sum, 'space', far)  2.59 us
  transfers between devices with their start and end apart: 16, of which 9 were waited for; matrix products, arithmetic and copies ran while one was open for 1% of the time, Pallas kernels for 12%

profile of v4, /device:TPU:0, one launch (start us, length us, event | category | flops | bytes accessed | tf_op | source)
XLA Modules:
  0.0 90.7 jit_solution(3173037944760250376)
XLA Ops:
  0.7 1.2 %fusion.59 = (f32[64,4,256]{2,1,0:T(4,128)S(1)}, f32[64,4,256]{2,1,0:T(4,128)S(1)}) fusion(f32[64,4,640]{2,1,0:T(4,128)} %bitcast.55), kind=kLoop, calls=%fused_computation.116 | loop fusion | bytes 1048576 | tf_op jit(solution)/shard_map/slice | solution.py:337
  1.8 1.5 %edges.2 = (bf16[4,64,160]{2,1,0:T(8,128)(2,1)S(1)}, bf16[4,64,160]{2,1,0:T(8,128)(2,1)S(1)}) custom-call(f32[64,4,256]{2,1,0:T(4,128)S(1)} %get-tuple-element.34.refs_0_, f32[64,4,256]{2,1,0:T(4,128)S(1)} %get-tuple-element.33.refs_1_), custom_call_target="tpu_custom_call" | custom-call | flops 1000000 | bytes 4000000 | tf_op jit(solution)/shard_map/edges/pallas_call | solution.py:318
  3.4 0.5 collective-permute-start
  3.9 0.8 collective-permute-start.1
  5.0 0.2 fusion.52.refs_1_.refs_5_.refs_2_.refs_3_.refs_7_.refs_4_
  5.2 0.8 copy-done.1
  6.0 2.9 %interior.2 = (bf16[4,480,256]{2,1,0:T(8,128)(2,1)S(1)}, bf16[4,320,384]{2,1,0:T(8,128)(2,1)S(1)}) custom-call(f32[64,4,640]{2,1,0:T(4,128)S(1)} %bitcast.56, bf16[3,640,256]{2,1,0:T(8,128)(2,1)S(1)} %pad.4.refs_0_.refs_3_.refs_2_.refs_5_, f32[1,256]{1,0:T(1,128)S(1)} %fusion.52.refs_1_.refs_5_.refs_2_.refs_3_.refs_7_.refs_4_), custom_call_target="tpu_custom_call" | custom-call | flops 2000000000 | bytes 4000000 | tf_op jit(solution)/shard_map/interior/pallas_call | solution.py:318
  9.0 3.8 %sending.2 = (f32[17,8,640]{2,1,0:T(8,128)S(1)}, bf16[3,320,256]{2,1,0:T(8,128)(2,1)S(1)}) custom-call(f32[3,128]{1,0:T(4,128)S(1)} %pad_maximum_fusion.real, f32[64,4,640]{2,1,0:T(4,128)S(1)} %bitcast.57, bf16[4,64,160]{2,1,0:T(8,128)(2,1)S(1)} %collective-permute-done.refs_0_, bf16[4,64,160]{2,1,0:T(8,128)(2,1)S(1)} %collective-permute-done.1.refs_1_, ...), custom_call_target="tpu_custom_call" | custom-call | flops 2000000000 | bytes 4000000 | tf_op jit(solution)/shard_map/sending/pallas_call | solution.py:318
  12.8 0.1 fusion
  12.9 2.5 %collective-permute-start.2 = (f16[17,8,640]{2,1,0:T(8,128)(2,1)S(1)}, f16[17,8,640]{2,1,0:T(8,128)(2,1)S(1)}, u32[]{:S(2)}, u32[]{:S(2)}) collective-permute-start(f16[17,8,640]{2,1,0:T(8,128)(2,1)S(1)} %fusion), channel_id=1, source_target_pairs={{0,4},{4,0},{8,12},{12,8},{16,20},{20,16},{24,28},{28,24},{1,5},{5... | collective-permute-start | bytes 522248 | tf_op jit(solution)/shard_map/ppermute | solution.py:460
  15.4 2.3 %keeping.2.refs_1_ = f32[17,8,640]{2,1,0:T(8,128)S(1)} custom-call(f32[3,128]{1,0:T(4,128)S(1)} %pad_maximum_fusion.real, f32[64,4,640]{2,1,0:T(4,128)S(1)} %bitcast.58, f32[64,4,640]{2,1,0:T(4,128)S(1)} %bitcast.64, bf16[3,64,2304]{2,1,0:T(8,128)(2,1)S(1)} %copy-done.2, f32[1,256]{1,0:T(1,128)S(1)} %fusion.52.refs_1_.refs_5_.refs_2_.refs_3_.refs_7_.refs_4_, ...), custom_call_target="tpu_custom_call" | custom-call | flops 2000000000 | bytes 4000000 | tf_op jit(solution)/shard_map/keeping/pallas_call | solution.py:318
  17.7 1.1 %collective-permute-done.2 = f16[17,8,640]{2,1,0:T(8,128)(2,1)S(1)} collective-permute-done((f16[17,8,640]{2,1,0:T(8,128)(2,1)S(1)}, f16[17,8,640]{2,1,0:T(8,128)(2,1)S(1)}, u32[]{:S(2)}, u32[]{:S(2)}) %collective-permute-start.2) | collective-permute-done | bytes 174112 | tf_op jit(solution)/shard_map/ppermute | solution.py:460
  18.9 0.1 add_select_fusion.9
  19.0 0.1 fusion.1
  19.1 2.1 %collective-permute-start.3 = (f16[17,8,640]{2,1,0:T(8,128)(2,1)S(1)}, f16[17,8,640]{2,1,0:T(8,128)(2,1)S(1)}, u32[]{:S(2)}, u32[]{:S(2)}) collective-permute-start(f16[17,8,640]{2,1,0:T(8,128)(2,1)S(1)} %fusion.1), channel_id=1, source_target_pairs={{0,8},{4,12},{8,0},{12,4},{16,24},{20,28},{24,16},{28,20},{1,9},{5... | collective-permute-start | bytes 522248 | tf_op jit(solution)/shard_map/ppermute | solution.py:460
  21.3 4.1 %collective-permute-done.3 = f16[17,8,640]{2,1,0:T(8,128)(2,1)S(1)} collective-permute-done((f16[17,8,640]{2,1,0:T(8,128)(2,1)S(1)}, f16[17,8,640]{2,1,0:T(8,128)(2,1)S(1)}, u32[]{:S(2)}, u32[]{:S(2)}) %collective-permute-start.3) | collective-permute-done | bytes 174112 | tf_op jit(solution)/shard_map/ppermute | solution.py:460
  25.4 0.1 add_select_fusion.8
  25.6 0.8 fusion.2
  26.4 3.5 %collective-permute-start.4 = (f16[17,8,640]{2,1,0:T(8,128)(2,1)}, f16[17,8,640]{2,1,0:T(8,128)(2,1)S(1)}, u32[]{:S(2)}, u32[]{:S(2)}) collective-permute-start(f16[17,8,640]{2,1,0:T(8,128)(2,1)} %fusion.2), channel_id=1, source_target_pairs={{0,16},{4,20},{8,24},{12,28},{16,0},{20,4},{24,8},{28,12},{1,17},{... | collective-permute-start | bytes 522248 | tf_op jit(solution)/shard_map/ppermute | solution.py:460
  29.9 9.0 %collective-permute-done.4 = f16[17,8,640]{2,1,0:T(8,128)(2,1)S(1)} collective-permute-done((f16[17,8,640]{2,1,0:T(8,128)(2,1)}, f16[17,8,640]{2,1,0:T(8,128)(2,1)S(1)}, u32[]{:S(2)}, u32[]{:S(2)}) %collective-permute-start.4) | collective-permute-done | bytes 174112 | tf_op jit(solution)/shard_map/ppermute | solution.py:460
  39.0 0.4 add_select_fusion.5
  39.4 0.1 fusion.4
  39.5 1.6 %collective-permute-start.5 = (f16[17,8,640]{2,1,0:T(8,128)(2,1)S(1)}, f16[17,8,640]{2,1,0:T(8,128)(2,1)S(1)}, u32[]{:S(2)}, u32[]{:S(2)}) collective-permute-start(f16[17,8,640]{2,1,0:T(8,128)(2,1)S(1)} %fusion.4), channel_id=1, source_target_pairs={{0,4},{4,0},{8,12},{12,8},{16,20},{20,16},{24,28},{28,24},{1,5},{5... | collective-permute-start | bytes 522248 | tf_op jit(solution)/shard_map/ppermute | solution.py:460
  41.2 4.7 %collective-permute-done.5 = f16[17,8,640]{2,1,0:T(8,128)(2,1)S(1)} collective-permute-done((f16[17,8,640]{2,1,0:T(8,128)(2,1)S(1)}, f16[17,8,640]{2,1,0:T(8,128)(2,1)S(1)}, u32[]{:S(2)}, u32[]{:S(2)}) %collective-permute-start.5) | collective-permute-done | bytes 174112 | tf_op jit(solution)/shard_map/ppermute | solution.py:460
  46.0 0.4 edges.3
  46.5 1.0 %collective-permute-start.7 = (bf16[4,64,160]{2,1,0:T(8,128)(2,1)S(1)}, bf16[4,64,160]{2,1,0:T(8,128)(2,1)S(1)}, u32[]{:S(2)}, u32[]{:S(2)}) collective-permute-start(bf16[4,64,160]{2,1,0:T(8,128)(2,1)S(1)} %get-tuple-element.24), channel_id=1, source_target_pairs={{1,2},{2,1},{5,6},{6,5},{9,10},{10,9},{13,14},{14,13},{17,18},{18,... | collective-permute-start | bytes 245768 | tf_op jit(solution)/shard_map/ppermute | solution.py:498
  47.5 2.5 %interior.3 = (bf16[4,480,256]{2,1,0:T(8,128)(2,1)S(1)}, bf16[4,320,384]{2,1,0:T(8,128)(2,1)S(1)}) custom-call(f32[64,4,640]{2,1,0:T(4,128)S(1)} %bitcast.60, f32[17,8,640]{2,1,0:T(8,128)S(1)} %multiply_select_fusion.8.refs_0_.refs_1_, f32[17,8,640]{2,1,0:T(8,128)S(1)} %get-tuple-element.38.refs_1_.refs_2_.refs_0_, ...), custom_call_target="tpu_custom_call" | custom-call | flops 2000000000 | bytes 4000000 | tf_op jit(solution)/shard_map/interior/pallas_call | solution.py:318
  50.0 3.9 %sending.3 = (f32[17,8,640]{2,1,0:T(8,128)S(1)}, bf16[3,320,256]{2,1,0:T(8,128)(2,1)S(1)}) custom-call(f32[3,128]{1,0:T(4,128)S(1)} %pad_maximum_fusion.real, f32[64,4,640]{2,1,0:T(4,128)S(1)} %bitcast.61, f32[17,8,640]{2,1,0:T(8,128)S(1)} %multiply_select_fusion.8.refs_0_.refs_1_, f32[17,8,640]{2,1,0:T(8,128)S(1)} %get-tuple-element.38.refs_1_.refs_2_.refs_0_, ...), custom_call_target="tpu_custom_call" | custom-call | flops 2000000000 | bytes 4000000 | tf_op jit(solution)/shard_map/sending/pallas_call | solution.py:318
  54.1 1.4 %collective-permute-start.8 = (f16[17,8,640]{2,1,0:T(8,128)(2,1)S(1)}, f16[17,8,640]{2,1,0:T(8,128)(2,1)S(1)}, u32[]{:S(2)}, u32[]{:S(2)}) collective-permute-start(f16[17,8,640]{2,1,0:T(8,128)(2,1)S(1)} %fusion.5), channel_id=1, source_target_pairs={{0,4},{4,0},{8,12},{12,8},{16,20},{20,16},{24,28},{28,24},{1,5},{5... | collective-permute-start | bytes 522248 | tf_op jit(solution)/shard_map/ppermute | solution.py:460
  55.5 2.4 %keeping.3.refs_5_.mine = f32[17,8,640]{2,1,0:T(8,128)S(1)} custom-call(f32[3,128]{1,0:T(4,128)S(1)} %pad_maximum_fusion.real, f32[64,4,640]{2,1,0:T(4,128)S(1)} %bitcast.62, f32[17,8,640]{2,1,0:T(8,128)S(1)} %multiply_select_fusion.8.refs_0_.refs_1_, f32[17,8,640]{2,1,0:T(8,128)S(1)} %get-tuple-element.38.refs_1_.refs_2_.refs_0_, ...), custom_call_target="tpu_custom_call" | custom-call | flops 2000000000 | bytes 4000000 | tf_op jit(solution)/shard_map/keeping/pallas_call | solution.py:318
  57.9 1.7 %collective-permute-done.8 = f16[17,8,640]{2,1,0:T(8,128)(2,1)S(1)} collective-permute-done((f16[17,8,640]{2,1,0:T(8,128)(2,1)S(1)}, f16[17,8,640]{2,1,0:T(8,128)(2,1)S(1)}, u32[]{:S(2)}, u32[]{:S(2)}) %collective-permute-start.8) | collective-permute-done | bytes 174112 | tf_op jit(solution)/shard_map/ppermute | solution.py:460
  59.6 0.1 add_select_fusion.4
  59.8 0.1 fusion.6
  59.9 1.0 %collective-permute-start.9 = (f16[17,8,640]{2,1,0:T(8,128)(2,1)S(1)}, f16[17,8,640]{2,1,0:T(8,128)(2,1)S(1)}, u32[]{:S(2)}, u32[]{:S(2)}) collective-permute-start(f16[17,8,640]{2,1,0:T(8,128)(2,1)S(1)} %fusion.6), channel_id=1, source_target_pairs={{0,8},{4,12},{8,0},{12,4},{16,24},{20,28},{24,16},{28,20},{1,9},{5... | collective-permute-start | bytes 522248 | tf_op jit(solution)/shard_map/ppermute | solution.py:460
  61.0 5.1 %collective-permute-done.9 = f16[17,8,640]{2,1,0:T(8,128)(2,1)S(1)} collective-permute-done((f16[17,8,640]{2,1,0:T(8,128)(2,1)S(1)}, f16[17,8,640]{2,1,0:T(8,128)(2,1)S(1)}, u32[]{:S(2)}, u32[]{:S(2)}) %collective-permute-start.9) | collective-permute-done | bytes 174112 | tf_op jit(solution)/shard_map/ppermute | solution.py:460
  66.1 0.1 add_select_fusion.3
  66.3 0.1 fusion.7
  66.4 1.9 %collective-permute-start.10 = (f16[17,8,640]{2,1,0:T(8,128)(2,1)S(1)}, f16[17,8,640]{2,1,0:T(8,128)(2,1)S(1)}, u32[]{:S(2)}, u32[]{:S(2)}) collective-permute-start(f16[17,8,640]{2,1,0:T(8,128)(2,1)S(1)} %fusion.7), channel_id=1, source_target_pairs={{0,16},{4,20},{8,24},{12,28},{16,0},{20,4},{24,8},{28,12},{1,17},{... | collective-permute-start | bytes 522248 | tf_op jit(solution)/shard_map/ppermute | solution.py:460
  68.3 10.0 %collective-permute-done.10 = f16[17,8,640]{2,1,0:T(8,128)(2,1)S(1)} collective-permute-done((f16[17,8,640]{2,1,0:T(8,128)(2,1)S(1)}, f16[17,8,640]{2,1,0:T(8,128)(2,1)S(1)}, u32[]{:S(2)}, u32[]{:S(2)}) %collective-permute-start.10) | collective-permute-done | bytes 174112 | tf_op jit(solution)/shard_map/ppermute | solution.py:460
  78.4 0.4 add_select_fusion
  78.8 0.3 changes.1
  79.2 0.1 collective-permute-start.11
  79.4 1.4 %collective-permute-start.12 = (f16[17,8,640]{2,1,0:T(8,128)(2,1)S(1)}, f16[17,8,640]{2,1,0:T(8,128)(2,1)S(1)}, u32[]{:S(2)}, u32[]{:S(2)}) collective-permute-start(f16[17,8,640]{2,1,0:T(8,128)(2,1)S(1)} %fusion.9), channel_id=1, source_target_pairs={{0,4},{4,0},{8,12},{12,8},{16,20},{20,16},{24,28},{28,24},{1,5},{5... | collective-permute-start | bytes 522248 | tf_op jit(solution)/shard_map/ppermute | solution.py:460
  80.8 0.8 collective-permute-start.13
  81.7 4.6 %collective-permute-done.12 = f16[17,8,640]{2,1,0:T(8,128)(2,1)S(1)} collective-permute-done((f16[17,8,640]{2,1,0:T(8,128)(2,1)S(1)}, f16[17,8,640]{2,1,0:T(8,128)(2,1)S(1)}, u32[]{:S(2)}, u32[]{:S(2)}) %collective-permute-start.12) | collective-permute-done | bytes 174112 | tf_op jit(solution)/shard_map/ppermute | solution.py:460
  86.5 1.0 %finish.1 = f32[64,4,640]{2,1,0:T(4,128)} custom-call(f32[17,8,640]{2,1,0:T(8,128)S(1)} %multiply_select_fusion.other, f32[17,8,640]{2,1,0:T(8,128)S(1)} %get-tuple-element.36.refs_4_.keep, f32[17,8,640]{2,1,0:T(8,128)S(1)} %get-tuple-element.27.yours, f32[17,8,640]{2,1,0:T(8,128)S(1)} %keeping.3.refs_5_.mine), custom_call_target="tpu_custom_call" | custom-call | flops 8000000000 | bytes 4000000 | tf_op jit(solution)/shard_map/finish/pallas_call | solution.py:404
  87.5 2.6 %collective-permute-done.15 = f32[8,128]{1,0:T(8,128)S(1)} collective-permute-done((f32[8,128]{1,0:T(8,128)S(1)}, f32[8,128]{1,0:T(8,128)S(1)}, u32[]{:S(2)}, u32[]{:S(2)}) %collective-permute-start.15) | collective-permute-done | bytes 4128 | tf_op jit(solution)/shard_map/ppermute | solution.py:523
  90.2 0.5 slice.97
  (62 shorter events, 1.3 us)
Async XLA Ops:
  0.6 4.3 %copy-start = (f32[64,256]{1,0:T(8,128)S(1)}, f32[64,256]{1,0:T(8,128)}, u32[]{:S(2)}) copy-start(f32[64,256]{1,0:T(8,128)} %param.11) | copy-start | bytes 196612
  0.6 4.2 %copy-start.5 = (bf16[3,256,576]{1,2,0:T(8,128)(2,1)S(1)}, bf16[3,256,576]{1,2,0:T(8,128)(2,1)}, u32[]{:S(2)}) copy-start(bf16[3,256,576]{1,2,0:T(8,128)(2,1)} %param.9) | copy-start | bytes 2654212
  3.4 5.6 %collective-permute-start = (bf16[4,64,160]{2,1,0:T(8,128)(2,1)S(1)}, bf16[4,64,160]{2,1,0:T(8,128)(2,1)S(1)}, u32[]{:S(2)}, u32[]{:S(2)}) collective-permute-start(bf16[4,64,160]{2,1,0:T(8,128)(2,1)S(1)} %get-tuple-element.17), channel_id=1, source_target_pairs={{0,1},{1,0},{2,3},{3,2},{4,5},{5,4},{6,7},{7,6},{8,9},{9,8},{10,11... | collective-permute-start | bytes 245768 | tf_op jit(solution)/shard_map/ppermute | solution.py:497
  3.9 0.8 copy-start.6
  3.9 5.1 %collective-permute-start.1 = (bf16[4,64,160]{2,1,0:T(8,128)(2,1)S(1)}, bf16[4,64,160]{2,1,0:T(8,128)(2,1)S(1)}, u32[]{:S(2)}, u32[]{:S(2)}) collective-permute-start(bf16[4,64,160]{2,1,0:T(8,128)(2,1)S(1)} %get-tuple-element.18), channel_id=1, source_target_pairs={{1,2},{2,1},{5,6},{6,5},{9,10},{10,9},{13,14},{14,13},{17,18},{18,... | collective-permute-start | bytes 245768 | tf_op jit(solution)/shard_map/ppermute | solution.py:498
  4.9 1.1 %copy-start.1 = (f32[1,64,4,640]{3,2,1,0:T(4,128)S(1)}, f32[1,64,4,640]{3,2,1,0:T(4,128)}, u32[]{:S(2)}) copy-start(f32[1,64,4,640]{3,2,1,0:T(4,128)} %param.6) | copy-start | bytes 1966084
  6.0 3.0 %copy-start.2 = (bf16[3,64,2304]{2,1,0:T(8,128)(2,1)S(1)}, bf16[3,64,2304]{2,1,0:T(8,128)(2,1)}, u32[]{:S(2)}) copy-start(bf16[3,64,2304]{2,1,0:T(8,128)(2,1)} %refs_3_.1) | copy-start | bytes 2654212
  6.0 3.0 %copy-start.3 = (f32[1,64,4,640]{3,2,1,0:T(4,128)S(1)}, f32[1,64,4,640]{3,2,1,0:T(4,128)}, u32[]{:S(2)}) copy-start(f32[1,64,4,640]{3,2,1,0:T(4,128)} %param.7) | copy-start | bytes 1966084
  12.9 5.9 %collective-permute-start.2 = (f16[17,8,640]{2,1,0:T(8,128)(2,1)S(1)}, f16[17,8,640]{2,1,0:T(8,128)(2,1)S(1)}, u32[]{:S(2)}, u32[]{:S(2)}) collective-permute-start(f16[17,8,640]{2,1,0:T(8,128)(2,1)S(1)} %fusion), channel_id=1, source_target_pairs={{0,4},{4,0},{8,12},{12,8},{16,20},{20,16},{24,28},{28,24},{1,5},{5... | collective-permute-start | bytes 522248 | tf_op jit(solution)/shard_map/ppermute | solution.py:460
  19.1 6.3 %collective-permute-start.3 = (f16[17,8,640]{2,1,0:T(8,128)(2,1)S(1)}, f16[17,8,640]{2,1,0:T(8,128)(2,1)S(1)}, u32[]{:S(2)}, u32[]{:S(2)}) collective-permute-start(f16[17,8,640]{2,1,0:T(8,128)(2,1)S(1)} %fusion.1), channel_id=1, source_target_pairs={{0,8},{4,12},{8,0},{12,4},{16,24},{20,28},{24,16},{28,20},{1,9},{5... | collective-permute-start | bytes 522248 | tf_op jit(solution)/shard_map/ppermute | solution.py:460
  26.4 12.5 %collective-permute-start.4 = (f16[17,8,640]{2,1,0:T(8,128)(2,1)}, f16[17,8,640]{2,1,0:T(8,128)(2,1)S(1)}, u32[]{:S(2)}, u32[]{:S(2)}) collective-permute-start(f16[17,8,640]{2,1,0:T(8,128)(2,1)} %fusion.2), channel_id=1, source_target_pairs={{0,16},{4,20},{8,24},{12,28},{16,0},{20,4},{24,8},{28,12},{1,17},{... | collective-permute-start | bytes 522248 | tf_op jit(solution)/shard_map/ppermute | solution.py:460
  39.5 6.3 %collective-permute-start.5 = (f16[17,8,640]{2,1,0:T(8,128)(2,1)S(1)}, f16[17,8,640]{2,1,0:T(8,128)(2,1)S(1)}, u32[]{:S(2)}, u32[]{:S(2)}) collective-permute-start(f16[17,8,640]{2,1,0:T(8,128)(2,1)S(1)} %fusion.4), channel_id=1, source_target_pairs={{0,4},{4,0},{8,12},{12,8},{16,20},{20,16},{24,28},{28,24},{1,5},{5... | collective-permute-start | bytes 522248 | tf_op jit(solution)/shard_map/ppermute | solution.py:460
  46.4 3.6 %collective-permute-start.6 = (bf16[4,64,160]{2,1,0:T(8,128)(2,1)S(1)}, bf16[4,64,160]{2,1,0:T(8,128)(2,1)S(1)}, u32[]{:S(2)}, u32[]{:S(2)}) collective-permute-start(bf16[4,64,160]{2,1,0:T(8,128)(2,1)S(1)} %get-tuple-element.23), channel_id=1, source_target_pairs={{0,1},{1,0},{2,3},{3,2},{4,5},{5,4},{6,7},{7,6},{8,9},{9,8},{10,11... | collective-permute-start | bytes 245768 | tf_op jit(solution)/shard_map/ppermute | solution.py:497
  46.5 3.6 %copy-start.4 = (f32[1,64,4,640]{3,2,1,0:T(4,128)S(1)}, f32[1,64,4,640]{3,2,1,0:T(4,128)}, u32[]{:S(2)}) copy-start(f32[1,64,4,640]{3,2,1,0:T(4,128)} %param.7) | copy-start | bytes 1966084
  46.5 3.6 %collective-permute-start.7 = (bf16[4,64,160]{2,1,0:T(8,128)(2,1)S(1)}, bf16[4,64,160]{2,1,0:T(8,128)(2,1)S(1)}, u32[]{:S(2)}, u32[]{:S(2)}) collective-permute-start(bf16[4,64,160]{2,1,0:T(8,128)(2,1)S(1)} %get-tuple-element.24), channel_id=1, source_target_pairs={{1,2},{2,1},{5,6},{6,5},{9,10},{10,9},{13,14},{14,13},{17,18},{18,... | collective-permute-start | bytes 245768 | tf_op jit(solution)/shard_map/ppermute | solution.py:498
  54.1 5.5 %collective-permute-start.8 = (f16[17,8,640]{2,1,0:T(8,128)(2,1)S(1)}, f16[17,8,640]{2,1,0:T(8,128)(2,1)S(1)}, u32[]{:S(2)}, u32[]{:S(2)}) collective-permute-start(f16[17,8,640]{2,1,0:T(8,128)(2,1)S(1)} %fusion.5), channel_id=1, source_target_pairs={{0,4},{4,0},{8,12},{12,8},{16,20},{20,16},{24,28},{28,24},{1,5},{5... | collective-permute-start | bytes 522248 | tf_op jit(solution)/shard_map/ppermute | solution.py:460
  59.9 6.2 %collective-permute-start.9 = (f16[17,8,640]{2,1,0:T(8,128)(2,1)S(1)}, f16[17,8,640]{2,1,0:T(8,128)(2,1)S(1)}, u32[]{:S(2)}, u32[]{:S(2)}) collective-permute-start(f16[17,8,640]{2,1,0:T(8,128)(2,1)S(1)} %fusion.6), channel_id=1, source_target_pairs={{0,8},{4,12},{8,0},{12,4},{16,24},{20,28},{24,16},{28,20},{1,9},{5... | collective-permute-start | bytes 522248 | tf_op jit(solution)/shard_map/ppermute | solution.py:460
  66.4 11.9 %collective-permute-start.10 = (f16[17,8,640]{2,1,0:T(8,128)(2,1)S(1)}, f16[17,8,640]{2,1,0:T(8,128)(2,1)S(1)}, u32[]{:S(2)}, u32[]{:S(2)}) collective-permute-start(f16[17,8,640]{2,1,0:T(8,128)(2,1)S(1)} %fusion.7), channel_id=1, source_target_pairs={{0,16},{4,20},{8,24},{12,28},{16,0},{20,4},{24,8},{28,12},{1,17},{... | collective-permute-start | bytes 522248 | tf_op jit(solution)/shard_map/ppermute | solution.py:460
  79.2 1.6 %collective-permute-start.11 = (f32[2,8,128]{2,1,0:T(8,128)S(1)}, f32[2,8,128]{2,1,0:T(8,128)S(1)}, u32[]{:S(2)}, u32[]{:S(2)}) collective-permute-start(f32[2,8,128]{2,1,0:T(8,128)S(1)} %changes.1), channel_id=1, source_target_pairs={{0,1},{1,0},{2,3},{3,2},{4,5},{5,4},{6,7},{7,6},{8,9},{9,8},{10,11... | collective-permute-start | bytes 24584 | tf_op jit(solution)/shard_map/ppermute | solution.py:511
  79.4 6.9 %collective-permute-start.12 = (f16[17,8,640]{2,1,0:T(8,128)(2,1)S(1)}, f16[17,8,640]{2,1,0:T(8,128)(2,1)S(1)}, u32[]{:S(2)}, u32[]{:S(2)}) collective-permute-start(f16[17,8,640]{2,1,0:T(8,128)(2,1)S(1)} %fusion.9), channel_id=1, source_target_pairs={{0,4},{4,0},{8,12},{12,8},{16,20},{20,16},{24,28},{28,24},{1,5},{5... | collective-permute-start | bytes 522248 | tf_op jit(solution)/shard_map/ppermute | solution.py:460
  80.8 6.8 %collective-permute-start.14 = (f32[8,128]{1,0:T(8,128)S(1)}, f32[8,128]{1,0:T(8,128)S(1)}, u32[]{:S(2)}, u32[]{:S(2)}) collective-permute-start(f32[8,128]{1,0:T(8,128)S(1)} %get-tuple-element.41), channel_id=1, source_target_pairs={{0,6},{1,7},{2,4},{3,5},{4,2},{5,3},{6,0},{7,1},{8,14},{9,15},{10,... | collective-permute-start | bytes 12296 | tf_op jit(solution)/shard_map/ppermute | solution.py:522
  80.8 6.7 %collective-permute-start.13 = (f32[8,128]{1,0:T(8,128)S(1)}, f32[8,128]{1,0:T(8,128)S(1)}, u32[]{:S(2)}, u32[]{:S(2)}) collective-permute-start(f32[8,128]{1,0:T(8,128)S(1)} %get-tuple-element.41), channel_id=1, source_target_pairs={{0,4},{1,5},{2,6},{3,7},{4,0},{5,1},{6,2},{7,3},{8,12},{9,13},{10,... | collective-permute-start | bytes 12296 | tf_op jit(solution)/shard_map/ppermute | solution.py:521
  86.5 3.7 %collective-permute-start.15 = (f32[8,128]{1,0:T(8,128)S(1)}, f32[8,128]{1,0:T(8,128)S(1)}, u32[]{:S(2)}, u32[]{:S(2)}) collective-permute-start(f32[8,128]{1,0:T(8,128)S(1)} %get-tuple-element.29), channel_id=1, source_target_pairs={{0,2},{1,3},{2,0},{3,1},{4,6},{5,7},{6,4},{7,5},{8,10},{9,11},{10,... | collective-permute-start | bytes 12296 | tf_op jit(solution)/shard_map/ppermute | solution.py:523

commit v5 on v4

--- a/solution.py
+++ b/solution.py
@@ -46,18 +46,15 @@
 
 
 class Frames:
-    def __init__(self, odd, parity):
-        self.odd, self.parity = odd, parity
-
-    def pick(self, ref, v):
-        count = ref.shape[1]
-        return jnp.where(self.odd, ref[:, v, :], ref[:, count - 1 - v, :])
+    def __init__(self, parity):
+        self.parity = parity
 
     def slot(self, v):
         return jnp.where(self.parity == 1, v % 2, (v + 1) % 2)
 
-    def load(self, ref, v):
+    def load(self, halves, v):
         tiles = C // SUB
+        ref = halves[0] if v < 2 else halves[1]
         return ref[pl.ds(self.slot(v) * tiles, tiles)].reshape(C, ref.shape[2])
 
     def store(self, ref, v, value):
@@ -66,14 +63,6 @@
 
     def tap(self, a):
         return jnp.where(self.parity == 1, a, 2 - a)
-
-
-def entering_of(frames, flags, guesses, halves, v):
-    start = frames.pick(guesses, v)
-    if halves is None:
-        return start
-    other, keep = halves
-    return jnp.where(flags.anchor, start, frames.load(other if v < 2 else keep, v))
 
 
 class Flags:
@@ -92,27 +81,37 @@
     return (0 if v < 2 else 2) + frames.slot(v)
 
 
-def edges_kernel(later, *refs):
+def ends_of(flags, frames, halves, inner, outer):
+    edge = 2 * COLS
+    for half, ref in enumerate(halves):
+        length = ref.shape[2]
+        for slot in range(2):
+            slabs = pl.ds(slot * (C // SUB), C // SUB)
+            head = ref[slabs, :, 0:edge].reshape(C, edge).astype(jnp.bfloat16)
+            tail = ref[slabs, :, length - edge : length].reshape(C, edge).astype(jnp.bfloat16)
+            inner[2 * half + slot] = jnp.where(flags.even_block, tail, head)
+            outer[2 * half + slot] = jnp.where(flags.even_block, head, tail)
+
+
+def edges_kernel(other, keep, inner, outer):
     flags = Flags()
-    frames = Frames(flags.odd, flags.parity)
-    edge = 2 * COLS
-    if later:
-        guesses, other, keep, inner, outer = refs
-        count, length = guesses.shape[1:]
-    else:
-        low, high, inner, outer = refs
-        count, wide = low.shape[1:]
-    for v in range(count):
-        if later:
-            latent = entering_of(frames, flags, guesses, (other, keep), v)
-            head, tail = latent[:, :edge], latent[:, length - edge :]
-        else:
-            head = frames.pick(low, v)[:, :edge]
-            tail = frames.pick(high, v)[:, wide - edge :]
-        head, tail = head.astype(jnp.bfloat16), tail.astype(jnp.bfloat16)
-        at = halo_slot(frames, v)
-        inner[at] = jnp.where(flags.even_block, tail, head)
-        outer[at] = jnp.where(flags.even_block, head, tail)
+    ends_of(flags, Frames(flags.parity), (other, keep), inner, outer)
+
+
+def arrange_kernel(with_ends, values, other, keep, *ends):
+    flags = Flags()
+    channels, count, length = values.shape
+    tiles = channels // SUB
+    for slot in range(count // 2):
+        low = values[:, slot, :].reshape(tiles, SUB, length)
+        high = values[:, count // 2 + slot, :].reshape(tiles, SUB, length)
+        slabs = pl.ds(slot * tiles, tiles)
+        other[slabs] = jnp.where(flags.odd, low, high)
+        keep[slabs] = jnp.where(flags.odd, high, low)
+    for ref in (other, keep):
+        ref[ref.shape[0] - 1] = jnp.zeros((SUB, length), jnp.float32)
+    if with_ends:
+        ends_of(flags, Frames(flags.parity), (other, keep), *ends)
 
 
 def near_frames(v, count):
@@ -140,17 +139,15 @@
     return value / (1.0 + jnp.exp(-value))
 
 
-def interior_kernel(later, guesses, *refs):
+def interior_kernel(other, keep, first, temb, hidden, own, spread):
     flags = Flags()
-    frames = Frames(flags.odd, flags.parity)
-    halves, refs = split(later, refs)
-    first, temb, hidden, own, spread = refs
-    count, length = guesses.shape[1:]
+    frames = Frames(flags.parity)
+    count, length = spread.shape[:2]
     edge = 2 * COLS
     inside = length - edge
 
     def prepare(v):
-        left, mixed, right = spread_columns(entering_of(frames, flags, guesses, halves, v))
+        left, mixed, right = spread_columns(frames.load((other, keep), v))
         spread[v, :, 0:128] = left
         spread[v, :, 128:192] = mixed[:, :64]
         spread[v, pl.ds(0, length - COLS), 192:256] = mixed[COLS:, 64:]
@@ -177,15 +174,12 @@
 
 
 class Rest:
-    def __init__(self, real, guesses, halves, noise, first, second, temb, inside, ends):
+    def __init__(self, real, halves, noise, first, second, temb, inside, ends):
         self.flags = Flags(real)
-        self.frames = Frames(self.flags.odd, self.flags.parity)
-        self.guesses, self.halves, self.noise = guesses, halves, noise
+        self.frames = Frames(self.flags.parity)
+        self.halves, self.noise = halves, noise
         self.first, self.second, self.temb, self.inside, self.ends = first, second, temb, inside, ends
-        self.channels, self.count, self.length = guesses.shape
-
-    def entering(self, v):
-        return entering_of(self.frames, self.flags, self.guesses, self.halves, v)
+        self.channels, self.count, self.length = C, inside.shape[0], halves[0].shape[2]
 
     def prepare(self, v, inner, outer, own, spread):
         edge = 2 * COLS
@@ -194,14 +188,15 @@
         even = self.flags.even_block
         both = jnp.concatenate([jnp.where(even, far, near), jnp.where(even, near, far)], axis=1)
         left, mixed, right = spread_columns(both)
-        spread[v, pl.ds(edge, 2 * edge), :] = own[v]
+        ref, i = spread[v]
+        ref[i, pl.ds(edge, 2 * edge), :] = own[v]
         for low, high, rows in ((0, 128, left), (128, 192, mixed[:, :64]), (256, 384, right)):
-            spread[v, pl.ds(0, edge), low:high] = rows[:edge]
-            spread[v, pl.ds(3 * edge, edge), low:high] = rows[edge:]
-        spread[v, pl.ds(0, COLS), 192:256] = mixed[COLS:edge, 64:]
-        spread[v, pl.ds(COLS, COLS), 192:256] = own[v, pl.ds(0, COLS), 0:64]
-        spread[v, pl.ds(3 * edge - COLS, edge), 192:256] = mixed[edge:, 64:]
-        spread[v, pl.ds(3 * edge + COLS, COLS), 192:256] = jnp.zeros((COLS, 64), jnp.bfloat16)
+            ref[i, pl.ds(0, edge), low:high] = rows[:edge]
+            ref[i, pl.ds(3 * edge, edge), low:high] = rows[edge:]
+        ref[i, pl.ds(0, COLS), 192:256] = mixed[COLS:edge, 64:]
+        ref[i, pl.ds(COLS, COLS), 192:256] = own[v, pl.ds(0, COLS), 0:64]
+        ref[i, pl.ds(3 * edge - COLS, edge), 192:256] = mixed[edge:, 64:]
+        ref[i, pl.ds(3 * edge + COLS, COLS), 192:256] = jnp.zeros((COLS, 64), jnp.bfloat16)
 
     def edge_rows(self, v, spread):
         edge = 2 * COLS
@@ -211,7 +206,7 @@
             rows.append(
                 jnp.concatenate(
                     [
-                        spread[v + a - 1, pl.ds(group + b * COLS, edge), low:high]
+                        spread[v + a - 1][0][spread[v + a - 1][1], pl.ds(group + b * COLS, edge), low:high]
                         for a in near_frames(v, self.count)
                         for b, low, high in WINDOWS
                     ],
@@ -246,7 +241,7 @@
             ],
             axis=1,
         )
-        latent, noise = self.entering(v), self.frames.pick(self.noise, v)
+        latent, noise = self.frames.load(self.halves, v), self.frames.load(self.noise, v)
         base = flags.keep * latent + flags.spread * noise + jnp.where(flags.anchor, latent, 0.0)
         chunk = length // 2
         column = lax.broadcasted_iota(jnp.int32, (1, chunk), 1) % COLS
@@ -281,33 +276,27 @@
         ref[ref.shape[0] - 1] = jnp.broadcast_to(exponent, (SUB, self.length))
 
 
-def split(later, refs):
-    return (tuple(refs[:2]), refs[2:]) if later else (None, refs)
-
-
-def sending_kernel(later, real, guesses, *refs):
-    halves, refs = split(later, refs)
-    inner, outer, noise, first, second, temb, inside, own, yours, ends_out, ends_own, spread = refs
-    ends = {0: (ends_own, 0), 1: (ends_out, 0), 2: (ends_out, 1), 3: (ends_out, 2)}
-    work = Rest(real, guesses, halves, noise, first, second, temb, inside, ends)
+def sending_kernel(real, other, keep, noise_other, inner, outer, first, second, temb, inside, own, yours, *rest):
+    ends_out, spread_out, ends_own, spread_own = rest
+    ends = {0: (ends_own, 0), 1: (ends_out, 0), 2: (ends_out, 1)}
+    spread = {0: (spread_own, 0), 1: (spread_own, 1), 2: (spread_out, 0), 3: (spread_out, 1)}
+    work = Rest(real, (other, keep), (noise_other, None), first, second, temb, inside, ends)
     work.prepare(0, inner, outer, own, spread)
     work.prepare(1, inner, outer, own, spread)
     work.edge_rows(0, spread)
     work.prepare(2, inner, outer, own, spread)
     work.edge_rows(1, spread)
+    work.prepare(3, inner, outer, own, spread)
     peaks = [work.second_conv(0, yours)]
-    work.prepare(3, inner, outer, own, spread)
     work.edge_rows(2, spread)
     peaks.append(work.second_conv(1, yours))
-    work.edge_rows(3, spread)
     work.mark(yours, peaks)
 
 
-def keeping_kernel(later, real, guesses, *refs):
-    halves, refs = split(later, refs)
-    noise, second, temb, inside, ends_in, mine = refs
-    ends = {1: (ends_in, 0), 2: (ends_in, 1), 3: (ends_in, 2)}
-    work = Rest(real, guesses, halves, noise, None, second, temb, inside, ends)
+def keeping_kernel(real, keep, noise_keep, first, second, temb, inside, ends_in, spread_in, mine, ends_own):
+    ends = {1: (ends_in, 0), 2: (ends_in, 1), 3: (ends_own, 0)}
+    work = Rest(real, (keep, keep), (None, noise_keep), first, second, temb, inside, ends)
+    work.edge_rows(3, {2: (spread_in, 0), 3: (spread_in, 1)})
     work.mark(mine, [work.second_conv(2, mine), work.second_conv(3, mine)])
 
 
@@ -327,26 +316,28 @@
     )(*arrays)
 
 
-def edges(guesses, halves):
-    channels, frames, length = guesses.shape
-    shape = jax.ShapeDtypeStruct((frames, channels, 2 * COLS), jnp.bfloat16)
-    kernel = functools.partial(edges_kernel, halves is not None)
-    if halves is not None:
-        return call(kernel, "edges", (guesses,) + halves, (shape, shape))
-    wide = -(-2 * COLS // 128) * 128
-    return call(kernel, "edges", (guesses[..., :wide], guesses[..., length - wide :]), (shape, shape))
-
-
-def denoise(real, guesses, halves, inner, outer, noise, first, second, temb):
-    channels, frames, length = guesses.shape
+def edges(other, keep):
+    shape = jax.ShapeDtypeStruct((2 * other.shape[0] // (C // SUB), C, 2 * COLS), jnp.bfloat16)
+    return call(edges_kernel, "edges", (other, keep), (shape, shape))
+
+
+def arrange(values, with_ends):
+    channels, frames, length = values.shape
+    half = jax.ShapeDtypeStruct((frames // 2 * channels // SUB + 1, SUB, length), jnp.float32)
+    ends = jax.ShapeDtypeStruct((frames, channels, 2 * COLS), jnp.bfloat16)
+    shapes = (half, half) + ((ends, ends) if with_ends else ())
+    return call(functools.partial(arrange_kernel, with_ends), "arrange", (values,), shapes)
+
+
+def denoise(real, other, keep, noise, inner, outer, first, second, temb):
+    length = other.shape[2]
+    frames = inner.shape[0]
     width = temb.shape[1]
-    half = jax.ShapeDtypeStruct((frames // 2 * channels // SUB + 1, SUB, length), jnp.float32)
-    later = halves is not None
-    start = (guesses,) + (halves or ())
+    half = jax.ShapeDtypeStruct(other.shape, jnp.float32)
     inside, own = call(
-        functools.partial(interior_kernel, later),
+        interior_kernel,
         "interior",
-        start + (first, temb),
+        (other, keep, first, temb),
         (
             jax.ShapeDtypeStruct((frames, length - 2 * COLS, width), jnp.bfloat16),
             jax.ShapeDtypeStruct((frames, 4 * COLS, 384), jnp.bfloat16),
@@ -356,21 +347,23 @@
         limit=6,
     )
     ends = (4 * COLS, width)
-    yours, ends_mid = call(
-        functools.partial(sending_kernel, later),
+    spread = (2, 8 * COLS, 384)
+    yours, ends_mid, spread_mid = call(
+        sending_kernel,
         "sending",
-        (real,) + start + (inner, outer, noise, first, second, temb, inside, own),
-        (half, jax.ShapeDtypeStruct((3,) + ends, jnp.bfloat16)),
-        [pltpu.VMEM((1,) + ends, jnp.bfloat16), pltpu.VMEM((frames, 8 * COLS, 384), jnp.bfloat16)],
+        (real, other, keep, noise[0], inner, outer, first, second, temb, inside, own),
+        (half, jax.ShapeDtypeStruct((2,) + ends, jnp.bfloat16), jax.ShapeDtypeStruct(spread, jnp.bfloat16)),
+        [pltpu.VMEM((1,) + ends, jnp.bfloat16), pltpu.VMEM(spread, jnp.bfloat16)],
         2_000_000_000,
         limit=6,
     )
     (mine,) = call(
-        functools.partial(keeping_kernel, later),
+        keeping_kernel,
         "keeping",
-        (real,) + start + (noise, second, temb, inside, ends_mid),
+        (real, keep, noise[1], first, second, temb, inside, ends_mid, spread_mid),
         (half,),
-        flops=2_000_000_000,
+        [pltpu.VMEM((1,) + ends, jnp.bfloat16)],
+        2_000_000_000,
         limit=6,
     )
     return yours, mine
@@ -413,15 +406,10 @@
     )(*halves)
 
 
-def changes_kernel(*refs):
-    *sweeps, sums = refs
-    tiles = 2 * C // SUB
-
-    def reached(before, term):
-        return before[pl.ds(0, tiles)] + term[pl.ds(0, tiles)]
-
-    for i, at in enumerate((0, 2)):
-        change = reached(sweeps[4 + at], sweeps[5 + at]) - reached(sweeps[at], sweeps[1 + at])
+def changes_kernel(own1, theirs1, own2, theirs2, sums):
+    slabs = pl.ds(0, 2 * C // SUB)
+    for i, (one, two) in enumerate(((own1, own2), (theirs1, theirs2))):
+        change = two[slabs] - one[slabs]
         square = jnp.sum(change * change, axis=0)
         total = jnp.sum(jnp.sum(square, axis=0, keepdims=True), axis=1, keepdims=True)
         sums[i] = jnp.broadcast_to(total, sums.shape[1:])
@@ -455,9 +443,9 @@
     return jnp.where(condition, half, jnp.where(is_mark(half), -100.0, 0.0))
 
 
-def exchange(half, distance):
+def exchange(half, flip):
     steps = lax.axis_size("step")
-    return decoded(lax.ppermute(coded(half), "step", [(i, i ^ distance) for i in range(steps)]))
+    return decoded(lax.ppermute(coded(half), "step", [(i, i ^ flip) for i in range(steps)]))
 
 
 def prefix(yours, mine, step_index):
@@ -468,13 +456,13 @@
     before = masked(total, False)
     distance = 2
     while distance < steps:
-        got = exchange(total, distance)
+        got = exchange(total, 2 * distance - 2)
         before = added(before, masked(got, (step_index // distance) % 2 == 1))
         total = added(total, got)
         distance *= 2
     keep = added(before, masked(partner, odd))
     give = added(before, masked(mine, jnp.logical_not(odd)))
-    return exchange(give, 1), keep, (keep, mine, give, partner)
+    return exchange(give, 1), keep, (keep + mine, give + partner)
 
 
 def local(guesses, noise, timesteps, conv_first, conv_second, time_weight):
@@ -492,17 +480,18 @@
     temb = time_embed(pair[0, : C // 2], time_weight).reshape(1, -1)
     first = jnp.pad(conv_first.transpose(0, 2, 1), ((0, 0), (0, C), (0, 0)))
 
-    def sweep(halves):
-        near, far = edges(start_latent, halves)
+    def sweep(other, keep, near, far):
         inner = lax.ppermute(near, "space", inner_pairs)
         outer = lax.ppermute(far, "space", outer_pairs)
-        yours, mine = denoise(
-            real, start_latent, halves, inner, outer, noise_step, first, conv_second, temb
-        )
+        yours, mine = denoise(real, other, keep, noise_halves, inner, outer, first, conv_second, temb)
         return yours, mine, prefix(yours, mine, step_index)
 
-    _, _, (other1, keep1, reached1) = sweep(None)
-    yours2, mine2, (other2, keep2, reached2) = sweep((other1, keep1))
+    other0, keep0, near, far = arrange(start_latent, True)
+    noise_halves = arrange(noise_step, False)
+    _, _, (other1, keep1, reached1) = sweep(other0, keep0, near, far)
+    is_anchor = step_index == 0
+    other1, keep1 = jnp.where(is_anchor, other0, other1), jnp.where(is_anchor, keep0, keep1)
+    yours2, mine2, (other2, keep2, reached2) = sweep(other1, keep1, *edges(other1, keep1))
     sums = change_sums(reached1, reached2)
     steps = lax.axis_size("step")
     cell_count = start_latent.size * space

time: 90.9 us -> 88.3 us (0.971)
  waiting for transfers between devices: 43 us -> 27.3 us
  starting transfers between devices: 19 us -> 31 us
  other arithmetic: 3.67 us -> 5.6 us
  Pallas kernels: 21 us -> 19.1 us
  local copies, waits for them, and re-layouts: 2.64 us -> 3.7 us
    ppermute x8, waiting for transfers between devices: 40.4 us -> 26.7 us  [exchange(): lax.ppermute(coded(half), 'step', [(i, i ^ flip) for i in range(steps)])]
    ppermute x8, starting transfers between devices: 15.5 us -> 19.6 us  [exchange(): lax.ppermute(coded(half), 'step', [(i, i ^ flip) for i in range(steps)])]
    ppermute x1, starting transfers between devices: 0.07 us -> 3.84 us  [local(): lax.ppermute(near_sum, 'space', far)]
    ppermute x1, starting transfers between devices: 0.07 us -> 3.8 us  [local(): lax.ppermute(sums[1], ('step', 'space'), cross)]
    ppermute x1, waiting for transfers between devices: 2.59 us -> 0.59 us  [local(): lax.ppermute(near_sum, 'space', far)]
    pallas_call x9 -> x10, Pallas kernels: 20.1 us -> 18.2 us  [call(): pl.pallas_call(kernel, out_shape=out_shape, in_specs=[WHOLE] * len(arrays...]
    add x0 -> x2, other arithmetic: none -> 1.85 us  [prefix(): return (exchange(give, 1), keep, (keep + mine, give + partner))]
    pad x1, local copies, waits for them, and re-layouts: 0.07 us -> 1.34 us  [local(): first = jnp.pad(conv_first.transpose(0, 2, 1), ((0, 0), (0, C), (0, 0)))]
  transfers between devices with their start and end apart: 16 -> 16, of which waited for: 9 -> 9; matrix products, arithmetic and copies ran while one was open for 1% -> 2% of each run, Pallas kernels for 12% -> 12%
where the time goes in v5:
time: 88.3 us; the launch traced here: 88.1 us
  starting transfers between devices  31 us (35%)
  waiting for transfers between devices  27.3 us (31%)
  Pallas kernels  19.1 us (22%)
  other arithmetic  5.6 us (6%)
  local copies, waits for them, and re-layouts  3.7 us (4%)
  between operations  1.1 us (1%)
    ppermute x8, waiting for transfers between devices, exchange(): lax.ppermute(coded(half), 'step', [(i, i ^ flip) for i in range(steps)])  26.7 us
    ppermute x8, starting transfers between devices, exchange(): lax.ppermute(coded(half), 'step', [(i, i ^ flip) for i in range(steps)])  19.6 us
    pallas_call x10, Pallas kernels, call(): pl.pallas_call(kernel, out_shape=out_shape, in_specs=[WHOLE] * len(arrays...  18.2 us
    ppermute x1, starting transfers between devices, local(): lax.ppermute(near_sum, 'space', far)  3.84 us
    ppermute x1, starting transfers between devices, local(): lax.ppermute(sums[1], ('step', 'space'), cross)  3.8 us
    add x2, other arithmetic, prefix(): return (exchange(give, 1), keep, (keep + mine, give + partner))  1.85 us
    ppermute x2, starting transfers between devices, sweep(): outer = lax.ppermute(far, 'space', outer_pairs)  1.77 us
    unnamed x18, local copies, waits for them, and re-layouts  1.77 us
  transfers between devices with their start and end apart: 16, of which 9 were waited for; matrix products, arithmetic and copies ran while one was open for 2% of the time, Pallas kernels for 12%

profile of v5, /device:TPU:0, one launch (start us, length us, event | category | flops | bytes accessed | tf_op | source)
XLA Modules:
  0.0 88.1 jit_solution(16537807374169002542)
XLA Ops:
  0.7 1.1 %copy-done.1 = f32[1,64,4,640]{3,2,1,0:T(4,128)S(1)} copy-done((f32[1,64,4,640]{3,2,1,0:T(4,128)S(1)}, f32[1,64,4,640]{3,2,1,0:T(4,128)}, u32[]{:S(2)}) %copy-start.1) | copy-done | bytes 655384
  1.8 0.4 arrange.2
  2.2 0.5 collective-permute-start
  2.7 0.8 collective-permute-start.1
  3.6 0.2 arrange.3
  3.9 1.3 %pad.4.first = bf16[3,640,256]{2,1,0:T(8,128)(2,1)S(1)} pad(bf16[3,576,256]{2,1,0:T(8,128)(2,1)} %bitcast.57, bf16[]{:T(256)} %constant.98.clone.1), padding=0_0x0_64x0_0 | pad | bytes 1867778 | tf_op jit(solution)/shard_map/jit(_pad)/pad | solution.py:481
  5.3 0.2 fusion.55.temb
  5.5 2.4 %interior.2 = (bf16[4,480,256]{2,1,0:T(8,128)(2,1)S(1)}, bf16[4,320,384]{2,1,0:T(8,128)(2,1)S(1)}) custom-call(f32[17,8,640]{2,1,0:T(8,128)S(1)} %get-tuple-element.24.other, f32[17,8,640]{2,1,0:T(8,128)S(1)} %get-tuple-element.22.keep, bf16[3,640,256]{2,1,0:T(8,128)(2,1)S(1)} %pad.4.first, f32[1,256]{1,0:T(1,128)S(1)} %fusion.55.temb), custom_call_target="tpu_custom_call" | custom-call | flops 2000000000 | bytes 4000000 | tf_op jit(solution)/shard_map/interior/pallas_call | solution.py:307
  7.9 3.7 %sending.2 = (f32[17,8,640]{2,1,0:T(8,128)S(1)}, bf16[2,320,256]{2,1,0:T(8,128)(2,1)S(1)}, bf16[2,640,384]{2,1,0:T(8,128)(2,1)S(1)}) custom-call(f32[3,128]{1,0:T(4,128)S(1)} %pad_maximum_fusion.real, f32[17,8,640]{2,1,0:T(8,128)S(1)} %get-tuple-element.24.other, f32[17,8,640]{2,1,0:T(8,128)S(1)} %get-tuple-element.22.keep, ...), custom_call_target="tpu_custom_call" | custom-call | flops 2000000000 | bytes 4000000 | tf_op jit(solution)/shard_map/sending/pallas_call | solution.py:307
  11.8 2.5 %collective-permute-start.2 = (f16[17,8,640]{2,1,0:T(8,128)(2,1)S(1)}, f16[17,8,640]{2,1,0:T(8,128)(2,1)S(1)}, u32[]{:S(2)}, u32[]{:S(2)}) collective-permute-start(f16[17,8,640]{2,1,0:T(8,128)(2,1)S(1)} %fusion), channel_id=1, source_target_pairs={{0,4},{4,0},{8,12},{12,8},{16,20},{20,16},{24,28},{28,24},{1,5},{5... | collective-permute-start | bytes 522248 | tf_op jit(solution)/shard_map/ppermute | solution.py:448
  14.3 2.5 %keeping.2 = f32[17,8,640]{2,1,0:T(8,128)S(1)} custom-call(f32[3,128]{1,0:T(4,128)S(1)} %pad_maximum_fusion.real, f32[17,8,640]{2,1,0:T(8,128)S(1)} %get-tuple-element.22.keep, f32[17,8,640]{2,1,0:T(8,128)S(1)} %get-tuple-element.23.noise_keep, bf16[3,640,256]{2,1,0:T(8,128)(2,1)S(1)} %pad.4.first, bf16[3,64,2304]{2,1,0:T(8,128)(2,1)S(1)} %copy-done.3, ...), custom_call_target="tpu_custom_call" | custom-call | flops 2000000000 | bytes 4000000 | tf_op jit(solution)/shard_map/keeping/pallas_call | solution.py:307
  16.8 0.9 %collective-permute-done.2 = f16[17,8,640]{2,1,0:T(8,128)(2,1)S(1)} collective-permute-done((f16[17,8,640]{2,1,0:T(8,128)(2,1)S(1)}, f16[17,8,640]{2,1,0:T(8,128)(2,1)S(1)}, u32[]{:S(2)}, u32[]{:S(2)}) %collective-permute-start.2) | collective-permute-done | bytes 174112 | tf_op jit(solution)/shard_map/ppermute | solution.py:448
  17.7 0.1 add_select_fusion.9
  18.0 2.1 %collective-permute-start.3 = (f16[17,8,640]{2,1,0:T(8,128)(2,1)S(1)}, f16[17,8,640]{2,1,0:T(8,128)(2,1)S(1)}, u32[]{:S(2)}, u32[]{:S(2)}) collective-permute-start(f16[17,8,640]{2,1,0:T(8,128)(2,1)S(1)} %fusion.1), channel_id=1, source_target_pairs={{0,8},{4,12},{8,0},{12,4},{16,24},{20,28},{24,16},{28,20},{1,9},{5... | collective-permute-start | bytes 522248 | tf_op jit(solution)/shard_map/ppermute | solution.py:448
  20.2 4.1 %collective-permute-done.3 = f16[17,8,640]{2,1,0:T(8,128)(2,1)S(1)} collective-permute-done((f16[17,8,640]{2,1,0:T(8,128)(2,1)S(1)}, f16[17,8,640]{2,1,0:T(8,128)(2,1)S(1)}, u32[]{:S(2)}, u32[]{:S(2)}) %collective-permute-start.3) | collective-permute-done | bytes 174112 | tf_op jit(solution)/shard_map/ppermute | solution.py:448
  24.3 0.6 copy-done.6
  24.9 0.1 add_select_fusion.8
  25.1 0.8 fusion.2
  25.9 4.5 %collective-permute-start.4 = (f16[17,8,640]{2,1,0:T(8,128)(2,1)}, f16[17,8,640]{2,1,0:T(8,128)(2,1)}, u32[]{:S(2)}, u32[]{:S(2)}) collective-permute-start(f16[17,8,640]{2,1,0:T(8,128)(2,1)} %fusion.2), channel_id=1, source_target_pairs={{0,24},{4,28},{8,16},{12,20},{16,8},{20,12},{24,0},{28,4},{1,25},{... | collective-permute-start | bytes 522248 | tf_op jit(solution)/shard_map/ppermute | solution.py:448
  30.4 5.5 %collective-permute-done.4 = f16[17,8,640]{2,1,0:T(8,128)(2,1)} collective-permute-done((f16[17,8,640]{2,1,0:T(8,128)(2,1)}, f16[17,8,640]{2,1,0:T(8,128)(2,1)}, u32[]{:S(2)}, u32[]{:S(2)}) %collective-permute-start.4) | collective-permute-done | bytes 174112 | tf_op jit(solution)/shard_map/ppermute | solution.py:448
  35.9 0.9 %convert_element_type.77 = f32[17,8,640]{2,1,0:T(8,128)S(1)} convert(f16[17,8,640]{2,1,0:T(8,128)(2,1)} %collective-permute-done.4) | non-fusion elementwise | flops 87040 | bytes 522240 | tf_op jit(solution)/shard_map/convert_element_type | solution.py:434
  36.9 1.4 %fusion.11 = (f32[17,8,640]{2,1,0:T(8,128)S(1)}, f32[17,8,640]{2,1,0:T(8,128)S(1)}, f32[17,8,640]{2,1,0:T(8,128)S(1)}, f32[17,8,640]{2,1,0:T(8,128)S(1)}) fusion(f16[17,8,640]{2,1,0:T(8,128)(2,1)S(1)} %collective-permute-done.2, f32[8,640]{1,0:T(8,128)S(1)} %fusion.54, pred[17]{0:T(512)(128)(4,1)S(1)} %iota_compare_fusion, f32[17,8,640]{2,1,0:T(8,128)S(1)} %keeping.2, ...), kind=kLoop, calls=%fused_computation.37 | loop fusion | flops 2785280 | bytes 2672730 | tf_op jit(solution)/shard_map/add | solution.py:465
  38.4 1.6 %collective-permute-start.5 = (f16[17,8,640]{2,1,0:T(8,128)(2,1)S(1)}, f16[17,8,640]{2,1,0:T(8,128)(2,1)S(1)}, u32[]{:S(2)}, u32[]{:S(2)}) collective-permute-start(f16[17,8,640]{2,1,0:T(8,128)(2,1)S(1)} %fusion.4), channel_id=1, source_target_pairs={{0,4},{4,0},{8,12},{12,8},{16,20},{20,16},{24,28},{28,24},{1,5},{5... | collective-permute-start | bytes 522248 | tf_op jit(solution)/shard_map/ppermute | solution.py:448
  40.0 4.7 %collective-permute-done.5 = f16[17,8,640]{2,1,0:T(8,128)(2,1)S(1)} collective-permute-done((f16[17,8,640]{2,1,0:T(8,128)(2,1)S(1)}, f16[17,8,640]{2,1,0:T(8,128)(2,1)S(1)}, u32[]{:S(2)}, u32[]{:S(2)}) %collective-permute-start.5) | collective-permute-done | bytes 174112 | tf_op jit(solution)/shard_map/ppermute | solution.py:448
  44.7 0.1 fusion.5.other
  44.9 0.2 edges.1
  45.1 1.0 %collective-permute-start.7 = (bf16[4,64,160]{2,1,0:T(8,128)(2,1)S(1)}, bf16[4,64,160]{2,1,0:T(8,128)(2,1)S(1)}, u32[]{:S(2)}, u32[]{:S(2)}) collective-permute-start(bf16[4,64,160]{2,1,0:T(8,128)(2,1)S(1)} %get-tuple-element.35), channel_id=1, source_target_pairs={{1,2},{2,1},{5,6},{6,5},{9,10},{10,9},{13,14},{14,13},{17,18},{18,... | collective-permute-start | bytes 245768 | tf_op jit(solution)/shard_map/ppermute | solution.py:485
  46.1 2.4 %interior.3 = (bf16[4,480,256]{2,1,0:T(8,128)(2,1)S(1)}, bf16[4,320,384]{2,1,0:T(8,128)(2,1)S(1)}) custom-call(f32[17,8,640]{2,1,0:T(8,128)S(1)} %fusion.5.other, f32[17,8,640]{2,1,0:T(8,128)S(1)} %get-tuple-element.54.keep, bf16[3,640,256]{2,1,0:T(8,128)(2,1)S(1)} %pad.4.first, f32[1,256]{1,0:T(1,128)S(1)} %fusion.55.temb), custom_call_target="tpu_custom_call" | custom-call | flops 2000000000 | bytes 4000000 | tf_op jit(solution)/shard_map/interior/pallas_call | solution.py:307
  48.5 3.7 %sending.3 = (f32[17,8,640]{2,1,0:T(8,128)S(1)}, bf16[2,320,256]{2,1,0:T(8,128)(2,1)S(1)}, bf16[2,640,384]{2,1,0:T(8,128)(2,1)S(1)}) custom-call(f32[3,128]{1,0:T(4,128)S(1)} %pad_maximum_fusion.real, f32[17,8,640]{2,1,0:T(8,128)S(1)} %fusion.5.other, f32[17,8,640]{2,1,0:T(8,128)S(1)} %get-tuple-element.54.keep, f32[17,8,640]{2,1,0:T(8,128)S(1)} %copy-done.5, ...), custom_call_target="tpu_custom_call" | custom-call | flops 2000000000 | bytes 4000000 | tf_op jit(solution)/shard_map/sending/pallas_call | solution.py:307
  52.4 1.5 %collective-permute-start.8 = (f16[17,8,640]{2,1,0:T(8,128)(2,1)S(1)}, f16[17,8,640]{2,1,0:T(8,128)(2,1)S(1)}, u32[]{:S(2)}, u32[]{:S(2)}) collective-permute-start(f16[17,8,640]{2,1,0:T(8,128)(2,1)S(1)} %fusion.6), channel_id=1, source_target_pairs={{0,4},{4,0},{8,12},{12,8},{16,20},{20,16},{24,28},{28,24},{1,5},{5... | collective-permute-start | bytes 522248 | tf_op jit(solution)/shard_map/ppermute | solution.py:448
  53.9 2.5 %keeping.3.mine = f32[17,8,640]{2,1,0:T(8,128)S(1)} custom-call(f32[3,128]{1,0:T(4,128)S(1)} %pad_maximum_fusion.real, f32[17,8,640]{2,1,0:T(8,128)S(1)} %get-tuple-element.54.keep, f32[17,8,640]{2,1,0:T(8,128)S(1)} %get-tuple-element.23.noise_keep, bf16[3,640,256]{2,1,0:T(8,128)(2,1)S(1)} %pad.4.first, bf16[3,64,2304]{2,1,0:T(8,128)(2,1)S(1)} %copy-done.3, ...), custom_call_target="tpu_custom_call" | custom-call | flops 2000000000 | bytes 4000000 | tf_op jit(solution)/shard_map/keeping/pallas_call | solution.py:307
  56.4 1.6 %collective-permute-done.8 = f16[17,8,640]{2,1,0:T(8,128)(2,1)S(1)} collective-permute-done((f16[17,8,640]{2,1,0:T(8,128)(2,1)S(1)}, f16[17,8,640]{2,1,0:T(8,128)(2,1)S(1)}, u32[]{:S(2)}, u32[]{:S(2)}) %collective-permute-start.8) | collective-permute-done | bytes 174112 | tf_op jit(solution)/shard_map/ppermute | solution.py:448
  58.0 0.1 add_select_fusion.4
  58.2 3.3 %collective-permute-start.9 = (f16[17,8,640]{2,1,0:T(8,128)(2,1)S(1)}, f16[17,8,640]{2,1,0:T(8,128)(2,1)S(1)}, u32[]{:S(2)}, u32[]{:S(2)}) collective-permute-start(f16[17,8,640]{2,1,0:T(8,128)(2,1)S(1)} %fusion.7), channel_id=1, source_target_pairs={{0,8},{4,12},{8,0},{12,4},{16,24},{20,28},{24,16},{28,20},{1,9},{5... | collective-permute-start | bytes 522248 | tf_op jit(solution)/shard_map/ppermute | solution.py:448
  61.5 3.6 %collective-permute-done.9 = f16[17,8,640]{2,1,0:T(8,128)(2,1)S(1)} collective-permute-done((f16[17,8,640]{2,1,0:T(8,128)(2,1)S(1)}, f16[17,8,640]{2,1,0:T(8,128)(2,1)S(1)}, u32[]{:S(2)}, u32[]{:S(2)}) %collective-permute-start.9) | collective-permute-done | bytes 174112 | tf_op jit(solution)/shard_map/ppermute | solution.py:448
  65.1 0.1 add_select_fusion.3
  65.4 2.5 %collective-permute-start.10 = (f16[17,8,640]{2,1,0:T(8,128)(2,1)S(1)}, f16[17,8,640]{2,1,0:T(8,128)(2,1)S(1)}, u32[]{:S(2)}, u32[]{:S(2)}) collective-permute-start(f16[17,8,640]{2,1,0:T(8,128)(2,1)S(1)} %fusion.8), channel_id=1, source_target_pairs={{0,24},{4,28},{8,16},{12,20},{16,8},{20,12},{24,0},{28,4},{1,25},{... | collective-permute-start | bytes 522248 | tf_op jit(solution)/shard_map/ppermute | solution.py:448
  67.9 6.2 %collective-permute-done.10 = f16[17,8,640]{2,1,0:T(8,128)(2,1)S(1)} collective-permute-done((f16[17,8,640]{2,1,0:T(8,128)(2,1)S(1)}, f16[17,8,640]{2,1,0:T(8,128)(2,1)S(1)}, u32[]{:S(2)}, u32[]{:S(2)}) %collective-permute-start.10) | collective-permute-done | bytes 174112 | tf_op jit(solution)/shard_map/ppermute | solution.py:448
  74.2 0.5 fusion.12
  74.7 0.2 changes.1
  74.9 0.3 collective-permute-start.11
  75.3 1.6 %collective-permute-start.12 = (f16[17,8,640]{2,1,0:T(8,128)(2,1)S(1)}, f16[17,8,640]{2,1,0:T(8,128)(2,1)S(1)}, u32[]{:S(2)}, u32[]{:S(2)}) collective-permute-start(f16[17,8,640]{2,1,0:T(8,128)(2,1)S(1)} %fusion.10), channel_id=1, source_target_pairs={{0,4},{4,0},{8,12},{12,8},{16,20},{20,16},{24,28},{28,24},{1,5},{5... | collective-permute-start | bytes 522248 | tf_op jit(solution)/shard_map/ppermute | solution.py:448
  76.9 3.8 %collective-permute-start.14 = (f32[8,128]{1,0:T(8,128)S(1)}, f32[8,128]{1,0:T(8,128)S(1)}, u32[]{:S(2)}, u32[]{:S(2)}) collective-permute-start(f32[8,128]{1,0:T(8,128)S(1)} %get-tuple-element.55), channel_id=1, source_target_pairs={{0,6},{1,7},{2,4},{3,5},{4,2},{5,3},{6,0},{7,1},{8,14},{9,15},{10,... | collective-permute-start | bytes 12296 | tf_op jit(solution)/shard_map/ppermute | solution.py:511
  80.7 1.1 %collective-permute-start.13 = (f32[8,128]{1,0:T(8,128)S(1)}, f32[8,128]{1,0:T(8,128)S(1)}, u32[]{:S(2)}, u32[]{:S(2)}) collective-permute-start(f32[8,128]{1,0:T(8,128)S(1)} %get-tuple-element.55), channel_id=1, source_target_pairs={{0,4},{1,5},{2,6},{3,7},{4,0},{5,1},{6,2},{7,3},{8,12},{9,13},{10,... | collective-permute-start | bytes 12296 | tf_op jit(solution)/shard_map/ppermute | solution.py:510
  82.1 3.8 %collective-permute-start.15 = (f32[8,128]{1,0:T(8,128)S(1)}, f32[8,128]{1,0:T(8,128)S(1)}, u32[]{:S(2)}, u32[]{:S(2)}) collective-permute-start(f32[8,128]{1,0:T(8,128)S(1)} %get-tuple-element.41), channel_id=1, source_target_pairs={{0,2},{1,3},{2,0},{3,1},{4,6},{5,7},{6,4},{7,5},{8,10},{9,11},{10,... | collective-permute-start | bytes 12296 | tf_op jit(solution)/shard_map/ppermute | solution.py:512
  86.0 1.0 %finish.1 = f32[64,4,640]{2,1,0:T(4,128)} custom-call(f32[17,8,640]{2,1,0:T(8,128)S(1)} %multiply_select_fusion.other, f32[17,8,640]{2,1,0:T(8,128)S(1)} %get-tuple-element.52.keep, f32[17,8,640]{2,1,0:T(8,128)S(1)} %get-tuple-element.39.yours, f32[17,8,640]{2,1,0:T(8,128)S(1)} %keeping.3.mine), custom_call_target="tpu_custom_call" | custom-call | flops 8000000000 | bytes 4000000 | tf_op jit(solution)/shard_map/finish/pallas_call | solution.py:397
  87.0 0.6 collective-permute-done.15
  87.6 0.5 slice.89
  (66 shorter events, 1.7 us)
Async XLA Ops:
  0.6 4.6 %copy-start = (f32[64,256]{1,0:T(8,128)S(1)}, f32[64,256]{1,0:T(8,128)}, u32[]{:S(2)}) copy-start(f32[64,256]{1,0:T(8,128)} %param.11) | copy-start | bytes 196612
  0.6 1.1 %copy-start.1 = (f32[1,64,4,640]{3,2,1,0:T(4,128)S(1)}, f32[1,64,4,640]{3,2,1,0:T(4,128)}, u32[]{:S(2)}) copy-start(f32[1,64,4,640]{3,2,1,0:T(4,128)} %param.6) | copy-start | bytes 1966084
  1.8 1.9 %copy-start.2 = (f32[1,64,4,640]{3,2,1,0:T(4,128)S(1)}, f32[1,64,4,640]{3,2,1,0:T(4,128)}, u32[]{:S(2)}) copy-start(f32[1,64,4,640]{3,2,1,0:T(4,128)} %param.7) | copy-start | bytes 1966084
  2.2 5.8 %collective-permute-start = (bf16[4,64,160]{2,1,0:T(8,128)(2,1)S(1)}, bf16[4,64,160]{2,1,0:T(8,128)(2,1)S(1)}, u32[]{:S(2)}, u32[]{:S(2)}) collective-permute-start(bf16[4,64,160]{2,1,0:T(8,128)(2,1)S(1)} %get-tuple-element.27), channel_id=1, source_target_pairs={{0,1},{1,0},{2,3},{3,2},{4,5},{5,4},{6,7},{7,6},{8,9},{9,8},{10,11... | collective-permute-start | bytes 245768 | tf_op jit(solution)/shard_map/ppermute | solution.py:484
  2.7 0.8 copy-start.8
  2.7 5.2 %collective-permute-start.1 = (bf16[4,64,160]{2,1,0:T(8,128)(2,1)S(1)}, bf16[4,64,160]{2,1,0:T(8,128)(2,1)S(1)}, u32[]{:S(2)}, u32[]{:S(2)}) collective-permute-start(bf16[4,64,160]{2,1,0:T(8,128)(2,1)S(1)} %get-tuple-element.28), channel_id=1, source_target_pairs={{1,2},{2,1},{5,6},{6,5},{9,10},{10,9},{13,14},{14,13},{17,18},{18,... | collective-permute-start | bytes 245768 | tf_op jit(solution)/shard_map/ppermute | solution.py:485
  3.9 4.1 %copy-start.4 = (f32[17,8,640]{2,1,0:T(8,128)}, f32[17,8,640]{2,1,0:T(8,128)S(1)}, u32[]{:S(2)}) copy-start(f32[17,8,640]{2,1,0:T(8,128)S(1)} %get-tuple-element.26.noise_other) | copy-start | bytes 1044484
  5.5 2.5 %copy-start.3 = (bf16[3,64,2304]{2,1,0:T(8,128)(2,1)S(1)}, bf16[3,64,2304]{2,1,0:T(8,128)(2,1)}, u32[]{:S(2)}) copy-start(bf16[3,64,2304]{2,1,0:T(8,128)(2,1)} %second.7) | copy-start | bytes 2654212
  11.8 5.9 %collective-permute-start.2 = (f16[17,8,640]{2,1,0:T(8,128)(2,1)S(1)}, f16[17,8,640]{2,1,0:T(8,128)(2,1)S(1)}, u32[]{:S(2)}, u32[]{:S(2)}) collective-permute-start(f16[17,8,640]{2,1,0:T(8,128)(2,1)S(1)} %fusion), channel_id=1, source_target_pairs={{0,4},{4,0},{8,12},{12,8},{16,20},{20,16},{24,28},{28,24},{1,5},{5... | collective-permute-start | bytes 522248 | tf_op jit(solution)/shard_map/ppermute | solution.py:448
  18.0 6.3 %collective-permute-start.3 = (f16[17,8,640]{2,1,0:T(8,128)(2,1)S(1)}, f16[17,8,640]{2,1,0:T(8,128)(2,1)S(1)}, u32[]{:S(2)}, u32[]{:S(2)}) collective-permute-start(f16[17,8,640]{2,1,0:T(8,128)(2,1)S(1)} %fusion.1), channel_id=1, source_target_pairs={{0,8},{4,12},{8,0},{12,4},{16,24},{20,28},{24,16},{28,20},{1,9},{5... | collective-permute-start | bytes 522248 | tf_op jit(solution)/shard_map/ppermute | solution.py:448
  24.3 0.7 copy-start.6
  25.9 10.0 %collective-permute-start.4 = (f16[17,8,640]{2,1,0:T(8,128)(2,1)}, f16[17,8,640]{2,1,0:T(8,128)(2,1)}, u32[]{:S(2)}, u32[]{:S(2)}) collective-permute-start(f16[17,8,640]{2,1,0:T(8,128)(2,1)} %fusion.2), channel_id=1, source_target_pairs={{0,24},{4,28},{8,16},{12,20},{16,8},{20,12},{24,0},{28,4},{1,25},{... | collective-permute-start | bytes 522248 | tf_op jit(solution)/shard_map/ppermute | solution.py:448
  30.4 6.5 %copy-start.7 = (f16[17,8,640]{2,1,0:T(8,128)(2,1)S(1)}, f16[17,8,640]{2,1,0:T(8,128)(2,1)}, u32[]{:S(2)}) copy-start(f16[17,8,640]{2,1,0:T(8,128)(2,1)} %copy-done.6) | copy-start | bytes 522244
  38.4 6.3 %collective-permute-start.5 = (f16[17,8,640]{2,1,0:T(8,128)(2,1)S(1)}, f16[17,8,640]{2,1,0:T(8,128)(2,1)S(1)}, u32[]{:S(2)}, u32[]{:S(2)}) collective-permute-start(f16[17,8,640]{2,1,0:T(8,128)(2,1)S(1)} %fusion.4), channel_id=1, source_target_pairs={{0,4},{4,0},{8,12},{12,8},{16,20},{20,16},{24,28},{28,24},{1,5},{5... | collective-permute-start | bytes 522248 | tf_op jit(solution)/shard_map/ppermute | solution.py:448
  45.0 3.5 %collective-permute-start.6 = (bf16[4,64,160]{2,1,0:T(8,128)(2,1)S(1)}, bf16[4,64,160]{2,1,0:T(8,128)(2,1)S(1)}, u32[]{:S(2)}, u32[]{:S(2)}) collective-permute-start(bf16[4,64,160]{2,1,0:T(8,128)(2,1)S(1)} %get-tuple-element.34), channel_id=1, source_target_pairs={{0,1},{1,0},{2,3},{3,2},{4,5},{5,4},{6,7},{7,6},{8,9},{9,8},{10,11... | collective-permute-start | bytes 245768 | tf_op jit(solution)/shard_map/ppermute | solution.py:484
  45.1 3.4 %copy-start.5 = (f32[17,8,640]{2,1,0:T(8,128)S(1)}, f32[17,8,640]{2,1,0:T(8,128)}, u32[]{:S(2)}) copy-start(f32[17,8,640]{2,1,0:T(8,128)} %copy-done.4) | copy-start | bytes 1044484
  45.1 3.4 %collective-permute-start.7 = (bf16[4,64,160]{2,1,0:T(8,128)(2,1)S(1)}, bf16[4,64,160]{2,1,0:T(8,128)(2,1)S(1)}, u32[]{:S(2)}, u32[]{:S(2)}) collective-permute-start(bf16[4,64,160]{2,1,0:T(8,128)(2,1)S(1)} %get-tuple-element.35), channel_id=1, source_target_pairs={{1,2},{2,1},{5,6},{6,5},{9,10},{10,9},{13,14},{14,13},{17,18},{18,... | collective-permute-start | bytes 245768 | tf_op jit(solution)/shard_map/ppermute | solution.py:485
  52.4 5.5 %collective-permute-start.8 = (f16[17,8,640]{2,1,0:T(8,128)(2,1)S(1)}, f16[17,8,640]{2,1,0:T(8,128)(2,1)S(1)}, u32[]{:S(2)}, u32[]{:S(2)}) collective-permute-start(f16[17,8,640]{2,1,0:T(8,128)(2,1)S(1)} %fusion.6), channel_id=1, source_target_pairs={{0,4},{4,0},{8,12},{12,8},{16,20},{20,16},{24,28},{28,24},{1,5},{5... | collective-permute-start | bytes 522248 | tf_op jit(solution)/shard_map/ppermute | solution.py:448
  58.2 6.8 %collective-permute-start.9 = (f16[17,8,640]{2,1,0:T(8,128)(2,1)S(1)}, f16[17,8,640]{2,1,0:T(8,128)(2,1)S(1)}, u32[]{:S(2)}, u32[]{:S(2)}) collective-permute-start(f16[17,8,640]{2,1,0:T(8,128)(2,1)S(1)} %fusion.7), channel_id=1, source_target_pairs={{0,8},{4,12},{8,0},{12,4},{16,24},{20,28},{24,16},{28,20},{1,9},{5... | collective-permute-start | bytes 522248 | tf_op jit(solution)/shard_map/ppermute | solution.py:448
  65.4 8.8 %collective-permute-start.10 = (f16[17,8,640]{2,1,0:T(8,128)(2,1)S(1)}, f16[17,8,640]{2,1,0:T(8,128)(2,1)S(1)}, u32[]{:S(2)}, u32[]{:S(2)}) collective-permute-start(f16[17,8,640]{2,1,0:T(8,128)(2,1)S(1)} %fusion.8), channel_id=1, source_target_pairs={{0,24},{4,28},{8,16},{12,20},{16,8},{20,12},{24,0},{28,4},{1,25},{... | collective-permute-start | bytes 522248 | tf_op jit(solution)/shard_map/ppermute | solution.py:448
  74.9 2.0 %collective-permute-start.11 = (f32[2,8,128]{2,1,0:T(8,128)S(1)}, f32[2,8,128]{2,1,0:T(8,128)S(1)}, u32[]{:S(2)}, u32[]{:S(2)}) collective-permute-start(f32[2,8,128]{2,1,0:T(8,128)S(1)} %changes.1), channel_id=1, source_target_pairs={{0,1},{1,0},{2,3},{3,2},{4,5},{5,4},{6,7},{7,6},{8,9},{9,8},{10,11... | collective-permute-start | bytes 24584 | tf_op jit(solution)/shard_map/ppermute | solution.py:500
  75.3 6.6 %collective-permute-start.12 = (f16[17,8,640]{2,1,0:T(8,128)(2,1)S(1)}, f16[17,8,640]{2,1,0:T(8,128)(2,1)S(1)}, u32[]{:S(2)}, u32[]{:S(2)}) collective-permute-start(f16[17,8,640]{2,1,0:T(8,128)(2,1)S(1)} %fusion.10), channel_id=1, source_target_pairs={{0,4},{4,0},{8,12},{12,8},{16,20},{20,16},{24,28},{28,24},{1,5},{5... | collective-permute-start | bytes 522248 | tf_op jit(solution)/shard_map/ppermute | solution.py:448
  76.9 10.0 %collective-permute-start.14 = (f32[8,128]{1,0:T(8,128)S(1)}, f32[8,128]{1,0:T(8,128)S(1)}, u32[]{:S(2)}, u32[]{:S(2)}) collective-permute-start(f32[8,128]{1,0:T(8,128)S(1)} %get-tuple-element.55), channel_id=1, source_target_pairs={{0,6},{1,7},{2,4},{3,5},{4,2},{5,3},{6,0},{7,1},{8,14},{9,15},{10,... | collective-permute-start | bytes 12296 | tf_op jit(solution)/shard_map/ppermute | solution.py:511
  80.7 6.2 %collective-permute-start.13 = (f32[8,128]{1,0:T(8,128)S(1)}, f32[8,128]{1,0:T(8,128)S(1)}, u32[]{:S(2)}, u32[]{:S(2)}) collective-permute-start(f32[8,128]{1,0:T(8,128)S(1)} %get-tuple-element.55), channel_id=1, source_target_pairs={{0,4},{1,5},{2,6},{3,7},{4,0},{5,1},{6,2},{7,3},{8,12},{9,13},{10,... | collective-permute-start | bytes 12296 | tf_op jit(solution)/shard_map/ppermute | solution.py:510
  82.1 5.4 %collective-permute-start.15 = (f32[8,128]{1,0:T(8,128)S(1)}, f32[8,128]{1,0:T(8,128)S(1)}, u32[]{:S(2)}, u32[]{:S(2)}) collective-permute-start(f32[8,128]{1,0:T(8,128)S(1)} %get-tuple-element.41), channel_id=1, source_target_pairs={{0,2},{1,3},{2,0},{3,1},{4,6},{5,7},{6,4},{7,5},{8,10},{9,11},{10,... | collective-permute-start | bytes 12296 | tf_op jit(solution)/shard_map/ppermute | solution.py:512

commit v6 on v5

--- a/solution.py
+++ b/solution.py
@@ -478,20 +478,29 @@
     pair = lax.optimization_barrier(jnp.broadcast_to(timestep_pair[:, None], (2, 128)))
     real = jnp.stack(coefficients(pair))
     temb = time_embed(pair[0, : C // 2], time_weight).reshape(1, -1)
-    first = jnp.pad(conv_first.transpose(0, 2, 1), ((0, 0), (0, C), (0, 0)))
-
-    def sweep(other, keep, near, far):
+    def weights_of(conv):
+        return jnp.pad(conv.transpose(0, 2, 1), ((0, 0), (0, C), (0, 0)))
+
+    first = weights_of(conv_first)
+    first, start_latent = lax.optimization_barrier((first, start_latent))
+
+    def sweep(first, other, keep, noise, near, far):
         inner = lax.ppermute(near, "space", inner_pairs)
         outer = lax.ppermute(far, "space", outer_pairs)
-        yours, mine = denoise(real, other, keep, noise_halves, inner, outer, first, conv_second, temb)
-        return yours, mine, prefix(yours, mine, step_index)
-
+        return denoise(real, other, keep, noise, inner, outer, first, conv_second, temb)
+
+    is_anchor = step_index == 0
     other0, keep0, near, far = arrange(start_latent, True)
-    noise_halves = arrange(noise_step, False)
-    _, _, (other1, keep1, reached1) = sweep(other0, keep0, near, far)
-    is_anchor = step_index == 0
+    yours1, mine1 = sweep(first, other0, keep0, arrange(noise_step, False), near, far)
+    mine1, conv_first, start_latent, noise_step = lax.optimization_barrier(
+        (mine1, conv_first, start_latent, noise_step)
+    )
+    first, noise_halves = weights_of(conv_first), arrange(noise_step, False)
+    other0, keep0 = arrange(start_latent, False)
+    other1, keep1, reached1 = prefix(yours1, mine1, step_index)
     other1, keep1 = jnp.where(is_anchor, other0, other1), jnp.where(is_anchor, keep0, keep1)
-    yours2, mine2, (other2, keep2, reached2) = sweep(other1, keep1, *edges(other1, keep1))
+    yours2, mine2 = sweep(first, other1, keep1, noise_halves, *edges(other1, keep1))
+    other2, keep2, reached2 = prefix(yours2, mine2, step_index)
     sums = change_sums(reached1, reached2)
     steps = lax.axis_size("step")
     cell_count = start_latent.size * space

time: 88.3 us -> 83.8 us (0.949)
  other arithmetic: 5.6 us -> 3.09 us
  local copies, waits for them, and re-layouts: 3.7 us -> 2.05 us
  waiting for transfers between devices: 27.3 us -> 25.8 us
    unnamed x18 -> x12, local copies, waits for them, and re-layouts: 1.77 us -> 0.09 us
    ppermute x8, waiting for transfers between devices: 26.7 us -> 25.2 us  [exchange(): lax.ppermute(coded(half), 'step', [(i, i ^ flip) for i in range(steps)])]
    add x2, other arithmetic: 1.85 us -> 0.93 us  [prefix(): return (exchange(give, 1), keep, (keep + mine, give + partner))]
    convert_element_type x8, other arithmetic: 1.12 us -> 0.2 us  [decoded(): half = message.astype(jnp.float32)]
    pallas_call x10 -> x12, Pallas kernels: 18.2 us -> 18.6 us  [call(): pl.pallas_call(kernel, out_shape=out_shape, in_specs=[WHOLE] * len(arrays...]
  transfers between devices with their start and end apart: 16 -> 16, of which waited for: 9 -> 8; matrix products, arithmetic and copies ran while one was open for 2% -> 1% of each run, Pallas kernels for 12% -> 14%
where the time goes in v6:
time: 83.8 us; the launch traced here: 83.7 us
  starting transfers between devices  31.8 us (38%)
  waiting for transfers between devices  25.8 us (31%)
  Pallas kernels  19.5 us (23%)
  other arithmetic  3.09 us (4%)
  local copies, waits for them, and re-layouts  2.05 us (2%)
  between operations  1.1 us (1%)
    ppermute x8, waiting for transfers between devices, exchange(): lax.ppermute(coded(half), 'step', [(i, i ^ flip) for i in range(steps)])  25.2 us
    ppermute x8, starting transfers between devices, exchange(): lax.ppermute(coded(half), 'step', [(i, i ^ flip) for i in range(steps)])  20.3 us
    pallas_call x12, Pallas kernels, call(): pl.pallas_call(kernel, out_shape=out_shape, in_specs=[WHOLE] * len(arrays...  18.6 us
    ppermute x1, starting transfers between devices, local(): lax.ppermute(near_sum, 'space', far)  3.96 us
    ppermute x1, starting transfers between devices, local(): lax.ppermute(sums[1], ('step', 'space'), cross)  3.87 us
  transfers between devices with their start and end apart: 16, of which 8 were waited for; matrix products, arithmetic and copies ran while one was open for 1% of the time, Pallas kernels for 14%

profile of v6, /device:TPU:0, one launch (start us, length us, event | category | flops | bytes accessed | tf_op | source)
XLA Modules:
  0.0 83.7 jit_solution(801775708649620440)
XLA Ops:
  0.7 1.3 %pad.7.first = bf16[3,640,256]{2,1,0:T(8,128)(2,1)S(1)} pad(bf16[3,576,256]{2,1,0:T(8,128)(2,1)} %bitcast.60, bf16[]{:T(256)} %constant.98.clone.1), padding=0_0x0_64x0_0 | pad | bytes 1867778 | tf_op jit(solution)/shard_map/jit(_pad)/pad | solution.py:482
  2.0 0.4 arrange.4
  2.4 0.5 collective-permute-start
  2.9 0.8 collective-permute-start.1
  3.9 0.2 arrange.5
  4.2 0.2 fusion.55.temb
  4.4 2.4 %interior.2 = (bf16[4,480,256]{2,1,0:T(8,128)(2,1)S(1)}, bf16[4,320,384]{2,1,0:T(8,128)(2,1)S(1)}) custom-call(f32[17,8,640]{2,1,0:T(8,128)S(1)} %get-tuple-element.36.other, f32[17,8,640]{2,1,0:T(8,128)S(1)} %get-tuple-element.33.keep, bf16[3,640,256]{2,1,0:T(8,128)(2,1)S(1)} %pad.7.first, f32[1,256]{1,0:T(1,128)S(1)} %fusion.55.temb), custom_call_target="tpu_custom_call" | custom-call | flops 2000000000 | bytes 4000000 | tf_op jit(solution)/shard_map/interior/pallas_call | solution.py:307
  6.8 3.7 %sending.2 = (f32[17,8,640]{2,1,0:T(8,128)S(1)}, bf16[2,320,256]{2,1,0:T(8,128)(2,1)S(1)}, bf16[2,640,384]{2,1,0:T(8,128)(2,1)S(1)}) custom-call(f32[3,128]{1,0:T(4,128)S(1)} %pad_maximum_fusion.real, f32[17,8,640]{2,1,0:T(8,128)S(1)} %get-tuple-element.36.other, f32[17,8,640]{2,1,0:T(8,128)S(1)} %get-tuple-element.33.keep, ...), custom_call_target="tpu_custom_call" | custom-call | flops 2000000000 | bytes 4000000 | tf_op jit(solution)/shard_map/sending/pallas_call | solution.py:307
  10.6 0.1 fusion
  10.7 2.5 %collective-permute-start.2 = (f16[17,8,640]{2,1,0:T(8,128)(2,1)S(1)}, f16[17,8,640]{2,1,0:T(8,128)(2,1)S(1)}, u32[]{:S(2)}, u32[]{:S(2)}) collective-permute-start(f16[17,8,640]{2,1,0:T(8,128)(2,1)S(1)} %fusion), channel_id=1, source_target_pairs={{0,4},{4,0},{8,12},{12,8},{16,20},{20,16},{24,28},{28,24},{1,5},{5... | collective-permute-start | bytes 522248 | tf_op jit(solution)/shard_map/ppermute | solution.py:448
  13.2 2.5 %keeping.2 = f32[17,8,640]{2,1,0:T(8,128)S(1)} custom-call(f32[3,128]{1,0:T(4,128)S(1)} %pad_maximum_fusion.real, f32[17,8,640]{2,1,0:T(8,128)S(1)} %get-tuple-element.33.keep, f32[17,8,640]{2,1,0:T(8,128)S(1)} %get-tuple-element.34.noise_keep, bf16[3,640,256]{2,1,0:T(8,128)(2,1)S(1)} %pad.7.first, bf16[3,64,2304]{2,1,0:T(8,128)(2,1)S(1)} %copy-done.3, ...), custom_call_target="tpu_custom_call" | custom-call | flops 2000000000 | bytes 4000000 | tf_op jit(solution)/shard_map/keeping/pallas_call | solution.py:307
  15.6 0.9 %collective-permute-done.2 = f16[17,8,640]{2,1,0:T(8,128)(2,1)S(1)} collective-permute-done((f16[17,8,640]{2,1,0:T(8,128)(2,1)S(1)}, f16[17,8,640]{2,1,0:T(8,128)(2,1)S(1)}, u32[]{:S(2)}, u32[]{:S(2)}) %collective-permute-start.2) | collective-permute-done | bytes 174112 | tf_op jit(solution)/shard_map/ppermute | solution.py:448
  16.6 0.1 add_select_fusion.9
  16.9 2.1 %collective-permute-start.3 = (f16[17,8,640]{2,1,0:T(8,128)(2,1)S(1)}, f16[17,8,640]{2,1,0:T(8,128)(2,1)S(1)}, u32[]{:S(2)}, u32[]{:S(2)}) collective-permute-start(f16[17,8,640]{2,1,0:T(8,128)(2,1)S(1)} %fusion.1), channel_id=1, source_target_pairs={{0,8},{4,12},{8,0},{12,4},{16,24},{20,28},{24,16},{28,20},{1,9},{5... | collective-permute-start | bytes 522248 | tf_op jit(solution)/shard_map/ppermute | solution.py:448
  19.0 4.0 %collective-permute-done.3 = f16[17,8,640]{2,1,0:T(8,128)(2,1)S(1)} collective-permute-done((f16[17,8,640]{2,1,0:T(8,128)(2,1)S(1)}, f16[17,8,640]{2,1,0:T(8,128)(2,1)S(1)}, u32[]{:S(2)}, u32[]{:S(2)}) %collective-permute-start.3) | collective-permute-done | bytes 174112 | tf_op jit(solution)/shard_map/ppermute | solution.py:448
  23.0 0.1 add_select_fusion.8
  23.3 4.4 %collective-permute-start.4 = (f16[17,8,640]{2,1,0:T(8,128)(2,1)S(1)}, f16[17,8,640]{2,1,0:T(8,128)(2,1)S(1)}, u32[]{:S(2)}, u32[]{:S(2)}) collective-permute-start(f16[17,8,640]{2,1,0:T(8,128)(2,1)S(1)} %fusion.2), channel_id=1, source_target_pairs={{0,24},{4,28},{8,16},{12,20},{16,8},{20,12},{24,0},{28,4},{1,25},{... | collective-permute-start | bytes 522248 | tf_op jit(solution)/shard_map/ppermute | solution.py:448
  27.7 0.2 arrange.6
  28.0 5.0 %collective-permute-done.4 = f16[17,8,640]{2,1,0:T(8,128)(2,1)S(1)} collective-permute-done((f16[17,8,640]{2,1,0:T(8,128)(2,1)S(1)}, f16[17,8,640]{2,1,0:T(8,128)(2,1)S(1)}, u32[]{:S(2)}, u32[]{:S(2)}) %collective-permute-start.4) | collective-permute-done | bytes 174112 | tf_op jit(solution)/shard_map/ppermute | solution.py:448
  33.1 0.5 fusion.11
  33.7 1.8 %collective-permute-start.5 = (f16[17,8,640]{2,1,0:T(8,128)(2,1)S(1)}, f16[17,8,640]{2,1,0:T(8,128)(2,1)S(1)}, u32[]{:S(2)}, u32[]{:S(2)}) collective-permute-start(f16[17,8,640]{2,1,0:T(8,128)(2,1)S(1)} %fusion.4), channel_id=1, source_target_pairs={{0,4},{4,0},{8,12},{12,8},{16,20},{20,16},{24,28},{28,24},{1,5},{5... | collective-permute-start | bytes 522248 | tf_op jit(solution)/shard_map/ppermute | solution.py:448
  35.6 0.2 arrange.7
  35.8 4.3 %collective-permute-done.5 = f16[17,8,640]{2,1,0:T(8,128)(2,1)S(1)} collective-permute-done((f16[17,8,640]{2,1,0:T(8,128)(2,1)S(1)}, f16[17,8,640]{2,1,0:T(8,128)(2,1)S(1)}, u32[]{:S(2)}, u32[]{:S(2)}) %collective-permute-start.5) | collective-permute-done | bytes 174112 | tf_op jit(solution)/shard_map/ppermute | solution.py:448
  40.2 0.1 fusion.5.other
  40.3 0.2 edges.1
  40.6 0.8 %collective-permute-start.7 = (bf16[4,64,160]{2,1,0:T(8,128)(2,1)S(1)}, bf16[4,64,160]{2,1,0:T(8,128)(2,1)S(1)}, u32[]{:S(2)}, u32[]{:S(2)}) collective-permute-start(bf16[4,64,160]{2,1,0:T(8,128)(2,1)S(1)} %get-tuple-element.55), channel_id=1, source_target_pairs={{1,2},{2,1},{5,6},{6,5},{9,10},{10,9},{13,14},{14,13},{17,18},{18,... | collective-permute-start | bytes 245768 | tf_op jit(solution)/shard_map/ppermute | solution.py:489
  41.4 2.4 %interior.3 = (bf16[4,480,256]{2,1,0:T(8,128)(2,1)S(1)}, bf16[4,320,384]{2,1,0:T(8,128)(2,1)S(1)}) custom-call(f32[17,8,640]{2,1,0:T(8,128)S(1)} %fusion.5.other, f32[17,8,640]{2,1,0:T(8,128)S(1)} %get-tuple-element.74.keep, bf16[3,640,256]{2,1,0:T(8,128)(2,1)S(1)} %pad.8.first, f32[1,256]{1,0:T(1,128)S(1)} %fusion.55.temb), custom_call_target="tpu_custom_call" | custom-call | flops 2000000000 | bytes 4000000 | tf_op jit(solution)/shard_map/interior/pallas_call | solution.py:307
  43.8 3.7 %sending.3 = (f32[17,8,640]{2,1,0:T(8,128)S(1)}, bf16[2,320,256]{2,1,0:T(8,128)(2,1)S(1)}, bf16[2,640,384]{2,1,0:T(8,128)(2,1)S(1)}) custom-call(f32[3,128]{1,0:T(4,128)S(1)} %pad_maximum_fusion.real, f32[17,8,640]{2,1,0:T(8,128)S(1)} %fusion.5.other, f32[17,8,640]{2,1,0:T(8,128)S(1)} %get-tuple-element.74.keep, ...), custom_call_target="tpu_custom_call" | custom-call | flops 2000000000 | bytes 4000000 | tf_op jit(solution)/shard_map/sending/pallas_call | solution.py:307
  47.6 1.7 %collective-permute-start.8 = (f16[17,8,640]{2,1,0:T(8,128)(2,1)S(1)}, f16[17,8,640]{2,1,0:T(8,128)(2,1)S(1)}, u32[]{:S(2)}, u32[]{:S(2)}) collective-permute-start(f16[17,8,640]{2,1,0:T(8,128)(2,1)S(1)} %fusion.6), channel_id=1, source_target_pairs={{0,4},{4,0},{8,12},{12,8},{16,20},{20,16},{24,28},{28,24},{1,5},{5... | collective-permute-start | bytes 522248 | tf_op jit(solution)/shard_map/ppermute | solution.py:448
  49.4 2.5 %keeping.3.mine = f32[17,8,640]{2,1,0:T(8,128)S(1)} custom-call(f32[3,128]{1,0:T(4,128)S(1)} %pad_maximum_fusion.real, f32[17,8,640]{2,1,0:T(8,128)S(1)} %get-tuple-element.74.keep, f32[17,8,640]{2,1,0:T(8,128)S(1)} %get-tuple-element.49.noise_keep, bf16[3,640,256]{2,1,0:T(8,128)(2,1)S(1)} %pad.8.first, bf16[3,64,2304]{2,1,0:T(8,128)(2,1)S(1)} %copy-done.3, ...), custom_call_target="tpu_custom_call" | custom-call | flops 2000000000 | bytes 4000000 | tf_op jit(solution)/shard_map/keeping/pallas_call | solution.py:307
  51.9 1.3 %collective-permute-done.8 = f16[17,8,640]{2,1,0:T(8,128)(2,1)S(1)} collective-permute-done((f16[17,8,640]{2,1,0:T(8,128)(2,1)S(1)}, f16[17,8,640]{2,1,0:T(8,128)(2,1)S(1)}, u32[]{:S(2)}, u32[]{:S(2)}) %collective-permute-start.8) | collective-permute-done | bytes 174112 | tf_op jit(solution)/shard_map/ppermute | solution.py:448
  53.2 0.1 add_select_fusion.4
  53.5 3.6 %collective-permute-start.9 = (f16[17,8,640]{2,1,0:T(8,128)(2,1)S(1)}, f16[17,8,640]{2,1,0:T(8,128)(2,1)S(1)}, u32[]{:S(2)}, u32[]{:S(2)}) collective-permute-start(f16[17,8,640]{2,1,0:T(8,128)(2,1)S(1)} %fusion.7), channel_id=1, source_target_pairs={{0,8},{4,12},{8,0},{12,4},{16,24},{20,28},{24,16},{28,20},{1,9},{5... | collective-permute-start | bytes 522248 | tf_op jit(solution)/shard_map/ppermute | solution.py:448
  57.0 3.5 %collective-permute-done.9 = f16[17,8,640]{2,1,0:T(8,128)(2,1)S(1)} collective-permute-done((f16[17,8,640]{2,1,0:T(8,128)(2,1)S(1)}, f16[17,8,640]{2,1,0:T(8,128)(2,1)S(1)}, u32[]{:S(2)}, u32[]{:S(2)}) %collective-permute-start.9) | collective-permute-done | bytes 174112 | tf_op jit(solution)/shard_map/ppermute | solution.py:448
  60.6 0.1 add_select_fusion.3
  60.8 0.1 fusion.8
  60.9 2.5 %collective-permute-start.10 = (f16[17,8,640]{2,1,0:T(8,128)(2,1)S(1)}, f16[17,8,640]{2,1,0:T(8,128)(2,1)S(1)}, u32[]{:S(2)}, u32[]{:S(2)}) collective-permute-start(f16[17,8,640]{2,1,0:T(8,128)(2,1)S(1)} %fusion.8), channel_id=1, source_target_pairs={{0,24},{4,28},{8,16},{12,20},{16,8},{20,12},{24,0},{28,4},{1,25},{... | collective-permute-start | bytes 522248 | tf_op jit(solution)/shard_map/ppermute | solution.py:448
  63.4 6.2 %collective-permute-done.10 = f16[17,8,640]{2,1,0:T(8,128)(2,1)S(1)} collective-permute-done((f16[17,8,640]{2,1,0:T(8,128)(2,1)S(1)}, f16[17,8,640]{2,1,0:T(8,128)(2,1)S(1)}, u32[]{:S(2)}, u32[]{:S(2)}) %collective-permute-start.10) | collective-permute-done | bytes 174112 | tf_op jit(solution)/shard_map/ppermute | solution.py:448
  69.7 0.5 fusion.12
  70.1 0.2 changes.1
  70.4 0.4 collective-permute-start.11
  70.8 1.6 %collective-permute-start.12 = (f16[17,8,640]{2,1,0:T(8,128)(2,1)S(1)}, f16[17,8,640]{2,1,0:T(8,128)(2,1)S(1)}, u32[]{:S(2)}, u32[]{:S(2)}) collective-permute-start(f16[17,8,640]{2,1,0:T(8,128)(2,1)S(1)} %fusion.10), channel_id=1, source_target_pairs={{0,4},{4,0},{8,12},{12,8},{16,20},{20,16},{24,28},{28,24},{1,5},{5... | collective-permute-start | bytes 522248 | tf_op jit(solution)/shard_map/ppermute | solution.py:448
  72.4 3.9 %collective-permute-start.14 = (f32[8,128]{1,0:T(8,128)S(1)}, f32[8,128]{1,0:T(8,128)S(1)}, u32[]{:S(2)}, u32[]{:S(2)}) collective-permute-start(f32[8,128]{1,0:T(8,128)S(1)} %get-tuple-element.75), channel_id=1, source_target_pairs={{0,6},{1,7},{2,4},{3,5},{4,2},{5,3},{6,0},{7,1},{8,14},{9,15},{10,... | collective-permute-start | bytes 12296 | tf_op jit(solution)/shard_map/ppermute | solution.py:520
  76.3 1.1 %collective-permute-start.13 = (f32[8,128]{1,0:T(8,128)S(1)}, f32[8,128]{1,0:T(8,128)S(1)}, u32[]{:S(2)}, u32[]{:S(2)}) collective-permute-start(f32[8,128]{1,0:T(8,128)S(1)} %get-tuple-element.75), channel_id=1, source_target_pairs={{0,4},{1,5},{2,6},{3,7},{4,0},{5,1},{6,2},{7,3},{8,12},{9,13},{10,... | collective-permute-start | bytes 12296 | tf_op jit(solution)/shard_map/ppermute | solution.py:519
  77.6 4.0 %collective-permute-start.15 = (f32[8,128]{1,0:T(8,128)S(1)}, f32[8,128]{1,0:T(8,128)S(1)}, u32[]{:S(2)}, u32[]{:S(2)}) collective-permute-start(f32[8,128]{1,0:T(8,128)S(1)} %get-tuple-element.61), channel_id=1, source_target_pairs={{0,2},{1,3},{2,0},{3,1},{4,6},{5,7},{6,4},{7,5},{8,10},{9,11},{10,... | collective-permute-start | bytes 12296 | tf_op jit(solution)/shard_map/ppermute | solution.py:521
  81.5 1.0 %finish.1 = f32[64,4,640]{2,1,0:T(4,128)} custom-call(f32[17,8,640]{2,1,0:T(8,128)S(1)} %multiply_select_fusion.other, f32[17,8,640]{2,1,0:T(8,128)S(1)} %get-tuple-element.72.keep, f32[17,8,640]{2,1,0:T(8,128)S(1)} %get-tuple-element.59.yours, f32[17,8,640]{2,1,0:T(8,128)S(1)} %keeping.3.mine), custom_call_target="tpu_custom_call" | custom-call | flops 8000000000 | bytes 4000000 | tf_op jit(solution)/shard_map/finish/pallas_call | solution.py:397
  82.5 0.6 collective-permute-done.15
  83.1 0.5 slice.89
  (63 shorter events, 1.6 us)
Async XLA Ops:
  0.6 3.5 %copy-start = (f32[64,256]{1,0:T(8,128)S(1)}, f32[64,256]{1,0:T(8,128)}, u32[]{:S(2)}) copy-start(f32[64,256]{1,0:T(8,128)} %param.11) | copy-start | bytes 196612
  0.6 1.4 %copy-start.1 = (f32[1,64,4,640]{3,2,1,0:T(4,128)S(1)}, f32[1,64,4,640]{3,2,1,0:T(4,128)}, u32[]{:S(2)}) copy-start(f32[1,64,4,640]{3,2,1,0:T(4,128)} %param.6) | copy-start | bytes 1966084
  2.0 1.9 %copy-start.2 = (f32[1,64,4,640]{3,2,1,0:T(4,128)S(1)}, f32[1,64,4,640]{3,2,1,0:T(4,128)}, u32[]{:S(2)}) copy-start(f32[1,64,4,640]{3,2,1,0:T(4,128)} %param.7) | copy-start | bytes 1966084
  2.4 4.4 %collective-permute-start = (bf16[4,64,160]{2,1,0:T(8,128)(2,1)S(1)}, bf16[4,64,160]{2,1,0:T(8,128)(2,1)S(1)}, u32[]{:S(2)}, u32[]{:S(2)}) collective-permute-start(bf16[4,64,160]{2,1,0:T(8,128)(2,1)S(1)} %get-tuple-element.39), channel_id=1, source_target_pairs={{0,1},{1,0},{2,3},{3,2},{4,5},{5,4},{6,7},{7,6},{8,9},{9,8},{10,11... | collective-permute-start | bytes 245768 | tf_op jit(solution)/shard_map/ppermute | solution.py:488
  2.9 0.8 copy-start.5
  2.9 3.9 %collective-permute-start.1 = (bf16[4,64,160]{2,1,0:T(8,128)(2,1)S(1)}, bf16[4,64,160]{2,1,0:T(8,128)(2,1)S(1)}, u32[]{:S(2)}, u32[]{:S(2)}) collective-permute-start(bf16[4,64,160]{2,1,0:T(8,128)(2,1)S(1)} %get-tuple-element.40), channel_id=1, source_target_pairs={{1,2},{2,1},{5,6},{6,5},{9,10},{10,9},{13,14},{14,13},{17,18},{18,... | collective-permute-start | bytes 245768 | tf_op jit(solution)/shard_map/ppermute | solution.py:489
  4.4 2.4 %copy-start.3 = (bf16[3,64,2304]{2,1,0:T(8,128)(2,1)S(1)}, bf16[3,64,2304]{2,1,0:T(8,128)(2,1)}, u32[]{:S(2)}) copy-start(bf16[3,64,2304]{2,1,0:T(8,128)(2,1)} %second.7) | copy-start | bytes 2654212
  10.7 5.9 %collective-permute-start.2 = (f16[17,8,640]{2,1,0:T(8,128)(2,1)S(1)}, f16[17,8,640]{2,1,0:T(8,128)(2,1)S(1)}, u32[]{:S(2)}, u32[]{:S(2)}) collective-permute-start(f16[17,8,640]{2,1,0:T(8,128)(2,1)S(1)} %fusion), channel_id=1, source_target_pairs={{0,4},{4,0},{8,12},{12,8},{16,20},{20,16},{24,28},{28,24},{1,5},{5... | collective-permute-start | bytes 522248 | tf_op jit(solution)/shard_map/ppermute | solution.py:448
  16.9 6.1 %collective-permute-start.3 = (f16[17,8,640]{2,1,0:T(8,128)(2,1)S(1)}, f16[17,8,640]{2,1,0:T(8,128)(2,1)S(1)}, u32[]{:S(2)}, u32[]{:S(2)}) collective-permute-start(f16[17,8,640]{2,1,0:T(8,128)(2,1)S(1)} %fusion.1), channel_id=1, source_target_pairs={{0,8},{4,12},{8,0},{12,4},{16,24},{20,28},{24,16},{28,20},{1,9},{5... | collective-permute-start | bytes 522248 | tf_op jit(solution)/shard_map/ppermute | solution.py:448
  23.3 9.7 %collective-permute-start.4 = (f16[17,8,640]{2,1,0:T(8,128)(2,1)S(1)}, f16[17,8,640]{2,1,0:T(8,128)(2,1)S(1)}, u32[]{:S(2)}, u32[]{:S(2)}) collective-permute-start(f16[17,8,640]{2,1,0:T(8,128)(2,1)S(1)} %fusion.2), channel_id=1, source_target_pairs={{0,24},{4,28},{8,16},{12,20},{16,8},{20,12},{24,0},{28,4},{1,25},{... | collective-permute-start | bytes 522248 | tf_op jit(solution)/shard_map/ppermute | solution.py:448
  33.0 2.5 %copy-start.4 = (bf16[3,256,576]{1,2,0:T(8,128)(2,1)S(1)}, bf16[3,256,576]{1,2,0:T(8,128)(2,1)}, u32[]{:S(2)}) copy-start(bf16[3,256,576]{1,2,0:T(8,128)(2,1)} %param.9) | copy-start | bytes 2654212
  33.7 6.4 %collective-permute-start.5 = (f16[17,8,640]{2,1,0:T(8,128)(2,1)S(1)}, f16[17,8,640]{2,1,0:T(8,128)(2,1)S(1)}, u32[]{:S(2)}, u32[]{:S(2)}) collective-permute-start(f16[17,8,640]{2,1,0:T(8,128)(2,1)S(1)} %fusion.4), channel_id=1, source_target_pairs={{0,4},{4,0},{8,12},{12,8},{16,20},{20,16},{24,28},{28,24},{1,5},{5... | collective-permute-start | bytes 522248 | tf_op jit(solution)/shard_map/ppermute | solution.py:448
  40.5 3.3 %collective-permute-start.6 = (bf16[4,64,160]{2,1,0:T(8,128)(2,1)S(1)}, bf16[4,64,160]{2,1,0:T(8,128)(2,1)S(1)}, u32[]{:S(2)}, u32[]{:S(2)}) collective-permute-start(bf16[4,64,160]{2,1,0:T(8,128)(2,1)S(1)} %get-tuple-element.54), channel_id=1, source_target_pairs={{0,1},{1,0},{2,3},{3,2},{4,5},{5,4},{6,7},{7,6},{8,9},{9,8},{10,11... | collective-permute-start | bytes 245768 | tf_op jit(solution)/shard_map/ppermute | solution.py:488
  40.6 3.2 %collective-permute-start.7 = (bf16[4,64,160]{2,1,0:T(8,128)(2,1)S(1)}, bf16[4,64,160]{2,1,0:T(8,128)(2,1)S(1)}, u32[]{:S(2)}, u32[]{:S(2)}) collective-permute-start(bf16[4,64,160]{2,1,0:T(8,128)(2,1)S(1)} %get-tuple-element.55), channel_id=1, source_target_pairs={{1,2},{2,1},{5,6},{6,5},{9,10},{10,9},{13,14},{14,13},{17,18},{18,... | collective-permute-start | bytes 245768 | tf_op jit(solution)/shard_map/ppermute | solution.py:489
  47.6 5.5 %collective-permute-start.8 = (f16[17,8,640]{2,1,0:T(8,128)(2,1)S(1)}, f16[17,8,640]{2,1,0:T(8,128)(2,1)S(1)}, u32[]{:S(2)}, u32[]{:S(2)}) collective-permute-start(f16[17,8,640]{2,1,0:T(8,128)(2,1)S(1)} %fusion.6), channel_id=1, source_target_pairs={{0,4},{4,0},{8,12},{12,8},{16,20},{20,16},{24,28},{28,24},{1,5},{5... | collective-permute-start | bytes 522248 | tf_op jit(solution)/shard_map/ppermute | solution.py:448
  53.5 7.1 %collective-permute-start.9 = (f16[17,8,640]{2,1,0:T(8,128)(2,1)S(1)}, f16[17,8,640]{2,1,0:T(8,128)(2,1)S(1)}, u32[]{:S(2)}, u32[]{:S(2)}) collective-permute-start(f16[17,8,640]{2,1,0:T(8,128)(2,1)S(1)} %fusion.7), channel_id=1, source_target_pairs={{0,8},{4,12},{8,0},{12,4},{16,24},{20,28},{24,16},{28,20},{1,9},{5... | collective-permute-start | bytes 522248 | tf_op jit(solution)/shard_map/ppermute | solution.py:448
  60.9 8.7 %collective-permute-start.10 = (f16[17,8,640]{2,1,0:T(8,128)(2,1)S(1)}, f16[17,8,640]{2,1,0:T(8,128)(2,1)S(1)}, u32[]{:S(2)}, u32[]{:S(2)}) collective-permute-start(f16[17,8,640]{2,1,0:T(8,128)(2,1)S(1)} %fusion.8), channel_id=1, source_target_pairs={{0,24},{4,28},{8,16},{12,20},{16,8},{20,12},{24,0},{28,4},{1,25},{... | collective-permute-start | bytes 522248 | tf_op jit(solution)/shard_map/ppermute | solution.py:448
  70.4 2.1 %collective-permute-start.11 = (f32[2,8,128]{2,1,0:T(8,128)S(1)}, f32[2,8,128]{2,1,0:T(8,128)S(1)}, u32[]{:S(2)}, u32[]{:S(2)}) collective-permute-start(f32[2,8,128]{2,1,0:T(8,128)S(1)} %changes.1), channel_id=1, source_target_pairs={{0,1},{1,0},{2,3},{3,2},{4,5},{5,4},{6,7},{7,6},{8,9},{9,8},{10,11... | collective-permute-start | bytes 24584 | tf_op jit(solution)/shard_map/ppermute | solution.py:509
  70.8 6.6 %collective-permute-start.12 = (f16[17,8,640]{2,1,0:T(8,128)(2,1)S(1)}, f16[17,8,640]{2,1,0:T(8,128)(2,1)S(1)}, u32[]{:S(2)}, u32[]{:S(2)}) collective-permute-start(f16[17,8,640]{2,1,0:T(8,128)(2,1)S(1)} %fusion.10), channel_id=1, source_target_pairs={{0,4},{4,0},{8,12},{12,8},{16,20},{20,16},{24,28},{28,24},{1,5},{5... | collective-permute-start | bytes 522248 | tf_op jit(solution)/shard_map/ppermute | solution.py:448
  72.4 10.1 %collective-permute-start.14 = (f32[8,128]{1,0:T(8,128)S(1)}, f32[8,128]{1,0:T(8,128)S(1)}, u32[]{:S(2)}, u32[]{:S(2)}) collective-permute-start(f32[8,128]{1,0:T(8,128)S(1)} %get-tuple-element.75), channel_id=1, source_target_pairs={{0,6},{1,7},{2,4},{3,5},{4,2},{5,3},{6,0},{7,1},{8,14},{9,15},{10,... | collective-permute-start | bytes 12296 | tf_op jit(solution)/shard_map/ppermute | solution.py:520
  76.3 6.2 %collective-permute-start.13 = (f32[8,128]{1,0:T(8,128)S(1)}, f32[8,128]{1,0:T(8,128)S(1)}, u32[]{:S(2)}, u32[]{:S(2)}) collective-permute-start(f32[8,128]{1,0:T(8,128)S(1)} %get-tuple-element.75), channel_id=1, source_target_pairs={{0,4},{1,5},{2,6},{3,7},{4,0},{5,1},{6,2},{7,3},{8,12},{9,13},{10,... | collective-permute-start | bytes 12296 | tf_op jit(solution)/shard_map/ppermute | solution.py:519
  77.6 5.5 %collective-permute-start.15 = (f32[8,128]{1,0:T(8,128)S(1)}, f32[8,128]{1,0:T(8,128)S(1)}, u32[]{:S(2)}, u32[]{:S(2)}) collective-permute-start(f32[8,128]{1,0:T(8,128)S(1)} %get-tuple-element.61), channel_id=1, source_target_pairs={{0,2},{1,3},{2,0},{3,1},{4,6},{5,7},{6,4},{7,5},{8,10},{9,11},{10,... | collective-permute-start | bytes 12296 | tf_op jit(solution)/shard_map/ppermute | solution.py:521

commit v7 on v6

--- a/solution.py
+++ b/solution.py
@@ -11,6 +11,7 @@
 C = 64
 COLS = 80
 SUB = 8
+LANES = 128
 NT = (((1,), (1,)), ((), ()))
 MEGA = 2**20
 
@@ -45,6 +46,28 @@
     )
 
 
+def frame_tiles(ref):
+    return ref.shape[0] // 2
+
+
+def frame_of(ref, slot):
+    tiles = frame_tiles(ref)
+    value = ref[pl.ds(slot * tiles, tiles)].reshape(C // SUB, -1, SUB, LANES)
+    return jnp.concatenate([value[:, i].reshape(C, LANES) for i in range(value.shape[1])], axis=1)
+
+
+def put_frame(ref, slot, value):
+    across = value.shape[1] // LANES
+    for row in range(C // SUB):
+        for i in range(across):
+            tile = value[row * SUB : (row + 1) * SUB, i * LANES : (i + 1) * LANES]
+            ref[slot * frame_tiles(ref) + row * across + i] = tile
+
+
+def length_of(ref):
+    return frame_tiles(ref) * SUB * LANES // C
+
+
 class Frames:
     def __init__(self, parity):
         self.parity = parity
@@ -53,13 +76,10 @@
         return jnp.where(self.parity == 1, v % 2, (v + 1) % 2)
 
     def load(self, halves, v):
-        tiles = C // SUB
-        ref = halves[0] if v < 2 else halves[1]
-        return ref[pl.ds(self.slot(v) * tiles, tiles)].reshape(C, ref.shape[2])
+        return frame_of(halves[0] if v < 2 else halves[1], self.slot(v))
 
     def store(self, ref, v, value):
-        tiles = C // SUB
-        ref[pl.ds(self.slot(v) * tiles, tiles)] = value.reshape(tiles, SUB, ref.shape[2])
+        put_frame(ref, self.slot(v), value)
 
     def tap(self, a):
         return jnp.where(self.parity == 1, a, 2 - a)
@@ -84,11 +104,11 @@
 def ends_of(flags, frames, halves, inner, outer):
     edge = 2 * COLS
     for half, ref in enumerate(halves):
-        length = ref.shape[2]
+        length = length_of(ref)
         for slot in range(2):
-            slabs = pl.ds(slot * (C // SUB), C // SUB)
-            head = ref[slabs, :, 0:edge].reshape(C, edge).astype(jnp.bfloat16)
-            tail = ref[slabs, :, length - edge : length].reshape(C, edge).astype(jnp.bfloat16)
+            values = frame_of(ref, slot)
+            head = values[:, :edge].astype(jnp.bfloat16)
+            tail = values[:, length - edge :].astype(jnp.bfloat16)
             inner[2 * half + slot] = jnp.where(flags.even_block, tail, head)
             outer[2 * half + slot] = jnp.where(flags.even_block, head, tail)
 
@@ -100,16 +120,13 @@
 
 def arrange_kernel(with_ends, values, other, keep, *ends):
     flags = Flags()
-    channels, count, length = values.shape
-    tiles = channels // SUB
+    count = values.shape[1]
     for slot in range(count // 2):
-        low = values[:, slot, :].reshape(tiles, SUB, length)
-        high = values[:, count // 2 + slot, :].reshape(tiles, SUB, length)
-        slabs = pl.ds(slot * tiles, tiles)
-        other[slabs] = jnp.where(flags.odd, low, high)
-        keep[slabs] = jnp.where(flags.odd, high, low)
+        low, high = values[:, slot, :], values[:, count // 2 + slot, :]
+        put_frame(other, slot, jnp.where(flags.odd, low, high))
+        put_frame(keep, slot, jnp.where(flags.odd, high, low))
     for ref in (other, keep):
-        ref[ref.shape[0] - 1] = jnp.zeros((SUB, length), jnp.float32)
+        ref[ref.shape[0] - 1] = jnp.zeros((SUB, LANES), jnp.float32)
     if with_ends:
         ends_of(flags, Frames(flags.parity), (other, keep), *ends)
 
@@ -179,7 +196,7 @@
         self.frames = Frames(self.flags.parity)
         self.halves, self.noise = halves, noise
         self.first, self.second, self.temb, self.inside, self.ends = first, second, temb, inside, ends
-        self.channels, self.count, self.length = C, inside.shape[0], halves[0].shape[2]
+        self.channels, self.count, self.length = C, inside.shape[0], inside.shape[1] + 2 * COLS
 
     def prepare(self, v, inner, outer, own, spread):
         edge = 2 * COLS
@@ -273,7 +290,7 @@
     def mark(self, ref, peaks):
         peak = jnp.max(functools.reduce(jnp.maximum, peaks), axis=1, keepdims=True)
         exponent = jnp.clip(jnp.ceil(jnp.log(peak) * (1.0 / math.log(2.0))) + 1.0, -100.0, 126.0)
-        ref[ref.shape[0] - 1] = jnp.broadcast_to(exponent, (SUB, self.length))
+        ref[ref.shape[0] - 1] = jnp.broadcast_to(exponent, (SUB, LANES))
 
 
 def sending_kernel(real, other, keep, noise_other, inner, outer, first, second, temb, inside, own, yours, *rest):
@@ -317,20 +334,20 @@
 
 
 def edges(other, keep):
-    shape = jax.ShapeDtypeStruct((2 * other.shape[0] // (C // SUB), C, 2 * COLS), jnp.bfloat16)
+    shape = jax.ShapeDtypeStruct((4, C, 2 * COLS), jnp.bfloat16)
     return call(edges_kernel, "edges", (other, keep), (shape, shape))
 
 
 def arrange(values, with_ends):
     channels, frames, length = values.shape
-    half = jax.ShapeDtypeStruct((frames // 2 * channels // SUB + 1, SUB, length), jnp.float32)
+    half = jax.ShapeDtypeStruct((frames // 2 * channels * length // (SUB * LANES) + 1, SUB, LANES), jnp.float32)
     ends = jax.ShapeDtypeStruct((frames, channels, 2 * COLS), jnp.bfloat16)
     shapes = (half, half) + ((ends, ends) if with_ends else ())
     return call(functools.partial(arrange_kernel, with_ends), "arrange", (values,), shapes)
 
 
 def denoise(real, other, keep, noise, inner, outer, first, second, temb):
-    length = other.shape[2]
+    length = length_of(other)
     frames = inner.shape[0]
     width = temb.shape[1]
     half = jax.ShapeDtypeStruct(other.shape, jnp.float32)
@@ -372,20 +389,22 @@
 def finish_kernel(other, keep, yours, mine, out, states, done):
     flags = Flags()
     channels, count, length = states.shape
-    tiles = C // SUB
     group = channels // 4
+    rows, across = group // SUB, length // LANES
     copies = []
     for at in range(0, channels, group):
         for frame in range(count):
             low = frame < count // 2
-            slabs = pl.ds((frame % 2) * tiles + at // SUB, group // SUB)
+            slabs = pl.ds((frame % 2) * frame_tiles(keep) + at // SUB * across, rows * across)
 
             def part(first_ref, second_ref):
-                one, two = first_ref[slabs].reshape(group, length), second_ref[slabs].reshape(group, length)
+                one, two = first_ref[slabs], second_ref[slabs]
                 return jnp.where(flags.odd, one, two) if low else jnp.where(flags.odd, two, one)
 
             before = jnp.where(flags.anchor, 0.0, part(other, keep))
-            states[pl.ds(at, group), frame, :] = before + part(yours, mine)
+            value = (before + part(yours, mine)).reshape(rows, across, SUB, LANES)
+            columns = [value[:, i].reshape(group, LANES) for i in range(across)]
+            states[pl.ds(at, group), frame, :] = jnp.concatenate(columns, axis=1)
         place = pl.ds(at, group)
         copies.append(pltpu.make_async_copy(states.at[place], out.at[place], done.at[len(copies)]))
         copies[-1].start()
@@ -407,7 +426,7 @@
 
 
 def changes_kernel(own1, theirs1, own2, theirs2, sums):
-    slabs = pl.ds(0, 2 * C // SUB)
+    slabs = pl.ds(0, own1.shape[0] - 1)
     for i, (one, two) in enumerate(((own1, own2), (theirs1, theirs2))):
         change = two[slabs] - one[slabs]
         square = jnp.sum(change * change, axis=0)
@@ -508,20 +527,11 @@
     while 2 * distance < space:
         sums = sums + lax.ppermute(sums, "space", [(i, i ^ distance) for i in range(space)])
         distance *= 2
-    swap = [(k * space + s, (k ^ 1) * space + s) for k in range(steps) for s in range(space)]
-    cross = [(k * space + s, (k ^ 1) * space + (s ^ distance)) for k in range(steps) for s in range(space)]
-    far = [(i, i ^ distance) for i in range(space)]
-    near_sum, other2 = lax.optimization_barrier((sums[0], other2))
-    if space == 1:
-        others = (lax.ppermute(sums[1], ("step", "space"), swap),)
-    else:
-        others = (
-            lax.ppermute(sums[1], ("step", "space"), swap),
-            lax.ppermute(sums[1], ("step", "space"), cross),
-            lax.ppermute(near_sum, "space", far),
-        )
+    total = sums[0] + lax.ppermute(sums[1], "step", [(i, i ^ 1) for i in range(steps)])
+    if space > 1:
+        total = total + lax.ppermute(total, "space", [(i, i ^ distance) for i in range(space)])
     states = finish(start_latent, other2, keep2, yours2, mine2)
-    total = functools.reduce(jnp.add, others, sums[0])
+    total, states = lax.optimization_barrier((total, states))
     changes = lax.optimization_barrier(jnp.sqrt(total / cell_count))[0, :1]
     return (states[None], changes)
 

time: 83.8 us -> 82.1 us (0.980)
  starting transfers between devices: 31.8 us -> 25.9 us
  waiting for transfers between devices: 25.8 us -> 28.1 us
  Pallas kernels: 19.5 us -> 20.5 us
    ppermute x3 -> x2, starting transfers between devices: 8.94 us -> 4.9 us  [the longest x1 3.38 us: local(): lax.ppermute(total, 'space', [(i, i ^ distance) for i in range(space)])]
    ppermute x3 -> x2, waiting for transfers between devices: 0.59 us -> 2.94 us  [the longest x1 1.58 us: local(): lax.ppermute(total, 'space', [(i, i ^ distance) for i in range(space)])]
    ppermute x8, starting transfers between devices: 20.3 us -> 18.4 us  [exchange(): lax.ppermute(coded(half), 'step', [(i, i ^ flip) for i in range(steps)])]
    pallas_call x12, Pallas kernels: 18.6 us -> 19.6 us  [call(): pl.pallas_call(kernel, out_shape=out_shape, in_specs=[WHOLE] * len(arrays...]
    ppermute x8, waiting for transfers between devices: 25.2 us -> 24.3 us  [exchange(): lax.ppermute(coded(half), 'step', [(i, i ^ flip) for i in range(steps)])]
    ppermute x1, waiting for transfers between devices: 0.01 us -> 0.85 us  [local(): lax.ppermute(sums, 'space', [(i, i ^ distance) for i in range(space)])]
  transfers between devices with their start and end apart: 16 -> 15, of which waited for: 8 -> 10; matrix products, arithmetic and copies ran while one was open for 1% -> 1% of each run, Pallas kernels for 14% -> 14%
where the time goes in v7:
time: 82.1 us; the launch traced here: 81.4 us
  waiting for transfers between devices  28.1 us (34%)
  starting transfers between devices  25.9 us (32%)
  Pallas kernels  20.5 us (25%)
  other arithmetic  3.53 us (4%)
  local copies, waits for them, and re-layouts  2.05 us (2%)
  between operations  1.1 us (1%)
    ppermute x8, waiting for transfers between devices, exchange(): lax.ppermute(coded(half), 'step', [(i, i ^ flip) for i in range(steps)])  24.3 us
    pallas_call x12, Pallas kernels, call(): pl.pallas_call(kernel, out_shape=out_shape, in_specs=[WHOLE] * len(arrays...  19.6 us
    ppermute x8, starting transfers between devices, exchange(): lax.ppermute(coded(half), 'step', [(i, i ^ flip) for i in range(steps)])  18.4 us
    ppermute x1, starting transfers between devices, local(): lax.ppermute(total, 'space', [(i, i ^ distance) for i in range(space)])  3.38 us
  transfers between devices with their start and end apart: 15, of which 10 were waited for; matrix products, arithmetic and copies ran while one was open for 1% of the time, Pallas kernels for 14%

profile of v7, /device:TPU:0, one launch (start us, length us, event | category | flops | bytes accessed | tf_op | source)
XLA Modules:
  0.0 81.4 jit_solution(16590251226931397599)
XLA Ops:
  0.7 1.3 %pad.7.first = bf16[3,640,256]{2,1,0:T(8,128)(2,1)S(1)} pad(bf16[3,576,256]{2,1,0:T(8,128)(2,1)} %bitcast.60, bf16[]{:T(256)} %constant.98.clone.1), padding=0_0x0_64x0_0 | pad | bytes 1867778 | tf_op jit(solution)/shard_map/jit(_pad)/pad | solution.py:501
  2.0 0.6 arrange.4
  2.7 0.5 collective-permute-start
  3.2 0.8 collective-permute-start.1
  4.1 0.5 arrange.5
  4.7 0.2 fusion.56.temb
  4.9 2.4 %interior.2 = (bf16[4,480,256]{2,1,0:T(8,128)(2,1)S(1)}, bf16[4,320,384]{2,1,0:T(8,128)(2,1)S(1)}) custom-call(f32[81,8,128]{2,1,0:T(8,128)S(1)} %get-tuple-element.36.other, f32[81,8,128]{2,1,0:T(8,128)S(1)} %get-tuple-element.33.keep, bf16[3,640,256]{2,1,0:T(8,128)(2,1)S(1)} %pad.7.first, f32[1,256]{1,0:T(1,128)S(1)} %fusion.56.temb), custom_call_target="tpu_custom_call" | custom-call | flops 2000000000 | bytes 4000000 | tf_op jit(solution)/shard_map/interior/pallas_call | solution.py:324
  7.3 3.7 %sending.2 = (f32[81,8,128]{2,1,0:T(8,128)S(1)}, bf16[2,320,256]{2,1,0:T(8,128)(2,1)S(1)}, bf16[2,640,384]{2,1,0:T(8,128)(2,1)S(1)}) custom-call(f32[3,128]{1,0:T(4,128)S(1)} %pad_maximum_fusion.real, f32[81,8,128]{2,1,0:T(8,128)S(1)} %get-tuple-element.36.other, f32[81,8,128]{2,1,0:T(8,128)S(1)} %get-tuple-element.33.keep, ...), custom_call_target="tpu_custom_call" | custom-call | flops 2000000000 | bytes 4000000 | tf_op jit(solution)/shard_map/sending/pallas_call | solution.py:324
  11.0 0.2 fusion
  11.2 2.5 %collective-permute-start.2 = (f16[81,8,128]{2,1,0:T(8,128)(2,1)S(1)}, f16[81,8,128]{2,1,0:T(8,128)(2,1)S(1)}, u32[]{:S(2)}, u32[]{:S(2)}) collective-permute-start(f16[81,8,128]{2,1,0:T(8,128)(2,1)S(1)} %fusion), channel_id=1, source_target_pairs={{0,4},{4,0},{8,12},{12,8},{16,20},{20,16},{24,28},{28,24},{1,5},{5... | collective-permute-start | bytes 497672 | tf_op jit(solution)/shard_map/ppermute | solution.py:467
  13.7 2.5 %keeping.2 = f32[81,8,128]{2,1,0:T(8,128)S(1)} custom-call(f32[3,128]{1,0:T(4,128)S(1)} %pad_maximum_fusion.real, f32[81,8,128]{2,1,0:T(8,128)S(1)} %get-tuple-element.33.keep, f32[81,8,128]{2,1,0:T(8,128)S(1)} %get-tuple-element.34.noise_keep, bf16[3,640,256]{2,1,0:T(8,128)(2,1)S(1)} %pad.7.first, bf16[3,64,2304]{2,1,0:T(8,128)(2,1)S(1)} %copy-done.3, ...), custom_call_target="tpu_custom_call" | custom-call | flops 2000000000 | bytes 4000000 | tf_op jit(solution)/shard_map/keeping/pallas_call | solution.py:324
  16.2 0.9 %collective-permute-done.2 = f16[81,8,128]{2,1,0:T(8,128)(2,1)S(1)} collective-permute-done((f16[81,8,128]{2,1,0:T(8,128)(2,1)S(1)}, f16[81,8,128]{2,1,0:T(8,128)(2,1)S(1)}, u32[]{:S(2)}, u32[]{:S(2)}) %collective-permute-start.2) | collective-permute-done | bytes 165920 | tf_op jit(solution)/shard_map/ppermute | solution.py:467
  17.0 0.2 add_select_fusion.9
  17.4 2.1 %collective-permute-start.3 = (f16[81,8,128]{2,1,0:T(8,128)(2,1)S(1)}, f16[81,8,128]{2,1,0:T(8,128)(2,1)S(1)}, u32[]{:S(2)}, u32[]{:S(2)}) collective-permute-start(f16[81,8,128]{2,1,0:T(8,128)(2,1)S(1)} %fusion.1), channel_id=1, source_target_pairs={{0,8},{4,12},{8,0},{12,4},{16,24},{20,28},{24,16},{28,20},{1,9},{5... | collective-permute-start | bytes 497672 | tf_op jit(solution)/shard_map/ppermute | solution.py:467
  19.5 3.9 %collective-permute-done.3 = f16[81,8,128]{2,1,0:T(8,128)(2,1)S(1)} collective-permute-done((f16[81,8,128]{2,1,0:T(8,128)(2,1)S(1)}, f16[81,8,128]{2,1,0:T(8,128)(2,1)S(1)}, u32[]{:S(2)}, u32[]{:S(2)}) %collective-permute-start.3) | collective-permute-done | bytes 165920 | tf_op jit(solution)/shard_map/ppermute | solution.py:467
  23.5 0.2 add_select_fusion.8
  23.9 4.6 %collective-permute-start.4 = (f16[81,8,128]{2,1,0:T(8,128)(2,1)S(1)}, f16[81,8,128]{2,1,0:T(8,128)(2,1)S(1)}, u32[]{:S(2)}, u32[]{:S(2)}) collective-permute-start(f16[81,8,128]{2,1,0:T(8,128)(2,1)S(1)} %fusion.2), channel_id=1, source_target_pairs={{0,24},{4,28},{8,16},{12,20},{16,8},{20,12},{24,0},{28,4},{1,25},{... | collective-permute-start | bytes 497672 | tf_op jit(solution)/shard_map/ppermute | solution.py:467
  28.4 0.5 arrange.6
  28.9 4.6 %collective-permute-done.4 = f16[81,8,128]{2,1,0:T(8,128)(2,1)S(1)} collective-permute-done((f16[81,8,128]{2,1,0:T(8,128)(2,1)S(1)}, f16[81,8,128]{2,1,0:T(8,128)(2,1)S(1)}, u32[]{:S(2)}, u32[]{:S(2)}) %collective-permute-start.4) | collective-permute-done | bytes 165920 | tf_op jit(solution)/shard_map/ppermute | solution.py:467
  33.5 0.4 fusion.11
  34.1 1.6 %collective-permute-start.5 = (f16[81,8,128]{2,1,0:T(8,128)(2,1)S(1)}, f16[81,8,128]{2,1,0:T(8,128)(2,1)S(1)}, u32[]{:S(2)}, u32[]{:S(2)}) collective-permute-start(f16[81,8,128]{2,1,0:T(8,128)(2,1)S(1)} %fusion.4), channel_id=1, source_target_pairs={{0,4},{4,0},{8,12},{12,8},{16,20},{20,16},{24,28},{28,24},{1,5},{5... | collective-permute-start | bytes 497672 | tf_op jit(solution)/shard_map/ppermute | solution.py:467
  35.8 0.5 arrange.7
  36.3 4.0 %collective-permute-done.5 = f16[81,8,128]{2,1,0:T(8,128)(2,1)S(1)} collective-permute-done((f16[81,8,128]{2,1,0:T(8,128)(2,1)S(1)}, f16[81,8,128]{2,1,0:T(8,128)(2,1)S(1)}, u32[]{:S(2)}, u32[]{:S(2)}) %collective-permute-start.5) | collective-permute-done | bytes 165920 | tf_op jit(solution)/shard_map/ppermute | solution.py:467
  40.3 0.2 fusion.5.other
  40.5 0.2 edges.1
  40.7 0.8 %collective-permute-start.7 = (bf16[4,64,160]{2,1,0:T(8,128)(2,1)S(1)}, bf16[4,64,160]{2,1,0:T(8,128)(2,1)S(1)}, u32[]{:S(2)}, u32[]{:S(2)}) collective-permute-start(bf16[4,64,160]{2,1,0:T(8,128)(2,1)S(1)} %get-tuple-element.55), channel_id=1, source_target_pairs={{1,2},{2,1},{5,6},{6,5},{9,10},{10,9},{13,14},{14,13},{17,18},{18,... | collective-permute-start | bytes 245768 | tf_op jit(solution)/shard_map/ppermute | solution.py:508
  41.6 2.4 %interior.3 = (bf16[4,480,256]{2,1,0:T(8,128)(2,1)S(1)}, bf16[4,320,384]{2,1,0:T(8,128)(2,1)S(1)}) custom-call(f32[81,8,128]{2,1,0:T(8,128)S(1)} %fusion.5.other, f32[81,8,128]{2,1,0:T(8,128)S(1)} %get-tuple-element.74.keep, bf16[3,640,256]{2,1,0:T(8,128)(2,1)S(1)} %pad.8.first, f32[1,256]{1,0:T(1,128)S(1)} %fusion.56.temb), custom_call_target="tpu_custom_call" | custom-call | flops 2000000000 | bytes 4000000 | tf_op jit(solution)/shard_map/interior/pallas_call | solution.py:324
  44.0 3.7 %sending.3 = (f32[81,8,128]{2,1,0:T(8,128)S(1)}, bf16[2,320,256]{2,1,0:T(8,128)(2,1)S(1)}, bf16[2,640,384]{2,1,0:T(8,128)(2,1)S(1)}) custom-call(f32[3,128]{1,0:T(4,128)S(1)} %pad_maximum_fusion.real, f32[81,8,128]{2,1,0:T(8,128)S(1)} %fusion.5.other, f32[81,8,128]{2,1,0:T(8,128)S(1)} %get-tuple-element.74.keep, ...), custom_call_target="tpu_custom_call" | custom-call | flops 2000000000 | bytes 4000000 | tf_op jit(solution)/shard_map/sending/pallas_call | solution.py:324
  47.7 0.2 fusion.6
  47.9 1.4 %collective-permute-start.8 = (f16[81,8,128]{2,1,0:T(8,128)(2,1)S(1)}, f16[81,8,128]{2,1,0:T(8,128)(2,1)S(1)}, u32[]{:S(2)}, u32[]{:S(2)}) collective-permute-start(f16[81,8,128]{2,1,0:T(8,128)(2,1)S(1)} %fusion.6), channel_id=1, source_target_pairs={{0,4},{4,0},{8,12},{12,8},{16,20},{20,16},{24,28},{28,24},{1,5},{5... | collective-permute-start | bytes 497672 | tf_op jit(solution)/shard_map/ppermute | solution.py:467
  49.4 2.5 %keeping.3.mine = f32[81,8,128]{2,1,0:T(8,128)S(1)} custom-call(f32[3,128]{1,0:T(4,128)S(1)} %pad_maximum_fusion.real, f32[81,8,128]{2,1,0:T(8,128)S(1)} %get-tuple-element.74.keep, f32[81,8,128]{2,1,0:T(8,128)S(1)} %get-tuple-element.49.noise_keep, bf16[3,640,256]{2,1,0:T(8,128)(2,1)S(1)} %pad.8.first, bf16[3,64,2304]{2,1,0:T(8,128)(2,1)S(1)} %copy-done.3, ...), custom_call_target="tpu_custom_call" | custom-call | flops 2000000000 | bytes 4000000 | tf_op jit(solution)/shard_map/keeping/pallas_call | solution.py:324
  51.8 1.5 %collective-permute-done.8 = f16[81,8,128]{2,1,0:T(8,128)(2,1)S(1)} collective-permute-done((f16[81,8,128]{2,1,0:T(8,128)(2,1)S(1)}, f16[81,8,128]{2,1,0:T(8,128)(2,1)S(1)}, u32[]{:S(2)}, u32[]{:S(2)}) %collective-permute-start.8) | collective-permute-done | bytes 165920 | tf_op jit(solution)/shard_map/ppermute | solution.py:467
  53.4 0.2 add_select_fusion.4
  53.7 3.1 %collective-permute-start.9 = (f16[81,8,128]{2,1,0:T(8,128)(2,1)S(1)}, f16[81,8,128]{2,1,0:T(8,128)(2,1)S(1)}, u32[]{:S(2)}, u32[]{:S(2)}) collective-permute-start(f16[81,8,128]{2,1,0:T(8,128)(2,1)S(1)} %fusion.7), channel_id=1, source_target_pairs={{0,8},{4,12},{8,0},{12,4},{16,24},{20,28},{24,16},{28,20},{1,9},{5... | collective-permute-start | bytes 497672 | tf_op jit(solution)/shard_map/ppermute | solution.py:467
  56.8 3.4 %collective-permute-done.9 = f16[81,8,128]{2,1,0:T(8,128)(2,1)S(1)} collective-permute-done((f16[81,8,128]{2,1,0:T(8,128)(2,1)S(1)}, f16[81,8,128]{2,1,0:T(8,128)(2,1)S(1)}, u32[]{:S(2)}, u32[]{:S(2)}) %collective-permute-start.9) | collective-permute-done | bytes 165920 | tf_op jit(solution)/shard_map/ppermute | solution.py:467
  60.6 2.5 %collective-permute-start.10 = (f16[81,8,128]{2,1,0:T(8,128)(2,1)S(1)}, f16[81,8,128]{2,1,0:T(8,128)(2,1)S(1)}, u32[]{:S(2)}, u32[]{:S(2)}) collective-permute-start(f16[81,8,128]{2,1,0:T(8,128)(2,1)S(1)} %fusion.8), channel_id=1, source_target_pairs={{0,24},{4,28},{8,16},{12,20},{16,8},{20,12},{24,0},{28,4},{1,25},{... | collective-permute-start | bytes 497672 | tf_op jit(solution)/shard_map/ppermute | solution.py:467
  63.1 6.0 %collective-permute-done.10 = f16[81,8,128]{2,1,0:T(8,128)(2,1)S(1)} collective-permute-done((f16[81,8,128]{2,1,0:T(8,128)(2,1)S(1)}, f16[81,8,128]{2,1,0:T(8,128)(2,1)S(1)}, u32[]{:S(2)}, u32[]{:S(2)}) %collective-permute-start.10) | collective-permute-done | bytes 165920 | tf_op jit(solution)/shard_map/ppermute | solution.py:467
  69.2 0.4 fusion.12
  69.7 0.2 changes.1
  69.9 0.3 collective-permute-start.11
  70.2 0.9 %collective-permute-done.11 = f32[2,8,128]{2,1,0:T(8,128)S(1)} collective-permute-done((f32[2,8,128]{2,1,0:T(8,128)S(1)}, f32[2,8,128]{2,1,0:T(8,128)S(1)}, u32[]{:S(2)}, u32[]{:S(2)}) %collective-permute-start.11) | collective-permute-done | bytes 8224 | tf_op jit(solution)/shard_map/ppermute | solution.py:528
  71.1 1.5 %collective-permute-start.12 = (f32[8,128]{1,0:T(8,128)S(1)}, f32[8,128]{1,0:T(8,128)S(1)}, u32[]{:S(2)}, u32[]{:S(2)}) collective-permute-start(f32[8,128]{1,0:T(8,128)S(1)} %slice_bitcast_fusion), channel_id=1, source_target_pairs={{0,4},{4,0},{8,12},{12,8},{16,20},{20,16},{24,28},{28,24},{1,5},{5... | collective-permute-start | bytes 12296 | tf_op jit(solution)/shard_map/ppermute | solution.py:530
  72.8 0.6 collective-permute-start.14
  73.3 1.4 %collective-permute-done.12 = f32[8,128]{1,0:T(8,128)S(1)} collective-permute-done((f32[8,128]{1,0:T(8,128)S(1)}, f32[8,128]{1,0:T(8,128)S(1)}, u32[]{:S(2)}, u32[]{:S(2)}) %collective-permute-start.12) | collective-permute-done | bytes 4128 | tf_op jit(solution)/shard_map/ppermute | solution.py:530
  74.7 3.4 %collective-permute-start.13 = (f32[8,128]{1,0:T(8,128)S(1)}, f32[8,128]{1,0:T(8,128)S(1)}, u32[]{:S(2)}, u32[]{:S(2)}) collective-permute-start(f32[8,128]{1,0:T(8,128)S(1)} %fusion.19), channel_id=1, source_target_pairs={{0,2},{1,3},{2,0},{3,1},{4,6},{5,7},{6,4},{7,5},{8,10},{9,11},{10,... | collective-permute-start | bytes 12296 | tf_op jit(solution)/shard_map/ppermute | solution.py:532
  78.1 1.6 %collective-permute-done.13 = f32[8,128]{1,0:T(8,128)S(1)} collective-permute-done((f32[8,128]{1,0:T(8,128)S(1)}, f32[8,128]{1,0:T(8,128)S(1)}, u32[]{:S(2)}, u32[]{:S(2)}) %collective-permute-start.13) | collective-permute-done | bytes 4128 | tf_op jit(solution)/shard_map/ppermute | solution.py:532
  79.9 1.0 %finish.1 = f32[64,4,640]{2,1,0:T(4,128)} custom-call(f32[81,8,128]{2,1,0:T(8,128)S(1)} %multiply_select_fusion.other, f32[81,8,128]{2,1,0:T(8,128)S(1)} %get-tuple-element.72.keep, f32[81,8,128]{2,1,0:T(8,128)S(1)} %get-tuple-element.59.yours, f32[81,8,128]{2,1,0:T(8,128)S(1)} %keeping.3.mine), custom_call_target="tpu_custom_call" | custom-call | flops 8000000000 | bytes 4000000 | tf_op jit(solution)/shard_map/finish/pallas_call | solution.py:416
  80.9 0.5 slice.87
  (63 shorter events, 2.0 us)
Async XLA Ops:
  0.6 4.0 %copy-start = (f32[64,256]{1,0:T(8,128)S(1)}, f32[64,256]{1,0:T(8,128)}, u32[]{:S(2)}) copy-start(f32[64,256]{1,0:T(8,128)} %param.11) | copy-start | bytes 196612
  0.6 1.4 %copy-start.1 = (f32[1,64,4,640]{3,2,1,0:T(4,128)S(1)}, f32[1,64,4,640]{3,2,1,0:T(4,128)}, u32[]{:S(2)}) copy-start(f32[1,64,4,640]{3,2,1,0:T(4,128)} %param.6) | copy-start | bytes 1966084
  2.0 2.2 %copy-start.2 = (f32[1,64,4,640]{3,2,1,0:T(4,128)S(1)}, f32[1,64,4,640]{3,2,1,0:T(4,128)}, u32[]{:S(2)}) copy-start(f32[1,64,4,640]{3,2,1,0:T(4,128)} %param.7) | copy-start | bytes 1966084
  2.7 4.6 %collective-permute-start = (bf16[4,64,160]{2,1,0:T(8,128)(2,1)S(1)}, bf16[4,64,160]{2,1,0:T(8,128)(2,1)S(1)}, u32[]{:S(2)}, u32[]{:S(2)}) collective-permute-start(bf16[4,64,160]{2,1,0:T(8,128)(2,1)S(1)} %get-tuple-element.39), channel_id=1, source_target_pairs={{0,1},{1,0},{2,3},{3,2},{4,5},{5,4},{6,7},{7,6},{8,9},{9,8},{10,11... | collective-permute-start | bytes 245768 | tf_op jit(solution)/shard_map/ppermute | solution.py:507
  3.2 0.8 copy-start.5
  3.2 4.1 %collective-permute-start.1 = (bf16[4,64,160]{2,1,0:T(8,128)(2,1)S(1)}, bf16[4,64,160]{2,1,0:T(8,128)(2,1)S(1)}, u32[]{:S(2)}, u32[]{:S(2)}) collective-permute-start(bf16[4,64,160]{2,1,0:T(8,128)(2,1)S(1)} %get-tuple-element.40), channel_id=1, source_target_pairs={{1,2},{2,1},{5,6},{6,5},{9,10},{10,9},{13,14},{14,13},{17,18},{18,... | collective-permute-start | bytes 245768 | tf_op jit(solution)/shard_map/ppermute | solution.py:508
  4.9 2.4 %copy-start.3 = (bf16[3,64,2304]{2,1,0:T(8,128)(2,1)S(1)}, bf16[3,64,2304]{2,1,0:T(8,128)(2,1)}, u32[]{:S(2)}) copy-start(bf16[3,64,2304]{2,1,0:T(8,128)(2,1)} %second.7) | copy-start | bytes 2654212
  11.2 5.8 %collective-permute-start.2 = (f16[81,8,128]{2,1,0:T(8,128)(2,1)S(1)}, f16[81,8,128]{2,1,0:T(8,128)(2,1)S(1)}, u32[]{:S(2)}, u32[]{:S(2)}) collective-permute-start(f16[81,8,128]{2,1,0:T(8,128)(2,1)S(1)} %fusion), channel_id=1, source_target_pairs={{0,4},{4,0},{8,12},{12,8},{16,20},{20,16},{24,28},{28,24},{1,5},{5... | collective-permute-start | bytes 497672 | tf_op jit(solution)/shard_map/ppermute | solution.py:467
  17.4 6.1 %collective-permute-start.3 = (f16[81,8,128]{2,1,0:T(8,128)(2,1)S(1)}, f16[81,8,128]{2,1,0:T(8,128)(2,1)S(1)}, u32[]{:S(2)}, u32[]{:S(2)}) collective-permute-start(f16[81,8,128]{2,1,0:T(8,128)(2,1)S(1)} %fusion.1), channel_id=1, source_target_pairs={{0,8},{4,12},{8,0},{12,4},{16,24},{20,28},{24,16},{28,20},{1,9},{5... | collective-permute-start | bytes 497672 | tf_op jit(solution)/shard_map/ppermute | solution.py:467
  23.9 9.6 %collective-permute-start.4 = (f16[81,8,128]{2,1,0:T(8,128)(2,1)S(1)}, f16[81,8,128]{2,1,0:T(8,128)(2,1)S(1)}, u32[]{:S(2)}, u32[]{:S(2)}) collective-permute-start(f16[81,8,128]{2,1,0:T(8,128)(2,1)S(1)} %fusion.2), channel_id=1, source_target_pairs={{0,24},{4,28},{8,16},{12,20},{16,8},{20,12},{24,0},{28,4},{1,25},{... | collective-permute-start | bytes 497672 | tf_op jit(solution)/shard_map/ppermute | solution.py:467
  33.5 2.2 %copy-start.4 = (bf16[3,256,576]{1,2,0:T(8,128)(2,1)S(1)}, bf16[3,256,576]{1,2,0:T(8,128)(2,1)}, u32[]{:S(2)}) copy-start(bf16[3,256,576]{1,2,0:T(8,128)(2,1)} %param.9) | copy-start | bytes 2654212
  34.1 6.1 %collective-permute-start.5 = (f16[81,8,128]{2,1,0:T(8,128)(2,1)S(1)}, f16[81,8,128]{2,1,0:T(8,128)(2,1)S(1)}, u32[]{:S(2)}, u32[]{:S(2)}) collective-permute-start(f16[81,8,128]{2,1,0:T(8,128)(2,1)S(1)} %fusion.4), channel_id=1, source_target_pairs={{0,4},{4,0},{8,12},{12,8},{16,20},{20,16},{24,28},{28,24},{1,5},{5... | collective-permute-start | bytes 497672 | tf_op jit(solution)/shard_map/ppermute | solution.py:467
  40.7 3.3 %collective-permute-start.6 = (bf16[4,64,160]{2,1,0:T(8,128)(2,1)S(1)}, bf16[4,64,160]{2,1,0:T(8,128)(2,1)S(1)}, u32[]{:S(2)}, u32[]{:S(2)}) collective-permute-start(bf16[4,64,160]{2,1,0:T(8,128)(2,1)S(1)} %get-tuple-element.54), channel_id=1, source_target_pairs={{0,1},{1,0},{2,3},{3,2},{4,5},{5,4},{6,7},{7,6},{8,9},{9,8},{10,11... | collective-permute-start | bytes 245768 | tf_op jit(solution)/shard_map/ppermute | solution.py:507
  40.7 3.3 %collective-permute-start.7 = (bf16[4,64,160]{2,1,0:T(8,128)(2,1)S(1)}, bf16[4,64,160]{2,1,0:T(8,128)(2,1)S(1)}, u32[]{:S(2)}, u32[]{:S(2)}) collective-permute-start(bf16[4,64,160]{2,1,0:T(8,128)(2,1)S(1)} %get-tuple-element.55), channel_id=1, source_target_pairs={{1,2},{2,1},{5,6},{6,5},{9,10},{10,9},{13,14},{14,13},{17,18},{18,... | collective-permute-start | bytes 245768 | tf_op jit(solution)/shard_map/ppermute | solution.py:508
  47.9 5.4 %collective-permute-start.8 = (f16[81,8,128]{2,1,0:T(8,128)(2,1)S(1)}, f16[81,8,128]{2,1,0:T(8,128)(2,1)S(1)}, u32[]{:S(2)}, u32[]{:S(2)}) collective-permute-start(f16[81,8,128]{2,1,0:T(8,128)(2,1)S(1)} %fusion.6), channel_id=1, source_target_pairs={{0,4},{4,0},{8,12},{12,8},{16,20},{20,16},{24,28},{28,24},{1,5},{5... | collective-permute-start | bytes 497672 | tf_op jit(solution)/shard_map/ppermute | solution.py:467
  53.7 6.5 %collective-permute-start.9 = (f16[81,8,128]{2,1,0:T(8,128)(2,1)S(1)}, f16[81,8,128]{2,1,0:T(8,128)(2,1)S(1)}, u32[]{:S(2)}, u32[]{:S(2)}) collective-permute-start(f16[81,8,128]{2,1,0:T(8,128)(2,1)S(1)} %fusion.7), channel_id=1, source_target_pairs={{0,8},{4,12},{8,0},{12,4},{16,24},{20,28},{24,16},{28,20},{1,9},{5... | collective-permute-start | bytes 497672 | tf_op jit(solution)/shard_map/ppermute | solution.py:467
  60.6 8.6 %collective-permute-start.10 = (f16[81,8,128]{2,1,0:T(8,128)(2,1)S(1)}, f16[81,8,128]{2,1,0:T(8,128)(2,1)S(1)}, u32[]{:S(2)}, u32[]{:S(2)}) collective-permute-start(f16[81,8,128]{2,1,0:T(8,128)(2,1)S(1)} %fusion.8), channel_id=1, source_target_pairs={{0,24},{4,28},{8,16},{12,20},{16,8},{20,12},{24,0},{28,4},{1,25},{... | collective-permute-start | bytes 497672 | tf_op jit(solution)/shard_map/ppermute | solution.py:467
  69.9 1.2 %collective-permute-start.11 = (f32[2,8,128]{2,1,0:T(8,128)S(1)}, f32[2,8,128]{2,1,0:T(8,128)S(1)}, u32[]{:S(2)}, u32[]{:S(2)}) collective-permute-start(f32[2,8,128]{2,1,0:T(8,128)S(1)} %changes.1), channel_id=1, source_target_pairs={{0,1},{1,0},{2,3},{3,2},{4,5},{5,4},{6,7},{7,6},{8,9},{9,8},{10,11... | collective-permute-start | bytes 24584 | tf_op jit(solution)/shard_map/ppermute | solution.py:528
  71.1 3.6 %collective-permute-start.12 = (f32[8,128]{1,0:T(8,128)S(1)}, f32[8,128]{1,0:T(8,128)S(1)}, u32[]{:S(2)}, u32[]{:S(2)}) collective-permute-start(f32[8,128]{1,0:T(8,128)S(1)} %slice_bitcast_fusion), channel_id=1, source_target_pairs={{0,4},{4,0},{8,12},{12,8},{16,20},{20,16},{24,28},{28,24},{1,5},{5... | collective-permute-start | bytes 12296 | tf_op jit(solution)/shard_map/ppermute | solution.py:530
  72.8 6.9 %collective-permute-start.14 = (f16[81,8,128]{2,1,0:T(8,128)(2,1)S(1)}, f16[81,8,128]{2,1,0:T(8,128)(2,1)S(1)}, u32[]{:S(2)}, u32[]{:S(2)}) collective-permute-start(f16[81,8,128]{2,1,0:T(8,128)(2,1)S(1)} %fusion.10), channel_id=1, source_target_pairs={{0,4},{4,0},{8,12},{12,8},{16,20},{20,16},{24,28},{28,24},{1,5},{5... | collective-permute-start | bytes 497672 | tf_op jit(solution)/shard_map/ppermute | solution.py:467
  74.7 5.0 %collective-permute-start.13 = (f32[8,128]{1,0:T(8,128)S(1)}, f32[8,128]{1,0:T(8,128)S(1)}, u32[]{:S(2)}, u32[]{:S(2)}) collective-permute-start(f32[8,128]{1,0:T(8,128)S(1)} %fusion.19), channel_id=1, source_target_pairs={{0,2},{1,3},{2,0},{3,1},{4,6},{5,7},{6,4},{7,5},{8,10},{9,11},{10,... | collective-permute-start | bytes 12296 | tf_op jit(solution)/shard_map/ppermute | solution.py:532

commit v8 on v7

--- a/solution.py
+++ b/solution.py
@@ -12,6 +12,7 @@
 COLS = 80
 SUB = 8
 LANES = 128
+WIDE = -(-2 * COLS // LANES) * LANES
 NT = (((1,), (1,)), ((), ()))
 MEGA = 2**20
 
@@ -102,13 +103,12 @@
 
 
 def ends_of(flags, frames, halves, inner, outer):
-    edge = 2 * COLS
     for half, ref in enumerate(halves):
         length = length_of(ref)
         for slot in range(2):
             values = frame_of(ref, slot)
-            head = values[:, :edge].astype(jnp.bfloat16)
-            tail = values[:, length - edge :].astype(jnp.bfloat16)
+            head = values[:, :WIDE].astype(jnp.bfloat16)
+            tail = values[:, length - WIDE :].astype(jnp.bfloat16)
             inner[2 * half + slot] = jnp.where(flags.even_block, tail, head)
             outer[2 * half + slot] = jnp.where(flags.even_block, head, tail)
 
@@ -135,9 +135,8 @@
     return [a for a in range(3) if 0 <= v + a - 1 < count]
 
 
-def spread_columns(values):
+def spread_columns(values, column):
     n = values.shape[1]
-    column = lax.broadcasted_iota(jnp.int32, (1, n), 1) % COLS
     before = jnp.where(column >= 1, pltpu.roll(values, 1, 1), 0.0).astype(jnp.bfloat16)
     after = jnp.where(column <= COLS - 2, pltpu.roll(values, n - 1, 1), 0.0).astype(jnp.bfloat16)
     center = values.astype(jnp.bfloat16)
@@ -164,7 +163,8 @@
     inside = length - edge
 
     def prepare(v):
-        left, mixed, right = spread_columns(frames.load((other, keep), v))
+        column = lax.broadcasted_iota(jnp.int32, (1, length), 1) % COLS
+        left, mixed, right = spread_columns(frames.load((other, keep), v), column)
         spread[v, :, 0:128] = left
         spread[v, :, 128:192] = mixed[:, :64]
         spread[v, pl.ds(0, length - COLS), 192:256] = mixed[COLS:, 64:]
@@ -203,16 +203,22 @@
         at = halo_slot(self.frames, v)
         near, far = inner[at].astype(jnp.float32), outer[at].astype(jnp.float32)
         even = self.flags.even_block
-        both = jnp.concatenate([jnp.where(even, far, near), jnp.where(even, near, far)], axis=1)
-        left, mixed, right = spread_columns(both)
+        above, below = jnp.where(even, far, near), jnp.where(even, near, far)
+        total = 2 * WIDE - LANES
+        lane = lax.broadcasted_iota(jnp.int32, (1, total), 1)
+        shared = jnp.where(lane[:, :LANES] < LANES // 2, below[:, WIDE - LANES :], above[:, :LANES])
+        both = jnp.concatenate([below[:, : WIDE - LANES], shared, above[:, LANES:]], axis=1)
+        at = total - edge
+        column = jnp.where(lane < total // 2, lane, lane + (-at % COLS)) % COLS
+        left, mixed, right = spread_columns(both, column)
         ref, i = spread[v]
         ref[i, pl.ds(edge, 2 * edge), :] = own[v]
         for low, high, rows in ((0, 128, left), (128, 192, mixed[:, :64]), (256, 384, right)):
-            ref[i, pl.ds(0, edge), low:high] = rows[:edge]
-            ref[i, pl.ds(3 * edge, edge), low:high] = rows[edge:]
-        ref[i, pl.ds(0, COLS), 192:256] = mixed[COLS:edge, 64:]
+            ref[i, pl.ds(0, edge), low:high] = rows[at:]
+            ref[i, pl.ds(3 * edge, edge), low:high] = rows[:edge]
+        ref[i, pl.ds(0, COLS), 192:256] = mixed[at + COLS :, 64:]
         ref[i, pl.ds(COLS, COLS), 192:256] = own[v, pl.ds(0, COLS), 0:64]
-        ref[i, pl.ds(3 * edge - COLS, edge), 192:256] = mixed[edge:, 64:]
+        ref[i, pl.ds(3 * edge - COLS, edge), 192:256] = mixed[:edge, 64:]
         ref[i, pl.ds(3 * edge + COLS, COLS), 192:256] = jnp.zeros((COLS, 64), jnp.bfloat16)
 
     def edge_rows(self, v, spread):
@@ -258,7 +264,7 @@
             ],
             axis=1,
         )
-        latent, noise = self.frames.load(self.halves, v), self.frames.load(self.noise, v)
+        latent, noise = self.frames.load(self.halves, v), self.noise_of(v)
         base = flags.keep * latent + flags.spread * noise + jnp.where(flags.anchor, latent, 0.0)
         chunk = length // 2
         column = lax.broadcasted_iota(jnp.int32, (1, chunk), 1) % COLS
@@ -287,17 +293,22 @@
         self.frames.store(out, v, result)
         return jnp.max(jnp.abs(result), axis=0, keepdims=True)
 
+    def noise_of(self, v):
+        if len(self.noise.shape) == 3 and self.noise.shape[1] == self.count:
+            return jnp.where(self.flags.odd, self.noise[:, v, :], self.noise[:, self.count - 1 - v, :])
+        return frame_of(self.noise, self.frames.slot(v))
+
     def mark(self, ref, peaks):
         peak = jnp.max(functools.reduce(jnp.maximum, peaks), axis=1, keepdims=True)
         exponent = jnp.clip(jnp.ceil(jnp.log(peak) * (1.0 / math.log(2.0))) + 1.0, -100.0, 126.0)
         ref[ref.shape[0] - 1] = jnp.broadcast_to(exponent, (SUB, LANES))
 
 
-def sending_kernel(real, other, keep, noise_other, inner, outer, first, second, temb, inside, own, yours, *rest):
+def sending_kernel(real, other, keep, noise, inner, outer, first, second, temb, inside, own, yours, *rest):
     ends_out, spread_out, ends_own, spread_own = rest
     ends = {0: (ends_own, 0), 1: (ends_out, 0), 2: (ends_out, 1)}
     spread = {0: (spread_own, 0), 1: (spread_own, 1), 2: (spread_out, 0), 3: (spread_out, 1)}
-    work = Rest(real, (other, keep), (noise_other, None), first, second, temb, inside, ends)
+    work = Rest(real, (other, keep), noise, first, second, temb, inside, ends)
     work.prepare(0, inner, outer, own, spread)
     work.prepare(1, inner, outer, own, spread)
     work.edge_rows(0, spread)
@@ -310,9 +321,9 @@
     work.mark(yours, peaks)
 
 
-def keeping_kernel(real, keep, noise_keep, first, second, temb, inside, ends_in, spread_in, mine, ends_own):
+def keeping_kernel(real, keep, noise, first, second, temb, inside, ends_in, spread_in, mine, ends_own):
     ends = {1: (ends_in, 0), 2: (ends_in, 1), 3: (ends_own, 0)}
-    work = Rest(real, (keep, keep), (None, noise_keep), first, second, temb, inside, ends)
+    work = Rest(real, (keep, keep), noise, first, second, temb, inside, ends)
     work.edge_rows(3, {2: (spread_in, 0), 3: (spread_in, 1)})
     work.mark(mine, [work.second_conv(2, mine), work.second_conv(3, mine)])
 
@@ -334,14 +345,14 @@
 
 
 def edges(other, keep):
-    shape = jax.ShapeDtypeStruct((4, C, 2 * COLS), jnp.bfloat16)
+    shape = jax.ShapeDtypeStruct((4, C, WIDE), jnp.bfloat16)
     return call(edges_kernel, "edges", (other, keep), (shape, shape))
 
 
 def arrange(values, with_ends):
     channels, frames, length = values.shape
     half = jax.ShapeDtypeStruct((frames // 2 * channels * length // (SUB * LANES) + 1, SUB, LANES), jnp.float32)
-    ends = jax.ShapeDtypeStruct((frames, channels, 2 * COLS), jnp.bfloat16)
+    ends = jax.ShapeDtypeStruct((frames, channels, WIDE), jnp.bfloat16)
     shapes = (half, half) + ((ends, ends) if with_ends else ())
     return call(functools.partial(arrange_kernel, with_ends), "arrange", (values,), shapes)
 
@@ -510,7 +521,7 @@
 
     is_anchor = step_index == 0
     other0, keep0, near, far = arrange(start_latent, True)
-    yours1, mine1 = sweep(first, other0, keep0, arrange(noise_step, False), near, far)
+    yours1, mine1 = sweep(first, other0, keep0, (noise_step, noise_step), near, far)
     mine1, conv_first, start_latent, noise_step = lax.optimization_barrier(
         (mine1, conv_first, start_latent, noise_step)
     )

time: 82.1 us -> 81.2 us (0.989)
  Pallas kernels: 20.5 us -> 19.6 us
    ppermute x1, starting transfers between devices: 3.38 us -> 2 us  [local(): lax.ppermute(total, 'space', [(i, i ^ distance) for i in range(space)])]
    ppermute x8, starting transfers between devices: 18.4 us -> 19.6 us  [exchange(): lax.ppermute(coded(half), 'step', [(i, i ^ flip) for i in range(steps)])]
    pallas_call x12 -> x11, Pallas kernels: 19.6 us -> 18.6 us  [call(): pl.pallas_call(kernel, out_shape=out_shape, in_specs=[WHOLE] * len(arrays...]
  transfers between devices with their start and end apart: 15 -> 15, of which waited for: 10 -> 11; matrix products, arithmetic and copies ran while one was open for 1% -> 1% of each run, Pallas kernels for 14% -> 13%
where the time goes in v8:
time: 81.2 us; the launch traced here: 79.8 us
  waiting for transfers between devices  27.8 us (34%)
  starting transfers between devices  25.6 us (32%)
  Pallas kernels  19.6 us (24%)
  other arithmetic  3.52 us (4%)
  local copies, waits for them, and re-layouts  2.06 us (3%)
  between operations  1.08 us (1%)
    ppermute x8, waiting for transfers between devices, exchange(): lax.ppermute(coded(half), 'step', [(i, i ^ flip) for i in range(steps)])  23.9 us
    ppermute x8, starting transfers between devices, exchange(): lax.ppermute(coded(half), 'step', [(i, i ^ flip) for i in range(steps)])  19.6 us
    pallas_call x11, Pallas kernels, call(): pl.pallas_call(kernel, out_shape=out_shape, in_specs=[WHOLE] * len(arrays...  18.6 us
    ppermute x1, starting transfers between devices, local(): lax.ppermute(total, 'space', [(i, i ^ distance) for i in range(space)])  2 us
    ppermute x2, starting transfers between devices, sweep(): outer = lax.ppermute(far, 'space', outer_pairs)  1.64 us
  transfers between devices with their start and end apart: 15, of which 11 were waited for; matrix products, arithmetic and copies ran while one was open for 1% of the time, Pallas kernels for 13%

profile of v8, /device:TPU:0, one launch (start us, length us, event | category | flops | bytes accessed | tf_op | source)
XLA Modules:
  0.0 79.8 jit_solution(16665532055354550197)
XLA Ops:
  0.7 1.3 %pad.7.first = bf16[3,640,256]{2,1,0:T(8,128)(2,1)S(1)} pad(bf16[3,576,256]{2,1,0:T(8,128)(2,1)} %bitcast.61, bf16[]{:T(256)} %constant.98.clone.1), padding=0_0x0_64x0_0 | pad | bytes 1867778 | tf_op jit(solution)/shard_map/jit(_pad)/pad | solution.py:512
  2.0 0.6 arrange.3
  2.6 0.5 collective-permute-start
  3.1 0.8 collective-permute-start.1
  4.1 0.2 fusion.56.temb
  4.3 2.4 %interior.2 = (bf16[4,480,256]{2,1,0:T(8,128)(2,1)S(1)}, bf16[4,320,384]{2,1,0:T(8,128)(2,1)S(1)}) custom-call(f32[81,8,128]{2,1,0:T(8,128)S(1)} %get-tuple-element.33.other, f32[81,8,128]{2,1,0:T(8,128)S(1)} %get-tuple-element.31.keep, bf16[3,640,256]{2,1,0:T(8,128)(2,1)S(1)} %pad.7.first, f32[1,256]{1,0:T(1,128)S(1)} %fusion.56.temb), custom_call_target="tpu_custom_call" | custom-call | flops 2000000000 | bytes 4000000 | tf_op jit(solution)/shard_map/interior/pallas_call | solution.py:335
  6.8 3.6 %sending.2 = (f32[81,8,128]{2,1,0:T(8,128)S(1)}, bf16[2,320,256]{2,1,0:T(8,128)(2,1)S(1)}, bf16[2,640,384]{2,1,0:T(8,128)(2,1)S(1)}) custom-call(f32[3,128]{1,0:T(4,128)S(1)} %pad_maximum_fusion.real, f32[81,8,128]{2,1,0:T(8,128)S(1)} %get-tuple-element.33.other, f32[81,8,128]{2,1,0:T(8,128)S(1)} %get-tuple-element.31.keep, f32[64,4,640]{2,1,0:T(4,128)S(1)} %bitcast.58, ...), custom_call_target="tpu_custom_call" | custom-call | flops 2000000000 | bytes 4000000 | tf_op jit(solution)/shard_map/sending/pallas_call | solution.py:335
  10.4 0.2 fusion
  10.5 2.5 %collective-permute-start.2 = (f16[81,8,128]{2,1,0:T(8,128)(2,1)S(1)}, f16[81,8,128]{2,1,0:T(8,128)(2,1)S(1)}, u32[]{:S(2)}, u32[]{:S(2)}) collective-permute-start(f16[81,8,128]{2,1,0:T(8,128)(2,1)S(1)} %fusion), channel_id=1, source_target_pairs={{0,4},{4,0},{8,12},{12,8},{16,20},{20,16},{24,28},{28,24},{1,5},{5... | collective-permute-start | bytes 497672 | tf_op jit(solution)/shard_map/ppermute | solution.py:478
  13.0 2.5 %keeping.2 = f32[81,8,128]{2,1,0:T(8,128)S(1)} custom-call(f32[3,128]{1,0:T(4,128)S(1)} %pad_maximum_fusion.real, f32[81,8,128]{2,1,0:T(8,128)S(1)} %get-tuple-element.31.keep, f32[64,4,640]{2,1,0:T(4,128)S(1)} %bitcast.59, bf16[3,640,256]{2,1,0:T(8,128)(2,1)S(1)} %pad.7.first, bf16[3,64,2304]{2,1,0:T(8,128)(2,1)S(1)} %copy-done.3, ...), custom_call_target="tpu_custom_call" | custom-call | flops 2000000000 | bytes 4000000 | tf_op jit(solution)/shard_map/keeping/pallas_call | solution.py:335
  15.6 0.8 collective-permute-done.2
  16.4 0.2 add_select_fusion.9
  16.7 2.1 %collective-permute-start.3 = (f16[81,8,128]{2,1,0:T(8,128)(2,1)S(1)}, f16[81,8,128]{2,1,0:T(8,128)(2,1)S(1)}, u32[]{:S(2)}, u32[]{:S(2)}) collective-permute-start(f16[81,8,128]{2,1,0:T(8,128)(2,1)S(1)} %fusion.1), channel_id=1, source_target_pairs={{0,8},{4,12},{8,0},{12,4},{16,24},{20,28},{24,16},{28,20},{1,9},{5... | collective-permute-start | bytes 497672 | tf_op jit(solution)/shard_map/ppermute | solution.py:478
  18.9 3.5 %collective-permute-done.3 = f16[81,8,128]{2,1,0:T(8,128)(2,1)S(1)} collective-permute-done((f16[81,8,128]{2,1,0:T(8,128)(2,1)S(1)}, f16[81,8,128]{2,1,0:T(8,128)(2,1)S(1)}, u32[]{:S(2)}, u32[]{:S(2)}) %collective-permute-start.3) | collective-permute-done | bytes 165920 | tf_op jit(solution)/shard_map/ppermute | solution.py:478
  22.4 0.2 add_select_fusion.8
  22.8 4.4 %collective-permute-start.4 = (f16[81,8,128]{2,1,0:T(8,128)(2,1)S(1)}, f16[81,8,128]{2,1,0:T(8,128)(2,1)S(1)}, u32[]{:S(2)}, u32[]{:S(2)}) collective-permute-start(f16[81,8,128]{2,1,0:T(8,128)(2,1)S(1)} %fusion.2), channel_id=1, source_target_pairs={{0,24},{4,28},{8,16},{12,20},{16,8},{20,12},{24,0},{28,4},{1,25},{... | collective-permute-start | bytes 497672 | tf_op jit(solution)/shard_map/ppermute | solution.py:478
  27.2 0.5 arrange.4
  27.7 4.4 %collective-permute-done.4 = f16[81,8,128]{2,1,0:T(8,128)(2,1)S(1)} collective-permute-done((f16[81,8,128]{2,1,0:T(8,128)(2,1)S(1)}, f16[81,8,128]{2,1,0:T(8,128)(2,1)S(1)}, u32[]{:S(2)}, u32[]{:S(2)}) %collective-permute-start.4) | collective-permute-done | bytes 165920 | tf_op jit(solution)/shard_map/ppermute | solution.py:478
  32.1 0.4 fusion.11
  32.8 1.9 %collective-permute-start.5 = (f16[81,8,128]{2,1,0:T(8,128)(2,1)S(1)}, f16[81,8,128]{2,1,0:T(8,128)(2,1)S(1)}, u32[]{:S(2)}, u32[]{:S(2)}) collective-permute-start(f16[81,8,128]{2,1,0:T(8,128)(2,1)S(1)} %fusion.4), channel_id=1, source_target_pairs={{0,4},{4,0},{8,12},{12,8},{16,20},{20,16},{24,28},{28,24},{1,5},{5... | collective-permute-start | bytes 497672 | tf_op jit(solution)/shard_map/ppermute | solution.py:478
  34.8 0.5 arrange.5
  35.2 3.9 %collective-permute-done.5 = f16[81,8,128]{2,1,0:T(8,128)(2,1)S(1)} collective-permute-done((f16[81,8,128]{2,1,0:T(8,128)(2,1)S(1)}, f16[81,8,128]{2,1,0:T(8,128)(2,1)S(1)}, u32[]{:S(2)}, u32[]{:S(2)}) %collective-permute-start.5) | collective-permute-done | bytes 165920 | tf_op jit(solution)/shard_map/ppermute | solution.py:478
  39.2 0.2 fusion.5.other
  39.5 0.8 %collective-permute-start.7 = (bf16[4,64,256]{2,1,0:T(8,128)(2,1)S(1)}, bf16[4,64,256]{2,1,0:T(8,128)(2,1)S(1)}, u32[]{:S(2)}, u32[]{:S(2)}) collective-permute-start(bf16[4,64,256]{2,1,0:T(8,128)(2,1)S(1)} %get-tuple-element.51), channel_id=1, source_target_pairs={{1,2},{2,1},{5,6},{6,5},{9,10},{10,9},{13,14},{14,13},{17,18},{18,... | collective-permute-start | bytes 393224 | tf_op jit(solution)/shard_map/ppermute | solution.py:519
  40.4 2.4 %interior.3 = (bf16[4,480,256]{2,1,0:T(8,128)(2,1)S(1)}, bf16[4,320,384]{2,1,0:T(8,128)(2,1)S(1)}) custom-call(f32[81,8,128]{2,1,0:T(8,128)S(1)} %fusion.5.other, f32[81,8,128]{2,1,0:T(8,128)S(1)} %get-tuple-element.70.keep, bf16[3,640,256]{2,1,0:T(8,128)(2,1)S(1)} %pad.8.first, f32[1,256]{1,0:T(1,128)S(1)} %fusion.56.temb), custom_call_target="tpu_custom_call" | custom-call | flops 2000000000 | bytes 4000000 | tf_op jit(solution)/shard_map/interior/pallas_call | solution.py:335
  42.8 3.5 %sending.3 = (f32[81,8,128]{2,1,0:T(8,128)S(1)}, bf16[2,320,256]{2,1,0:T(8,128)(2,1)S(1)}, bf16[2,640,384]{2,1,0:T(8,128)(2,1)S(1)}) custom-call(f32[3,128]{1,0:T(4,128)S(1)} %pad_maximum_fusion.real, f32[81,8,128]{2,1,0:T(8,128)S(1)} %fusion.5.other, f32[81,8,128]{2,1,0:T(8,128)S(1)} %get-tuple-element.70.keep, f32[81,8,128]{2,1,0:T(8,128)S(1)} %get-tuple-element.49.noise, ...), custom_call_target="tpu_custom_call" | custom-call | flops 2000000000 | bytes 4000000 | tf_op jit(solution)/shard_map/sending/pallas_call | solution.py:335
  46.3 0.2 fusion.6
  46.5 1.8 %collective-permute-start.8 = (f16[81,8,128]{2,1,0:T(8,128)(2,1)S(1)}, f16[81,8,128]{2,1,0:T(8,128)(2,1)S(1)}, u32[]{:S(2)}, u32[]{:S(2)}) collective-permute-start(f16[81,8,128]{2,1,0:T(8,128)(2,1)S(1)} %fusion.6), channel_id=1, source_target_pairs={{0,4},{4,0},{8,12},{12,8},{16,20},{20,16},{24,28},{28,24},{1,5},{5... | collective-permute-start | bytes 497672 | tf_op jit(solution)/shard_map/ppermute | solution.py:478
  48.3 2.5 %keeping.3.mine = f32[81,8,128]{2,1,0:T(8,128)S(1)} custom-call(f32[3,128]{1,0:T(4,128)S(1)} %pad_maximum_fusion.real, f32[81,8,128]{2,1,0:T(8,128)S(1)} %get-tuple-element.70.keep, f32[81,8,128]{2,1,0:T(8,128)S(1)} %get-tuple-element.45.noise, bf16[3,640,256]{2,1,0:T(8,128)(2,1)S(1)} %pad.8.first, bf16[3,64,2304]{2,1,0:T(8,128)(2,1)S(1)} %copy-done.3, ...), custom_call_target="tpu_custom_call" | custom-call | flops 2000000000 | bytes 4000000 | tf_op jit(solution)/shard_map/keeping/pallas_call | solution.py:335
  50.8 1.1 %collective-permute-done.8 = f16[81,8,128]{2,1,0:T(8,128)(2,1)S(1)} collective-permute-done((f16[81,8,128]{2,1,0:T(8,128)(2,1)S(1)}, f16[81,8,128]{2,1,0:T(8,128)(2,1)S(1)}, u32[]{:S(2)}, u32[]{:S(2)}) %collective-permute-start.8) | collective-permute-done | bytes 165920 | tf_op jit(solution)/shard_map/ppermute | solution.py:478
  51.9 0.2 add_select_fusion.4
  52.3 3.6 %collective-permute-start.9 = (f16[81,8,128]{2,1,0:T(8,128)(2,1)S(1)}, f16[81,8,128]{2,1,0:T(8,128)(2,1)S(1)}, u32[]{:S(2)}, u32[]{:S(2)}) collective-permute-start(f16[81,8,128]{2,1,0:T(8,128)(2,1)S(1)} %fusion.7), channel_id=1, source_target_pairs={{0,8},{4,12},{8,0},{12,4},{16,24},{20,28},{24,16},{28,20},{1,9},{5... | collective-permute-start | bytes 497672 | tf_op jit(solution)/shard_map/ppermute | solution.py:478
  55.9 3.4 %collective-permute-done.9 = f16[81,8,128]{2,1,0:T(8,128)(2,1)S(1)} collective-permute-done((f16[81,8,128]{2,1,0:T(8,128)(2,1)S(1)}, f16[81,8,128]{2,1,0:T(8,128)(2,1)S(1)}, u32[]{:S(2)}, u32[]{:S(2)}) %collective-permute-start.9) | collective-permute-done | bytes 165920 | tf_op jit(solution)/shard_map/ppermute | solution.py:478
  59.4 0.2 add_select_fusion.3
  59.7 2.5 %collective-permute-start.10 = (f16[81,8,128]{2,1,0:T(8,128)(2,1)S(1)}, f16[81,8,128]{2,1,0:T(8,128)(2,1)S(1)}, u32[]{:S(2)}, u32[]{:S(2)}) collective-permute-start(f16[81,8,128]{2,1,0:T(8,128)(2,1)S(1)} %fusion.8), channel_id=1, source_target_pairs={{0,24},{4,28},{8,16},{12,20},{16,8},{20,12},{24,0},{28,4},{1,25},{... | collective-permute-start | bytes 497672 | tf_op jit(solution)/shard_map/ppermute | solution.py:478
  62.2 6.1 %collective-permute-done.10 = f16[81,8,128]{2,1,0:T(8,128)(2,1)S(1)} collective-permute-done((f16[81,8,128]{2,1,0:T(8,128)(2,1)S(1)}, f16[81,8,128]{2,1,0:T(8,128)(2,1)S(1)}, u32[]{:S(2)}, u32[]{:S(2)}) %collective-permute-start.10) | collective-permute-done | bytes 165920 | tf_op jit(solution)/shard_map/ppermute | solution.py:478
  68.3 0.4 fusion.12
  68.8 0.2 changes.1
  69.0 0.3 collective-permute-start.11
  69.3 0.9 %collective-permute-done.11 = f32[2,8,128]{2,1,0:T(8,128)S(1)} collective-permute-done((f32[2,8,128]{2,1,0:T(8,128)S(1)}, f32[2,8,128]{2,1,0:T(8,128)S(1)}, u32[]{:S(2)}, u32[]{:S(2)}) %collective-permute-start.11) | collective-permute-done | bytes 8224 | tf_op jit(solution)/shard_map/ppermute | solution.py:539
  70.2 1.5 %collective-permute-start.12 = (f32[8,128]{1,0:T(8,128)S(1)}, f32[8,128]{1,0:T(8,128)S(1)}, u32[]{:S(2)}, u32[]{:S(2)}) collective-permute-start(f32[8,128]{1,0:T(8,128)S(1)} %slice_bitcast_fusion), channel_id=1, source_target_pairs={{0,4},{4,0},{8,12},{12,8},{16,20},{20,16},{24,28},{28,24},{1,5},{5... | collective-permute-start | bytes 12296 | tf_op jit(solution)/shard_map/ppermute | solution.py:541
  71.9 0.6 collective-permute-start.14
  72.4 1.4 %collective-permute-done.12 = f32[8,128]{1,0:T(8,128)S(1)} collective-permute-done((f32[8,128]{1,0:T(8,128)S(1)}, f32[8,128]{1,0:T(8,128)S(1)}, u32[]{:S(2)}, u32[]{:S(2)}) %collective-permute-start.12) | collective-permute-done | bytes 4128 | tf_op jit(solution)/shard_map/ppermute | solution.py:541
  73.8 2.0 %collective-permute-start.13 = (f32[8,128]{1,0:T(8,128)S(1)}, f32[8,128]{1,0:T(8,128)S(1)}, u32[]{:S(2)}, u32[]{:S(2)}) collective-permute-start(f32[8,128]{1,0:T(8,128)S(1)} %fusion.19), channel_id=1, source_target_pairs={{0,2},{1,3},{2,0},{3,1},{4,6},{5,7},{6,4},{7,5},{8,10},{9,11},{10,... | collective-permute-start | bytes 12296 | tf_op jit(solution)/shard_map/ppermute | solution.py:543
  75.8 1.6 %collective-permute-done.13 = f32[8,128]{1,0:T(8,128)S(1)} collective-permute-done((f32[8,128]{1,0:T(8,128)S(1)}, f32[8,128]{1,0:T(8,128)S(1)}, u32[]{:S(2)}, u32[]{:S(2)}) %collective-permute-start.13) | collective-permute-done | bytes 4128 | tf_op jit(solution)/shard_map/ppermute | solution.py:543
  77.4 0.7 collective-permute-done.14
  78.3 1.0 %finish.1 = f32[64,4,640]{2,1,0:T(4,128)} custom-call(f32[81,8,128]{2,1,0:T(8,128)S(1)} %multiply_select_fusion.other, f32[81,8,128]{2,1,0:T(8,128)S(1)} %get-tuple-element.68.keep, f32[81,8,128]{2,1,0:T(8,128)S(1)} %get-tuple-element.55.yours, f32[81,8,128]{2,1,0:T(8,128)S(1)} %keeping.3.mine), custom_call_target="tpu_custom_call" | custom-call | flops 8000000000 | bytes 4000000 | tf_op jit(solution)/shard_map/finish/pallas_call | solution.py:427
  79.3 0.5 slice.87
  (62 shorter events, 1.9 us)
Async XLA Ops:
  0.6 3.5 %copy-start = (f32[64,256]{1,0:T(8,128)S(1)}, f32[64,256]{1,0:T(8,128)}, u32[]{:S(2)}) copy-start(f32[64,256]{1,0:T(8,128)} %param.11) | copy-start | bytes 196612
  0.6 1.4 %copy-start.1 = (f32[1,64,4,640]{3,2,1,0:T(4,128)S(1)}, f32[1,64,4,640]{3,2,1,0:T(4,128)}, u32[]{:S(2)}) copy-start(f32[1,64,4,640]{3,2,1,0:T(4,128)} %param.6) | copy-start | bytes 1966084
  2.6 4.1 %collective-permute-start = (bf16[4,64,256]{2,1,0:T(8,128)(2,1)S(1)}, bf16[4,64,256]{2,1,0:T(8,128)(2,1)S(1)}, u32[]{:S(2)}, u32[]{:S(2)}) collective-permute-start(bf16[4,64,256]{2,1,0:T(8,128)(2,1)S(1)} %get-tuple-element.35), channel_id=1, source_target_pairs={{0,1},{1,0},{2,3},{3,2},{4,5},{5,4},{6,7},{7,6},{8,9},{9,8},{10,11... | collective-permute-start | bytes 393224 | tf_op jit(solution)/shard_map/ppermute | solution.py:518
  3.1 0.8 %copy-start.5 = (s32[1,2]{1,0:T(1,128)S(1)}, s32[1,2]{1,0:T(1,128)}, u32[]{:S(2)}) copy-start(s32[1,2]{1,0:T(1,128)} %param.8) | copy-start | bytes 28
  3.1 3.6 %collective-permute-start.1 = (bf16[4,64,256]{2,1,0:T(8,128)(2,1)S(1)}, bf16[4,64,256]{2,1,0:T(8,128)(2,1)S(1)}, u32[]{:S(2)}, u32[]{:S(2)}) collective-permute-start(bf16[4,64,256]{2,1,0:T(8,128)(2,1)S(1)} %get-tuple-element.36), channel_id=1, source_target_pairs={{1,2},{2,1},{5,6},{6,5},{9,10},{10,9},{13,14},{14,13},{17,18},{18,... | collective-permute-start | bytes 393224 | tf_op jit(solution)/shard_map/ppermute | solution.py:519
  4.3 2.4 %copy-start.2 = (f32[1,64,4,640]{3,2,1,0:T(4,128)S(1)}, f32[1,64,4,640]{3,2,1,0:T(4,128)}, u32[]{:S(2)}) copy-start(f32[1,64,4,640]{3,2,1,0:T(4,128)} %param.7) | copy-start | bytes 1966084
  4.3 2.4 %copy-start.3 = (bf16[3,64,2304]{2,1,0:T(8,128)(2,1)S(1)}, bf16[3,64,2304]{2,1,0:T(8,128)(2,1)}, u32[]{:S(2)}) copy-start(bf16[3,64,2304]{2,1,0:T(8,128)(2,1)} %second.7) | copy-start | bytes 2654212
  10.5 5.8 %collective-permute-start.2 = (f16[81,8,128]{2,1,0:T(8,128)(2,1)S(1)}, f16[81,8,128]{2,1,0:T(8,128)(2,1)S(1)}, u32[]{:S(2)}, u32[]{:S(2)}) collective-permute-start(f16[81,8,128]{2,1,0:T(8,128)(2,1)S(1)} %fusion), channel_id=1, source_target_pairs={{0,4},{4,0},{8,12},{12,8},{16,20},{20,16},{24,28},{28,24},{1,5},{5... | collective-permute-start | bytes 497672 | tf_op jit(solution)/shard_map/ppermute | solution.py:478
  16.7 5.7 %collective-permute-start.3 = (f16[81,8,128]{2,1,0:T(8,128)(2,1)S(1)}, f16[81,8,128]{2,1,0:T(8,128)(2,1)S(1)}, u32[]{:S(2)}, u32[]{:S(2)}) collective-permute-start(f16[81,8,128]{2,1,0:T(8,128)(2,1)S(1)} %fusion.1), channel_id=1, source_target_pairs={{0,8},{4,12},{8,0},{12,4},{16,24},{20,28},{24,16},{28,20},{1,9},{5... | collective-permute-start | bytes 497672 | tf_op jit(solution)/shard_map/ppermute | solution.py:478
  22.8 9.3 %collective-permute-start.4 = (f16[81,8,128]{2,1,0:T(8,128)(2,1)S(1)}, f16[81,8,128]{2,1,0:T(8,128)(2,1)S(1)}, u32[]{:S(2)}, u32[]{:S(2)}) collective-permute-start(f16[81,8,128]{2,1,0:T(8,128)(2,1)S(1)} %fusion.2), channel_id=1, source_target_pairs={{0,24},{4,28},{8,16},{12,20},{16,8},{20,12},{24,0},{28,4},{1,25},{... | collective-permute-start | bytes 497672 | tf_op jit(solution)/shard_map/ppermute | solution.py:478
  32.1 2.6 %copy-start.4 = (bf16[3,256,576]{1,2,0:T(8,128)(2,1)S(1)}, bf16[3,256,576]{1,2,0:T(8,128)(2,1)}, u32[]{:S(2)}) copy-start(bf16[3,256,576]{1,2,0:T(8,128)(2,1)} %param.9) | copy-start | bytes 2654212
  32.8 6.4 %collective-permute-start.5 = (f16[81,8,128]{2,1,0:T(8,128)(2,1)S(1)}, f16[81,8,128]{2,1,0:T(8,128)(2,1)S(1)}, u32[]{:S(2)}, u32[]{:S(2)}) collective-permute-start(f16[81,8,128]{2,1,0:T(8,128)(2,1)S(1)} %fusion.4), channel_id=1, source_target_pairs={{0,4},{4,0},{8,12},{12,8},{16,20},{20,16},{24,28},{28,24},{1,5},{5... | collective-permute-start | bytes 497672 | tf_op jit(solution)/shard_map/ppermute | solution.py:478
  39.4 3.3 %collective-permute-start.6 = (bf16[4,64,256]{2,1,0:T(8,128)(2,1)S(1)}, bf16[4,64,256]{2,1,0:T(8,128)(2,1)S(1)}, u32[]{:S(2)}, u32[]{:S(2)}) collective-permute-start(bf16[4,64,256]{2,1,0:T(8,128)(2,1)S(1)} %get-tuple-element.50), channel_id=1, source_target_pairs={{0,1},{1,0},{2,3},{3,2},{4,5},{5,4},{6,7},{7,6},{8,9},{9,8},{10,11... | collective-permute-start | bytes 393224 | tf_op jit(solution)/shard_map/ppermute | solution.py:518
  39.5 3.3 %collective-permute-start.7 = (bf16[4,64,256]{2,1,0:T(8,128)(2,1)S(1)}, bf16[4,64,256]{2,1,0:T(8,128)(2,1)S(1)}, u32[]{:S(2)}, u32[]{:S(2)}) collective-permute-start(bf16[4,64,256]{2,1,0:T(8,128)(2,1)S(1)} %get-tuple-element.51), channel_id=1, source_target_pairs={{1,2},{2,1},{5,6},{6,5},{9,10},{10,9},{13,14},{14,13},{17,18},{18,... | collective-permute-start | bytes 393224 | tf_op jit(solution)/shard_map/ppermute | solution.py:519
  46.5 5.4 %collective-permute-start.8 = (f16[81,8,128]{2,1,0:T(8,128)(2,1)S(1)}, f16[81,8,128]{2,1,0:T(8,128)(2,1)S(1)}, u32[]{:S(2)}, u32[]{:S(2)}) collective-permute-start(f16[81,8,128]{2,1,0:T(8,128)(2,1)S(1)} %fusion.6), channel_id=1, source_target_pairs={{0,4},{4,0},{8,12},{12,8},{16,20},{20,16},{24,28},{28,24},{1,5},{5... | collective-permute-start | bytes 497672 | tf_op jit(solution)/shard_map/ppermute | solution.py:478
  52.3 7.0 %collective-permute-start.9 = (f16[81,8,128]{2,1,0:T(8,128)(2,1)S(1)}, f16[81,8,128]{2,1,0:T(8,128)(2,1)S(1)}, u32[]{:S(2)}, u32[]{:S(2)}) collective-permute-start(f16[81,8,128]{2,1,0:T(8,128)(2,1)S(1)} %fusion.7), channel_id=1, source_target_pairs={{0,8},{4,12},{8,0},{12,4},{16,24},{20,28},{24,16},{28,20},{1,9},{5... | collective-permute-start | bytes 497672 | tf_op jit(solution)/shard_map/ppermute | solution.py:478
  59.7 8.6 %collective-permute-start.10 = (f16[81,8,128]{2,1,0:T(8,128)(2,1)S(1)}, f16[81,8,128]{2,1,0:T(8,128)(2,1)S(1)}, u32[]{:S(2)}, u32[]{:S(2)}) collective-permute-start(f16[81,8,128]{2,1,0:T(8,128)(2,1)S(1)} %fusion.8), channel_id=1, source_target_pairs={{0,24},{4,28},{8,16},{12,20},{16,8},{20,12},{24,0},{28,4},{1,25},{... | collective-permute-start | bytes 497672 | tf_op jit(solution)/shard_map/ppermute | solution.py:478
  69.0 1.2 %collective-permute-start.11 = (f32[2,8,128]{2,1,0:T(8,128)S(1)}, f32[2,8,128]{2,1,0:T(8,128)S(1)}, u32[]{:S(2)}, u32[]{:S(2)}) collective-permute-start(f32[2,8,128]{2,1,0:T(8,128)S(1)} %changes.1), channel_id=1, source_target_pairs={{0,1},{1,0},{2,3},{3,2},{4,5},{5,4},{6,7},{7,6},{8,9},{9,8},{10,11... | collective-permute-start | bytes 24584 | tf_op jit(solution)/shard_map/ppermute | solution.py:539
  70.2 3.6 %collective-permute-start.12 = (f32[8,128]{1,0:T(8,128)S(1)}, f32[8,128]{1,0:T(8,128)S(1)}, u32[]{:S(2)}, u32[]{:S(2)}) collective-permute-start(f32[8,128]{1,0:T(8,128)S(1)} %slice_bitcast_fusion), channel_id=1, source_target_pairs={{0,4},{4,0},{8,12},{12,8},{16,20},{20,16},{24,28},{28,24},{1,5},{5... | collective-permute-start | bytes 12296 | tf_op jit(solution)/shard_map/ppermute | solution.py:541
  71.9 6.2 %collective-permute-start.14 = (f16[81,8,128]{2,1,0:T(8,128)(2,1)S(1)}, f16[81,8,128]{2,1,0:T(8,128)(2,1)S(1)}, u32[]{:S(2)}, u32[]{:S(2)}) collective-permute-start(f16[81,8,128]{2,1,0:T(8,128)(2,1)S(1)} %fusion.10), channel_id=1, source_target_pairs={{0,4},{4,0},{8,12},{12,8},{16,20},{20,16},{24,28},{28,24},{1,5},{5... | collective-permute-start | bytes 497672 | tf_op jit(solution)/shard_map/ppermute | solution.py:478
  73.8 3.6 %collective-permute-start.13 = (f32[8,128]{1,0:T(8,128)S(1)}, f32[8,128]{1,0:T(8,128)S(1)}, u32[]{:S(2)}, u32[]{:S(2)}) collective-permute-start(f32[8,128]{1,0:T(8,128)S(1)} %fusion.19), channel_id=1, source_target_pairs={{0,2},{1,3},{2,0},{3,1},{4,6},{5,7},{6,4},{7,5},{8,10},{9,11},{10,... | collective-permute-start | bytes 12296 | tf_op jit(solution)/shard_map/ppermute | solution.py:543

commit v9 on v8

--- a/solution.py
+++ b/solution.py
@@ -266,7 +266,7 @@
         )
         latent, noise = self.frames.load(self.halves, v), self.noise_of(v)
         base = flags.keep * latent + flags.spread * noise + jnp.where(flags.anchor, latent, 0.0)
-        chunk = length // 2
+        chunk = length
         column = lax.broadcasted_iota(jnp.int32, (1, chunk), 1) % COLS
         predicted = []
         for start in range(0, length, chunk):
@@ -325,7 +325,7 @@
     ends = {1: (ends_in, 0), 2: (ends_in, 1), 3: (ends_own, 0)}
     work = Rest(real, (keep, keep), noise, first, second, temb, inside, ends)
     work.edge_rows(3, {2: (spread_in, 0), 3: (spread_in, 1)})
-    work.mark(mine, [work.second_conv(2, mine), work.second_conv(3, mine)])
+    work.mark(mine, [work.second_conv(3, mine), work.second_conv(2, mine)])
 
 
 WHOLE = pl.BlockSpec(memory_space=pltpu.VMEM)

time: 81.2 us -> 80.3 us (0.989)
  Pallas kernels: 19.6 us -> 17.9 us
    pallas_call x11, Pallas kernels: 18.6 us -> 17 us  [call(): pl.pallas_call(kernel, out_shape=out_shape, in_specs=[WHOLE] * len(arrays...]
    ppermute x8, waiting for transfers between devices: 23.9 us -> 24.8 us  [exchange(): lax.ppermute(coded(half), 'step', [(i, i ^ flip) for i in range(steps)])]
  transfers between devices with their start and end apart: 15 -> 15, of which waited for: 11 -> 11; matrix products, arithmetic and copies ran while one was open for 1% -> 1% of each run, Pallas kernels for 13% -> 12%
where the time goes in v9:
time: 80.3 us; the launch traced here: 79 us
  waiting for transfers between devices  28.6 us (36%)
  starting transfers between devices  25.6 us (32%)
  Pallas kernels  17.9 us (22%)
  other arithmetic  3.52 us (4%)
  local copies, waits for them, and re-layouts  2.06 us (3%)
  between operations  1.08 us (1%)
    ppermute x8, waiting for transfers between devices, exchange(): lax.ppermute(coded(half), 'step', [(i, i ^ flip) for i in range(steps)])  24.8 us
    ppermute x8, starting transfers between devices, exchange(): lax.ppermute(coded(half), 'step', [(i, i ^ flip) for i in range(steps)])  19.5 us
    pallas_call x11, Pallas kernels, call(): pl.pallas_call(kernel, out_shape=out_shape, in_specs=[WHOLE] * len(arrays...  17 us
    ppermute x1, starting transfers between devices, local(): lax.ppermute(total, 'space', [(i, i ^ distance) for i in range(space)])  1.99 us
    ppermute x2, starting transfers between devices, sweep(): outer = lax.ppermute(far, 'space', outer_pairs)  1.64 us
    ppermute x1, waiting for transfers between devices, local(): lax.ppermute(total, 'space', [(i, i ^ distance) for i in range(space)])  1.62 us
  transfers between devices with their start and end apart: 15, of which 11 were waited for; matrix products, arithmetic and copies ran while one was open for 1% of the time, Pallas kernels for 12%

profile of v9, /device:TPU:0, one launch (start us, length us, event | category | flops | bytes accessed | tf_op | source)
XLA Modules:
  0.0 79.0 jit_solution(7068087572756230677)
XLA Ops:
  0.7 1.3 %pad.7.first = bf16[3,640,256]{2,1,0:T(8,128)(2,1)S(1)} pad(bf16[3,576,256]{2,1,0:T(8,128)(2,1)} %bitcast.61, bf16[]{:T(256)} %constant.98.clone.1), padding=0_0x0_64x0_0 | pad | bytes 1867778 | tf_op jit(solution)/shard_map/jit(_pad)/pad | solution.py:512
  2.0 0.6 arrange.3
  2.6 0.5 collective-permute-start
  3.1 0.8 collective-permute-start.1
  4.1 0.2 fusion.56.temb
  4.3 2.4 %interior.2 = (bf16[4,480,256]{2,1,0:T(8,128)(2,1)S(1)}, bf16[4,320,384]{2,1,0:T(8,128)(2,1)S(1)}) custom-call(f32[81,8,128]{2,1,0:T(8,128)S(1)} %get-tuple-element.33.other, f32[81,8,128]{2,1,0:T(8,128)S(1)} %get-tuple-element.31.keep, bf16[3,640,256]{2,1,0:T(8,128)(2,1)S(1)} %pad.7.first, f32[1,256]{1,0:T(1,128)S(1)} %fusion.56.temb), custom_call_target="tpu_custom_call" | custom-call | flops 2000000000 | bytes 4000000 | tf_op jit(solution)/shard_map/interior/pallas_call | solution.py:335
  6.8 3.1 %sending.2 = (f32[81,8,128]{2,1,0:T(8,128)S(1)}, bf16[2,320,256]{2,1,0:T(8,128)(2,1)S(1)}, bf16[2,640,384]{2,1,0:T(8,128)(2,1)S(1)}) custom-call(f32[3,128]{1,0:T(4,128)S(1)} %pad_maximum_fusion.real, f32[81,8,128]{2,1,0:T(8,128)S(1)} %get-tuple-element.33.other, f32[81,8,128]{2,1,0:T(8,128)S(1)} %get-tuple-element.31.keep, f32[64,4,640]{2,1,0:T(4,128)S(1)} %bitcast.58, ...), custom_call_target="tpu_custom_call" | custom-call | flops 2000000000 | bytes 4000000 | tf_op jit(solution)/shard_map/sending/pallas_call | solution.py:335
  9.9 0.2 fusion
  10.1 2.5 %collective-permute-start.2 = (f16[81,8,128]{2,1,0:T(8,128)(2,1)S(1)}, f16[81,8,128]{2,1,0:T(8,128)(2,1)S(1)}, u32[]{:S(2)}, u32[]{:S(2)}) collective-permute-start(f16[81,8,128]{2,1,0:T(8,128)(2,1)S(1)} %fusion), channel_id=1, source_target_pairs={{0,4},{4,0},{8,12},{12,8},{16,20},{20,16},{24,28},{28,24},{1,5},{5... | collective-permute-start | bytes 497672 | tf_op jit(solution)/shard_map/ppermute | solution.py:478
  12.6 2.1 %keeping.2 = f32[81,8,128]{2,1,0:T(8,128)S(1)} custom-call(f32[3,128]{1,0:T(4,128)S(1)} %pad_maximum_fusion.real, f32[81,8,128]{2,1,0:T(8,128)S(1)} %get-tuple-element.31.keep, f32[64,4,640]{2,1,0:T(4,128)S(1)} %bitcast.59, bf16[3,640,256]{2,1,0:T(8,128)(2,1)S(1)} %pad.7.first, bf16[3,64,2304]{2,1,0:T(8,128)(2,1)S(1)} %copy-done.3, ...), custom_call_target="tpu_custom_call" | custom-call | flops 2000000000 | bytes 4000000 | tf_op jit(solution)/shard_map/keeping/pallas_call | solution.py:335
  14.7 1.2 %collective-permute-done.2 = f16[81,8,128]{2,1,0:T(8,128)(2,1)S(1)} collective-permute-done((f16[81,8,128]{2,1,0:T(8,128)(2,1)S(1)}, f16[81,8,128]{2,1,0:T(8,128)(2,1)S(1)}, u32[]{:S(2)}, u32[]{:S(2)}) %collective-permute-start.2) | collective-permute-done | bytes 165920 | tf_op jit(solution)/shard_map/ppermute | solution.py:478
  16.0 0.2 add_select_fusion.9
  16.3 2.1 %collective-permute-start.3 = (f16[81,8,128]{2,1,0:T(8,128)(2,1)S(1)}, f16[81,8,128]{2,1,0:T(8,128)(2,1)S(1)}, u32[]{:S(2)}, u32[]{:S(2)}) collective-permute-start(f16[81,8,128]{2,1,0:T(8,128)(2,1)S(1)} %fusion.1), channel_id=1, source_target_pairs={{0,8},{4,12},{8,0},{12,4},{16,24},{20,28},{24,16},{28,20},{1,9},{5... | collective-permute-start | bytes 497672 | tf_op jit(solution)/shard_map/ppermute | solution.py:478
  18.5 3.5 %collective-permute-done.3 = f16[81,8,128]{2,1,0:T(8,128)(2,1)S(1)} collective-permute-done((f16[81,8,128]{2,1,0:T(8,128)(2,1)S(1)}, f16[81,8,128]{2,1,0:T(8,128)(2,1)S(1)}, u32[]{:S(2)}, u32[]{:S(2)}) %collective-permute-start.3) | collective-permute-done | bytes 165920 | tf_op jit(solution)/shard_map/ppermute | solution.py:478
  22.0 0.2 add_select_fusion.8
  22.4 4.4 %collective-permute-start.4 = (f16[81,8,128]{2,1,0:T(8,128)(2,1)S(1)}, f16[81,8,128]{2,1,0:T(8,128)(2,1)S(1)}, u32[]{:S(2)}, u32[]{:S(2)}) collective-permute-start(f16[81,8,128]{2,1,0:T(8,128)(2,1)S(1)} %fusion.2), channel_id=1, source_target_pairs={{0,24},{4,28},{8,16},{12,20},{16,8},{20,12},{24,0},{28,4},{1,25},{... | collective-permute-start | bytes 497672 | tf_op jit(solution)/shard_map/ppermute | solution.py:478
  26.8 0.5 arrange.4
  27.2 4.4 %collective-permute-done.4 = f16[81,8,128]{2,1,0:T(8,128)(2,1)S(1)} collective-permute-done((f16[81,8,128]{2,1,0:T(8,128)(2,1)S(1)}, f16[81,8,128]{2,1,0:T(8,128)(2,1)S(1)}, u32[]{:S(2)}, u32[]{:S(2)}) %collective-permute-start.4) | collective-permute-done | bytes 165920 | tf_op jit(solution)/shard_map/ppermute | solution.py:478
  31.7 0.4 fusion.11
  32.3 2.0 %collective-permute-start.5 = (f16[81,8,128]{2,1,0:T(8,128)(2,1)S(1)}, f16[81,8,128]{2,1,0:T(8,128)(2,1)S(1)}, u32[]{:S(2)}, u32[]{:S(2)}) collective-permute-start(f16[81,8,128]{2,1,0:T(8,128)(2,1)S(1)} %fusion.4), channel_id=1, source_target_pairs={{0,4},{4,0},{8,12},{12,8},{16,20},{20,16},{24,28},{28,24},{1,5},{5... | collective-permute-start | bytes 497672 | tf_op jit(solution)/shard_map/ppermute | solution.py:478
  34.4 0.5 arrange.5
  34.8 3.9 %collective-permute-done.5 = f16[81,8,128]{2,1,0:T(8,128)(2,1)S(1)} collective-permute-done((f16[81,8,128]{2,1,0:T(8,128)(2,1)S(1)}, f16[81,8,128]{2,1,0:T(8,128)(2,1)S(1)}, u32[]{:S(2)}, u32[]{:S(2)}) %collective-permute-start.5) | collective-permute-done | bytes 165920 | tf_op jit(solution)/shard_map/ppermute | solution.py:478
  38.8 0.2 fusion.5.other
  39.1 0.8 %collective-permute-start.7 = (bf16[4,64,256]{2,1,0:T(8,128)(2,1)S(1)}, bf16[4,64,256]{2,1,0:T(8,128)(2,1)S(1)}, u32[]{:S(2)}, u32[]{:S(2)}) collective-permute-start(bf16[4,64,256]{2,1,0:T(8,128)(2,1)S(1)} %get-tuple-element.51), channel_id=1, source_target_pairs={{1,2},{2,1},{5,6},{6,5},{9,10},{10,9},{13,14},{14,13},{17,18},{18,... | collective-permute-start | bytes 393224 | tf_op jit(solution)/shard_map/ppermute | solution.py:519
  40.0 2.4 %interior.3 = (bf16[4,480,256]{2,1,0:T(8,128)(2,1)S(1)}, bf16[4,320,384]{2,1,0:T(8,128)(2,1)S(1)}) custom-call(f32[81,8,128]{2,1,0:T(8,128)S(1)} %fusion.5.other, f32[81,8,128]{2,1,0:T(8,128)S(1)} %get-tuple-element.70.keep, bf16[3,640,256]{2,1,0:T(8,128)(2,1)S(1)} %pad.8.first, f32[1,256]{1,0:T(1,128)S(1)} %fusion.56.temb), custom_call_target="tpu_custom_call" | custom-call | flops 2000000000 | bytes 4000000 | tf_op jit(solution)/shard_map/interior/pallas_call | solution.py:335
  42.4 3.1 %sending.3 = (f32[81,8,128]{2,1,0:T(8,128)S(1)}, bf16[2,320,256]{2,1,0:T(8,128)(2,1)S(1)}, bf16[2,640,384]{2,1,0:T(8,128)(2,1)S(1)}) custom-call(f32[3,128]{1,0:T(4,128)S(1)} %pad_maximum_fusion.real, f32[81,8,128]{2,1,0:T(8,128)S(1)} %fusion.5.other, f32[81,8,128]{2,1,0:T(8,128)S(1)} %get-tuple-element.70.keep, f32[81,8,128]{2,1,0:T(8,128)S(1)} %get-tuple-element.49.noise, ...), custom_call_target="tpu_custom_call" | custom-call | flops 2000000000 | bytes 4000000 | tf_op jit(solution)/shard_map/sending/pallas_call | solution.py:335
  45.5 0.2 fusion.6
  45.7 1.8 %collective-permute-start.8 = (f16[81,8,128]{2,1,0:T(8,128)(2,1)S(1)}, f16[81,8,128]{2,1,0:T(8,128)(2,1)S(1)}, u32[]{:S(2)}, u32[]{:S(2)}) collective-permute-start(f16[81,8,128]{2,1,0:T(8,128)(2,1)S(1)} %fusion.6), channel_id=1, source_target_pairs={{0,4},{4,0},{8,12},{12,8},{16,20},{20,16},{24,28},{28,24},{1,5},{5... | collective-permute-start | bytes 497672 | tf_op jit(solution)/shard_map/ppermute | solution.py:478
  47.5 2.1 %keeping.3.mine = f32[81,8,128]{2,1,0:T(8,128)S(1)} custom-call(f32[3,128]{1,0:T(4,128)S(1)} %pad_maximum_fusion.real, f32[81,8,128]{2,1,0:T(8,128)S(1)} %get-tuple-element.70.keep, f32[81,8,128]{2,1,0:T(8,128)S(1)} %get-tuple-element.45.noise, bf16[3,640,256]{2,1,0:T(8,128)(2,1)S(1)} %pad.8.first, bf16[3,64,2304]{2,1,0:T(8,128)(2,1)S(1)} %copy-done.3, ...), custom_call_target="tpu_custom_call" | custom-call | flops 2000000000 | bytes 4000000 | tf_op jit(solution)/shard_map/keeping/pallas_call | solution.py:335
  49.5 1.6 %collective-permute-done.8 = f16[81,8,128]{2,1,0:T(8,128)(2,1)S(1)} collective-permute-done((f16[81,8,128]{2,1,0:T(8,128)(2,1)S(1)}, f16[81,8,128]{2,1,0:T(8,128)(2,1)S(1)}, u32[]{:S(2)}, u32[]{:S(2)}) %collective-permute-start.8) | collective-permute-done | bytes 165920 | tf_op jit(solution)/shard_map/ppermute | solution.py:478
  51.1 0.2 add_select_fusion.4
  51.4 3.6 %collective-permute-start.9 = (f16[81,8,128]{2,1,0:T(8,128)(2,1)S(1)}, f16[81,8,128]{2,1,0:T(8,128)(2,1)S(1)}, u32[]{:S(2)}, u32[]{:S(2)}) collective-permute-start(f16[81,8,128]{2,1,0:T(8,128)(2,1)S(1)} %fusion.7), channel_id=1, source_target_pairs={{0,8},{4,12},{8,0},{12,4},{16,24},{20,28},{24,16},{28,20},{1,9},{5... | collective-permute-start | bytes 497672 | tf_op jit(solution)/shard_map/ppermute | solution.py:478
  55.1 3.4 %collective-permute-done.9 = f16[81,8,128]{2,1,0:T(8,128)(2,1)S(1)} collective-permute-done((f16[81,8,128]{2,1,0:T(8,128)(2,1)S(1)}, f16[81,8,128]{2,1,0:T(8,128)(2,1)S(1)}, u32[]{:S(2)}, u32[]{:S(2)}) %collective-permute-start.9) | collective-permute-done | bytes 165920 | tf_op jit(solution)/shard_map/ppermute | solution.py:478
  58.5 0.2 add_select_fusion.3
  58.9 2.5 %collective-permute-start.10 = (f16[81,8,128]{2,1,0:T(8,128)(2,1)S(1)}, f16[81,8,128]{2,1,0:T(8,128)(2,1)S(1)}, u32[]{:S(2)}, u32[]{:S(2)}) collective-permute-start(f16[81,8,128]{2,1,0:T(8,128)(2,1)S(1)} %fusion.8), channel_id=1, source_target_pairs={{0,24},{4,28},{8,16},{12,20},{16,8},{20,12},{24,0},{28,4},{1,25},{... | collective-permute-start | bytes 497672 | tf_op jit(solution)/shard_map/ppermute | solution.py:478
  61.4 6.1 %collective-permute-done.10 = f16[81,8,128]{2,1,0:T(8,128)(2,1)S(1)} collective-permute-done((f16[81,8,128]{2,1,0:T(8,128)(2,1)S(1)}, f16[81,8,128]{2,1,0:T(8,128)(2,1)S(1)}, u32[]{:S(2)}, u32[]{:S(2)}) %collective-permute-start.10) | collective-permute-done | bytes 165920 | tf_op jit(solution)/shard_map/ppermute | solution.py:478
  67.5 0.4 fusion.12
  67.9 0.2 changes.1
  68.2 0.3 collective-permute-start.11
  68.5 0.9 %collective-permute-done.11 = f32[2,8,128]{2,1,0:T(8,128)S(1)} collective-permute-done((f32[2,8,128]{2,1,0:T(8,128)S(1)}, f32[2,8,128]{2,1,0:T(8,128)S(1)}, u32[]{:S(2)}, u32[]{:S(2)}) %collective-permute-start.11) | collective-permute-done | bytes 8224 | tf_op jit(solution)/shard_map/ppermute | solution.py:539
  69.4 1.5 %collective-permute-start.12 = (f32[8,128]{1,0:T(8,128)S(1)}, f32[8,128]{1,0:T(8,128)S(1)}, u32[]{:S(2)}, u32[]{:S(2)}) collective-permute-start(f32[8,128]{1,0:T(8,128)S(1)} %slice_bitcast_fusion), channel_id=1, source_target_pairs={{0,4},{4,0},{8,12},{12,8},{16,20},{20,16},{24,28},{28,24},{1,5},{5... | collective-permute-start | bytes 12296 | tf_op jit(solution)/shard_map/ppermute | solution.py:541
  71.0 0.6 collective-permute-start.14
  71.6 1.4 %collective-permute-done.12 = f32[8,128]{1,0:T(8,128)S(1)} collective-permute-done((f32[8,128]{1,0:T(8,128)S(1)}, f32[8,128]{1,0:T(8,128)S(1)}, u32[]{:S(2)}, u32[]{:S(2)}) %collective-permute-start.12) | collective-permute-done | bytes 4128 | tf_op jit(solution)/shard_map/ppermute | solution.py:541
  73.0 2.0 %collective-permute-start.13 = (f32[8,128]{1,0:T(8,128)S(1)}, f32[8,128]{1,0:T(8,128)S(1)}, u32[]{:S(2)}, u32[]{:S(2)}) collective-permute-start(f32[8,128]{1,0:T(8,128)S(1)} %fusion.19), channel_id=1, source_target_pairs={{0,2},{1,3},{2,0},{3,1},{4,6},{5,7},{6,4},{7,5},{8,10},{9,11},{10,... | collective-permute-start | bytes 12296 | tf_op jit(solution)/shard_map/ppermute | solution.py:543
  75.0 1.6 %collective-permute-done.13 = f32[8,128]{1,0:T(8,128)S(1)} collective-permute-done((f32[8,128]{1,0:T(8,128)S(1)}, f32[8,128]{1,0:T(8,128)S(1)}, u32[]{:S(2)}, u32[]{:S(2)}) %collective-permute-start.13) | collective-permute-done | bytes 4128 | tf_op jit(solution)/shard_map/ppermute | solution.py:543
  76.6 0.7 collective-permute-done.14
  77.5 1.0 %finish.1 = f32[64,4,640]{2,1,0:T(4,128)} custom-call(f32[81,8,128]{2,1,0:T(8,128)S(1)} %multiply_select_fusion.other, f32[81,8,128]{2,1,0:T(8,128)S(1)} %get-tuple-element.68.keep, f32[81,8,128]{2,1,0:T(8,128)S(1)} %get-tuple-element.55.yours, f32[81,8,128]{2,1,0:T(8,128)S(1)} %keeping.3.mine), custom_call_target="tpu_custom_call" | custom-call | flops 8000000000 | bytes 4000000 | tf_op jit(solution)/shard_map/finish/pallas_call | solution.py:427
  78.5 0.5 slice.87
  (62 shorter events, 1.9 us)
Async XLA Ops:
  0.6 3.5 %copy-start = (f32[64,256]{1,0:T(8,128)S(1)}, f32[64,256]{1,0:T(8,128)}, u32[]{:S(2)}) copy-start(f32[64,256]{1,0:T(8,128)} %param.11) | copy-start | bytes 196612
  0.6 1.4 %copy-start.1 = (f32[1,64,4,640]{3,2,1,0:T(4,128)S(1)}, f32[1,64,4,640]{3,2,1,0:T(4,128)}, u32[]{:S(2)}) copy-start(f32[1,64,4,640]{3,2,1,0:T(4,128)} %param.6) | copy-start | bytes 1966084
  2.6 4.1 %collective-permute-start = (bf16[4,64,256]{2,1,0:T(8,128)(2,1)S(1)}, bf16[4,64,256]{2,1,0:T(8,128)(2,1)S(1)}, u32[]{:S(2)}, u32[]{:S(2)}) collective-permute-start(bf16[4,64,256]{2,1,0:T(8,128)(2,1)S(1)} %get-tuple-element.35), channel_id=1, source_target_pairs={{0,1},{1,0},{2,3},{3,2},{4,5},{5,4},{6,7},{7,6},{8,9},{9,8},{10,11... | collective-permute-start | bytes 393224 | tf_op jit(solution)/shard_map/ppermute | solution.py:518
  3.1 0.8 %copy-start.5 = (s32[1,2]{1,0:T(1,128)S(1)}, s32[1,2]{1,0:T(1,128)}, u32[]{:S(2)}) copy-start(s32[1,2]{1,0:T(1,128)} %param.8) | copy-start | bytes 28
  3.1 3.6 %collective-permute-start.1 = (bf16[4,64,256]{2,1,0:T(8,128)(2,1)S(1)}, bf16[4,64,256]{2,1,0:T(8,128)(2,1)S(1)}, u32[]{:S(2)}, u32[]{:S(2)}) collective-permute-start(bf16[4,64,256]{2,1,0:T(8,128)(2,1)S(1)} %get-tuple-element.36), channel_id=1, source_target_pairs={{1,2},{2,1},{5,6},{6,5},{9,10},{10,9},{13,14},{14,13},{17,18},{18,... | collective-permute-start | bytes 393224 | tf_op jit(solution)/shard_map/ppermute | solution.py:519
  4.3 2.4 %copy-start.2 = (f32[1,64,4,640]{3,2,1,0:T(4,128)S(1)}, f32[1,64,4,640]{3,2,1,0:T(4,128)}, u32[]{:S(2)}) copy-start(f32[1,64,4,640]{3,2,1,0:T(4,128)} %param.7) | copy-start | bytes 1966084
  4.3 2.4 %copy-start.3 = (bf16[3,64,2304]{2,1,0:T(8,128)(2,1)S(1)}, bf16[3,64,2304]{2,1,0:T(8,128)(2,1)}, u32[]{:S(2)}) copy-start(bf16[3,64,2304]{2,1,0:T(8,128)(2,1)} %second.7) | copy-start | bytes 2654212
  10.1 5.8 %collective-permute-start.2 = (f16[81,8,128]{2,1,0:T(8,128)(2,1)S(1)}, f16[81,8,128]{2,1,0:T(8,128)(2,1)S(1)}, u32[]{:S(2)}, u32[]{:S(2)}) collective-permute-start(f16[81,8,128]{2,1,0:T(8,128)(2,1)S(1)} %fusion), channel_id=1, source_target_pairs={{0,4},{4,0},{8,12},{12,8},{16,20},{20,16},{24,28},{28,24},{1,5},{5... | collective-permute-start | bytes 497672 | tf_op jit(solution)/shard_map/ppermute | solution.py:478
  16.3 5.7 %collective-permute-start.3 = (f16[81,8,128]{2,1,0:T(8,128)(2,1)S(1)}, f16[81,8,128]{2,1,0:T(8,128)(2,1)S(1)}, u32[]{:S(2)}, u32[]{:S(2)}) collective-permute-start(f16[81,8,128]{2,1,0:T(8,128)(2,1)S(1)} %fusion.1), channel_id=1, source_target_pairs={{0,8},{4,12},{8,0},{12,4},{16,24},{20,28},{24,16},{28,20},{1,9},{5... | collective-permute-start | bytes 497672 | tf_op jit(solution)/shard_map/ppermute | solution.py:478
  22.4 9.3 %collective-permute-start.4 = (f16[81,8,128]{2,1,0:T(8,128)(2,1)S(1)}, f16[81,8,128]{2,1,0:T(8,128)(2,1)S(1)}, u32[]{:S(2)}, u32[]{:S(2)}) collective-permute-start(f16[81,8,128]{2,1,0:T(8,128)(2,1)S(1)} %fusion.2), channel_id=1, source_target_pairs={{0,24},{4,28},{8,16},{12,20},{16,8},{20,12},{24,0},{28,4},{1,25},{... | collective-permute-start | bytes 497672 | tf_op jit(solution)/shard_map/ppermute | solution.py:478
  31.7 2.6 %copy-start.4 = (bf16[3,256,576]{1,2,0:T(8,128)(2,1)S(1)}, bf16[3,256,576]{1,2,0:T(8,128)(2,1)}, u32[]{:S(2)}) copy-start(bf16[3,256,576]{1,2,0:T(8,128)(2,1)} %param.9) | copy-start | bytes 2654212
  32.3 6.4 %collective-permute-start.5 = (f16[81,8,128]{2,1,0:T(8,128)(2,1)S(1)}, f16[81,8,128]{2,1,0:T(8,128)(2,1)S(1)}, u32[]{:S(2)}, u32[]{:S(2)}) collective-permute-start(f16[81,8,128]{2,1,0:T(8,128)(2,1)S(1)} %fusion.4), channel_id=1, source_target_pairs={{0,4},{4,0},{8,12},{12,8},{16,20},{20,16},{24,28},{28,24},{1,5},{5... | collective-permute-start | bytes 497672 | tf_op jit(solution)/shard_map/ppermute | solution.py:478
  39.0 3.3 %collective-permute-start.6 = (bf16[4,64,256]{2,1,0:T(8,128)(2,1)S(1)}, bf16[4,64,256]{2,1,0:T(8,128)(2,1)S(1)}, u32[]{:S(2)}, u32[]{:S(2)}) collective-permute-start(bf16[4,64,256]{2,1,0:T(8,128)(2,1)S(1)} %get-tuple-element.50), channel_id=1, source_target_pairs={{0,1},{1,0},{2,3},{3,2},{4,5},{5,4},{6,7},{7,6},{8,9},{9,8},{10,11... | collective-permute-start | bytes 393224 | tf_op jit(solution)/shard_map/ppermute | solution.py:518
  39.1 3.3 %collective-permute-start.7 = (bf16[4,64,256]{2,1,0:T(8,128)(2,1)S(1)}, bf16[4,64,256]{2,1,0:T(8,128)(2,1)S(1)}, u32[]{:S(2)}, u32[]{:S(2)}) collective-permute-start(bf16[4,64,256]{2,1,0:T(8,128)(2,1)S(1)} %get-tuple-element.51), channel_id=1, source_target_pairs={{1,2},{2,1},{5,6},{6,5},{9,10},{10,9},{13,14},{14,13},{17,18},{18,... | collective-permute-start | bytes 393224 | tf_op jit(solution)/shard_map/ppermute | solution.py:519
  45.7 5.4 %collective-permute-start.8 = (f16[81,8,128]{2,1,0:T(8,128)(2,1)S(1)}, f16[81,8,128]{2,1,0:T(8,128)(2,1)S(1)}, u32[]{:S(2)}, u32[]{:S(2)}) collective-permute-start(f16[81,8,128]{2,1,0:T(8,128)(2,1)S(1)} %fusion.6), channel_id=1, source_target_pairs={{0,4},{4,0},{8,12},{12,8},{16,20},{20,16},{24,28},{28,24},{1,5},{5... | collective-permute-start | bytes 497672 | tf_op jit(solution)/shard_map/ppermute | solution.py:478
  51.4 7.0 %collective-permute-start.9 = (f16[81,8,128]{2,1,0:T(8,128)(2,1)S(1)}, f16[81,8,128]{2,1,0:T(8,128)(2,1)S(1)}, u32[]{:S(2)}, u32[]{:S(2)}) collective-permute-start(f16[81,8,128]{2,1,0:T(8,128)(2,1)S(1)} %fusion.7), channel_id=1, source_target_pairs={{0,8},{4,12},{8,0},{12,4},{16,24},{20,28},{24,16},{28,20},{1,9},{5... | collective-permute-start | bytes 497672 | tf_op jit(solution)/shard_map/ppermute | solution.py:478
  58.9 8.6 %collective-permute-start.10 = (f16[81,8,128]{2,1,0:T(8,128)(2,1)S(1)}, f16[81,8,128]{2,1,0:T(8,128)(2,1)S(1)}, u32[]{:S(2)}, u32[]{:S(2)}) collective-permute-start(f16[81,8,128]{2,1,0:T(8,128)(2,1)S(1)} %fusion.8), channel_id=1, source_target_pairs={{0,24},{4,28},{8,16},{12,20},{16,8},{20,12},{24,0},{28,4},{1,25},{... | collective-permute-start | bytes 497672 | tf_op jit(solution)/shard_map/ppermute | solution.py:478
  68.2 1.2 %collective-permute-start.11 = (f32[2,8,128]{2,1,0:T(8,128)S(1)}, f32[2,8,128]{2,1,0:T(8,128)S(1)}, u32[]{:S(2)}, u32[]{:S(2)}) collective-permute-start(f32[2,8,128]{2,1,0:T(8,128)S(1)} %changes.1), channel_id=1, source_target_pairs={{0,1},{1,0},{2,3},{3,2},{4,5},{5,4},{6,7},{7,6},{8,9},{9,8},{10,11... | collective-permute-start | bytes 24584 | tf_op jit(solution)/shard_map/ppermute | solution.py:539
  69.4 3.6 %collective-permute-start.12 = (f32[8,128]{1,0:T(8,128)S(1)}, f32[8,128]{1,0:T(8,128)S(1)}, u32[]{:S(2)}, u32[]{:S(2)}) collective-permute-start(f32[8,128]{1,0:T(8,128)S(1)} %slice_bitcast_fusion), channel_id=1, source_target_pairs={{0,4},{4,0},{8,12},{12,8},{16,20},{20,16},{24,28},{28,24},{1,5},{5... | collective-permute-start | bytes 12296 | tf_op jit(solution)/shard_map/ppermute | solution.py:541
  71.0 6.2 %collective-permute-start.14 = (f16[81,8,128]{2,1,0:T(8,128)(2,1)S(1)}, f16[81,8,128]{2,1,0:T(8,128)(2,1)S(1)}, u32[]{:S(2)}, u32[]{:S(2)}) collective-permute-start(f16[81,8,128]{2,1,0:T(8,128)(2,1)S(1)} %fusion.10), channel_id=1, source_target_pairs={{0,4},{4,0},{8,12},{12,8},{16,20},{20,16},{24,28},{28,24},{1,5},{5... | collective-permute-start | bytes 497672 | tf_op jit(solution)/shard_map/ppermute | solution.py:478
  73.0 3.6 %collective-permute-start.13 = (f32[8,128]{1,0:T(8,128)S(1)}, f32[8,128]{1,0:T(8,128)S(1)}, u32[]{:S(2)}, u32[]{:S(2)}) collective-permute-start(f32[8,128]{1,0:T(8,128)S(1)} %fusion.19), channel_id=1, source_target_pairs={{0,2},{1,3},{2,0},{3,1},{4,6},{5,7},{6,4},{7,5},{8,10},{9,11},{10,... | collective-permute-start | bytes 12296 | tf_op jit(solution)/shard_map/ppermute | solution.py:543

commit v10 on v9

--- a/solution.py
+++ b/solution.py
@@ -315,9 +315,8 @@
     work.prepare(2, inner, outer, own, spread)
     work.edge_rows(1, spread)
     work.prepare(3, inner, outer, own, spread)
-    peaks = [work.second_conv(0, yours)]
     work.edge_rows(2, spread)
-    peaks.append(work.second_conv(1, yours))
+    peaks = [work.second_conv(0, yours), work.second_conv(1, yours)]
     work.mark(yours, peaks)
 
 

time: 80.3 us -> 80.2 us (level)
  no operation moved by 1% of the time
where the time goes in v10:
time: 80.2 us; the launch traced here: 78.9 us
  waiting for transfers between devices  28.6 us (36%)
  starting transfers between devices  25.6 us (32%)
  Pallas kernels  17.8 us (22%)
  other arithmetic  3.52 us (4%)
  local copies, waits for them, and re-layouts  2.06 us (3%)
  between operations  1.08 us (1%)
    ppermute x8, waiting for transfers between devices, exchange(): lax.ppermute(coded(half), 'step', [(i, i ^ flip) for i in range(steps)])  24.7 us
    ppermute x8, starting transfers between devices, exchange(): lax.ppermute(coded(half), 'step', [(i, i ^ flip) for i in range(steps)])  19.6 us
    pallas_call x11, Pallas kernels, call(): pl.pallas_call(kernel, out_shape=out_shape, in_specs=[WHOLE] * len(arrays...  16.9 us
    ppermute x1, starting transfers between devices, local(): lax.ppermute(total, 'space', [(i, i ^ distance) for i in range(space)])  2 us
    ppermute x2, starting transfers between devices, sweep(): outer = lax.ppermute(far, 'space', outer_pairs)  1.64 us
  transfers between devices with their start and end apart: 15, of which 11 were waited for; matrix products, arithmetic and copies ran while one was open for 1% of the time, Pallas kernels for 12%

profile of v10, /device:TPU:0, one launch (start us, length us, event | category | flops | bytes accessed | tf_op | source)
XLA Modules:
  0.0 78.9 jit_solution(14393069336796970752)
XLA Ops:
  0.7 1.3 %pad.7.first = bf16[3,640,256]{2,1,0:T(8,128)(2,1)S(1)} pad(bf16[3,576,256]{2,1,0:T(8,128)(2,1)} %bitcast.61, bf16[]{:T(256)} %constant.98.clone.1), padding=0_0x0_64x0_0 | pad | bytes 1867778 | tf_op jit(solution)/shard_map/jit(_pad)/pad | solution.py:511
  2.0 0.6 arrange.3
  2.6 0.5 collective-permute-start
  3.1 0.8 collective-permute-start.1
  4.1 0.2 fusion.56.temb
  4.3 2.4 %interior.2 = (bf16[4,480,256]{2,1,0:T(8,128)(2,1)S(1)}, bf16[4,320,384]{2,1,0:T(8,128)(2,1)S(1)}) custom-call(f32[81,8,128]{2,1,0:T(8,128)S(1)} %get-tuple-element.33.other, f32[81,8,128]{2,1,0:T(8,128)S(1)} %get-tuple-element.31.keep, bf16[3,640,256]{2,1,0:T(8,128)(2,1)S(1)} %pad.7.first, f32[1,256]{1,0:T(1,128)S(1)} %fusion.56.temb), custom_call_target="tpu_custom_call" | custom-call | flops 2000000000 | bytes 4000000 | tf_op jit(solution)/shard_map/interior/pallas_call | solution.py:334
  6.8 3.1 %sending.2 = (f32[81,8,128]{2,1,0:T(8,128)S(1)}, bf16[2,320,256]{2,1,0:T(8,128)(2,1)S(1)}, bf16[2,640,384]{2,1,0:T(8,128)(2,1)S(1)}) custom-call(f32[3,128]{1,0:T(4,128)S(1)} %pad_maximum_fusion.real, f32[81,8,128]{2,1,0:T(8,128)S(1)} %get-tuple-element.33.other, f32[81,8,128]{2,1,0:T(8,128)S(1)} %get-tuple-element.31.keep, f32[64,4,640]{2,1,0:T(4,128)S(1)} %bitcast.58, ...), custom_call_target="tpu_custom_call" | custom-call | flops 2000000000 | bytes 4000000 | tf_op jit(solution)/shard_map/sending/pallas_call | solution.py:334
  9.9 0.2 fusion
  10.1 2.5 %collective-permute-start.2 = (f16[81,8,128]{2,1,0:T(8,128)(2,1)S(1)}, f16[81,8,128]{2,1,0:T(8,128)(2,1)S(1)}, u32[]{:S(2)}, u32[]{:S(2)}) collective-permute-start(f16[81,8,128]{2,1,0:T(8,128)(2,1)S(1)} %fusion), channel_id=1, source_target_pairs={{0,4},{4,0},{8,12},{12,8},{16,20},{20,16},{24,28},{28,24},{1,5},{5... | collective-permute-start | bytes 497672 | tf_op jit(solution)/shard_map/ppermute | solution.py:477
  12.6 2.1 %keeping.2 = f32[81,8,128]{2,1,0:T(8,128)S(1)} custom-call(f32[3,128]{1,0:T(4,128)S(1)} %pad_maximum_fusion.real, f32[81,8,128]{2,1,0:T(8,128)S(1)} %get-tuple-element.31.keep, f32[64,4,640]{2,1,0:T(4,128)S(1)} %bitcast.59, bf16[3,640,256]{2,1,0:T(8,128)(2,1)S(1)} %pad.7.first, bf16[3,64,2304]{2,1,0:T(8,128)(2,1)S(1)} %copy-done.3, ...), custom_call_target="tpu_custom_call" | custom-call | flops 2000000000 | bytes 4000000 | tf_op jit(solution)/shard_map/keeping/pallas_call | solution.py:334
  14.7 1.2 %collective-permute-done.2 = f16[81,8,128]{2,1,0:T(8,128)(2,1)S(1)} collective-permute-done((f16[81,8,128]{2,1,0:T(8,128)(2,1)S(1)}, f16[81,8,128]{2,1,0:T(8,128)(2,1)S(1)}, u32[]{:S(2)}, u32[]{:S(2)}) %collective-permute-start.2) | collective-permute-done | bytes 165920 | tf_op jit(solution)/shard_map/ppermute | solution.py:477
  15.9 0.2 add_select_fusion.9
  16.3 2.1 %collective-permute-start.3 = (f16[81,8,128]{2,1,0:T(8,128)(2,1)S(1)}, f16[81,8,128]{2,1,0:T(8,128)(2,1)S(1)}, u32[]{:S(2)}, u32[]{:S(2)}) collective-permute-start(f16[81,8,128]{2,1,0:T(8,128)(2,1)S(1)} %fusion.1), channel_id=1, source_target_pairs={{0,8},{4,12},{8,0},{12,4},{16,24},{20,28},{24,16},{28,20},{1,9},{5... | collective-permute-start | bytes 497672 | tf_op jit(solution)/shard_map/ppermute | solution.py:477
  18.4 3.5 %collective-permute-done.3 = f16[81,8,128]{2,1,0:T(8,128)(2,1)S(1)} collective-permute-done((f16[81,8,128]{2,1,0:T(8,128)(2,1)S(1)}, f16[81,8,128]{2,1,0:T(8,128)(2,1)S(1)}, u32[]{:S(2)}, u32[]{:S(2)}) %collective-permute-start.3) | collective-permute-done | bytes 165920 | tf_op jit(solution)/shard_map/ppermute | solution.py:477
  22.0 0.2 add_select_fusion.8
  22.3 4.4 %collective-permute-start.4 = (f16[81,8,128]{2,1,0:T(8,128)(2,1)S(1)}, f16[81,8,128]{2,1,0:T(8,128)(2,1)S(1)}, u32[]{:S(2)}, u32[]{:S(2)}) collective-permute-start(f16[81,8,128]{2,1,0:T(8,128)(2,1)S(1)} %fusion.2), channel_id=1, source_target_pairs={{0,24},{4,28},{8,16},{12,20},{16,8},{20,12},{24,0},{28,4},{1,25},{... | collective-permute-start | bytes 497672 | tf_op jit(solution)/shard_map/ppermute | solution.py:477
  26.7 0.5 arrange.4
  27.2 4.4 %collective-permute-done.4 = f16[81,8,128]{2,1,0:T(8,128)(2,1)S(1)} collective-permute-done((f16[81,8,128]{2,1,0:T(8,128)(2,1)S(1)}, f16[81,8,128]{2,1,0:T(8,128)(2,1)S(1)}, u32[]{:S(2)}, u32[]{:S(2)}) %collective-permute-start.4) | collective-permute-done | bytes 165920 | tf_op jit(solution)/shard_map/ppermute | solution.py:477
  31.7 0.4 fusion.11
  32.3 1.9 %collective-permute-start.5 = (f16[81,8,128]{2,1,0:T(8,128)(2,1)S(1)}, f16[81,8,128]{2,1,0:T(8,128)(2,1)S(1)}, u32[]{:S(2)}, u32[]{:S(2)}) collective-permute-start(f16[81,8,128]{2,1,0:T(8,128)(2,1)S(1)} %fusion.4), channel_id=1, source_target_pairs={{0,4},{4,0},{8,12},{12,8},{16,20},{20,16},{24,28},{28,24},{1,5},{5... | collective-permute-start | bytes 497672 | tf_op jit(solution)/shard_map/ppermute | solution.py:477
  34.3 0.5 arrange.5
  34.8 3.9 %collective-permute-done.5 = f16[81,8,128]{2,1,0:T(8,128)(2,1)S(1)} collective-permute-done((f16[81,8,128]{2,1,0:T(8,128)(2,1)S(1)}, f16[81,8,128]{2,1,0:T(8,128)(2,1)S(1)}, u32[]{:S(2)}, u32[]{:S(2)}) %collective-permute-start.5) | collective-permute-done | bytes 165920 | tf_op jit(solution)/shard_map/ppermute | solution.py:477
  38.7 0.2 fusion.5.other
  39.0 0.8 %collective-permute-start.7 = (bf16[4,64,256]{2,1,0:T(8,128)(2,1)S(1)}, bf16[4,64,256]{2,1,0:T(8,128)(2,1)S(1)}, u32[]{:S(2)}, u32[]{:S(2)}) collective-permute-start(bf16[4,64,256]{2,1,0:T(8,128)(2,1)S(1)} %get-tuple-element.51), channel_id=1, source_target_pairs={{1,2},{2,1},{5,6},{6,5},{9,10},{10,9},{13,14},{14,13},{17,18},{18,... | collective-permute-start | bytes 393224 | tf_op jit(solution)/shard_map/ppermute | solution.py:518
  39.9 2.4 %interior.3 = (bf16[4,480,256]{2,1,0:T(8,128)(2,1)S(1)}, bf16[4,320,384]{2,1,0:T(8,128)(2,1)S(1)}) custom-call(f32[81,8,128]{2,1,0:T(8,128)S(1)} %fusion.5.other, f32[81,8,128]{2,1,0:T(8,128)S(1)} %get-tuple-element.70.keep, bf16[3,640,256]{2,1,0:T(8,128)(2,1)S(1)} %pad.8.first, f32[1,256]{1,0:T(1,128)S(1)} %fusion.56.temb), custom_call_target="tpu_custom_call" | custom-call | flops 2000000000 | bytes 4000000 | tf_op jit(solution)/shard_map/interior/pallas_call | solution.py:334
  42.3 3.1 %sending.3 = (f32[81,8,128]{2,1,0:T(8,128)S(1)}, bf16[2,320,256]{2,1,0:T(8,128)(2,1)S(1)}, bf16[2,640,384]{2,1,0:T(8,128)(2,1)S(1)}) custom-call(f32[3,128]{1,0:T(4,128)S(1)} %pad_maximum_fusion.real, f32[81,8,128]{2,1,0:T(8,128)S(1)} %fusion.5.other, f32[81,8,128]{2,1,0:T(8,128)S(1)} %get-tuple-element.70.keep, f32[81,8,128]{2,1,0:T(8,128)S(1)} %get-tuple-element.49.noise, ...), custom_call_target="tpu_custom_call" | custom-call | flops 2000000000 | bytes 4000000 | tf_op jit(solution)/shard_map/sending/pallas_call | solution.py:334
  45.4 0.2 fusion.6
  45.5 1.8 %collective-permute-start.8 = (f16[81,8,128]{2,1,0:T(8,128)(2,1)S(1)}, f16[81,8,128]{2,1,0:T(8,128)(2,1)S(1)}, u32[]{:S(2)}, u32[]{:S(2)}) collective-permute-start(f16[81,8,128]{2,1,0:T(8,128)(2,1)S(1)} %fusion.6), channel_id=1, source_target_pairs={{0,4},{4,0},{8,12},{12,8},{16,20},{20,16},{24,28},{28,24},{1,5},{5... | collective-permute-start | bytes 497672 | tf_op jit(solution)/shard_map/ppermute | solution.py:477
  47.3 2.0 %keeping.3.mine = f32[81,8,128]{2,1,0:T(8,128)S(1)} custom-call(f32[3,128]{1,0:T(4,128)S(1)} %pad_maximum_fusion.real, f32[81,8,128]{2,1,0:T(8,128)S(1)} %get-tuple-element.70.keep, f32[81,8,128]{2,1,0:T(8,128)S(1)} %get-tuple-element.45.noise, bf16[3,640,256]{2,1,0:T(8,128)(2,1)S(1)} %pad.8.first, bf16[3,64,2304]{2,1,0:T(8,128)(2,1)S(1)} %copy-done.3, ...), custom_call_target="tpu_custom_call" | custom-call | flops 2000000000 | bytes 4000000 | tf_op jit(solution)/shard_map/keeping/pallas_call | solution.py:334
  49.4 1.6 %collective-permute-done.8 = f16[81,8,128]{2,1,0:T(8,128)(2,1)S(1)} collective-permute-done((f16[81,8,128]{2,1,0:T(8,128)(2,1)S(1)}, f16[81,8,128]{2,1,0:T(8,128)(2,1)S(1)}, u32[]{:S(2)}, u32[]{:S(2)}) %collective-permute-start.8) | collective-permute-done | bytes 165920 | tf_op jit(solution)/shard_map/ppermute | solution.py:477
  51.0 0.2 add_select_fusion.4
  51.3 3.7 %collective-permute-start.9 = (f16[81,8,128]{2,1,0:T(8,128)(2,1)S(1)}, f16[81,8,128]{2,1,0:T(8,128)(2,1)S(1)}, u32[]{:S(2)}, u32[]{:S(2)}) collective-permute-start(f16[81,8,128]{2,1,0:T(8,128)(2,1)S(1)} %fusion.7), channel_id=1, source_target_pairs={{0,8},{4,12},{8,0},{12,4},{16,24},{20,28},{24,16},{28,20},{1,9},{5... | collective-permute-start | bytes 497672 | tf_op jit(solution)/shard_map/ppermute | solution.py:477
  55.0 3.4 %collective-permute-done.9 = f16[81,8,128]{2,1,0:T(8,128)(2,1)S(1)} collective-permute-done((f16[81,8,128]{2,1,0:T(8,128)(2,1)S(1)}, f16[81,8,128]{2,1,0:T(8,128)(2,1)S(1)}, u32[]{:S(2)}, u32[]{:S(2)}) %collective-permute-start.9) | collective-permute-done | bytes 165920 | tf_op jit(solution)/shard_map/ppermute | solution.py:477
  58.4 0.2 add_select_fusion.3
  58.8 2.6 %collective-permute-start.10 = (f16[81,8,128]{2,1,0:T(8,128)(2,1)S(1)}, f16[81,8,128]{2,1,0:T(8,128)(2,1)S(1)}, u32[]{:S(2)}, u32[]{:S(2)}) collective-permute-start(f16[81,8,128]{2,1,0:T(8,128)(2,1)S(1)} %fusion.8), channel_id=1, source_target_pairs={{0,24},{4,28},{8,16},{12,20},{16,8},{20,12},{24,0},{28,4},{1,25},{... | collective-permute-start | bytes 497672 | tf_op jit(solution)/shard_map/ppermute | solution.py:477
  61.3 6.0 %collective-permute-done.10 = f16[81,8,128]{2,1,0:T(8,128)(2,1)S(1)} collective-permute-done((f16[81,8,128]{2,1,0:T(8,128)(2,1)S(1)}, f16[81,8,128]{2,1,0:T(8,128)(2,1)S(1)}, u32[]{:S(2)}, u32[]{:S(2)}) %collective-permute-start.10) | collective-permute-done | bytes 165920 | tf_op jit(solution)/shard_map/ppermute | solution.py:477
  67.4 0.4 fusion.12
  67.8 0.2 changes.1
  68.1 0.3 collective-permute-start.11
  68.4 0.9 %collective-permute-done.11 = f32[2,8,128]{2,1,0:T(8,128)S(1)} collective-permute-done((f32[2,8,128]{2,1,0:T(8,128)S(1)}, f32[2,8,128]{2,1,0:T(8,128)S(1)}, u32[]{:S(2)}, u32[]{:S(2)}) %collective-permute-start.11) | collective-permute-done | bytes 8224 | tf_op jit(solution)/shard_map/ppermute | solution.py:538
  69.3 1.5 %collective-permute-start.12 = (f32[8,128]{1,0:T(8,128)S(1)}, f32[8,128]{1,0:T(8,128)S(1)}, u32[]{:S(2)}, u32[]{:S(2)}) collective-permute-start(f32[8,128]{1,0:T(8,128)S(1)} %slice_bitcast_fusion), channel_id=1, source_target_pairs={{0,4},{4,0},{8,12},{12,8},{16,20},{20,16},{24,28},{28,24},{1,5},{5... | collective-permute-start | bytes 12296 | tf_op jit(solution)/shard_map/ppermute | solution.py:540
  70.9 0.6 collective-permute-start.14
  71.5 1.4 %collective-permute-done.12 = f32[8,128]{1,0:T(8,128)S(1)} collective-permute-done((f32[8,128]{1,0:T(8,128)S(1)}, f32[8,128]{1,0:T(8,128)S(1)}, u32[]{:S(2)}, u32[]{:S(2)}) %collective-permute-start.12) | collective-permute-done | bytes 4128 | tf_op jit(solution)/shard_map/ppermute | solution.py:540
  72.9 2.0 %collective-permute-start.13 = (f32[8,128]{1,0:T(8,128)S(1)}, f32[8,128]{1,0:T(8,128)S(1)}, u32[]{:S(2)}, u32[]{:S(2)}) collective-permute-start(f32[8,128]{1,0:T(8,128)S(1)} %fusion.19), channel_id=1, source_target_pairs={{0,2},{1,3},{2,0},{3,1},{4,6},{5,7},{6,4},{7,5},{8,10},{9,11},{10,... | collective-permute-start | bytes 12296 | tf_op jit(solution)/shard_map/ppermute | solution.py:542
  74.9 1.6 %collective-permute-done.13 = f32[8,128]{1,0:T(8,128)S(1)} collective-permute-done((f32[8,128]{1,0:T(8,128)S(1)}, f32[8,128]{1,0:T(8,128)S(1)}, u32[]{:S(2)}, u32[]{:S(2)}) %collective-permute-start.13) | collective-permute-done | bytes 4128 | tf_op jit(solution)/shard_map/ppermute | solution.py:542
  76.5 0.7 collective-permute-done.14
  77.4 1.0 %finish.1 = f32[64,4,640]{2,1,0:T(4,128)} custom-call(f32[81,8,128]{2,1,0:T(8,128)S(1)} %multiply_select_fusion.other, f32[81,8,128]{2,1,0:T(8,128)S(1)} %get-tuple-element.68.keep, f32[81,8,128]{2,1,0:T(8,128)S(1)} %get-tuple-element.55.yours, f32[81,8,128]{2,1,0:T(8,128)S(1)} %keeping.3.mine), custom_call_target="tpu_custom_call" | custom-call | flops 8000000000 | bytes 4000000 | tf_op jit(solution)/shard_map/finish/pallas_call | solution.py:426
  78.4 0.5 slice.87
  (62 shorter events, 1.9 us)
Async XLA Ops:
  0.6 3.5 %copy-start = (f32[64,256]{1,0:T(8,128)S(1)}, f32[64,256]{1,0:T(8,128)}, u32[]{:S(2)}) copy-start(f32[64,256]{1,0:T(8,128)} %param.11) | copy-start | bytes 196612
  0.6 1.4 %copy-start.1 = (f32[1,64,4,640]{3,2,1,0:T(4,128)S(1)}, f32[1,64,4,640]{3,2,1,0:T(4,128)}, u32[]{:S(2)}) copy-start(f32[1,64,4,640]{3,2,1,0:T(4,128)} %param.6) | copy-start | bytes 1966084
  2.6 4.1 %collective-permute-start = (bf16[4,64,256]{2,1,0:T(8,128)(2,1)S(1)}, bf16[4,64,256]{2,1,0:T(8,128)(2,1)S(1)}, u32[]{:S(2)}, u32[]{:S(2)}) collective-permute-start(bf16[4,64,256]{2,1,0:T(8,128)(2,1)S(1)} %get-tuple-element.35), channel_id=1, source_target_pairs={{0,1},{1,0},{2,3},{3,2},{4,5},{5,4},{6,7},{7,6},{8,9},{9,8},{10,11... | collective-permute-start | bytes 393224 | tf_op jit(solution)/shard_map/ppermute | solution.py:517
  3.1 0.8 %copy-start.5 = (s32[1,2]{1,0:T(1,128)S(1)}, s32[1,2]{1,0:T(1,128)}, u32[]{:S(2)}) copy-start(s32[1,2]{1,0:T(1,128)} %param.8) | copy-start | bytes 28
  3.1 3.6 %collective-permute-start.1 = (bf16[4,64,256]{2,1,0:T(8,128)(2,1)S(1)}, bf16[4,64,256]{2,1,0:T(8,128)(2,1)S(1)}, u32[]{:S(2)}, u32[]{:S(2)}) collective-permute-start(bf16[4,64,256]{2,1,0:T(8,128)(2,1)S(1)} %get-tuple-element.36), channel_id=1, source_target_pairs={{1,2},{2,1},{5,6},{6,5},{9,10},{10,9},{13,14},{14,13},{17,18},{18,... | collective-permute-start | bytes 393224 | tf_op jit(solution)/shard_map/ppermute | solution.py:518
  4.3 2.4 %copy-start.2 = (f32[1,64,4,640]{3,2,1,0:T(4,128)S(1)}, f32[1,64,4,640]{3,2,1,0:T(4,128)}, u32[]{:S(2)}) copy-start(f32[1,64,4,640]{3,2,1,0:T(4,128)} %param.7) | copy-start | bytes 1966084
  4.3 2.4 %copy-start.3 = (bf16[3,64,2304]{2,1,0:T(8,128)(2,1)S(1)}, bf16[3,64,2304]{2,1,0:T(8,128)(2,1)}, u32[]{:S(2)}) copy-start(bf16[3,64,2304]{2,1,0:T(8,128)(2,1)} %second.7) | copy-start | bytes 2654212
  10.1 5.8 %collective-permute-start.2 = (f16[81,8,128]{2,1,0:T(8,128)(2,1)S(1)}, f16[81,8,128]{2,1,0:T(8,128)(2,1)S(1)}, u32[]{:S(2)}, u32[]{:S(2)}) collective-permute-start(f16[81,8,128]{2,1,0:T(8,128)(2,1)S(1)} %fusion), channel_id=1, source_target_pairs={{0,4},{4,0},{8,12},{12,8},{16,20},{20,16},{24,28},{28,24},{1,5},{5... | collective-permute-start | bytes 497672 | tf_op jit(solution)/shard_map/ppermute | solution.py:477
  16.3 5.7 %collective-permute-start.3 = (f16[81,8,128]{2,1,0:T(8,128)(2,1)S(1)}, f16[81,8,128]{2,1,0:T(8,128)(2,1)S(1)}, u32[]{:S(2)}, u32[]{:S(2)}) collective-permute-start(f16[81,8,128]{2,1,0:T(8,128)(2,1)S(1)} %fusion.1), channel_id=1, source_target_pairs={{0,8},{4,12},{8,0},{12,4},{16,24},{20,28},{24,16},{28,20},{1,9},{5... | collective-permute-start | bytes 497672 | tf_op jit(solution)/shard_map/ppermute | solution.py:477
  22.3 9.3 %collective-permute-start.4 = (f16[81,8,128]{2,1,0:T(8,128)(2,1)S(1)}, f16[81,8,128]{2,1,0:T(8,128)(2,1)S(1)}, u32[]{:S(2)}, u32[]{:S(2)}) collective-permute-start(f16[81,8,128]{2,1,0:T(8,128)(2,1)S(1)} %fusion.2), channel_id=1, source_target_pairs={{0,24},{4,28},{8,16},{12,20},{16,8},{20,12},{24,0},{28,4},{1,25},{... | collective-permute-start | bytes 497672 | tf_op jit(solution)/shard_map/ppermute | solution.py:477
  31.7 2.6 %copy-start.4 = (bf16[3,256,576]{1,2,0:T(8,128)(2,1)S(1)}, bf16[3,256,576]{1,2,0:T(8,128)(2,1)}, u32[]{:S(2)}) copy-start(bf16[3,256,576]{1,2,0:T(8,128)(2,1)} %param.9) | copy-start | bytes 2654212
  32.3 6.4 %collective-permute-start.5 = (f16[81,8,128]{2,1,0:T(8,128)(2,1)S(1)}, f16[81,8,128]{2,1,0:T(8,128)(2,1)S(1)}, u32[]{:S(2)}, u32[]{:S(2)}) collective-permute-start(f16[81,8,128]{2,1,0:T(8,128)(2,1)S(1)} %fusion.4), channel_id=1, source_target_pairs={{0,4},{4,0},{8,12},{12,8},{16,20},{20,16},{24,28},{28,24},{1,5},{5... | collective-permute-start | bytes 497672 | tf_op jit(solution)/shard_map/ppermute | solution.py:477
  38.9 3.3 %collective-permute-start.6 = (bf16[4,64,256]{2,1,0:T(8,128)(2,1)S(1)}, bf16[4,64,256]{2,1,0:T(8,128)(2,1)S(1)}, u32[]{:S(2)}, u32[]{:S(2)}) collective-permute-start(bf16[4,64,256]{2,1,0:T(8,128)(2,1)S(1)} %get-tuple-element.50), channel_id=1, source_target_pairs={{0,1},{1,0},{2,3},{3,2},{4,5},{5,4},{6,7},{7,6},{8,9},{9,8},{10,11... | collective-permute-start | bytes 393224 | tf_op jit(solution)/shard_map/ppermute | solution.py:517
  39.0 3.3 %collective-permute-start.7 = (bf16[4,64,256]{2,1,0:T(8,128)(2,1)S(1)}, bf16[4,64,256]{2,1,0:T(8,128)(2,1)S(1)}, u32[]{:S(2)}, u32[]{:S(2)}) collective-permute-start(bf16[4,64,256]{2,1,0:T(8,128)(2,1)S(1)} %get-tuple-element.51), channel_id=1, source_target_pairs={{1,2},{2,1},{5,6},{6,5},{9,10},{10,9},{13,14},{14,13},{17,18},{18,... | collective-permute-start | bytes 393224 | tf_op jit(solution)/shard_map/ppermute | solution.py:518
  45.5 5.4 %collective-permute-start.8 = (f16[81,8,128]{2,1,0:T(8,128)(2,1)S(1)}, f16[81,8,128]{2,1,0:T(8,128)(2,1)S(1)}, u32[]{:S(2)}, u32[]{:S(2)}) collective-permute-start(f16[81,8,128]{2,1,0:T(8,128)(2,1)S(1)} %fusion.6), channel_id=1, source_target_pairs={{0,4},{4,0},{8,12},{12,8},{16,20},{20,16},{24,28},{28,24},{1,5},{5... | collective-permute-start | bytes 497672 | tf_op jit(solution)/shard_map/ppermute | solution.py:477
  51.3 7.1 %collective-permute-start.9 = (f16[81,8,128]{2,1,0:T(8,128)(2,1)S(1)}, f16[81,8,128]{2,1,0:T(8,128)(2,1)S(1)}, u32[]{:S(2)}, u32[]{:S(2)}) collective-permute-start(f16[81,8,128]{2,1,0:T(8,128)(2,1)S(1)} %fusion.7), channel_id=1, source_target_pairs={{0,8},{4,12},{8,0},{12,4},{16,24},{20,28},{24,16},{28,20},{1,9},{5... | collective-permute-start | bytes 497672 | tf_op jit(solution)/shard_map/ppermute | solution.py:477
  58.8 8.6 %collective-permute-start.10 = (f16[81,8,128]{2,1,0:T(8,128)(2,1)S(1)}, f16[81,8,128]{2,1,0:T(8,128)(2,1)S(1)}, u32[]{:S(2)}, u32[]{:S(2)}) collective-permute-start(f16[81,8,128]{2,1,0:T(8,128)(2,1)S(1)} %fusion.8), channel_id=1, source_target_pairs={{0,24},{4,28},{8,16},{12,20},{16,8},{20,12},{24,0},{28,4},{1,25},{... | collective-permute-start | bytes 497672 | tf_op jit(solution)/shard_map/ppermute | solution.py:477
  68.1 1.2 %collective-permute-start.11 = (f32[2,8,128]{2,1,0:T(8,128)S(1)}, f32[2,8,128]{2,1,0:T(8,128)S(1)}, u32[]{:S(2)}, u32[]{:S(2)}) collective-permute-start(f32[2,8,128]{2,1,0:T(8,128)S(1)} %changes.1), channel_id=1, source_target_pairs={{0,1},{1,0},{2,3},{3,2},{4,5},{5,4},{6,7},{7,6},{8,9},{9,8},{10,11... | collective-permute-start | bytes 24584 | tf_op jit(solution)/shard_map/ppermute | solution.py:538
  69.3 3.6 %collective-permute-start.12 = (f32[8,128]{1,0:T(8,128)S(1)}, f32[8,128]{1,0:T(8,128)S(1)}, u32[]{:S(2)}, u32[]{:S(2)}) collective-permute-start(f32[8,128]{1,0:T(8,128)S(1)} %slice_bitcast_fusion), channel_id=1, source_target_pairs={{0,4},{4,0},{8,12},{12,8},{16,20},{20,16},{24,28},{28,24},{1,5},{5... | collective-permute-start | bytes 12296 | tf_op jit(solution)/shard_map/ppermute | solution.py:540
  70.9 6.2 %collective-permute-start.14 = (f16[81,8,128]{2,1,0:T(8,128)(2,1)S(1)}, f16[81,8,128]{2,1,0:T(8,128)(2,1)S(1)}, u32[]{:S(2)}, u32[]{:S(2)}) collective-permute-start(f16[81,8,128]{2,1,0:T(8,128)(2,1)S(1)} %fusion.10), channel_id=1, source_target_pairs={{0,4},{4,0},{8,12},{12,8},{16,20},{20,16},{24,28},{28,24},{1,5},{5... | collective-permute-start | bytes 497672 | tf_op jit(solution)/shard_map/ppermute | solution.py:477
  72.9 3.6 %collective-permute-start.13 = (f32[8,128]{1,0:T(8,128)S(1)}, f32[8,128]{1,0:T(8,128)S(1)}, u32[]{:S(2)}, u32[]{:S(2)}) collective-permute-start(f32[8,128]{1,0:T(8,128)S(1)} %fusion.19), channel_id=1, source_target_pairs={{0,2},{1,3},{2,0},{3,1},{4,6},{5,7},{6,4},{7,5},{8,10},{9,11},{10,... | collective-permute-start | bytes 12296 | tf_op jit(solution)/shard_map/ppermute | solution.py:542
